TPU v7x, 128 devices: a whole 4x4x4 slice. The times are simulated.
128 devices in a mesh: rep: 8 (over z, core), fsdp: 16 (over y, x).
Axes of the slice: x: 4, y: 4, z: 4, core: 2. Of those that a mesh axis runs over, the one named last changes fastest.
Arguments:
- gradient: bfloat16 [8, 4, 128, 13824], P('rep', None, 'fsdp'), may hold values from -6 to 6
- momentum: float32 [8, 4, 128, 13824], P('rep', None, 'fsdp'), may hold values from -6 to 6
- params: bfloat16 [4, 128, 13824], P(None, 'fsdp'), may hold values from -6 to 6
- bands: int32 [8, 4, 128, 216, 2], P('rep', None, 'fsdp'), may hold values from 0 to 7, as said below
Outputs:
- new_momentum: float32 [8, 4, 128, 13824], P('rep', None, 'fsdp')
- new_params: bfloat16 [4, 128, 13824], replicated
Inputs may be any that keep to these rules, and one draw needn't show every extreme that they name: The 2 bands of one block of one replica differ.
All inputs are finite; a program needn't handle non-finite values.
Results may differ from a plain program's by a relative error of at most 0.0059.
Values may be sent and summed in bfloat16 or wider, within the bound.
No kernel may reach another device: no remote copies, remote signals or barrier semaphores. Data moves between devices by JAX's collectives and lax.ppermute only.
A program may use at most 256 MiB of HBM per device.

v0:
```python
import math

import jax
import jax.numpy as jnp
from jax import lax
from jax.sharding import PartitionSpec as P

GROUP = 64
BANDS = 8


decay_rate = 0.9
step_size = 1.0


def cosine_table():
    freqs = jnp.arange(GROUP).astype(jnp.float32)
    samples = jnp.arange(GROUP).astype(jnp.float32)
    scales = jnp.where(freqs == 0, math.sqrt(1.0 / GROUP), math.sqrt(2.0 / GROUP))
    return scales[:, None] * jnp.cos(
        math.pi * (2.0 * samples[None, :] + 1.0) * freqs[:, None] / (2.0 * GROUP)
    )


def decode_update(values, band_ids, params, cosines, replicas):
    highest = lax.Precision.HIGHEST
    layers = params.shape[0]
    rows_here = params.shape[1]
    width = params.shape[2]
    blocks = width // GROUP
    chosen = (band_ids[..., None] == jnp.arange(BANDS)).astype(jnp.float32)
    restored = jnp.einsum("alrcsb,alrcsj->lrcbj", chosen, values, precision=highest) / replicas
    decoded = jnp.einsum(
        "lrck,kn->lrcn",
        restored.reshape(layers, rows_here, blocks, GROUP),
        cosines,
        precision=highest,
    )
    decoded = decoded.reshape(layers, rows_here, width)
    return (params.astype(jnp.float32) - step_size * decoded).astype(jnp.bfloat16)


def update_layers(gradient, momentum, params, bands, cosines):
    highest = lax.Precision.HIGHEST
    layers = params.shape[0]
    rows_here = params.shape[1]
    width = params.shape[2]
    blocks = width // GROUP
    replicas = lax.axis_size("rep")
    merged = decay_rate * momentum[0] + gradient[0].astype(jnp.float32)
    grouped = merged.reshape(layers, rows_here, blocks, GROUP)
    spectra = jnp.einsum("lrcn,kn->lrck", grouped, cosines, precision=highest)
    banded = spectra.reshape(layers, rows_here, blocks, BANDS, 8)
    own_bands = bands[0]
    chosen = (own_bands[..., None] == jnp.arange(BANDS)).astype(jnp.float32)
    picked = jnp.einsum("lrcsb,lrcbj->lrcsj", chosen, banded, precision=highest)
    kept_mask = jnp.sum(chosen, axis=3)
    remain = banded * (1.0 - kept_mask[..., None])
    new_momentum = jnp.einsum(
        "lrck,kn->lrcn",
        remain.reshape(layers, rows_here, blocks, GROUP),
        cosines,
        precision=highest,
    )
    new_momentum = new_momentum.reshape(1, layers, rows_here, width)
    all_values, all_bands = (
        lax.all_gather(picked[None].astype(jnp.bfloat16), "rep", axis=0, tiled=True).astype(
            jnp.float32
        ),
        lax.all_gather(own_bands[None], "rep", axis=0, tiled=True),
    )
    updated = decode_update(all_values, all_bands, params, cosines, replicas)
    gathered = lax.all_gather(updated, "fsdp", axis=1, tiled=True)
    return (new_momentum, gathered)


def shards(gradient, momentum, params, bands):
    cosines = cosine_table()
    layers = params.shape[0]
    results = [
        update_layers(
            gradient[:, position : position + 1],
            momentum[:, position : position + 1],
            params[position : position + 1],
            bands[:, position : position + 1],
            cosines,
        )
        for position in range(layers)
    ]
    new_momentum = jnp.concatenate([item[0] for item in results], axis=1)
    new_params = jnp.concatenate([item[1] for item in results], axis=0)
    return (new_momentum, new_params)


def solution(mesh):
    in_specs = (
        P("rep", None, "fsdp", None),
        P("rep", None, "fsdp", None),
        P(None, "fsdp", None),
        P("rep", None, "fsdp", None, None),
    )
    out_specs = (P("rep", None, "fsdp", None), P())
    return jax.shard_map(shards, mesh=mesh, in_specs=in_specs, out_specs=out_specs, check_vma=False)
```

profile of v0, /device:TPU:1, one launch (start us, length us, event | category | flops | bytes accessed | tf_op | source)
XLA Modules:
  0.0 552.4 jit_solution(12083332863728493834)
XLA Ops:
  14.2 16.3 %all_gather.45 = s32[8,1,8,216,2]{3,2,4,1,0:T(8,128)} all-gather(s32[1,1,8,216,2]{3,2,4,1,0:T(8,128)S(1)} %copy.261), channel_id=1, replica_groups=mesh['rep'=8,'fsdp'=16] {'rep'}, dimensions={0}, use_global_device_ids=true | all-gather | bytes 124416 | tf_op jit(solution)/shard_map/all_gather | solution.py:70
  30.6 13.8 %all_gather.39 = s32[8,1,8,216,2]{3,2,4,1,0:T(8,128)} all-gather(s32[1,1,8,216,2]{3,2,4,1,0:T(8,128)S(1)} %copy.259), channel_id=1, replica_groups=mesh['rep'=8,'fsdp'=16] {'rep'}, dimensions={0}, use_global_device_ids=true | all-gather | bytes 124416 | tf_op jit(solution)/shard_map/all_gather | solution.py:70
  44.4 12.7 %all_gather.42 = s32[8,1,8,216,2]{3,2,4,1,0:T(8,128)S(1)} all-gather(s32[1,1,8,216,2]{3,2,4,1,0:T(8,128)S(1)} %copy.260), channel_id=1, replica_groups=mesh['rep'=8,'fsdp'=16] {'rep'}, dimensions={0}, use_global_device_ids=true | all-gather | bytes 124416 | tf_op jit(solution)/shard_map/all_gather | solution.py:70
  57.1 13.3 %all_gather.36 = s32[8,1,8,216,2]{3,2,4,1,0:T(8,128)S(1)} all-gather(s32[1,1,8,216,2]{3,2,4,1,0:T(8,128)S(1)} %copy.258), channel_id=1, replica_groups=mesh['rep'=8,'fsdp'=16] {'rep'}, dimensions={0}, use_global_device_ids=true | all-gather | bytes 124416 | tf_op jit(solution)/shard_map/all_gather | solution.py:70
  73.6 2.3 copy.197
  75.9 2.4 copy.211
  78.3 2.9 convert_add_fusion.3
  85.6 3.9 fusion.66
  89.5 3.9 fusion.56
  95.6 3.9 fusion.52
  101.6 3.9 fusion.54
  105.6 5.2 copy.206
  110.8 9.1 %fusion.26 = bf16[8,216,2,8]{3,2,1,0:T(2,128)(2,1)} fusion(f32[8,216,8,8]{3,2,1,0:T(8,128)} %copy.206, s32[8,216,2]{2,1,0:T(8,128)} %bitcast.120), kind=kOutput, calls=%fused_computation.32 | convolution fusion | flops 2709504 | bytes 511488 | tf_op jit(solution)/shard_map/lrcsb,lrcbj->lrcsj/dot_general | solution.py:56
  119.9 2.8 copy.207
  122.7 14.6 %all-gather.2 = bf16[64,216,2,8]{1,3,2,0:T(8,128)(2,1)} all-gather(bf16[8,216,2,8]{1,3,2,0:T(8,128)(2,1)} %copy.207), channel_id=4, replica_groups=mesh['rep'=8,'fsdp'=16] {'rep'}, dimensions={0}, use_global_device_ids=true | all-gather | bytes 497664 | tf_op jit(solution)/shard_map/all_gather | solution.py:67
  137.3 6.5 %copy.208 = bf16[8,8,216,2,8]{4,0,3,2,1:T(8,128)(2,1)} copy(bf16[8,8,216,2,8]{2,4,3,1,0:T(8,128)(2,1)} %bitcast.113) | data formatting | bytes 884736 | tf_op jit(solution)/shard_map/reshape.93
  143.8 8.9 %bitcast_multiply_fusion.1 = f32[8,216,8,8]{3,2,1,0:T(8,128)} fusion(bf16[8,8,216,2,8]{4,0,3,2,1:T(8,128)(2,1)} %copy.208, s32[8,8,216,2]{0,3,2,1:T(2,128)} %copy.204), kind=kOutput, calls=%fused_computation.10 | convolution fusion | flops 3870720 | bytes 995328 | tf_op jit(solution)/shard_map/alrcsb,alrcsj->lrcbj/dot_general | solution.py:32
  152.7 5.6 %copy.209 = f32[8,216,8,8]{1,3,2,0:T(8,128)} copy(f32[8,216,8,8]{3,2,1,0:T(8,128)} %bitcast_multiply_fusion.1) | data formatting | bytes 884736 | tf_op jit(solution)/shard_map/div | solution.py:32
  158.3 3.6 fusion.38
  164.1 5.2 copy.213
  169.3 9.1 %fusion.29 = bf16[8,216,2,8]{3,2,1,0:T(2,128)(2,1)} fusion(f32[8,216,8,8]{3,2,1,0:T(8,128)} %copy.213, s32[8,216,2]{2,1,0:T(8,128)} %bitcast.119), kind=kOutput, calls=%fused_computation.33 | convolution fusion | flops 2709504 | bytes 511488 | tf_op jit(solution)/shard_map/lrcsb,lrcbj->lrcsj/dot_general | solution.py:56
  178.4 2.8 copy.214
  181.3 14.6 %all-gather.3 = bf16[64,216,2,8]{1,3,2,0:T(8,128)(2,1)} all-gather(bf16[8,216,2,8]{1,3,2,0:T(8,128)(2,1)} %copy.214), channel_id=5, replica_groups=mesh['rep'=8,'fsdp'=16] {'rep'}, dimensions={0}, use_global_device_ids=true | all-gather | bytes 497664 | tf_op jit(solution)/shard_map/all_gather | solution.py:67
  195.9 6.5 %copy.215 = bf16[8,8,216,2,8]{4,0,3,2,1:T(8,128)(2,1)} copy(bf16[8,8,216,2,8]{2,4,3,1,0:T(8,128)(2,1)} %bitcast.114) | data formatting | bytes 884736 | tf_op jit(solution)/shard_map/reshape.105
  202.4 8.9 %bitcast_multiply_fusion = f32[8,216,8,8]{3,2,1,0:T(8,128)} fusion(bf16[8,8,216,2,8]{4,0,3,2,1:T(8,128)(2,1)} %copy.215, s32[8,8,216,2]{0,3,2,1:T(2,128)} %copy.211), kind=kOutput, calls=%fused_computation.9 | convolution fusion | flops 3870720 | bytes 995328 | tf_op jit(solution)/shard_map/alrcsb,alrcsj->lrcbj/dot_general | solution.py:32
  211.2 5.6 %copy.216 = f32[8,216,8,8]{1,3,2,0:T(8,128)} copy(f32[8,216,8,8]{3,2,1,0:T(8,128)} %bitcast_multiply_fusion) | data formatting | bytes 884736 | tf_op jit(solution)/shard_map/div | solution.py:32
  216.9 3.6 fusion.36
  222.7 5.2 copy.199
  227.9 9.1 %fusion.23 = bf16[8,216,2,8]{3,2,1,0:T(2,128)(2,1)} fusion(f32[8,216,8,8]{3,2,1,0:T(8,128)} %copy.199, s32[8,216,2]{2,1,0:T(8,128)} %bitcast.118), kind=kOutput, calls=%fused_computation.31 | convolution fusion | flops 2709504 | bytes 511488 | tf_op jit(solution)/shard_map/lrcsb,lrcbj->lrcsj/dot_general | solution.py:56
  237.0 2.8 copy.200
  239.8 14.6 %all-gather.1 = bf16[64,216,2,8]{1,3,2,0:T(8,128)(2,1)} all-gather(bf16[8,216,2,8]{1,3,2,0:T(8,128)(2,1)} %copy.200), channel_id=3, replica_groups=mesh['rep'=8,'fsdp'=16] {'rep'}, dimensions={0}, use_global_device_ids=true | all-gather | bytes 497664 | tf_op jit(solution)/shard_map/all_gather | solution.py:67
  254.5 6.5 %copy.201 = bf16[8,8,216,2,8]{4,0,3,2,1:T(8,128)(2,1)} copy(bf16[8,8,216,2,8]{2,4,3,1,0:T(8,128)(2,1)} %bitcast.115) | data formatting | bytes 884736 | tf_op jit(solution)/shard_map/reshape.81
  261.0 8.3 %bitcast_multiply_fusion.2 = f32[8,216,8,8]{3,2,1,0:T(8,128)} fusion(bf16[8,8,216,2,8]{4,0,3,2,1:T(8,128)(2,1)} %copy.201, s32[8,8,216,2]{0,3,2,1:T(2,128)S(1)} %copy.197), kind=kOutput, calls=%fused_computation.11 | convolution fusion | flops 3870720 | bytes 995328 | tf_op jit(solution)/shard_map/alrcsb,alrcsj->lrcbj/dot_general | solution.py:32
  269.3 5.7 %copy.202 = f32[8,216,8,8]{1,3,2,0:T(8,128)} copy(f32[8,216,8,8]{3,2,1,0:T(8,128)} %bitcast_multiply_fusion.2) | data formatting | bytes 884736 | tf_op jit(solution)/shard_map/div | solution.py:32
  275.0 2.7 fusion.40
  278.7 4.4 copy.192
  283.1 9.0 %fusion.20 = bf16[8,216,2,8]{3,2,1,0:T(2,128)(2,1)} fusion(f32[8,216,8,8]{3,2,1,0:T(8,128)} %copy.192, s32[8,216,2]{2,1,0:T(8,128)S(1)} %bitcast.117), kind=kOutput, calls=%fused_computation.30 | convolution fusion | flops 2709504 | bytes 511488 | tf_op jit(solution)/shard_map/lrcsb,lrcbj->lrcsj/dot_general | solution.py:56
  292.1 2.2 copy.193
  294.3 13.6 %all-gather = bf16[64,216,2,8]{1,3,2,0:T(8,128)(2,1)S(1)} all-gather(bf16[8,216,2,8]{1,3,2,0:T(8,128)(2,1)S(1)} %copy.193), channel_id=2, replica_groups=mesh['rep'=8,'fsdp'=16] {'rep'}, dimensions={0}, use_global_device_ids=true | all-gather | bytes 497664 | tf_op jit(solution)/shard_map/all_gather | solution.py:67
  307.9 5.4 copy.194
  313.3 8.3 %bitcast_multiply_fusion.3 = f32[8,216,8,8]{3,2,1,0:T(8,128)} fusion(bf16[8,8,216,2,8]{4,0,3,2,1:T(8,128)(2,1)} %copy.194, s32[8,8,216,2]{0,3,2,1:T(2,128)S(1)} %copy.190), kind=kOutput, calls=%fused_computation.12 | convolution fusion | flops 3870720 | bytes 995328 | tf_op jit(solution)/shard_map/alrcsb,alrcsj->lrcbj/dot_general | solution.py:32
  321.7 5.1 copy.195
  329.4 2.8 subtract_convert_fusion.3
  344.5 37.3 %all-gather.9.cloned.1.call-done = bf16[1,128,13824]{2,1,0:T(8,128)(2,1)} async-done(((bf16[1,8,13824]{2,1,0:T(8,128)(2,1)}), bf16[1,128,13824]{2,1,0:T(8,128)(2,1)}) %all-gather.9.cloned.1.call-update) | async-done | bytes 3538960 | tf_op jit(solution)/shard_map/all_gather | solution.py:73
  381.8 50.3 %all-gather.11.cloned.1.call-done = bf16[1,128,13824]{2,1,0:T(8,128)(2,1)} async-done(((bf16[1,8,13824]{2,1,0:T(8,128)(2,1)}), bf16[1,128,13824]{2,1,0:T(8,128)(2,1)}) %all-gather.11.cloned.1.call-update) | async-done | bytes 3538960 | tf_op jit(solution)/shard_map/all_gather | solution.py:73
  432.1 50.4 %all-gather.15.cloned.1.call-done = bf16[1,128,13824]{2,1,0:T(8,128)(2,1)} async-done(((bf16[1,8,13824]{2,1,0:T(8,128)(2,1)}), bf16[1,128,13824]{2,1,0:T(8,128)(2,1)}) %all-gather.15.cloned.1.call-update) | async-done | bytes 3538960 | tf_op jit(solution)/shard_map/all_gather | solution.py:73
  482.5 50.2 %all-gather.13.cloned.1.call-done = bf16[1,128,13824]{2,1,0:T(8,128)(2,1)} async-done(((bf16[1,8,13824]{2,1,0:T(8,128)(2,1)}), bf16[1,128,13824]{2,1,0:T(8,128)(2,1)}) %all-gather.13.cloned.1.call-update) | async-done | bytes 3538960 | tf_op jit(solution)/shard_map/all_gather | solution.py:73
  532.7 13.0 %pad_maximum_fusion = bf16[4,128,13824]{2,1,0:T(8,128)(2,1)} fusion(bf16[1,128,13824]{2,1,0:T(8,128)(2,1)} %all-gather.15.cloned.1.call-done, bf16[1,128,13824]{2,1,0:T(8,128)(2,1)} %all-gather.13.cloned.1.call-done, bf16[1,128,13824]{2,1,0:T(8,128)(2,1)} %all-gather.11.cloned.1.call-done, bf16[1,128,13824]{2,1,0:T(8,128)(2,1)} %all-gather.9.cloned.1.call-done), kind=kLoop, calls=%fused_computation | loop fusion | flops 21233664 | bytes 28311552 | tf_op jit(solution)/shard_map/concatenate | solution.py:91
  (81 shorter events, 38.9 us)
Async XLA Ops:
  7.2 374.6 %all-gather.9.cloned.1.call-start = ((), (), s32[]{:S(2)}) async-start(), calls=%async_computation | async-start | bytes 3760128 | tf_op jit(solution)/shard_map/all_gather | solution.py:73
  10.4 60.0 %copy-start.6 = (s32[1,1,8,216,2]{3,2,4,1,0:T(8,128)}, s32[1,1,8,216,2]{3,2,4,1,0:T(8,128)S(1)}, u32[]{:S(2)}) copy-start(s32[1,1,8,216,2]{3,2,4,1,0:T(8,128)S(1)} %copy.259) | copy-start | bytes 41476
  11.7 58.7 %copy-start.8 = (s32[1,1,8,216,2]{3,2,4,1,0:T(8,128)}, s32[1,1,8,216,2]{3,2,4,1,0:T(8,128)S(1)}, u32[]{:S(2)}) copy-start(s32[1,1,8,216,2]{3,2,4,1,0:T(8,128)S(1)} %copy.260) | copy-start | bytes 41476
  13.0 57.5 %copy-start.10 = (s32[1,1,8,216,2]{3,2,4,1,0:T(8,128)}, s32[1,1,8,216,2]{3,2,4,1,0:T(8,128)S(1)}, u32[]{:S(2)}) copy-start(s32[1,1,8,216,2]{3,2,4,1,0:T(8,128)S(1)} %copy.258) | copy-start | bytes 41476
  269.3 5.7 %copy-start.12 = (f32[64]{0:T(128)S(1)}, f32[64]{0:T(128)}, u32[]{:S(2)}) copy-start(f32[64]{0:T(128)} %iota_convert_fusion) | copy-start | bytes 772
  269.3 5.7 %copy-start.13 = (f32[64]{0:T(128)S(1)}, f32[64]{0:T(128)}, u32[]{:S(2)}) copy-start(f32[64]{0:T(128)} %get-tuple-element.22) | copy-start | bytes 772
  269.3 5.7 %copy-start.14 = (f32[64]{0:T(128)S(1)}, f32[64]{0:T(128)}, u32[]{:S(2)}) copy-start(f32[64]{0:T(128)} %get-tuple-element.23) | copy-start | bytes 772
  269.3 9.4 %copy-start.3 = (f32[8,216,64]{1,2,0:T(8,128)S(1)}, f32[8,216,64]{1,2,0:T(8,128)}, u32[]{:S(2)}) copy-start(f32[8,216,64]{1,2,0:T(8,128)} %fusion.66) | copy-start | bytes 1327108
  278.7 4.4 copy-start.5
  321.6 12.7 %copy-start.7 = (s32[1,1,8,216,2]{3,2,4,1,0:T(8,128)S(1)}, s32[1,1,8,216,2]{3,2,4,1,0:T(8,128)}, u32[]{:S(2)}) copy-start(s32[1,1,8,216,2]{3,2,4,1,0:T(8,128)} %copy-done.6) | copy-start | bytes 41476
  321.6 12.7 %copy-start.9 = (s32[1,1,8,216,2]{3,2,4,1,0:T(8,128)S(1)}, s32[1,1,8,216,2]{3,2,4,1,0:T(8,128)}, u32[]{:S(2)}) copy-start(s32[1,1,8,216,2]{3,2,4,1,0:T(8,128)} %copy-done.8) | copy-start | bytes 41476
  321.7 12.7 %copy-start.11 = (s32[1,1,8,216,2]{3,2,4,1,0:T(8,128)S(1)}, s32[1,1,8,216,2]{3,2,4,1,0:T(8,128)}, u32[]{:S(2)}) copy-start(s32[1,1,8,216,2]{3,2,4,1,0:T(8,128)} %copy-done.10) | copy-start | bytes 41476
  326.7 10.5 %copy-start.2 = (f32[8,216,64]{1,2,0:T(8,128)S(1)}, f32[8,216,64]{1,2,0:T(8,128)}, u32[]{:S(2)}) copy-start(f32[8,216,64]{1,2,0:T(8,128)} %fusion.56) | copy-start | bytes 1327108
  326.7 12.5 %copy-start.1 = (f32[8,216,64]{1,2,0:T(8,128)S(1)}, f32[8,216,64]{1,2,0:T(8,128)}, u32[]{:S(2)}) copy-start(f32[8,216,64]{1,2,0:T(8,128)} %fusion.52) | copy-start | bytes 1327108
  329.4 11.8 %copy-start = (f32[8,216,64]{1,2,0:T(8,128)S(1)}, f32[8,216,64]{1,2,0:T(8,128)}, u32[]{:S(2)}) copy-start(f32[8,216,64]{1,2,0:T(8,128)} %fusion.54) | copy-start | bytes 1327108
  332.2 99.9 %all-gather.11.cloned.1.call-start = ((), (), s32[]{:S(2)}) async-start(), calls=%async_computation.1 | async-start | bytes 3760128 | tf_op jit(solution)/shard_map/all_gather | solution.py:73
  333.0 149.5 %all-gather.15.cloned.1.call-start = ((), (), s32[]{:S(2)}) async-start(), calls=%async_computation.3 | async-start | bytes 3760128 | tf_op jit(solution)/shard_map/all_gather | solution.py:73
  333.7 199.0 %all-gather.13.cloned.1.call-start = ((), (), s32[]{:S(2)}) async-start(), calls=%async_computation.2 | async-start | bytes 3760128 | tf_op jit(solution)/shard_map/all_gather | solution.py:73
  337.2 6.0 %copy-start.4 = (f32[1,1,8,13824]{3,2,1,0:T(8,128)S(1)}, f32[1,1,8,13824]{3,2,1,0:T(8,128)}, u32[]{:S(2)}) copy-start(f32[1,1,8,13824]{3,2,1,0:T(8,128)} %reshape.362) | copy-start | bytes 1327108
Sparse Core Ops, SparseCore 0:
  332.3 49.4 all-gather.8
  383.9 48.1 all-gather.10
  434.3 48.1 all-gather.14
  484.5 48.1 all-gather.12
where the time goes:
time: 557 us; the launch traced here: 552 us
  waiting for transfers between devices  190 us (34%)
  blocking collectives  114 us (20%)
  local copies, waits for them, and re-layouts  108 us (19%)
  matrix products  105 us (19%)
  other arithmetic  21.3 us (4%)
  between operations  14.3 us (3%)
    all_gather x4, waiting for transfers between devices, update_layers(): gathered = lax.all_gather(updated, 'fsdp', axis=1, tiled=True)  188 us
    all_gather x4, blocking collectives, update_layers(): lax.all_gather(picked[None].astype(jnp.bfloat16), 'rep', axis=0, tiled=True)  57.4 us
    all_gather x4, blocking collectives, update_layers(): lax.all_gather(own_bands[None], 'rep', axis=0, tiled=True)  56.2 us
    another operation x8, local copies, waits for them, and re-layouts  44.9 us
    dot_general x4, matrix products, update_layers(): picked = jnp.einsum('lrcsb,lrcbj->lrcsj', chosen, banded, precision=highest)  36.4 us
    dot_general x4, matrix products, decode_update(): jnp.einsum('alrcsb,alrcsj->lrcbj', chosen, values, precision=highest)  34.4 us
    div x4, local copies, waits for them, and re-layouts, decode_update(): jnp.einsum('alrcsb,alrcsj->lrcbj', chosen, values, precision=highest)  22.1 us
    dot_general x4, matrix products, update_layers(): spectra = jnp.einsum('lrcn,kn->lrck', grouped, cosines, precision=highest)  15.7 us
  transfers between devices with their start and end apart: 4, of which 4 were waited for; matrix products, arithmetic and copies ran while one was open for 2% of the time, Pallas kernels for 0%

commit v1 on v0

v1 whole, which is shorter than its diff:
```python
import math

import jax
import jax.numpy as jnp
import numpy as np
from jax import lax
from jax.experimental import pallas as pl
from jax.experimental.pallas import tpu as pltpu
from jax.sharding import PartitionSpec as P

GROUP = 64
BANDS = 8
LAYERS = 4
ROWS_HERE = 8
WIDTH = 13824
HALF = WIDTH // 2
QUARTER = HALF // 2
WIDE = 256
LANES = 128
REPS = 8

decay_rate = 0.9
step_size = 1.0
VMEM_LIMIT = 48 * 1024 * 1024


def cosine_table():
    k = np.arange(GROUP, dtype=np.float64)
    n = np.arange(GROUP, dtype=np.float64)
    scale = np.where(k == 0, math.sqrt(1.0 / GROUP), math.sqrt(2.0 / GROUP))
    return scale[:, None] * np.cos(math.pi * (2.0 * n[None, :] + 1.0) * k[:, None] / (2.0 * GROUP))


def split_table(table):
    high = jnp.asarray(table, jnp.float32).astype(jnp.bfloat16)
    low = (jnp.asarray(table, jnp.float32) - high.astype(jnp.float32)).astype(jnp.bfloat16)
    return jnp.stack([high, low])


def dot3(x, table_ref):
    high = x.astype(jnp.bfloat16)
    low = (x - high.astype(jnp.float32)).astype(jnp.bfloat16)
    total = jnp.dot(high, table_ref[1], preferred_element_type=jnp.float32)
    total += jnp.dot(low, table_ref[0], preferred_element_type=jnp.float32)
    return total + jnp.dot(high, table_ref[0], preferred_element_type=jnp.float32)


def stacked(x):
    return jnp.concatenate([x[:, at : at + WIDE] for at in range(0, x.shape[1], WIDE)], axis=0)


def merge_and_pick(bands_ref, gradient_ref, momentum_ref, forward_ref):
    merged = decay_rate * momentum_ref[0, 0] + gradient_ref[0, 0].astype(jnp.float32)
    merged = stacked(merged)
    spectra = dot3(merged, forward_ref)
    lane = lax.broadcasted_iota(jnp.int32, (ROWS_HERE, LANES), 1)
    upper = lax.shift_right_logical(lane, 6)
    band = lax.bitwise_and(lax.shift_right_logical(lane, 3), 7)
    tiles = []
    for tile in range(WIDTH // LANES):
        part = tile // 64
        index = upper + (2 * tile - LANES * part)
        first = jnp.take_along_axis(bands_ref[0, 0, :, part * LANES : (part + 1) * LANES], index, axis=1)
        second = jnp.take_along_axis(bands_ref[0, 1, :, part * LANES : (part + 1) * LANES], index, axis=1)
        row = (tile // 2) * ROWS_HERE
        column = (tile % 2) * LANES
        values = spectra[row : row + ROWS_HERE, column : column + LANES]
        tiles.append(jnp.where((first == band) | (second == band), values, 0.0))
    return merged, tiles


def pick_kernel(bands_ref, gradient_ref, momentum_ref, forward_ref, picked_ref):
    _, tiles = merge_and_pick(bands_ref, gradient_ref, momentum_ref, forward_ref)
    for tile, values in enumerate(tiles):
        side, at = divmod(tile, HALF // LANES)
        picked_ref[side, :, at * LANES : (at + 1) * LANES] = values.astype(jnp.bfloat16)


def momentum_kernel(bands_ref, gradient_ref, momentum_ref, forward_ref, inverse_ref, out_ref):
    merged, tiles = merge_and_pick(bands_ref, gradient_ref, momentum_ref, forward_ref)
    wide = [jnp.concatenate(tiles[at : at + 2], axis=1) for at in range(0, len(tiles), 2)]
    kept = merged - dot3(jnp.concatenate(wide, axis=0), inverse_ref)
    for at in range(WIDTH // WIDE):
        out_ref[0, 0, :, at * WIDE : (at + 1) * WIDE] = kept[at * ROWS_HERE : (at + 1) * ROWS_HERE]


def decode_kernel(place_ref, received_ref, params_ref, inverse_ref, out_ref):
    del place_ref
    total = received_ref[0].astype(jnp.float32)
    for replica in range(1, REPS):
        total += received_ref[replica].astype(jnp.float32)
    restored = stacked(total * (1.0 / REPS))
    restored = jnp.concatenate([restored, jnp.zeros((ROWS_HERE, WIDE), jnp.float32)], axis=0)
    decoded = dot3(restored, inverse_ref)
    for at in range(HALF // WIDE):
        before = params_ref[0, :, at * WIDE : (at + 1) * WIDE].astype(jnp.float32)
        after = before - step_size * decoded[at * ROWS_HERE : (at + 1) * ROWS_HERE]
        after = after.astype(jnp.bfloat16)
        for part in range(2):
            column = at * WIDE + part * LANES
            side, column = divmod(column, QUARTER)
            out_ref[side, :, column : column + LANES] = after[:, part * LANES : (part + 1) * LANES]


def copy_all(pairs, sems):
    copies = [pltpu.make_async_copy(src, dst, sems.at[i]) for i, (src, dst) in enumerate(pairs)]
    for copy in copies:
        copy.start()
    for copy in copies:
        copy.wait()


def bring_together(place, blocks, which, out_shapes, targets):
    def kernel(place_ref, *refs):
        ins, outs, sems = refs[: len(blocks)], refs[len(blocks) : -1], refs[-1]
        pairs = []
        for k, block in enumerate(ins):
            source = lax.rem(place_ref[which] + (4 - k), 4)
            pairs += targets(outs, block, source)
        copy_all(pairs, sems)

    count = len(blocks) * len(out_shapes)
    return pl.pallas_call(
        kernel,
        out_shape=out_shapes,
        in_specs=[pl.BlockSpec(memory_space=pltpu.SMEM)] + [pl.BlockSpec(memory_space=pl.ANY)] * len(blocks),
        out_specs=[pl.BlockSpec(memory_space=pl.ANY)] * len(out_shapes),
        scratch_shapes=[pltpu.SemaphoreType.DMA((count,))],
        cost_estimate=pl.CostEstimate(flops=0, bytes_accessed=2 * sum(b.size * 2 for b in blocks), transcendentals=0),
    )(place, *blocks)


def write_blocks(place, whole, items):
    blocks = [item[0] for item in items]

    def kernel(place_ref, *refs):
        ins, out, sems = refs[: len(blocks)], refs[-2], refs[-1]
        y, x, core = place_ref[1], place_ref[2], place_ref[3]
        pairs = []
        for block, (_, axis, first, steps, other) in zip(ins, items):
            side = core if other == 0 else 1 - core
            layers = pl.ds(first, 2)
            if axis == "y":
                column = pl.multiple_of(side * HALF, LANES)
                target = out.at[layers, lax.rem(y + (4 - steps), 4), :, :, pl.ds(column, QUARTER)]
            else:
                column = pl.multiple_of(side * HALF + QUARTER, LANES)
                target = out.at[layers, :, lax.rem(x + (4 - steps), 4), :, pl.ds(column, QUARTER)]
            pairs.append((block, target))
        copy_all(pairs, sems)

    any_space = pl.BlockSpec(memory_space=pl.ANY)
    operands = [place] + blocks
    specs = [pl.BlockSpec(memory_space=pltpu.SMEM)] + [any_space] * len(blocks)
    aliases = {}
    if whole is not None:
        aliases = {len(operands): 0}
        operands.append(whole)
        specs.append(any_space)
    return pl.pallas_call(
        kernel,
        out_shape=jax.ShapeDtypeStruct((LAYERS, 4, 4, ROWS_HERE, WIDTH), jnp.bfloat16),
        in_specs=specs,
        out_specs=any_space,
        scratch_shapes=[pltpu.SemaphoreType.DMA((len(blocks),))],
        input_output_aliases=aliases,
        cost_estimate=pl.CostEstimate(flops=0, bytes_accessed=2 * sum(b.size * 2 for b in blocks), transcendentals=0),
    )(*operands)


def shift_z(x, steps):
    return lax.ppermute(x, "rep", [(r, (r + 2 * steps) % 8) for r in range(8)])


def shift_core(x):
    return lax.ppermute(x, "rep", [(r, r ^ 1) for r in range(8)])


def shift_plane(x, axis, steps):
    pairs = []
    for y in range(4):
        for u in range(4):
            if axis == "y":
                pairs.append((y * 4 + u, (y + steps) % 4 * 4 + u))
            else:
                pairs.append((y * 4 + u, y * 4 + (u + steps) % 4))
    return lax.ppermute(x, "fsdp", pairs)


def shards(gradient, momentum, params, bands):
    rep, fsdp = lax.axis_index("rep"), lax.axis_index("fsdp")
    place = jnp.stack([rep // 2, fsdp // 4, fsdp % 4, rep % 2]).astype(jnp.int32)
    table = cosine_table()
    forward = split_table(np.kron(np.eye(WIDE // GROUP), table.T))
    inverse = split_table(np.kron(np.eye(WIDE // GROUP), table))
    blocks = WIDTH // GROUP
    by_layer = jnp.pad(jnp.transpose(bands[0], (0, 3, 1, 2)), ((0, 0), (0, 0), (0, 0), (0, WIDE - blocks)))

    row_spec = pl.BlockSpec((1, 1, ROWS_HERE, WIDTH), lambda l: (0, l, 0, 0))
    bands_spec = pl.BlockSpec((1, 2, ROWS_HERE, WIDE), lambda l: (l, 0, 0, 0))
    table_spec = pl.BlockSpec((2, WIDE, WIDE), lambda l: (0, 0, 0))
    dot_flops = 2 * 3 * LAYERS * ROWS_HERE * WIDTH * WIDE
    picked = pl.pallas_call(
        pick_kernel,
        grid=(LAYERS,),
        in_specs=[bands_spec, row_spec, row_spec, table_spec],
        out_specs=pl.BlockSpec((2, ROWS_HERE, HALF), lambda l: (l, 0, 0)),
        out_shape=jax.ShapeDtypeStruct((REPS, ROWS_HERE, HALF), jnp.bfloat16),
        compiler_params=pltpu.CompilerParams(vmem_limit_bytes=VMEM_LIMIT),
        cost_estimate=pl.CostEstimate(flops=dot_flops, bytes_accessed=4 * 1024 * 1024, transcendentals=0),
    )(by_layer, gradient, momentum, forward)
    received = lax.all_to_all(picked, "rep", 0, 0, tiled=True)

    piece = pl.pallas_call(
        decode_kernel,
        grid_spec=pltpu.PrefetchScalarGridSpec(
            num_scalar_prefetch=1,
            grid=(1,),
            in_specs=[
                pl.BlockSpec((REPS, ROWS_HERE, HALF), lambda i, at: (0, 0, 0)),
                pl.BlockSpec((1, ROWS_HERE, HALF), lambda i, at: (at[0], 0, at[3])),
                pl.BlockSpec((2, WIDE, WIDE), lambda i, at: (0, 0, 0)),
            ],
            out_specs=pl.BlockSpec((2, ROWS_HERE, QUARTER), lambda i, at: (0, 0, 0)),
        ),
        out_shape=jax.ShapeDtypeStruct((2, ROWS_HERE, QUARTER), jnp.bfloat16),
        compiler_params=pltpu.CompilerParams(vmem_limit_bytes=VMEM_LIMIT),
    )(place, received, params, inverse)

    along_z = [piece] + [shift_z(piece, k) for k in (1, 2, 3)]
    part = jax.ShapeDtypeStruct((LAYERS, ROWS_HERE, QUARTER), jnp.bfloat16)
    x_first, y_first = bring_together(
        place, along_z, 0, [part, part],
        lambda outs, block, source: [(block.at[side], outs[side].at[source]) for side in range(2)],
    )
    x_blocks = [x_first] + [shift_plane(x_first, "x", k) for k in (1, 2, 3)]
    y_blocks = [y_first] + [shift_plane(y_first, "y", k) for k in (1, 2, 3)]
    unit = jax.ShapeDtypeStruct((2, 4, ROWS_HERE, QUARTER), jnp.bfloat16)

    def by_halves(outs, block, source):
        return [(block.at[pl.ds(2 * i, 2)], outs[i].at[:, source]) for i in range(2)]

    x_units = bring_together(place, x_blocks, 2, [unit, unit], by_halves)
    y_units = bring_together(place, y_blocks, 1, [unit, unit], by_halves)

    own, near, far = [], [], []
    for axis, units in (("y", x_units), ("x", y_units)):
        for i, block in enumerate(units):
            own.append((block, axis, 2 * i, 0))
            before = shift_plane(block, axis, 1)
            after = shift_plane(block, axis, 3)
            near.append((before, axis, 2 * i, 1))
            near.append((after, axis, 2 * i, 3))
            onward = shift_plane(before, axis, 1) if i == 0 else shift_plane(after, axis, 3)
            far.append((onward, axis, 2 * i, 2))

    whole = None
    for group in (own, near, far):
        items = [item + (0,) for item in group] + [(shift_core(item[0]),) + item[1:] + (1,) for item in group]
        whole = write_blocks(place, whole, items)

    new_momentum = pl.pallas_call(
        momentum_kernel,
        grid=(LAYERS,),
        in_specs=[bands_spec, row_spec, row_spec, table_spec, table_spec],
        out_specs=row_spec,
        out_shape=jax.ShapeDtypeStruct(momentum.shape, jnp.float32),
        compiler_params=pltpu.CompilerParams(vmem_limit_bytes=VMEM_LIMIT),
        cost_estimate=pl.CostEstimate(flops=2 * dot_flops, bytes_accessed=6 * 1024 * 1024, transcendentals=0),
    )(by_layer, gradient, momentum, forward, inverse)
    return new_momentum, whole.reshape(LAYERS, 16 * ROWS_HERE, WIDTH)


def solution(mesh):
    in_specs = (
        P("rep", None, "fsdp", None),
        P("rep", None, "fsdp", None),
        P(None, "fsdp", None),
        P("rep", None, "fsdp", None, None),
    )
    out_specs = (P("rep", None, "fsdp", None), P())
    return jax.shard_map(shards, mesh=mesh, in_specs=in_specs, out_specs=out_specs, check_vma=False)
```

time: 557 us -> 628 us (1.13)
  Pallas kernels: 0 us -> 516 us
  waiting for transfers between devices: 190 us -> 48.1 us
  blocking collectives: 114 us -> 0 us
  matrix products: 105 us -> 0 us
  local copies, waits for them, and re-layouts: 108 us -> 14.6 us
  starting transfers between devices: 0.33 us -> 48.1 us
  other arithmetic: 21.3 us -> 0.08 us
  between operations: 14.3 us -> 1.14 us
    pallas_call x0 -> x9, Pallas kernels: none -> 516 us  [the longest x3 434 us: write_blocks(): pl.pallas_call(kernel, out_shape=jax.ShapeDtypeStruct((LAYERS, 4, 4, ROWS...]
    all_gather x4 -> x0, waiting for transfers between devices: 188 us -> none  [update_layers(): gathered = lax.all_gather(updated, 'fsdp', axis=1, tiled=True)]
    all_gather x8 -> x0, blocking collectives: 114 us -> none  [the longest x4 57.4 us: update_layers(): lax.all_gather(picked[None].astype(jnp.bfloat16), 'rep', axis=0, tiled=True)]
    dot_general x20 -> x0, matrix products: 105 us -> none  [the longest x4 36.4 us: update_layers(): picked = jnp.einsum('lrcsb,lrcbj->lrcsj', chosen, banded, precision=highest)]
    another operation x8 -> x0, local copies, waits for them, and re-layouts: 44.9 us -> none
    ppermute x0 -> x37, starting transfers between devices: none -> 41.3 us  [the longest x18 23.5 us: shift_plane(): return lax.ppermute(x, 'fsdp', pairs)]
    ppermute x0 -> x37, waiting for transfers between devices: none -> 34.8 us  [the longest x18 29.9 us: shift_plane(): return lax.ppermute(x, 'fsdp', pairs)]
    div x4 -> x0, local copies, waits for them, and re-layouts: 22.1 us -> none  [decode_update(): jnp.einsum('alrcsb,alrcsj->lrcbj', chosen, values, precision=highest)]
  transfers between devices with their start and end apart: 4 -> 38, of which waited for: 4 -> 11; matrix products, arithmetic and copies ran while one was open for 2% -> 0% of each run, Pallas kernels for 0% -> 62%
where the time goes in v1:
time: 628 us
  Pallas kernels  516 us (82%)
  starting transfers between devices  48.1 us (8%)
  waiting for transfers between devices  48.1 us (8%)
  local copies, waits for them, and re-layouts  14.6 us (2%)
    pallas_call x3, Pallas kernels, write_blocks(): pl.pallas_call(kernel, out_shape=jax.ShapeDtypeStruct((LAYERS, 4, 4, ROWS...  434 us
    pallas_call x3, Pallas kernels, bring_together(): pl.pallas_call(kernel, out_shape=out_shapes, in_specs=[pl.BlockSpec(memor...  72.5 us
    ppermute x18, waiting for transfers between devices, shift_plane(): return lax.ppermute(x, 'fsdp', pairs)  29.9 us
    ppermute x18, starting transfers between devices, shift_plane(): return lax.ppermute(x, 'fsdp', pairs)  23.5 us
    ppermute x16, starting transfers between devices, shift_core(): return lax.ppermute(x, 'rep', [(r, r ^ 1) for r in range(8)])  14.9 us
    unnamed x77, local copies, waits for them, and re-layouts  14.6 us
    all_to_all x1, waiting for transfers between devices, shards(): received = lax.all_to_all(picked, 'rep', 0, 0, tiled=True)  13.3 us
  transfers between devices with their start and end apart: 38, of which 11 were waited for; matrix products, arithmetic and copies ran while one was open for 0% of the time, Pallas kernels for 62%

profile of v1, /device:TPU:1, one launch (start us, length us, event | category | flops | bytes accessed | tf_op | source)
XLA Modules:
  0.0 627.7 jit_solution(9932725592346054114)
XLA Ops:
  1.5 1.5 copy-done
  3.0 1.2 copy-done.3
  4.1 0.9 copy-done.8
  5.1 3.2 shard_map.96
  8.3 6.8 %all-to-all-start = ((bf16[8,8,6912]{2,1,0:T(8,128)(2,1)}), bf16[8,8,6912]{2,1,0:T(8,128)(2,1)S(1)}, u32[]{:S(2)}, u32[]{:S(2)}) async-start(bf16[8,8,6912]{2,1,0:T(8,128)(2,1)} %shard_map.96), calls=%async_computation | async-start | bytes 1769472 | tf_op jit(solution)/shard_map/all_to_all | solution.py:212
  15.2 13.3 %all-to-all-done.received_ref = bf16[8,8,6912]{2,1,0:T(8,128)(2,1)S(1)} async-done(((bf16[8,8,6912]{2,1,0:T(8,128)(2,1)}), bf16[8,8,6912]{2,1,0:T(8,128)(2,1)S(1)}, u32[]{:S(2)}, u32[]{:S(2)}) %all-to-all-start) | async-done | bytes 884768 | tf_op jit(solution)/shard_map/all_to_all | solution.py:212
  28.5 1.2 copy-done.2
  29.6 0.9 copy-done.6
  31.8 1.8 collective-permute-start.1
  34.3 3.6 collective-permute-done.refs_1_
  37.9 1.2 collective-permute-done.2.refs_3_
  39.8 15.2 %shard_map.98 = (bf16[4,8,3456]{2,1,0:T(8,128)(2,1)}, bf16[4,8,3456]{2,1,0:T(8,128)(2,1)}) custom-call(s32[4]{0:T(128)} %copy-done.10, bf16[2,8,3456]{2,1,0:T(8,128)(2,1)} %copy-done.5, bf16[2,8,3456]{2,1,0:T(8,128)(2,1)} %copy-done.35, bf16[2,8,3456]{2,1,0:T(8,128)(2,1)} %copy-done.36, bf16[2,8,3456]{2,1,0:T(8,128)(2,1)} %copy-done.37), custom_call_target="tpu_custom_call" | custom-call | bytes 884736 | tf_op jit(solution)/shard_map/pallas_call | solution.py:123
  55.1 1.4 collective-permute-start.10
  56.4 2.6 collective-permute-start.11
  59.1 1.1 collective-permute-start.12
  60.1 1.2 collective-permute-start.3
  61.3 2.4 collective-permute-start.4
  63.8 1.2 collective-permute-start.5
  64.9 2.1 collective-permute-done.11.refs_2_
  68.5 28.6 %shard_map.100 = (bf16[2,4,8,3456]{3,2,1,0:T(8,128)(2,1)}, bf16[2,4,8,3456]{3,2,1,0:T(8,128)(2,1)}) custom-call(s32[4]{0:T(128)} %copy-done.10, bf16[4,8,3456]{2,1,0:T(8,128)(2,1)} %get-tuple-element.11.refs_0_, bf16[4,8,3456]{2,1,0:T(8,128)(2,1)} %copy-done.32, bf16[4,8,3456]{2,1,0:T(8,128)(2,1)} %copy-done.33, bf16[4,8,3456]{2,1,0:T(8,128)(2,1)} %copy-done.34), custom_call_target="tpu_custom_call" | custom-call | bytes 1769472 | tf_op jit(solution)/shard_map/pallas_call | solution.py:123
  97.1 3.4 collective-permute-start.35
  102.1 28.6 %shard_map.99 = (bf16[2,4,8,3456]{3,2,1,0:T(8,128)(2,1)}, bf16[2,4,8,3456]{3,2,1,0:T(8,128)(2,1)}) custom-call(s32[4]{0:T(128)} %copy-done.10, bf16[4,8,3456]{2,1,0:T(8,128)(2,1)} %get-tuple-element.8.refs_0_, bf16[4,8,3456]{2,1,0:T(8,128)(2,1)} %copy-done.29, bf16[4,8,3456]{2,1,0:T(8,128)(2,1)} %copy-done.30, bf16[4,8,3456]{2,1,0:T(8,128)(2,1)} %copy-done.31), custom_call_target="tpu_custom_call" | custom-call | bytes 1769472 | tf_op jit(solution)/shard_map/pallas_call | solution.py:123
  131.3 1.2 collective-permute-start.13
  132.5 1.5 collective-permute-start.23
  134.0 2.7 collective-permute-start.15
  136.9 7.1 %collective-permute-done.13.refs_4_ = bf16[2,4,8,3456]{3,2,1,0:T(8,128)(2,1)S(1)} collective-permute-done((bf16[2,4,8,3456]{3,2,1,0:T(8,128)(2,1)}, bf16[2,4,8,3456]{3,2,1,0:T(8,128)(2,1)S(1)}, u32[]{:S(2)}, u32[]{:S(2)}) %collective-permute-start.13) | collective-permute-done | bytes 442400 | tf_op jit(solution)/shard_map/ppermute | solution.py:187
  144.1 1.2 collective-permute-start.21
  145.5 8.0 %collective-permute-done.24.refs_6_ = bf16[2,4,8,3456]{3,2,1,0:T(8,128)(2,1)S(1)} collective-permute-done((bf16[2,4,8,3456]{3,2,1,0:T(8,128)(2,1)}, bf16[2,4,8,3456]{3,2,1,0:T(8,128)(2,1)S(1)}, u32[]{:S(2)}, u32[]{:S(2)}) %collective-permute-start.24) | collective-permute-done | bytes 442400 | tf_op jit(solution)/shard_map/ppermute | solution.py:187
  153.5 1.2 collective-permute-start.8
  154.7 1.5 collective-permute-start.29
  156.8 0.9 collective-permute-done.22.refs_2_
  157.8 2.4 collective-permute-start.32
  160.2 4.1 collective-permute-done.8.refs_3_
  164.3 2.2 collective-permute-start.25
  167.0 2.7 collective-permute-start.16
  169.9 2.4 collective-permute-start.9
  172.4 1.2 collective-permute-start.28
  173.6 6.4 %collective-permute-done.14.refs_2_ = bf16[2,4,8,3456]{3,2,1,0:T(8,128)(2,1)} collective-permute-done((bf16[2,4,8,3456]{3,2,1,0:T(8,128)(2,1)S(1)}, bf16[2,4,8,3456]{3,2,1,0:T(8,128)(2,1)}, u32[]{:S(2)}, u32[]{:S(2)}) %collective-permute-start.14) | collective-permute-done | bytes 442400 | tf_op jit(solution)/shard_map/ppermute | solution.py:187
  180.9 1.2 collective-permute-done.7.refs_0_
  182.1 1.5 collective-permute-start.17
  183.8 1.5 copy-done.1
  185.2 1.2 copy-done.4
  186.4 0.9 copy-done.7
  187.4 0.9 copy-done.9
  188.3 4.6 shard_map.95
  193.0 109.0 %shard_map.101.refs_16_ = bf16[4,4,4,8,13824]{4,3,2,1,0:T(8,128)(2,1)} custom-call(s32[4]{0:T(128)} %copy-done.10, bf16[2,4,8,3456]{3,2,1,0:T(8,128)(2,1)} %get-tuple-element.9.refs_0_, bf16[2,4,8,3456]{3,2,1,0:T(8,128)(2,1)} %get-tuple-element.10.refs_1_, bf16[2,4,8,3456]{3,2,1,0:T(8,128)(2,1)} %get-tuple-element.12.refs_2_, ...), custom_call_target="tpu_custom_call" | custom-call | bytes 7077888 | tf_op jit(solution)/shard_map/pallas_call | solution.py:160
  302.1 216.3 %shard_map.102.refs_8_ = bf16[4,4,4,8,13824]{4,3,2,1,0:T(8,128)(2,1)} custom-call(s32[4]{0:T(128)} %copy-done.10, bf16[2,4,8,3456]{3,2,1,0:T(8,128)(2,1)} %copy-done.19, bf16[2,4,8,3456]{3,2,1,0:T(8,128)(2,1)} %copy-done.20, bf16[2,4,8,3456]{3,2,1,0:T(8,128)(2,1)} %copy-done.21, ...), custom_call_target="tpu_custom_call", output_to_operand_aliasing={{}: (17, {})} | custom-call | bytes 14155776 | tf_op jit(solution)/shard_map/pallas_call | solution.py:160
  518.5 109.1 %shard_map.103 = bf16[4,4,4,8,13824]{4,3,2,1,0:T(8,128)(2,1)} custom-call(s32[4]{0:T(128)} %copy-done.10, bf16[2,4,8,3456]{3,2,1,0:T(8,128)(2,1)} %collective-permute-done.7.refs_0_, bf16[2,4,8,3456]{3,2,1,0:T(8,128)(2,1)} %collective-permute-done.9.refs_1_, bf16[2,4,8,3456]{3,2,1,0:T(8,128)(2,1)} %collective-permute-done.14.refs_2_, ...), custom_call_target="tpu_custom_call", output_to_operand_aliasing={{}: (9, {})} | custom-call | bytes 7077888 | tf_op jit(solution)/shard_map/pallas_call | solution.py:160
  (116 shorter events, 10.1 us)
Async XLA Ops:
  8.3 20.2 %all-to-all-start = ((bf16[8,8,6912]{2,1,0:T(8,128)(2,1)}), bf16[8,8,6912]{2,1,0:T(8,128)(2,1)S(1)}, u32[]{:S(2)}, u32[]{:S(2)}) async-start(bf16[8,8,6912]{2,1,0:T(8,128)(2,1)} %shard_map.96), calls=%async_computation | async-start | bytes 1769472 | tf_op jit(solution)/shard_map/all_to_all | solution.py:212
  31.4 6.4 %collective-permute-start = (bf16[2,8,3456]{2,1,0:T(8,128)(2,1)S(1)}, bf16[2,8,3456]{2,1,0:T(8,128)(2,1)S(1)}, u32[]{:S(2)}, u32[]{:S(2)}) collective-permute-start(bf16[2,8,3456]{2,1,0:T(8,128)(2,1)S(1)} %shard_map.97.refs_0_), channel_id=1, source_target_pairs={{0,32},{16,48},{32,64},{48,80},{64,96},{80,112},{96,0},{112,16},{1... | collective-permute-start | bytes 331784 | tf_op jit(solution)/shard_map/ppermute | solution.py:172
  31.8 6.1 collective-permute-start.1
  33.6 5.6 collective-permute-start.2
  55.1 8.7 %collective-permute-start.10 = (bf16[4,8,3456]{2,1,0:T(8,128)(2,1)}, bf16[4,8,3456]{2,1,0:T(8,128)(2,1)S(1)}, u32[]{:S(2)}, u32[]{:S(2)}) collective-permute-start(bf16[4,8,3456]{2,1,0:T(8,128)(2,1)} %get-tuple-element.11.refs_0_), channel_id=1, source_target_pairs={{0,4},{1,5},{2,6},{3,7},{4,8},{5,9},{6,10},{7,11},{8,12},{9,13},{1... | collective-permute-start | bytes 663560 | tf_op jit(solution)/shard_map/ppermute | solution.py:187
  56.4 10.6 %collective-permute-start.11 = (bf16[4,8,3456]{2,1,0:T(8,128)(2,1)}, bf16[4,8,3456]{2,1,0:T(8,128)(2,1)S(1)}, u32[]{:S(2)}, u32[]{:S(2)}) collective-permute-start(bf16[4,8,3456]{2,1,0:T(8,128)(2,1)} %get-tuple-element.11.refs_0_), channel_id=1, source_target_pairs={{0,8},{1,9},{2,10},{3,11},{4,12},{5,13},{6,14},{7,15},{8,0},{9,1},... | collective-permute-start | bytes 663560 | tf_op jit(solution)/shard_map/ppermute | solution.py:187
  59.1 8.0 %collective-permute-start.12 = (bf16[4,8,3456]{2,1,0:T(8,128)(2,1)}, bf16[4,8,3456]{2,1,0:T(8,128)(2,1)S(1)}, u32[]{:S(2)}, u32[]{:S(2)}) collective-permute-start(bf16[4,8,3456]{2,1,0:T(8,128)(2,1)} %get-tuple-element.11.refs_0_), channel_id=1, source_target_pairs={{0,12},{1,13},{2,14},{3,15},{4,0},{5,1},{6,2},{7,3},{8,4},{9,5},{1... | collective-permute-start | bytes 663560 | tf_op jit(solution)/shard_map/ppermute | solution.py:187
  60.1 40.5 %collective-permute-start.3 = (bf16[4,8,3456]{2,1,0:T(8,128)(2,1)}, bf16[4,8,3456]{2,1,0:T(8,128)(2,1)S(1)}, u32[]{:S(2)}, u32[]{:S(2)}) collective-permute-start(bf16[4,8,3456]{2,1,0:T(8,128)(2,1)} %get-tuple-element.8.refs_0_), channel_id=1, source_target_pairs={{0,1},{1,2},{2,3},{3,0},{4,5},{5,6},{6,7},{7,4},{8,9},{9,10},{10,1... | collective-permute-start | bytes 663560 | tf_op jit(solution)/shard_map/ppermute | solution.py:187
  61.3 39.3 %collective-permute-start.4 = (bf16[4,8,3456]{2,1,0:T(8,128)(2,1)}, bf16[4,8,3456]{2,1,0:T(8,128)(2,1)S(1)}, u32[]{:S(2)}, u32[]{:S(2)}) collective-permute-start(bf16[4,8,3456]{2,1,0:T(8,128)(2,1)} %get-tuple-element.8.refs_0_), channel_id=1, source_target_pairs={{0,2},{1,3},{2,0},{3,1},{4,6},{5,7},{6,4},{7,5},{8,10},{9,11},{10,... | collective-permute-start | bytes 663560 | tf_op jit(solution)/shard_map/ppermute | solution.py:187
  63.8 36.8 %collective-permute-start.5 = (bf16[4,8,3456]{2,1,0:T(8,128)(2,1)}, bf16[4,8,3456]{2,1,0:T(8,128)(2,1)S(1)}, u32[]{:S(2)}, u32[]{:S(2)}) collective-permute-start(bf16[4,8,3456]{2,1,0:T(8,128)(2,1)} %get-tuple-element.8.refs_0_), channel_id=1, source_target_pairs={{0,3},{1,0},{2,1},{3,2},{4,7},{5,4},{6,5},{7,6},{8,11},{9,8},{10,9... | collective-permute-start | bytes 663560 | tf_op jit(solution)/shard_map/ppermute | solution.py:187
  97.1 35.4 %collective-permute-start.35 = (bf16[2,4,8,3456]{3,2,1,0:T(8,128)(2,1)}, bf16[2,4,8,3456]{3,2,1,0:T(8,128)(2,1)S(1)}, u32[]{:S(2)}, u32[]{:S(2)}) collective-permute-start(bf16[2,4,8,3456]{3,2,1,0:T(8,128)(2,1)} %get-tuple-element.12.refs_2_), channel_id=1, source_target_pairs={{0,16},{16,0},{32,48},{48,32},{64,80},{80,64},{96,112},{112,96},{1... | collective-permute-start | bytes 1327112 | tf_op jit(solution)/shard_map/ppermute | solution.py:176
  100.5 33.5 %collective-permute-start.36 = (bf16[2,4,8,3456]{3,2,1,0:T(8,128)(2,1)}, bf16[2,4,8,3456]{3,2,1,0:T(8,128)(2,1)S(1)}, u32[]{:S(2)}, u32[]{:S(2)}) collective-permute-start(bf16[2,4,8,3456]{3,2,1,0:T(8,128)(2,1)} %get-tuple-element.13.refs_3_), channel_id=1, source_target_pairs={{0,16},{16,0},{32,48},{48,32},{64,80},{80,64},{96,112},{112,96},{1... | collective-permute-start | bytes 1327112 | tf_op jit(solution)/shard_map/ppermute | solution.py:176
  130.7 3.3 collective-permute-start.33
  131.2 5.5 collective-permute-start.34
  131.3 12.7 %collective-permute-start.13 = (bf16[2,4,8,3456]{3,2,1,0:T(8,128)(2,1)}, bf16[2,4,8,3456]{3,2,1,0:T(8,128)(2,1)S(1)}, u32[]{:S(2)}, u32[]{:S(2)}) collective-permute-start(bf16[2,4,8,3456]{3,2,1,0:T(8,128)(2,1)} %get-tuple-element.12.refs_2_), channel_id=1, source_target_pairs={{0,1},{1,2},{2,3},{3,0},{4,5},{5,6},{6,7},{7,4},{8,9},{9,10},{10,1... | collective-permute-start | bytes 1327112 | tf_op jit(solution)/shard_map/ppermute | solution.py:187
  132.5 60.4 %copy-start.11 = (bf16[2,4,8,3456]{3,2,1,0:T(8,128)(2,1)}, bf16[2,4,8,3456]{3,2,1,0:T(8,128)(2,1)S(1)}, u32[]{:S(2)}) copy-start(bf16[2,4,8,3456]{3,2,1,0:T(8,128)(2,1)S(1)} %collective-permute-done.35.refs_6_) | copy-start | bytes 1327108
  132.5 12.7 %collective-permute-start.23 = (bf16[2,4,8,3456]{3,2,1,0:T(8,128)(2,1)}, bf16[2,4,8,3456]{3,2,1,0:T(8,128)(2,1)S(1)}, u32[]{:S(2)}, u32[]{:S(2)}) collective-permute-start(bf16[2,4,8,3456]{3,2,1,0:T(8,128)(2,1)} %get-tuple-element.12.refs_2_), channel_id=1, source_target_pairs={{0,3},{1,0},{2,1},{3,2},{4,7},{5,4},{6,5},{7,6},{8,11},{9,8},{10,9... | collective-permute-start | bytes 1327112 | tf_op jit(solution)/shard_map/ppermute | solution.py:187
  134.0 59.0 %copy-start.12 = (bf16[2,4,8,3456]{3,2,1,0:T(8,128)(2,1)}, bf16[2,4,8,3456]{3,2,1,0:T(8,128)(2,1)S(1)}, u32[]{:S(2)}) copy-start(bf16[2,4,8,3456]{3,2,1,0:T(8,128)(2,1)S(1)} %collective-permute-done.36.refs_7_) | copy-start | bytes 1327108
  134.0 19.5 %collective-permute-start.24 = (bf16[2,4,8,3456]{3,2,1,0:T(8,128)(2,1)}, bf16[2,4,8,3456]{3,2,1,0:T(8,128)(2,1)S(1)}, u32[]{:S(2)}, u32[]{:S(2)}) collective-permute-start(bf16[2,4,8,3456]{3,2,1,0:T(8,128)(2,1)} %get-tuple-element.13.refs_3_), channel_id=1, source_target_pairs={{0,1},{1,2},{2,3},{3,0},{4,5},{5,6},{6,7},{7,4},{8,9},{9,10},{10,1... | collective-permute-start | bytes 1327112 | tf_op jit(solution)/shard_map/ppermute | solution.py:187
  134.0 59.0 %copy-start.13 = (bf16[2,4,8,3456]{3,2,1,0:T(8,128)(2,1)}, bf16[2,4,8,3456]{3,2,1,0:T(8,128)(2,1)S(1)}, u32[]{:S(2)}) copy-start(bf16[2,4,8,3456]{3,2,1,0:T(8,128)(2,1)S(1)} %collective-permute-done.33.refs_4_) | copy-start | bytes 1327108
  134.0 20.7 %collective-permute-start.15 = (bf16[2,4,8,3456]{3,2,1,0:T(8,128)(2,1)}, bf16[2,4,8,3456]{3,2,1,0:T(8,128)(2,1)S(1)}, u32[]{:S(2)}, u32[]{:S(2)}) collective-permute-start(bf16[2,4,8,3456]{3,2,1,0:T(8,128)(2,1)} %get-tuple-element.13.refs_3_), channel_id=1, source_target_pairs={{0,3},{1,0},{2,1},{3,2},{4,7},{5,4},{6,5},{7,6},{8,11},{9,8},{10,9... | collective-permute-start | bytes 1327112 | tf_op jit(solution)/shard_map/ppermute | solution.py:187
  136.7 56.3 %copy-start.15 = (bf16[2,4,8,3456]{3,2,1,0:T(8,128)(2,1)}, bf16[2,4,8,3456]{3,2,1,0:T(8,128)(2,1)S(1)}, u32[]{:S(2)}) copy-start(bf16[2,4,8,3456]{3,2,1,0:T(8,128)(2,1)S(1)} %collective-permute-done.34.refs_5_) | copy-start | bytes 1327108
  136.7 19.6 %collective-permute-start.6 = (bf16[2,4,8,3456]{3,2,1,0:T(8,128)(2,1)}, bf16[2,4,8,3456]{3,2,1,0:T(8,128)(2,1)S(1)}, u32[]{:S(2)}, u32[]{:S(2)}) collective-permute-start(bf16[2,4,8,3456]{3,2,1,0:T(8,128)(2,1)} %get-tuple-element.9.refs_0_), channel_id=1, source_target_pairs={{0,4},{1,5},{2,6},{3,7},{4,8},{5,9},{6,10},{7,11},{8,12},{9,13},{1... | collective-permute-start | bytes 1327112 | tf_op jit(solution)/shard_map/ppermute | solution.py:187
  144.0 158.0 %copy-start.14 = (bf16[2,4,8,3456]{3,2,1,0:T(8,128)(2,1)}, bf16[2,4,8,3456]{3,2,1,0:T(8,128)(2,1)S(1)}, u32[]{:S(2)}) copy-start(bf16[2,4,8,3456]{3,2,1,0:T(8,128)(2,1)S(1)} %collective-permute-done.13.refs_4_) | copy-start | bytes 1327108
  144.1 12.3 %collective-permute-start.21 = (bf16[2,4,8,3456]{3,2,1,0:T(8,128)(2,1)}, bf16[2,4,8,3456]{3,2,1,0:T(8,128)(2,1)S(1)}, u32[]{:S(2)}, u32[]{:S(2)}) collective-permute-start(bf16[2,4,8,3456]{3,2,1,0:T(8,128)(2,1)} %get-tuple-element.9.refs_0_), channel_id=1, source_target_pairs={{0,12},{1,13},{2,14},{3,15},{4,0},{5,1},{6,2},{7,3},{8,4},{9,5},{1... | collective-permute-start | bytes 1327112 | tf_op jit(solution)/shard_map/ppermute | solution.py:187
  145.2 156.8 %copy-start.16 = (bf16[2,4,8,3456]{3,2,1,0:T(8,128)(2,1)}, bf16[2,4,8,3456]{3,2,1,0:T(8,128)(2,1)S(1)}, u32[]{:S(2)}) copy-start(bf16[2,4,8,3456]{3,2,1,0:T(8,128)(2,1)S(1)} %collective-permute-done.23.refs_5_) | copy-start | bytes 1327108
  145.2 12.5 %collective-permute-start.22 = (bf16[2,4,8,3456]{3,2,1,0:T(8,128)(2,1)}, bf16[2,4,8,3456]{3,2,1,0:T(8,128)(2,1)S(1)}, u32[]{:S(2)}, u32[]{:S(2)}) collective-permute-start(bf16[2,4,8,3456]{3,2,1,0:T(8,128)(2,1)} %get-tuple-element.10.refs_1_), channel_id=1, source_target_pairs={{0,4},{1,5},{2,6},{3,7},{4,8},{5,9},{6,10},{7,11},{8,12},{9,13},{1... | collective-permute-start | bytes 1327112 | tf_op jit(solution)/shard_map/ppermute | solution.py:187
  153.5 148.5 %copy-start.17 = (bf16[2,4,8,3456]{3,2,1,0:T(8,128)(2,1)}, bf16[2,4,8,3456]{3,2,1,0:T(8,128)(2,1)S(1)}, u32[]{:S(2)}) copy-start(bf16[2,4,8,3456]{3,2,1,0:T(8,128)(2,1)S(1)} %collective-permute-done.24.refs_6_) | copy-start | bytes 1327108
  153.5 10.7 %collective-permute-start.8 = (bf16[2,4,8,3456]{3,2,1,0:T(8,128)(2,1)}, bf16[2,4,8,3456]{3,2,1,0:T(8,128)(2,1)}, u32[]{:S(2)}, u32[]{:S(2)}) collective-permute-start(bf16[2,4,8,3456]{3,2,1,0:T(8,128)(2,1)} %get-tuple-element.10.refs_1_), channel_id=1, source_target_pairs={{0,12},{1,13},{2,14},{3,15},{4,0},{5,1},{6,2},{7,3},{8,4},{9,5},{1... | collective-permute-start | bytes 1327112 | tf_op jit(solution)/shard_map/ppermute | solution.py:187
  154.7 28.8 %copy-start.18 = (bf16[2,4,8,3456]{3,2,1,0:T(8,128)(2,1)}, bf16[2,4,8,3456]{3,2,1,0:T(8,128)(2,1)S(1)}, u32[]{:S(2)}) copy-start(bf16[2,4,8,3456]{3,2,1,0:T(8,128)(2,1)S(1)} %collective-permute-done.15.refs_7_) | copy-start | bytes 1327108
  154.7 11.7 %collective-permute-start.29 = (bf16[2,4,8,3456]{3,2,1,0:T(8,128)(2,1)S(1)}, bf16[2,4,8,3456]{3,2,1,0:T(8,128)(2,1)S(1)}, u32[]{:S(2)}, u32[]{:S(2)}) collective-permute-start(bf16[2,4,8,3456]{3,2,1,0:T(8,128)(2,1)S(1)} %collective-permute-done.13.refs_4_), channel_id=1, source_target_pairs={{0,16},{16,0},{32,48},{48,32},{64,80},{80,64},{96,112},{112,96},{1... | collective-permute-start | bytes 1327112 | tf_op jit(solution)/shard_map/ppermute | solution.py:176
  156.3 27.3 %copy-start.19 = (bf16[2,4,8,3456]{3,2,1,0:T(8,128)(2,1)}, bf16[2,4,8,3456]{3,2,1,0:T(8,128)(2,1)S(1)}, u32[]{:S(2)}) copy-start(bf16[2,4,8,3456]{3,2,1,0:T(8,128)(2,1)S(1)} %collective-permute-done.6.refs_0_) | copy-start | bytes 1327108
  156.3 10.3 %collective-permute-start.30 = (bf16[2,4,8,3456]{3,2,1,0:T(8,128)(2,1)S(1)}, bf16[2,4,8,3456]{3,2,1,0:T(8,128)(2,1)S(1)}, u32[]{:S(2)}, u32[]{:S(2)}) collective-permute-start(bf16[2,4,8,3456]{3,2,1,0:T(8,128)(2,1)S(1)} %collective-permute-done.23.refs_5_), channel_id=1, source_target_pairs={{0,16},{16,0},{32,48},{48,32},{64,80},{80,64},{96,112},{112,96},{1... | collective-permute-start | bytes 1327112 | tf_op jit(solution)/shard_map/ppermute | solution.py:176
  156.4 27.2 %copy-start.20 = (bf16[2,4,8,3456]{3,2,1,0:T(8,128)(2,1)}, bf16[2,4,8,3456]{3,2,1,0:T(8,128)(2,1)S(1)}, u32[]{:S(2)}) copy-start(bf16[2,4,8,3456]{3,2,1,0:T(8,128)(2,1)S(1)} %collective-permute-done.21.refs_1_) | copy-start | bytes 1327108
  156.4 10.6 %collective-permute-start.31 = (bf16[2,4,8,3456]{3,2,1,0:T(8,128)(2,1)S(1)}, bf16[2,4,8,3456]{3,2,1,0:T(8,128)(2,1)S(1)}, u32[]{:S(2)}, u32[]{:S(2)}) collective-permute-start(bf16[2,4,8,3456]{3,2,1,0:T(8,128)(2,1)S(1)} %collective-permute-done.24.refs_6_), channel_id=1, source_target_pairs={{0,16},{16,0},{32,48},{48,32},{64,80},{80,64},{96,112},{112,96},{1... | collective-permute-start | bytes 1327112 | tf_op jit(solution)/shard_map/ppermute | solution.py:176
  157.8 9.2 %collective-permute-start.32 = (bf16[2,4,8,3456]{3,2,1,0:T(8,128)(2,1)S(1)}, bf16[2,4,8,3456]{3,2,1,0:T(8,128)(2,1)S(1)}, u32[]{:S(2)}, u32[]{:S(2)}) collective-permute-start(bf16[2,4,8,3456]{3,2,1,0:T(8,128)(2,1)S(1)} %collective-permute-done.15.refs_7_), channel_id=1, source_target_pairs={{0,16},{16,0},{32,48},{48,32},{64,80},{80,64},{96,112},{112,96},{1... | collective-permute-start | bytes 1327112 | tf_op jit(solution)/shard_map/ppermute | solution.py:176
  164.3 5.4 collective-permute-start.25
  166.4 3.5 collective-permute-start.26
  166.5 5.8 collective-permute-start.27
  167.0 13.0 %collective-permute-start.14 = (bf16[2,4,8,3456]{3,2,1,0:T(8,128)(2,1)S(1)}, bf16[2,4,8,3456]{3,2,1,0:T(8,128)(2,1)}, u32[]{:S(2)}, u32[]{:S(2)}) collective-permute-start(bf16[2,4,8,3456]{3,2,1,0:T(8,128)(2,1)S(1)} %collective-permute-done.13.refs_4_), channel_id=1, source_target_pairs={{0,1},{1,2},{2,3},{3,0},{4,5},{5,6},{6,7},{7,4},{8,9},{9,10},{10,1... | collective-permute-start | bytes 1327112 | tf_op jit(solution)/shard_map/ppermute | solution.py:187
  167.0 13.9 %collective-permute-start.16 = (bf16[2,4,8,3456]{3,2,1,0:T(8,128)(2,1)S(1)}, bf16[2,4,8,3456]{3,2,1,0:T(8,128)(2,1)}, u32[]{:S(2)}, u32[]{:S(2)}) collective-permute-start(bf16[2,4,8,3456]{3,2,1,0:T(8,128)(2,1)S(1)} %collective-permute-done.15.refs_7_), channel_id=1, source_target_pairs={{0,3},{1,0},{2,1},{3,2},{4,7},{5,4},{6,5},{7,6},{8,11},{9,8},{10,9... | collective-permute-start | bytes 1327112 | tf_op jit(solution)/shard_map/ppermute | solution.py:187
  169.7 12.4 %collective-permute-start.7 = (bf16[2,4,8,3456]{3,2,1,0:T(8,128)(2,1)S(1)}, bf16[2,4,8,3456]{3,2,1,0:T(8,128)(2,1)}, u32[]{:S(2)}, u32[]{:S(2)}) collective-permute-start(bf16[2,4,8,3456]{3,2,1,0:T(8,128)(2,1)S(1)} %collective-permute-done.6.refs_0_), channel_id=1, source_target_pairs={{0,4},{1,5},{2,6},{3,7},{4,8},{5,9},{6,10},{7,11},{8,12},{9,13},{1... | collective-permute-start | bytes 1327112 | tf_op jit(solution)/shard_map/ppermute | solution.py:187
  169.9 13.6 %collective-permute-start.9 = (bf16[2,4,8,3456]{3,2,1,0:T(8,128)(2,1)}, bf16[2,4,8,3456]{3,2,1,0:T(8,128)(2,1)}, u32[]{:S(2)}, u32[]{:S(2)}) collective-permute-start(bf16[2,4,8,3456]{3,2,1,0:T(8,128)(2,1)} %collective-permute-done.8.refs_3_), channel_id=1, source_target_pairs={{0,12},{1,13},{2,14},{3,15},{4,0},{5,1},{6,2},{7,3},{8,4},{9,5},{1... | collective-permute-start | bytes 1327112 | tf_op jit(solution)/shard_map/ppermute | solution.py:187
  172.4 129.7 %collective-permute-start.28 = (bf16[2,4,8,3456]{3,2,1,0:T(8,128)(2,1)}, bf16[2,4,8,3456]{3,2,1,0:T(8,128)(2,1)}, u32[]{:S(2)}, u32[]{:S(2)}) collective-permute-start(bf16[2,4,8,3456]{3,2,1,0:T(8,128)(2,1)} %collective-permute-done.8.refs_3_), channel_id=1, source_target_pairs={{0,16},{16,0},{32,48},{48,32},{64,80},{80,64},{96,112},{112,96},{1... | collective-permute-start | bytes 1327112 | tf_op jit(solution)/shard_map/ppermute | solution.py:176
  180.0 338.4 %collective-permute-start.19 = (bf16[2,4,8,3456]{3,2,1,0:T(8,128)(2,1)}, bf16[2,4,8,3456]{3,2,1,0:T(8,128)(2,1)}, u32[]{:S(2)}, u32[]{:S(2)}) collective-permute-start(bf16[2,4,8,3456]{3,2,1,0:T(8,128)(2,1)} %collective-permute-done.14.refs_2_), channel_id=1, source_target_pairs={{0,16},{16,0},{32,48},{48,32},{64,80},{80,64},{96,112},{112,96},{1... | collective-permute-start | bytes 1327112 | tf_op jit(solution)/shard_map/ppermute | solution.py:176
  180.9 337.6 %collective-permute-start.20 = (bf16[2,4,8,3456]{3,2,1,0:T(8,128)(2,1)}, bf16[2,4,8,3456]{3,2,1,0:T(8,128)(2,1)}, u32[]{:S(2)}, u32[]{:S(2)}) collective-permute-start(bf16[2,4,8,3456]{3,2,1,0:T(8,128)(2,1)} %collective-permute-done.16.refs_3_), channel_id=1, source_target_pairs={{0,16},{16,0},{32,48},{48,32},{64,80},{80,64},{96,112},{112,96},{1... | collective-permute-start | bytes 1327112 | tf_op jit(solution)/shard_map/ppermute | solution.py:176
  182.1 336.4 %collective-permute-start.17 = (bf16[2,4,8,3456]{3,2,1,0:T(8,128)(2,1)}, bf16[2,4,8,3456]{3,2,1,0:T(8,128)(2,1)}, u32[]{:S(2)}, u32[]{:S(2)}) collective-permute-start(bf16[2,4,8,3456]{3,2,1,0:T(8,128)(2,1)} %collective-permute-done.7.refs_0_), channel_id=1, source_target_pairs={{0,16},{16,0},{32,48},{48,32},{64,80},{80,64},{96,112},{112,96},{1... | collective-permute-start | bytes 1327112 | tf_op jit(solution)/shard_map/ppermute | solution.py:176
  183.7 334.8 %collective-permute-start.18 = (bf16[2,4,8,3456]{3,2,1,0:T(8,128)(2,1)}, bf16[2,4,8,3456]{3,2,1,0:T(8,128)(2,1)}, u32[]{:S(2)}, u32[]{:S(2)}) collective-permute-start(bf16[2,4,8,3456]{3,2,1,0:T(8,128)(2,1)} %collective-permute-done.9.refs_1_), channel_id=1, source_target_pairs={{0,16},{16,0},{32,48},{48,32},{64,80},{80,64},{96,112},{112,96},{1... | collective-permute-start | bytes 1327112 | tf_op jit(solution)/shard_map/ppermute | solution.py:176
  (28 other events, 184.3 us)

commit v2 on v1

--- a/solution.py
+++ b/solution.py
@@ -21,7 +21,7 @@
 
 decay_rate = 0.9
 step_size = 1.0
-VMEM_LIMIT = 48 * 1024 * 1024
+VMEM_LIMIT = 16 * 1024 * 1024
 
 
 def cosine_table():
@@ -112,20 +112,19 @@
 
 def bring_together(place, blocks, which, out_shapes, targets):
     def kernel(place_ref, *refs):
-        ins, outs, sems = refs[: len(blocks)], refs[len(blocks) : -1], refs[-1]
-        pairs = []
+        ins, outs = refs[: len(blocks)], refs[len(blocks) :]
         for k, block in enumerate(ins):
             source = lax.rem(place_ref[which] + (4 - k), 4)
-            pairs += targets(outs, block, source)
-        copy_all(pairs, sems)
-
-    count = len(blocks) * len(out_shapes)
+            for src, dst in targets(outs, block, source):
+                dst[...] = src[...]
+
+    vmem = pl.BlockSpec(memory_space=pltpu.VMEM)
     return pl.pallas_call(
         kernel,
         out_shape=out_shapes,
-        in_specs=[pl.BlockSpec(memory_space=pltpu.SMEM)] + [pl.BlockSpec(memory_space=pl.ANY)] * len(blocks),
-        out_specs=[pl.BlockSpec(memory_space=pl.ANY)] * len(out_shapes),
-        scratch_shapes=[pltpu.SemaphoreType.DMA((count,))],
+        in_specs=[pl.BlockSpec(memory_space=pltpu.SMEM)] + [vmem] * len(blocks),
+        out_specs=[vmem] * len(out_shapes),
+        compiler_params=pltpu.CompilerParams(vmem_limit_bytes=VMEM_LIMIT),
         cost_estimate=pl.CostEstimate(flops=0, bytes_accessed=2 * sum(b.size * 2 for b in blocks), transcendentals=0),
     )(place, *blocks)
 
@@ -151,7 +150,7 @@
 
     any_space = pl.BlockSpec(memory_space=pl.ANY)
     operands = [place] + blocks
-    specs = [pl.BlockSpec(memory_space=pltpu.SMEM)] + [any_space] * len(blocks)
+    specs = [pl.BlockSpec(memory_space=pltpu.SMEM)] + [pl.BlockSpec(memory_space=pltpu.VMEM)] * len(blocks)
     aliases = {}
     if whole is not None:
         aliases = {len(operands): 0}
@@ -164,6 +163,7 @@
         out_specs=any_space,
         scratch_shapes=[pltpu.SemaphoreType.DMA((len(blocks),))],
         input_output_aliases=aliases,
+        compiler_params=pltpu.CompilerParams(vmem_limit_bytes=VMEM_LIMIT),
         cost_estimate=pl.CostEstimate(flops=0, bytes_accessed=2 * sum(b.size * 2 for b in blocks), transcendentals=0),
     )(*operands)
 

time: 628 us -> 130 us (0.21)
  Pallas kernels: 516 us -> 18.9 us
    pallas_call x3, Pallas kernels: 434 us -> 8.39 us  [write_blocks(): pl.pallas_call(kernel, out_shape=jax.ShapeDtypeStruct((LAYERS, 4, 4, ROWS...]
    pallas_call x3, Pallas kernels: 72.5 us -> 1.8 us  [bring_together(): pl.pallas_call(kernel, out_shape=out_shapes, in_specs=[pl.BlockSpec(memor...]
    unnamed x77 -> x19, local copies, waits for them, and re-layouts: 14.6 us -> 11.1 us
  transfers between devices with their start and end apart: 38 -> 38, of which waited for: 11 -> 11; matrix products, arithmetic and copies ran while one was open for 0% -> 0% of each run, Pallas kernels for 62% -> 9%
where the time goes in v2:
time: 130 us
  starting transfers between devices  51 us (39%)
  waiting for transfers between devices  47.9 us (37%)
  Pallas kernels  18.9 us (15%)
  local copies, waits for them, and re-layouts  11.1 us (9%)
    ppermute x18, waiting for transfers between devices, shift_plane(): return lax.ppermute(x, 'fsdp', pairs)  29.7 us
    ppermute x18, starting transfers between devices, shift_plane(): return lax.ppermute(x, 'fsdp', pairs)  22.7 us
    ppermute x16, starting transfers between devices, shift_core(): return lax.ppermute(x, 'rep', [(r, r ^ 1) for r in range(8)])  18.7 us
    all_to_all x1, waiting for transfers between devices, shards(): received = lax.all_to_all(picked, 'rep', 0, 0, tiled=True)  13.3 us
    unnamed x19, local copies, waits for them, and re-layouts  11.1 us
    pallas_call x3, Pallas kernels, write_blocks(): pl.pallas_call(kernel, out_shape=jax.ShapeDtypeStruct((LAYERS, 4, 4, ROWS...  8.39 us
    all_to_all x1, starting transfers between devices, shards(): received = lax.all_to_all(picked, 'rep', 0, 0, tiled=True)  6.81 us
    ppermute x3, waiting for transfers between devices, shift_z(): return lax.ppermute(x, 'rep', [(r, (r + 2 * steps) % 8) for r in range(8)])  4.88 us
  transfers between devices with their start and end apart: 38, of which 11 were waited for; matrix products, arithmetic and copies ran while one was open for 0% of the time, Pallas kernels for 9%

profile of v2, /device:TPU:1, one launch (start us, length us, event | category | flops | bytes accessed | tf_op | source)
XLA Modules:
  0.0 129.9 jit_solution(13007513633151257688)
XLA Ops:
  1.5 1.5 %copy-done = f32[1,4,8,13824]{3,2,1,0:T(8,128)S(1)} copy-done((f32[1,4,8,13824]{3,2,1,0:T(8,128)S(1)}, f32[1,4,8,13824]{3,2,1,0:T(8,128)}, u32[]{:S(2)}) %copy-start) | copy-done | bytes 1769496
  3.0 1.2 copy-done.3
  4.1 0.9 copy-done.7
  5.1 3.2 %shard_map.96 = bf16[8,8,6912]{2,1,0:T(8,128)(2,1)} custom-call(s32[4,2,8,256]{3,2,1,0:T(8,128)S(1)} %pad.4.bands_ref, bf16[1,4,8,13824]{3,2,1,0:T(8,128)(2,1)S(1)} %copy-done.3, f32[1,4,8,13824]{3,2,1,0:T(8,128)S(1)} %copy-done, bf16[2,256,256]{2,1,0:T(8,128)(2,1)S(1)} %copy-done.7), custom_call_target="tpu_custom_call" | custom-call | flops 679477248 | bytes 4194304 | tf_op jit(solution)/shard_map/pallas_call | solution.py:203
  8.3 6.8 %all-to-all-start = ((bf16[8,8,6912]{2,1,0:T(8,128)(2,1)}), bf16[8,8,6912]{2,1,0:T(8,128)(2,1)S(1)}, u32[]{:S(2)}, u32[]{:S(2)}) async-start(bf16[8,8,6912]{2,1,0:T(8,128)(2,1)} %shard_map.96), calls=%async_computation | async-start | bytes 1769472 | tf_op jit(solution)/shard_map/all_to_all | solution.py:212
  15.2 13.3 %all-to-all-done.received_ref = bf16[8,8,6912]{2,1,0:T(8,128)(2,1)S(1)} async-done(((bf16[8,8,6912]{2,1,0:T(8,128)(2,1)}), bf16[8,8,6912]{2,1,0:T(8,128)(2,1)S(1)}, u32[]{:S(2)}, u32[]{:S(2)}) %all-to-all-start) | async-done | bytes 884768 | tf_op jit(solution)/shard_map/all_to_all | solution.py:212
  28.4 1.2 copy-done.2
  29.6 0.9 copy-done.5
  31.8 1.8 %collective-permute-start.1 = (bf16[2,8,3456]{2,1,0:T(8,128)(2,1)S(1)}, bf16[2,8,3456]{2,1,0:T(8,128)(2,1)S(1)}, u32[]{:S(2)}, u32[]{:S(2)}) collective-permute-start(bf16[2,8,3456]{2,1,0:T(8,128)(2,1)S(1)} %shard_map.97.refs_0_), channel_id=1, source_target_pairs={{0,64},{16,80},{32,96},{48,112},{64,0},{80,16},{96,32},{112,48},{1... | collective-permute-start | bytes 331784 | tf_op jit(solution)/shard_map/ppermute | solution.py:172
  34.3 3.6 %collective-permute-done.refs_1_ = bf16[2,8,3456]{2,1,0:T(8,128)(2,1)S(1)} collective-permute-done((bf16[2,8,3456]{2,1,0:T(8,128)(2,1)S(1)}, bf16[2,8,3456]{2,1,0:T(8,128)(2,1)S(1)}, u32[]{:S(2)}, u32[]{:S(2)}) %collective-permute-start) | collective-permute-done | bytes 110624 | tf_op jit(solution)/shard_map/ppermute | solution.py:172
  37.9 1.2 collective-permute-done.2.refs_3_
  39.7 1.4 %collective-permute-start.10 = (bf16[4,8,3456]{2,1,0:T(8,128)(2,1)S(1)}, bf16[4,8,3456]{2,1,0:T(8,128)(2,1)S(1)}, u32[]{:S(2)}, u32[]{:S(2)}) collective-permute-start(bf16[4,8,3456]{2,1,0:T(8,128)(2,1)S(1)} %get-tuple-element.11.refs_0_), channel_id=1, source_target_pairs={{0,4},{1,5},{2,6},{3,7},{4,8},{5,9},{6,10},{7,11},{8,12},{9,13},{1... | collective-permute-start | bytes 663560 | tf_op jit(solution)/shard_map/ppermute | solution.py:187
  41.1 2.6 %collective-permute-start.11 = (bf16[4,8,3456]{2,1,0:T(8,128)(2,1)S(1)}, bf16[4,8,3456]{2,1,0:T(8,128)(2,1)S(1)}, u32[]{:S(2)}, u32[]{:S(2)}) collective-permute-start(bf16[4,8,3456]{2,1,0:T(8,128)(2,1)S(1)} %get-tuple-element.11.refs_0_), channel_id=1, source_target_pairs={{0,8},{1,9},{2,10},{3,11},{4,12},{5,13},{6,14},{7,15},{8,0},{9,1},... | collective-permute-start | bytes 663560 | tf_op jit(solution)/shard_map/ppermute | solution.py:187
  43.7 1.1 collective-permute-start.12
  44.8 1.2 collective-permute-start.3
  46.0 2.4 %collective-permute-start.4 = (bf16[4,8,3456]{2,1,0:T(8,128)(2,1)S(1)}, bf16[4,8,3456]{2,1,0:T(8,128)(2,1)S(1)}, u32[]{:S(2)}, u32[]{:S(2)}) collective-permute-start(bf16[4,8,3456]{2,1,0:T(8,128)(2,1)S(1)} %get-tuple-element.8.refs_0_), channel_id=1, source_target_pairs={{0,2},{1,3},{2,0},{3,1},{4,6},{5,7},{6,4},{7,5},{8,10},{9,11},{10,... | collective-permute-start | bytes 663560 | tf_op jit(solution)/shard_map/ppermute | solution.py:187
  48.5 1.2 collective-permute-start.5
  49.6 2.0 %collective-permute-done.11.refs_2_ = bf16[4,8,3456]{2,1,0:T(8,128)(2,1)S(1)} collective-permute-done((bf16[4,8,3456]{2,1,0:T(8,128)(2,1)S(1)}, bf16[4,8,3456]{2,1,0:T(8,128)(2,1)S(1)}, u32[]{:S(2)}, u32[]{:S(2)}) %collective-permute-start.11) | collective-permute-done | bytes 221216 | tf_op jit(solution)/shard_map/ppermute | solution.py:187
  52.2 3.3 %collective-permute-start.35 = (bf16[2,4,8,3456]{3,2,1,0:T(8,128)(2,1)S(1)}, bf16[2,4,8,3456]{3,2,1,0:T(8,128)(2,1)S(1)}, u32[]{:S(2)}, u32[]{:S(2)}) collective-permute-start(bf16[2,4,8,3456]{3,2,1,0:T(8,128)(2,1)S(1)} %get-tuple-element.12.refs_2_), channel_id=1, source_target_pairs={{0,16},{16,0},{32,48},{48,32},{64,80},{80,64},{96,112},{112,96},{1... | collective-permute-start | bytes 1327112 | tf_op jit(solution)/shard_map/ppermute | solution.py:176
  56.3 4.1 %collective-permute-start.33 = (bf16[2,4,8,3456]{3,2,1,0:T(8,128)(2,1)S(1)}, bf16[2,4,8,3456]{3,2,1,0:T(8,128)(2,1)S(1)}, u32[]{:S(2)}, u32[]{:S(2)}) collective-permute-start(bf16[2,4,8,3456]{3,2,1,0:T(8,128)(2,1)S(1)} %get-tuple-element.9.refs_0_), channel_id=1, source_target_pairs={{0,16},{16,0},{32,48},{48,32},{64,80},{80,64},{96,112},{112,96},{1... | collective-permute-start | bytes 1327112 | tf_op jit(solution)/shard_map/ppermute | solution.py:176
  60.4 1.0 collective-permute-start.13
  61.4 1.7 %collective-permute-start.23 = (bf16[2,4,8,3456]{3,2,1,0:T(8,128)(2,1)S(1)}, bf16[2,4,8,3456]{3,2,1,0:T(8,128)(2,1)S(1)}, u32[]{:S(2)}, u32[]{:S(2)}) collective-permute-start(bf16[2,4,8,3456]{3,2,1,0:T(8,128)(2,1)S(1)} %get-tuple-element.12.refs_2_), channel_id=1, source_target_pairs={{0,3},{1,0},{2,1},{3,2},{4,7},{5,4},{6,5},{7,6},{8,11},{9,8},{10,9... | collective-permute-start | bytes 1327112 | tf_op jit(solution)/shard_map/ppermute | solution.py:187
  63.1 2.7 %collective-permute-start.15 = (bf16[2,4,8,3456]{3,2,1,0:T(8,128)(2,1)S(1)}, bf16[2,4,8,3456]{3,2,1,0:T(8,128)(2,1)S(1)}, u32[]{:S(2)}, u32[]{:S(2)}) collective-permute-start(bf16[2,4,8,3456]{3,2,1,0:T(8,128)(2,1)S(1)} %get-tuple-element.13.refs_3_), channel_id=1, source_target_pairs={{0,3},{1,0},{2,1},{3,2},{4,7},{5,4},{6,5},{7,6},{8,11},{9,8},{10,9... | collective-permute-start | bytes 1327112 | tf_op jit(solution)/shard_map/ppermute | solution.py:187
  66.2 6.8 %collective-permute-done.13.refs_4_ = bf16[2,4,8,3456]{3,2,1,0:T(8,128)(2,1)S(1)} collective-permute-done((bf16[2,4,8,3456]{3,2,1,0:T(8,128)(2,1)S(1)}, bf16[2,4,8,3456]{3,2,1,0:T(8,128)(2,1)S(1)}, u32[]{:S(2)}, u32[]{:S(2)}) %collective-permute-start.13) | collective-permute-done | bytes 442400 | tf_op jit(solution)/shard_map/ppermute | solution.py:187
  73.2 1.2 collective-permute-start.22
  74.4 8.0 %collective-permute-done.24.refs_6_ = bf16[2,4,8,3456]{3,2,1,0:T(8,128)(2,1)S(1)} collective-permute-done((bf16[2,4,8,3456]{3,2,1,0:T(8,128)(2,1)S(1)}, bf16[2,4,8,3456]{3,2,1,0:T(8,128)(2,1)S(1)}, u32[]{:S(2)}, u32[]{:S(2)}) %collective-permute-start.24) | collective-permute-done | bytes 442400 | tf_op jit(solution)/shard_map/ppermute | solution.py:187
  82.6 1.4 %collective-permute-start.29 = (bf16[2,4,8,3456]{3,2,1,0:T(8,128)(2,1)S(1)}, bf16[2,4,8,3456]{3,2,1,0:T(8,128)(2,1)S(1)}, u32[]{:S(2)}, u32[]{:S(2)}) collective-permute-start(bf16[2,4,8,3456]{3,2,1,0:T(8,128)(2,1)S(1)} %collective-permute-done.13.refs_4_), channel_id=1, source_target_pairs={{0,16},{16,0},{32,48},{48,32},{64,80},{80,64},{96,112},{112,96},{1... | collective-permute-start | bytes 1327112 | tf_op jit(solution)/shard_map/ppermute | solution.py:176
  84.1 1.4 %collective-permute-start.31 = (bf16[2,4,8,3456]{3,2,1,0:T(8,128)(2,1)S(1)}, bf16[2,4,8,3456]{3,2,1,0:T(8,128)(2,1)S(1)}, u32[]{:S(2)}, u32[]{:S(2)}) collective-permute-start(bf16[2,4,8,3456]{3,2,1,0:T(8,128)(2,1)S(1)} %collective-permute-done.24.refs_6_), channel_id=1, source_target_pairs={{0,16},{16,0},{32,48},{48,32},{64,80},{80,64},{96,112},{112,96},{1... | collective-permute-start | bytes 1327112 | tf_op jit(solution)/shard_map/ppermute | solution.py:176
  85.5 1.6 %collective-permute-done.22.refs_2_ = bf16[2,4,8,3456]{3,2,1,0:T(8,128)(2,1)S(1)} collective-permute-done((bf16[2,4,8,3456]{3,2,1,0:T(8,128)(2,1)S(1)}, bf16[2,4,8,3456]{3,2,1,0:T(8,128)(2,1)S(1)}, u32[]{:S(2)}, u32[]{:S(2)}) %collective-permute-start.22) | collective-permute-done | bytes 442400 | tf_op jit(solution)/shard_map/ppermute | solution.py:187
  87.1 2.0 %collective-permute-start.32 = (bf16[2,4,8,3456]{3,2,1,0:T(8,128)(2,1)S(1)}, bf16[2,4,8,3456]{3,2,1,0:T(8,128)(2,1)S(1)}, u32[]{:S(2)}, u32[]{:S(2)}) collective-permute-start(bf16[2,4,8,3456]{3,2,1,0:T(8,128)(2,1)S(1)} %collective-permute-done.15.refs_7_), channel_id=1, source_target_pairs={{0,16},{16,0},{32,48},{48,32},{64,80},{80,64},{96,112},{112,96},{1... | collective-permute-start | bytes 1327112 | tf_op jit(solution)/shard_map/ppermute | solution.py:176
  89.0 3.8 %collective-permute-done.8.refs_3_ = bf16[2,4,8,3456]{3,2,1,0:T(8,128)(2,1)S(1)} collective-permute-done((bf16[2,4,8,3456]{3,2,1,0:T(8,128)(2,1)S(1)}, bf16[2,4,8,3456]{3,2,1,0:T(8,128)(2,1)S(1)}, u32[]{:S(2)}, u32[]{:S(2)}) %collective-permute-start.8) | collective-permute-done | bytes 442400 | tf_op jit(solution)/shard_map/ppermute | solution.py:187
  92.8 2.2 %collective-permute-start.25 = (bf16[2,4,8,3456]{3,2,1,0:T(8,128)(2,1)S(1)}, bf16[2,4,8,3456]{3,2,1,0:T(8,128)(2,1)S(1)}, u32[]{:S(2)}, u32[]{:S(2)}) collective-permute-start(bf16[2,4,8,3456]{3,2,1,0:T(8,128)(2,1)S(1)} %collective-permute-done.6.refs_0_), channel_id=1, source_target_pairs={{0,16},{16,0},{32,48},{48,32},{64,80},{80,64},{96,112},{112,96},{1... | collective-permute-start | bytes 1327112 | tf_op jit(solution)/shard_map/ppermute | solution.py:176
  95.5 2.7 %collective-permute-start.16 = (bf16[2,4,8,3456]{3,2,1,0:T(8,128)(2,1)S(1)}, bf16[2,4,8,3456]{3,2,1,0:T(8,128)(2,1)S(1)}, u32[]{:S(2)}, u32[]{:S(2)}) collective-permute-start(bf16[2,4,8,3456]{3,2,1,0:T(8,128)(2,1)S(1)} %collective-permute-done.15.refs_7_), channel_id=1, source_target_pairs={{0,3},{1,0},{2,1},{3,2},{4,7},{5,4},{6,5},{7,6},{8,11},{9,8},{10,9... | collective-permute-start | bytes 1327112 | tf_op jit(solution)/shard_map/ppermute | solution.py:187
  98.2 1.3 collective-permute-start.7
  99.5 1.4 %collective-permute-start.9 = (bf16[2,4,8,3456]{3,2,1,0:T(8,128)(2,1)S(1)}, bf16[2,4,8,3456]{3,2,1,0:T(8,128)(2,1)S(1)}, u32[]{:S(2)}, u32[]{:S(2)}) collective-permute-start(bf16[2,4,8,3456]{3,2,1,0:T(8,128)(2,1)S(1)} %collective-permute-done.8.refs_3_), channel_id=1, source_target_pairs={{0,12},{1,13},{2,14},{3,15},{4,0},{5,1},{6,2},{7,3},{8,4},{9,5},{1... | collective-permute-start | bytes 1327112 | tf_op jit(solution)/shard_map/ppermute | solution.py:187
  100.9 1.2 collective-permute-start.28
  102.1 6.4 %collective-permute-done.14.refs_2_ = bf16[2,4,8,3456]{3,2,1,0:T(8,128)(2,1)S(1)} collective-permute-done((bf16[2,4,8,3456]{3,2,1,0:T(8,128)(2,1)S(1)}, bf16[2,4,8,3456]{3,2,1,0:T(8,128)(2,1)S(1)}, u32[]{:S(2)}, u32[]{:S(2)}) %collective-permute-start.14) | collective-permute-done | bytes 442400 | tf_op jit(solution)/shard_map/ppermute | solution.py:187
  108.5 0.9 collective-permute-start.19
  109.3 1.2 collective-permute-done.7.refs_0_
  110.5 1.5 %collective-permute-start.17 = (bf16[2,4,8,3456]{3,2,1,0:T(8,128)(2,1)S(1)}, bf16[2,4,8,3456]{3,2,1,0:T(8,128)(2,1)S(1)}, u32[]{:S(2)}, u32[]{:S(2)}) collective-permute-start(bf16[2,4,8,3456]{3,2,1,0:T(8,128)(2,1)S(1)} %collective-permute-done.7.refs_0_), channel_id=1, source_target_pairs={{0,16},{16,0},{32,48},{48,32},{64,80},{80,64},{96,112},{112,96},{1... | collective-permute-start | bytes 1327112 | tf_op jit(solution)/shard_map/ppermute | solution.py:176
  112.1 1.5 %copy-done.1 = f32[1,4,8,13824]{3,2,1,0:T(8,128)S(1)} copy-done((f32[1,4,8,13824]{3,2,1,0:T(8,128)S(1)}, f32[1,4,8,13824]{3,2,1,0:T(8,128)}, u32[]{:S(2)}) %copy-start.1) | copy-done | bytes 1769496
  113.6 1.2 copy-done.4
  114.8 0.9 copy-done.6
  115.7 0.9 copy-done.8
  116.7 4.6 %shard_map.95 = f32[1,4,8,13824]{3,2,1,0:T(8,128)} custom-call(s32[4,2,8,256]{3,2,1,0:T(8,128)S(1)} %pad.4.bands_ref, bf16[1,4,8,13824]{3,2,1,0:T(8,128)(2,1)S(1)} %copy-done.4, f32[1,4,8,13824]{3,2,1,0:T(8,128)S(1)} %copy-done.1, bf16[2,256,256]{2,1,0:T(8,128)(2,1)S(1)} %copy-done.8, bf16[2,256,256]{2,1,0:T(8,128)(2,1)S(1)} %copy-done.6), custom_call_target="tpu_custom_call" | custom-call | flops 1358954496 | bytes 6291456 | tf_op jit(solution)/shard_map/pallas_call | solution.py:262
  121.3 2.4 %shard_map.101.refs_16_ = bf16[4,4,4,8,13824]{4,3,2,1,0:T(8,128)(2,1)} custom-call(s32[4]{0:T(128)S(1)} %pad_add_fusion.place_ref, bf16[2,4,8,3456]{3,2,1,0:T(8,128)(2,1)S(1)} %get-tuple-element.9.refs_0_, bf16[2,4,8,3456]{3,2,1,0:T(8,128)(2,1)S(1)} %get-tuple-element.10.refs_1_, bf16[2,4,8,3456]{3,2,1,0:T(8,128)(2,1)S(1)} %get-tuple-element.12.refs_2_, ...), custom_call_target="tpu_custom_call" | custom-call | bytes 7077888 | tf_op jit(solution)/shard_map/pallas_call | solution.py:159
  123.7 3.6 %shard_map.102.refs_8_ = bf16[4,4,4,8,13824]{4,3,2,1,0:T(8,128)(2,1)} custom-call(s32[4]{0:T(128)S(1)} %pad_add_fusion.place_ref, bf16[2,4,8,3456]{3,2,1,0:T(8,128)(2,1)S(1)} %collective-permute-done.6.refs_0_, bf16[2,4,8,3456]{3,2,1,0:T(8,128)(2,1)S(1)} %collective-permute-done.21.refs_1_, ...), custom_call_target="tpu_custom_call", output_to_operand_aliasing={{}: (17, {})} | custom-call | bytes 14155776 | tf_op jit(solution)/shard_map/pallas_call | solution.py:159
  127.3 2.4 %shard_map.103 = bf16[4,4,4,8,13824]{4,3,2,1,0:T(8,128)(2,1)} custom-call(s32[4]{0:T(128)S(1)} %pad_add_fusion.place_ref, bf16[2,4,8,3456]{3,2,1,0:T(8,128)(2,1)S(1)} %collective-permute-done.7.refs_0_, bf16[2,4,8,3456]{3,2,1,0:T(8,128)(2,1)S(1)} %collective-permute-done.9.refs_1_, ...), custom_call_target="tpu_custom_call", output_to_operand_aliasing={{}: (9, {})} | custom-call | bytes 7077888 | tf_op jit(solution)/shard_map/pallas_call | solution.py:159
  (58 shorter events, 6.5 us)
Async XLA Ops:
  1.5 1.5 %copy-start = (f32[1,4,8,13824]{3,2,1,0:T(8,128)S(1)}, f32[1,4,8,13824]{3,2,1,0:T(8,128)}, u32[]{:S(2)}) copy-start(f32[1,4,8,13824]{3,2,1,0:T(8,128)} %momentum_ref.3) | copy-start | bytes 5308420
  3.0 1.2 copy-start.3
  4.1 0.9 copy-start.7
  8.3 20.2 %all-to-all-start = ((bf16[8,8,6912]{2,1,0:T(8,128)(2,1)}), bf16[8,8,6912]{2,1,0:T(8,128)(2,1)S(1)}, u32[]{:S(2)}, u32[]{:S(2)}) async-start(bf16[8,8,6912]{2,1,0:T(8,128)(2,1)} %shard_map.96), calls=%async_computation | async-start | bytes 1769472 | tf_op jit(solution)/shard_map/all_to_all | solution.py:212
  28.4 1.2 copy-start.2
  29.6 0.9 copy-start.5
  31.4 6.4 %collective-permute-start = (bf16[2,8,3456]{2,1,0:T(8,128)(2,1)S(1)}, bf16[2,8,3456]{2,1,0:T(8,128)(2,1)S(1)}, u32[]{:S(2)}, u32[]{:S(2)}) collective-permute-start(bf16[2,8,3456]{2,1,0:T(8,128)(2,1)S(1)} %shard_map.97.refs_0_), channel_id=1, source_target_pairs={{0,32},{16,48},{32,64},{48,80},{64,96},{80,112},{96,0},{112,16},{1... | collective-permute-start | bytes 331784 | tf_op jit(solution)/shard_map/ppermute | solution.py:172
  31.8 6.1 %collective-permute-start.1 = (bf16[2,8,3456]{2,1,0:T(8,128)(2,1)S(1)}, bf16[2,8,3456]{2,1,0:T(8,128)(2,1)S(1)}, u32[]{:S(2)}, u32[]{:S(2)}) collective-permute-start(bf16[2,8,3456]{2,1,0:T(8,128)(2,1)S(1)} %shard_map.97.refs_0_), channel_id=1, source_target_pairs={{0,64},{16,80},{32,96},{48,112},{64,0},{80,16},{96,32},{112,48},{1... | collective-permute-start | bytes 331784 | tf_op jit(solution)/shard_map/ppermute | solution.py:172
  33.6 5.6 %collective-permute-start.2 = (bf16[2,8,3456]{2,1,0:T(8,128)(2,1)S(1)}, bf16[2,8,3456]{2,1,0:T(8,128)(2,1)S(1)}, u32[]{:S(2)}, u32[]{:S(2)}) collective-permute-start(bf16[2,8,3456]{2,1,0:T(8,128)(2,1)S(1)} %shard_map.97.refs_0_), channel_id=1, source_target_pairs={{0,96},{16,112},{32,0},{48,16},{64,32},{80,48},{96,64},{112,80},{1... | collective-permute-start | bytes 331784 | tf_op jit(solution)/shard_map/ppermute | solution.py:172
  39.7 8.7 %collective-permute-start.10 = (bf16[4,8,3456]{2,1,0:T(8,128)(2,1)S(1)}, bf16[4,8,3456]{2,1,0:T(8,128)(2,1)S(1)}, u32[]{:S(2)}, u32[]{:S(2)}) collective-permute-start(bf16[4,8,3456]{2,1,0:T(8,128)(2,1)S(1)} %get-tuple-element.11.refs_0_), channel_id=1, source_target_pairs={{0,4},{1,5},{2,6},{3,7},{4,8},{5,9},{6,10},{7,11},{8,12},{9,13},{1... | collective-permute-start | bytes 663560 | tf_op jit(solution)/shard_map/ppermute | solution.py:187
  41.1 10.5 %collective-permute-start.11 = (bf16[4,8,3456]{2,1,0:T(8,128)(2,1)S(1)}, bf16[4,8,3456]{2,1,0:T(8,128)(2,1)S(1)}, u32[]{:S(2)}, u32[]{:S(2)}) collective-permute-start(bf16[4,8,3456]{2,1,0:T(8,128)(2,1)S(1)} %get-tuple-element.11.refs_0_), channel_id=1, source_target_pairs={{0,8},{1,9},{2,10},{3,11},{4,12},{5,13},{6,14},{7,15},{8,0},{9,1},... | collective-permute-start | bytes 663560 | tf_op jit(solution)/shard_map/ppermute | solution.py:187
  43.7 7.9 %collective-permute-start.12 = (bf16[4,8,3456]{2,1,0:T(8,128)(2,1)S(1)}, bf16[4,8,3456]{2,1,0:T(8,128)(2,1)S(1)}, u32[]{:S(2)}, u32[]{:S(2)}) collective-permute-start(bf16[4,8,3456]{2,1,0:T(8,128)(2,1)S(1)} %get-tuple-element.11.refs_0_), channel_id=1, source_target_pairs={{0,12},{1,13},{2,14},{3,15},{4,0},{5,1},{6,2},{7,3},{8,4},{9,5},{1... | collective-permute-start | bytes 663560 | tf_op jit(solution)/shard_map/ppermute | solution.py:187
  44.8 10.8 %collective-permute-start.3 = (bf16[4,8,3456]{2,1,0:T(8,128)(2,1)S(1)}, bf16[4,8,3456]{2,1,0:T(8,128)(2,1)S(1)}, u32[]{:S(2)}, u32[]{:S(2)}) collective-permute-start(bf16[4,8,3456]{2,1,0:T(8,128)(2,1)S(1)} %get-tuple-element.8.refs_0_), channel_id=1, source_target_pairs={{0,1},{1,2},{2,3},{3,0},{4,5},{5,6},{6,7},{7,4},{8,9},{9,10},{10,1... | collective-permute-start | bytes 663560 | tf_op jit(solution)/shard_map/ppermute | solution.py:187
  46.0 9.6 %collective-permute-start.4 = (bf16[4,8,3456]{2,1,0:T(8,128)(2,1)S(1)}, bf16[4,8,3456]{2,1,0:T(8,128)(2,1)S(1)}, u32[]{:S(2)}, u32[]{:S(2)}) collective-permute-start(bf16[4,8,3456]{2,1,0:T(8,128)(2,1)S(1)} %get-tuple-element.8.refs_0_), channel_id=1, source_target_pairs={{0,2},{1,3},{2,0},{3,1},{4,6},{5,7},{6,4},{7,5},{8,10},{9,11},{10,... | collective-permute-start | bytes 663560 | tf_op jit(solution)/shard_map/ppermute | solution.py:187
  48.5 7.2 %collective-permute-start.5 = (bf16[4,8,3456]{2,1,0:T(8,128)(2,1)S(1)}, bf16[4,8,3456]{2,1,0:T(8,128)(2,1)S(1)}, u32[]{:S(2)}, u32[]{:S(2)}) collective-permute-start(bf16[4,8,3456]{2,1,0:T(8,128)(2,1)S(1)} %get-tuple-element.8.refs_0_), channel_id=1, source_target_pairs={{0,3},{1,0},{2,1},{3,2},{4,7},{5,4},{6,5},{7,6},{8,11},{9,8},{10,9... | collective-permute-start | bytes 663560 | tf_op jit(solution)/shard_map/ppermute | solution.py:187
  52.2 9.2 %collective-permute-start.35 = (bf16[2,4,8,3456]{3,2,1,0:T(8,128)(2,1)S(1)}, bf16[2,4,8,3456]{3,2,1,0:T(8,128)(2,1)S(1)}, u32[]{:S(2)}, u32[]{:S(2)}) collective-permute-start(bf16[2,4,8,3456]{3,2,1,0:T(8,128)(2,1)S(1)} %get-tuple-element.12.refs_2_), channel_id=1, source_target_pairs={{0,16},{16,0},{32,48},{48,32},{64,80},{80,64},{96,112},{112,96},{1... | collective-permute-start | bytes 1327112 | tf_op jit(solution)/shard_map/ppermute | solution.py:176
  55.5 7.6 %collective-permute-start.36 = (bf16[2,4,8,3456]{3,2,1,0:T(8,128)(2,1)S(1)}, bf16[2,4,8,3456]{3,2,1,0:T(8,128)(2,1)S(1)}, u32[]{:S(2)}, u32[]{:S(2)}) collective-permute-start(bf16[2,4,8,3456]{3,2,1,0:T(8,128)(2,1)S(1)} %get-tuple-element.13.refs_3_), channel_id=1, source_target_pairs={{0,16},{16,0},{32,48},{48,32},{64,80},{80,64},{96,112},{112,96},{1... | collective-permute-start | bytes 1327112 | tf_op jit(solution)/shard_map/ppermute | solution.py:176
  56.3 6.8 %collective-permute-start.33 = (bf16[2,4,8,3456]{3,2,1,0:T(8,128)(2,1)S(1)}, bf16[2,4,8,3456]{3,2,1,0:T(8,128)(2,1)S(1)}, u32[]{:S(2)}, u32[]{:S(2)}) collective-permute-start(bf16[2,4,8,3456]{3,2,1,0:T(8,128)(2,1)S(1)} %get-tuple-element.9.refs_0_), channel_id=1, source_target_pairs={{0,16},{16,0},{32,48},{48,32},{64,80},{80,64},{96,112},{112,96},{1... | collective-permute-start | bytes 1327112 | tf_op jit(solution)/shard_map/ppermute | solution.py:176
  60.3 5.5 %collective-permute-start.34 = (bf16[2,4,8,3456]{3,2,1,0:T(8,128)(2,1)S(1)}, bf16[2,4,8,3456]{3,2,1,0:T(8,128)(2,1)S(1)}, u32[]{:S(2)}, u32[]{:S(2)}) collective-permute-start(bf16[2,4,8,3456]{3,2,1,0:T(8,128)(2,1)S(1)} %get-tuple-element.10.refs_1_), channel_id=1, source_target_pairs={{0,16},{16,0},{32,48},{48,32},{64,80},{80,64},{96,112},{112,96},{1... | collective-permute-start | bytes 1327112 | tf_op jit(solution)/shard_map/ppermute | solution.py:176
  60.4 12.5 %collective-permute-start.13 = (bf16[2,4,8,3456]{3,2,1,0:T(8,128)(2,1)S(1)}, bf16[2,4,8,3456]{3,2,1,0:T(8,128)(2,1)S(1)}, u32[]{:S(2)}, u32[]{:S(2)}) collective-permute-start(bf16[2,4,8,3456]{3,2,1,0:T(8,128)(2,1)S(1)} %get-tuple-element.12.refs_2_), channel_id=1, source_target_pairs={{0,1},{1,2},{2,3},{3,0},{4,5},{5,6},{6,7},{7,4},{8,9},{9,10},{10,1... | collective-permute-start | bytes 1327112 | tf_op jit(solution)/shard_map/ppermute | solution.py:187
  61.4 11.7 %collective-permute-start.23 = (bf16[2,4,8,3456]{3,2,1,0:T(8,128)(2,1)S(1)}, bf16[2,4,8,3456]{3,2,1,0:T(8,128)(2,1)S(1)}, u32[]{:S(2)}, u32[]{:S(2)}) collective-permute-start(bf16[2,4,8,3456]{3,2,1,0:T(8,128)(2,1)S(1)} %get-tuple-element.12.refs_2_), channel_id=1, source_target_pairs={{0,3},{1,0},{2,1},{3,2},{4,7},{5,4},{6,5},{7,6},{8,11},{9,8},{10,9... | collective-permute-start | bytes 1327112 | tf_op jit(solution)/shard_map/ppermute | solution.py:187
  63.1 19.3 %collective-permute-start.24 = (bf16[2,4,8,3456]{3,2,1,0:T(8,128)(2,1)S(1)}, bf16[2,4,8,3456]{3,2,1,0:T(8,128)(2,1)S(1)}, u32[]{:S(2)}, u32[]{:S(2)}) collective-permute-start(bf16[2,4,8,3456]{3,2,1,0:T(8,128)(2,1)S(1)} %get-tuple-element.13.refs_3_), channel_id=1, source_target_pairs={{0,1},{1,2},{2,3},{3,0},{4,5},{5,6},{6,7},{7,4},{8,9},{9,10},{10,1... | collective-permute-start | bytes 1327112 | tf_op jit(solution)/shard_map/ppermute | solution.py:187
  63.1 19.6 %collective-permute-start.15 = (bf16[2,4,8,3456]{3,2,1,0:T(8,128)(2,1)S(1)}, bf16[2,4,8,3456]{3,2,1,0:T(8,128)(2,1)S(1)}, u32[]{:S(2)}, u32[]{:S(2)}) collective-permute-start(bf16[2,4,8,3456]{3,2,1,0:T(8,128)(2,1)S(1)} %get-tuple-element.13.refs_3_), channel_id=1, source_target_pairs={{0,3},{1,0},{2,1},{3,2},{4,7},{5,4},{6,5},{7,6},{8,11},{9,8},{10,9... | collective-permute-start | bytes 1327112 | tf_op jit(solution)/shard_map/ppermute | solution.py:187
  65.8 18.3 %collective-permute-start.6 = (bf16[2,4,8,3456]{3,2,1,0:T(8,128)(2,1)S(1)}, bf16[2,4,8,3456]{3,2,1,0:T(8,128)(2,1)S(1)}, u32[]{:S(2)}, u32[]{:S(2)}) collective-permute-start(bf16[2,4,8,3456]{3,2,1,0:T(8,128)(2,1)S(1)} %get-tuple-element.9.refs_0_), channel_id=1, source_target_pairs={{0,4},{1,5},{2,6},{3,7},{4,8},{5,9},{6,10},{7,11},{8,12},{9,13},{1... | collective-permute-start | bytes 1327112 | tf_op jit(solution)/shard_map/ppermute | solution.py:187
  72.9 11.2 %collective-permute-start.21 = (bf16[2,4,8,3456]{3,2,1,0:T(8,128)(2,1)S(1)}, bf16[2,4,8,3456]{3,2,1,0:T(8,128)(2,1)S(1)}, u32[]{:S(2)}, u32[]{:S(2)}) collective-permute-start(bf16[2,4,8,3456]{3,2,1,0:T(8,128)(2,1)S(1)} %get-tuple-element.9.refs_0_), channel_id=1, source_target_pairs={{0,12},{1,13},{2,14},{3,15},{4,0},{5,1},{6,2},{7,3},{8,4},{9,5},{1... | collective-permute-start | bytes 1327112 | tf_op jit(solution)/shard_map/ppermute | solution.py:187
  73.2 13.9 %collective-permute-start.22 = (bf16[2,4,8,3456]{3,2,1,0:T(8,128)(2,1)S(1)}, bf16[2,4,8,3456]{3,2,1,0:T(8,128)(2,1)S(1)}, u32[]{:S(2)}, u32[]{:S(2)}) collective-permute-start(bf16[2,4,8,3456]{3,2,1,0:T(8,128)(2,1)S(1)} %get-tuple-element.10.refs_1_), channel_id=1, source_target_pairs={{0,4},{1,5},{2,6},{3,7},{4,8},{5,9},{6,10},{7,11},{8,12},{9,13},{1... | collective-permute-start | bytes 1327112 | tf_op jit(solution)/shard_map/ppermute | solution.py:187
  82.4 10.4 %collective-permute-start.8 = (bf16[2,4,8,3456]{3,2,1,0:T(8,128)(2,1)S(1)}, bf16[2,4,8,3456]{3,2,1,0:T(8,128)(2,1)S(1)}, u32[]{:S(2)}, u32[]{:S(2)}) collective-permute-start(bf16[2,4,8,3456]{3,2,1,0:T(8,128)(2,1)S(1)} %get-tuple-element.10.refs_1_), channel_id=1, source_target_pairs={{0,12},{1,13},{2,14},{3,15},{4,0},{5,1},{6,2},{7,3},{8,4},{9,5},{1... | collective-permute-start | bytes 1327112 | tf_op jit(solution)/shard_map/ppermute | solution.py:187
  82.6 12.4 %collective-permute-start.29 = (bf16[2,4,8,3456]{3,2,1,0:T(8,128)(2,1)S(1)}, bf16[2,4,8,3456]{3,2,1,0:T(8,128)(2,1)S(1)}, u32[]{:S(2)}, u32[]{:S(2)}) collective-permute-start(bf16[2,4,8,3456]{3,2,1,0:T(8,128)(2,1)S(1)} %collective-permute-done.13.refs_4_), channel_id=1, source_target_pairs={{0,16},{16,0},{32,48},{48,32},{64,80},{80,64},{96,112},{112,96},{1... | collective-permute-start | bytes 1327112 | tf_op jit(solution)/shard_map/ppermute | solution.py:176
  84.0 11.0 %collective-permute-start.30 = (bf16[2,4,8,3456]{3,2,1,0:T(8,128)(2,1)S(1)}, bf16[2,4,8,3456]{3,2,1,0:T(8,128)(2,1)S(1)}, u32[]{:S(2)}, u32[]{:S(2)}) collective-permute-start(bf16[2,4,8,3456]{3,2,1,0:T(8,128)(2,1)S(1)} %collective-permute-done.23.refs_5_), channel_id=1, source_target_pairs={{0,16},{16,0},{32,48},{48,32},{64,80},{80,64},{96,112},{112,96},{1... | collective-permute-start | bytes 1327112 | tf_op jit(solution)/shard_map/ppermute | solution.py:176
  84.1 11.4 %collective-permute-start.31 = (bf16[2,4,8,3456]{3,2,1,0:T(8,128)(2,1)S(1)}, bf16[2,4,8,3456]{3,2,1,0:T(8,128)(2,1)S(1)}, u32[]{:S(2)}, u32[]{:S(2)}) collective-permute-start(bf16[2,4,8,3456]{3,2,1,0:T(8,128)(2,1)S(1)} %collective-permute-done.24.refs_6_), channel_id=1, source_target_pairs={{0,16},{16,0},{32,48},{48,32},{64,80},{80,64},{96,112},{112,96},{1... | collective-permute-start | bytes 1327112 | tf_op jit(solution)/shard_map/ppermute | solution.py:176
  87.1 8.4 %collective-permute-start.32 = (bf16[2,4,8,3456]{3,2,1,0:T(8,128)(2,1)S(1)}, bf16[2,4,8,3456]{3,2,1,0:T(8,128)(2,1)S(1)}, u32[]{:S(2)}, u32[]{:S(2)}) collective-permute-start(bf16[2,4,8,3456]{3,2,1,0:T(8,128)(2,1)S(1)} %collective-permute-done.15.refs_7_), channel_id=1, source_target_pairs={{0,16},{16,0},{32,48},{48,32},{64,80},{80,64},{96,112},{112,96},{1... | collective-permute-start | bytes 1327112 | tf_op jit(solution)/shard_map/ppermute | solution.py:176
  92.8 5.4 %collective-permute-start.25 = (bf16[2,4,8,3456]{3,2,1,0:T(8,128)(2,1)S(1)}, bf16[2,4,8,3456]{3,2,1,0:T(8,128)(2,1)S(1)}, u32[]{:S(2)}, u32[]{:S(2)}) collective-permute-start(bf16[2,4,8,3456]{3,2,1,0:T(8,128)(2,1)S(1)} %collective-permute-done.6.refs_0_), channel_id=1, source_target_pairs={{0,16},{16,0},{32,48},{48,32},{64,80},{80,64},{96,112},{112,96},{1... | collective-permute-start | bytes 1327112 | tf_op jit(solution)/shard_map/ppermute | solution.py:176
  95.0 4.5 %collective-permute-start.26 = (bf16[2,4,8,3456]{3,2,1,0:T(8,128)(2,1)S(1)}, bf16[2,4,8,3456]{3,2,1,0:T(8,128)(2,1)S(1)}, u32[]{:S(2)}, u32[]{:S(2)}) collective-permute-start(bf16[2,4,8,3456]{3,2,1,0:T(8,128)(2,1)S(1)} %collective-permute-done.21.refs_1_), channel_id=1, source_target_pairs={{0,16},{16,0},{32,48},{48,32},{64,80},{80,64},{96,112},{112,96},{1... | collective-permute-start | bytes 1327112 | tf_op jit(solution)/shard_map/ppermute | solution.py:176
  95.0 5.9 %collective-permute-start.27 = (bf16[2,4,8,3456]{3,2,1,0:T(8,128)(2,1)S(1)}, bf16[2,4,8,3456]{3,2,1,0:T(8,128)(2,1)S(1)}, u32[]{:S(2)}, u32[]{:S(2)}) collective-permute-start(bf16[2,4,8,3456]{3,2,1,0:T(8,128)(2,1)S(1)} %collective-permute-done.22.refs_2_), channel_id=1, source_target_pairs={{0,16},{16,0},{32,48},{48,32},{64,80},{80,64},{96,112},{112,96},{1... | collective-permute-start | bytes 1327112 | tf_op jit(solution)/shard_map/ppermute | solution.py:176
  95.5 12.9 %collective-permute-start.14 = (bf16[2,4,8,3456]{3,2,1,0:T(8,128)(2,1)S(1)}, bf16[2,4,8,3456]{3,2,1,0:T(8,128)(2,1)S(1)}, u32[]{:S(2)}, u32[]{:S(2)}) collective-permute-start(bf16[2,4,8,3456]{3,2,1,0:T(8,128)(2,1)S(1)} %collective-permute-done.13.refs_4_), channel_id=1, source_target_pairs={{0,1},{1,2},{2,3},{3,0},{4,5},{5,6},{6,7},{7,4},{8,9},{9,10},{10,1... | collective-permute-start | bytes 1327112 | tf_op jit(solution)/shard_map/ppermute | solution.py:187
  95.5 13.8 %collective-permute-start.16 = (bf16[2,4,8,3456]{3,2,1,0:T(8,128)(2,1)S(1)}, bf16[2,4,8,3456]{3,2,1,0:T(8,128)(2,1)S(1)}, u32[]{:S(2)}, u32[]{:S(2)}) collective-permute-start(bf16[2,4,8,3456]{3,2,1,0:T(8,128)(2,1)S(1)} %collective-permute-done.15.refs_7_), channel_id=1, source_target_pairs={{0,3},{1,0},{2,1},{3,2},{4,7},{5,4},{6,5},{7,6},{8,11},{9,8},{10,9... | collective-permute-start | bytes 1327112 | tf_op jit(solution)/shard_map/ppermute | solution.py:187
  98.2 12.3 %collective-permute-start.7 = (bf16[2,4,8,3456]{3,2,1,0:T(8,128)(2,1)S(1)}, bf16[2,4,8,3456]{3,2,1,0:T(8,128)(2,1)S(1)}, u32[]{:S(2)}, u32[]{:S(2)}) collective-permute-start(bf16[2,4,8,3456]{3,2,1,0:T(8,128)(2,1)S(1)} %collective-permute-done.6.refs_0_), channel_id=1, source_target_pairs={{0,4},{1,5},{2,6},{3,7},{4,8},{5,9},{6,10},{7,11},{8,12},{9,13},{1... | collective-permute-start | bytes 1327112 | tf_op jit(solution)/shard_map/ppermute | solution.py:187
  99.5 12.5 %collective-permute-start.9 = (bf16[2,4,8,3456]{3,2,1,0:T(8,128)(2,1)S(1)}, bf16[2,4,8,3456]{3,2,1,0:T(8,128)(2,1)S(1)}, u32[]{:S(2)}, u32[]{:S(2)}) collective-permute-start(bf16[2,4,8,3456]{3,2,1,0:T(8,128)(2,1)S(1)} %collective-permute-done.8.refs_3_), channel_id=1, source_target_pairs={{0,12},{1,13},{2,14},{3,15},{4,0},{5,1},{6,2},{7,3},{8,4},{9,5},{1... | collective-permute-start | bytes 1327112 | tf_op jit(solution)/shard_map/ppermute | solution.py:187
  100.9 22.8 %collective-permute-start.28 = (bf16[2,4,8,3456]{3,2,1,0:T(8,128)(2,1)S(1)}, bf16[2,4,8,3456]{3,2,1,0:T(8,128)(2,1)S(1)}, u32[]{:S(2)}, u32[]{:S(2)}) collective-permute-start(bf16[2,4,8,3456]{3,2,1,0:T(8,128)(2,1)S(1)} %collective-permute-done.8.refs_3_), channel_id=1, source_target_pairs={{0,16},{16,0},{32,48},{48,32},{64,80},{80,64},{96,112},{112,96},{1... | collective-permute-start | bytes 1327112 | tf_op jit(solution)/shard_map/ppermute | solution.py:176
  108.5 18.8 %collective-permute-start.19 = (bf16[2,4,8,3456]{3,2,1,0:T(8,128)(2,1)S(1)}, bf16[2,4,8,3456]{3,2,1,0:T(8,128)(2,1)S(1)}, u32[]{:S(2)}, u32[]{:S(2)}) collective-permute-start(bf16[2,4,8,3456]{3,2,1,0:T(8,128)(2,1)S(1)} %collective-permute-done.14.refs_2_), channel_id=1, source_target_pairs={{0,16},{16,0},{32,48},{48,32},{64,80},{80,64},{96,112},{112,96},{1... | collective-permute-start | bytes 1327112 | tf_op jit(solution)/shard_map/ppermute | solution.py:176
  109.3 18.0 %collective-permute-start.20 = (bf16[2,4,8,3456]{3,2,1,0:T(8,128)(2,1)S(1)}, bf16[2,4,8,3456]{3,2,1,0:T(8,128)(2,1)S(1)}, u32[]{:S(2)}, u32[]{:S(2)}) collective-permute-start(bf16[2,4,8,3456]{3,2,1,0:T(8,128)(2,1)S(1)} %collective-permute-done.16.refs_3_), channel_id=1, source_target_pairs={{0,16},{16,0},{32,48},{48,32},{64,80},{80,64},{96,112},{112,96},{1... | collective-permute-start | bytes 1327112 | tf_op jit(solution)/shard_map/ppermute | solution.py:176
  110.5 16.8 %collective-permute-start.17 = (bf16[2,4,8,3456]{3,2,1,0:T(8,128)(2,1)S(1)}, bf16[2,4,8,3456]{3,2,1,0:T(8,128)(2,1)S(1)}, u32[]{:S(2)}, u32[]{:S(2)}) collective-permute-start(bf16[2,4,8,3456]{3,2,1,0:T(8,128)(2,1)S(1)} %collective-permute-done.7.refs_0_), channel_id=1, source_target_pairs={{0,16},{16,0},{32,48},{48,32},{64,80},{80,64},{96,112},{112,96},{1... | collective-permute-start | bytes 1327112 | tf_op jit(solution)/shard_map/ppermute | solution.py:176
  112.0 15.3 %collective-permute-start.18 = (bf16[2,4,8,3456]{3,2,1,0:T(8,128)(2,1)S(1)}, bf16[2,4,8,3456]{3,2,1,0:T(8,128)(2,1)S(1)}, u32[]{:S(2)}, u32[]{:S(2)}) collective-permute-start(bf16[2,4,8,3456]{3,2,1,0:T(8,128)(2,1)S(1)} %collective-permute-done.9.refs_1_), channel_id=1, source_target_pairs={{0,16},{16,0},{32,48},{48,32},{64,80},{80,64},{96,112},{112,96},{1... | collective-permute-start | bytes 1327112 | tf_op jit(solution)/shard_map/ppermute | solution.py:176
  112.1 1.5 %copy-start.1 = (f32[1,4,8,13824]{3,2,1,0:T(8,128)S(1)}, f32[1,4,8,13824]{3,2,1,0:T(8,128)}, u32[]{:S(2)}) copy-start(f32[1,4,8,13824]{3,2,1,0:T(8,128)} %momentum_ref.3) | copy-start | bytes 5308420
  113.6 1.2 copy-start.4
  114.8 0.9 copy-start.6
  115.7 0.9 copy-start.8

commit v3 on v0

v3 whole, which is shorter than its diff:
```python
import math

import jax
import jax.numpy as jnp
import numpy as np
from jax import lax
from jax.experimental import pallas as pl
from jax.experimental.pallas import tpu as pltpu
from jax.sharding import PartitionSpec as P

GROUP = 64
BANDS = 8
LAYERS = 4
ROWS_HERE = 8
WIDTH = 13824
HALF = WIDTH // 2
WIDE = 256
LANES = 128
REPS = 8
UNIT = 2
UNITS = LAYERS // UNIT

decay_rate = 0.9
step_size = 1.0
VMEM_LIMIT = 16 * 1024 * 1024


def cosine_table():
    k = np.arange(GROUP, dtype=np.float64)
    n = np.arange(GROUP, dtype=np.float64)
    scale = np.where(k == 0, math.sqrt(1.0 / GROUP), math.sqrt(2.0 / GROUP))
    return scale[:, None] * np.cos(math.pi * (2.0 * n[None, :] + 1.0) * k[:, None] / (2.0 * GROUP))


def split_table(table):
    high = jnp.asarray(table, jnp.float32).astype(jnp.bfloat16)
    low = (jnp.asarray(table, jnp.float32) - high.astype(jnp.float32)).astype(jnp.bfloat16)
    return jnp.stack([high, low])


def dot3(x, table_ref):
    high = x.astype(jnp.bfloat16)
    low = (x - high.astype(jnp.float32)).astype(jnp.bfloat16)
    total = jnp.dot(high, table_ref[1], preferred_element_type=jnp.float32)
    total += jnp.dot(low, table_ref[0], preferred_element_type=jnp.float32)
    return total + jnp.dot(high, table_ref[0], preferred_element_type=jnp.float32)


def stacked(x):
    return jnp.concatenate([x[:, at : at + WIDE] for at in range(0, x.shape[1], WIDE)], axis=0)


def pick_tiles(bands_ref, side, layers, spectra):
    lane = lax.broadcasted_iota(jnp.int32, (ROWS_HERE, LANES), 1)
    upper = lax.shift_right_logical(lane, 6)
    band = lax.bitwise_and(lax.shift_right_logical(lane, 3), 7)
    tiles = {}
    for i, layer in enumerate(layers):
        first_bands = bands_ref[layer, 0, side]
        second_bands = bands_ref[layer, 1, side]
        for tile in range(HALF // LANES):
            index = upper + 2 * tile
            first = jnp.take_along_axis(first_bands, index, axis=1)
            second = jnp.take_along_axis(second_bands, index, axis=1)
            row = (i * (HALF // WIDE) + tile // 2) * ROWS_HERE
            column = (tile % 2) * LANES
            values = spectra[row : row + ROWS_HERE, column : column + LANES]
            tiles[i, tile] = jnp.where((first == band) | (second == band), values, 0.0)
    return tiles


def merged_rows(gradient, momentum):
    merged = decay_rate * momentum + gradient.astype(jnp.float32)
    return jnp.concatenate([stacked(merged[i]) for i in range(merged.shape[0])], axis=0)


HBM = pl.BlockSpec(memory_space=pltpu.HBM)
VMEM = pl.BlockSpec(memory_space=pltpu.VMEM)
SMEM = pl.BlockSpec(memory_space=pltpu.SMEM)
HALF_UNIT = jax.ShapeDtypeStruct((UNIT, ROWS_HERE, HALF), jnp.bfloat16)


def cost(flops, size):
    return pl.CostEstimate(flops=flops, bytes_accessed=size, transcendentals=0)


def pick(place, by_layer, gradient, momentum, forward, units, own, received=None, params=None, inverse=None):
    count = len(units)
    extra = ([] if received is None else [received]) + ([] if params is None else [params]) + ([] if inverse is None else [inverse])
    n_extra = len(extra)
    out_shapes = [HALF_UNIT] * count
    if params is not None:
        out_shapes.append(HALF_UNIT)
    if inverse is not None:
        out_shapes.append(jax.ShapeDtypeStruct((2, WIDE, WIDE), jnp.bfloat16))

    def kernel(place_ref, bands_ref, gradient_ref, momentum_ref, forward_ref, *refs):
        extras, outs = refs[:n_extra], refs[n_extra : n_extra + len(out_shapes)]
        gradients, momenta, table, sems = refs[n_extra + len(out_shapes) :]
        core = place_ref[3]
        side = core if own else 1 - core
        columns = pl.ds(pl.multiple_of(side * HALF, LANES), HALF)
        pairs = [(forward_ref, table)]
        for i, unit in enumerate(units):
            layers = pl.ds(unit * UNIT, UNIT)
            pairs.append((gradient_ref.at[0, layers, :, columns], gradients.at[i]))
            pairs.append((momentum_ref.at[0, layers, :, columns], momenta.at[i]))
        at = 0 if received is None else 1
        if params is not None:
            pairs.append((extras[at].at[pl.ds(units[0] * UNIT, UNIT), :, columns], outs[count]))
            at += 1
        if inverse is not None:
            pairs.append((extras[at], outs[count + 1]))
        copies = [pltpu.make_async_copy(src, dst, sems.at[i]) for i, (src, dst) in enumerate(pairs)]
        for copy in copies:
            copy.start()
        copies[0].wait()
        for i, unit in enumerate(units):
            copies[1 + 2 * i].wait()
            copies[2 + 2 * i].wait()
            spectra = dot3(merged_rows(gradients[i], momenta[i]), table)
            layers = range(unit * UNIT, unit * UNIT + UNIT)
            for (layer, tile), values in pick_tiles(bands_ref, side, layers, spectra).items():
                where = (layer, slice(None), slice(tile * LANES, (tile + 1) * LANES))
                if received is not None:
                    values = values + extras[0][where].astype(jnp.float32)
                outs[i][where] = values.astype(jnp.bfloat16)
        for copy in copies[1 + 2 * count :]:
            copy.wait()

    extra_specs = ([] if received is None else [VMEM]) + [HBM] * (n_extra - (received is not None))
    return pl.pallas_call(
        kernel,
        out_shape=out_shapes,
        in_specs=[SMEM, VMEM, HBM, HBM, HBM] + extra_specs,
        out_specs=[VMEM] * len(out_shapes),
        scratch_shapes=[
            pltpu.VMEM((count, UNIT, ROWS_HERE, HALF), jnp.bfloat16),
            pltpu.VMEM((count, UNIT, ROWS_HERE, HALF), jnp.float32),
            pltpu.VMEM((2, WIDE, WIDE), jnp.bfloat16),
            pltpu.SemaphoreType.DMA((3 + 2 * count,)),
        ],
        compiler_params=pltpu.CompilerParams(vmem_limit_bytes=VMEM_LIMIT),
        cost_estimate=cost(6 * count * UNIT * ROWS_HERE * HALF * WIDE, count * 1500000),
    )(place, by_layer, gradient, momentum, forward, *extra)


def keep_rest(place, by_layer, gradient, momentum, forward, inverse, unit, before):
    def kernel(bands_ref, gradient_ref, momentum_ref, forward_ref, inverse_ref, *refs):
        out_ref, gradients, momenta, table, sems = refs[-5:]
        layers = pl.ds(unit * UNIT, UNIT)
        pairs = [(forward_ref, table)]
        for side in range(2):
            columns = pl.ds(side * HALF, HALF)
            pairs.append((gradient_ref.at[0, layers, :, columns], gradients.at[side]))
            pairs.append((momentum_ref.at[0, layers, :, columns], momenta.at[side]))
        copies = [pltpu.make_async_copy(src, dst, sems.at[i]) for i, (src, dst) in enumerate(pairs)]
        for copy in copies:
            copy.start()
        copies[0].wait()
        for side in range(2):
            copies[1 + 2 * side].wait()
            copies[2 + 2 * side].wait()
            merged = merged_rows(gradients[side], momenta[side])
            spectra = dot3(merged, table)
            tiles = pick_tiles(bands_ref, side, range(unit * UNIT, unit * UNIT + UNIT), spectra)
            wide = [
                jnp.concatenate([tiles[i, at], tiles[i, at + 1]], axis=1)
                for i in range(UNIT)
                for at in range(0, HALF // LANES, 2)
            ]
            kept = merged - dot3(jnp.concatenate(wide, axis=0), inverse_ref)
            for i in range(UNIT):
                for at in range(HALF // WIDE):
                    row = (i * (HALF // WIDE) + at) * ROWS_HERE
                    momenta[side, i, :, at * WIDE : (at + 1) * WIDE] = kept[row : row + ROWS_HERE]
            target = out_ref.at[0, layers, :, pl.ds(side * HALF, HALF)]
            copies.append(pltpu.make_async_copy(momenta.at[side], target, sems.at[5 + side]))
            copies[-1].start()
        copies[-2].wait()
        copies[-1].wait()

    operands = [by_layer, gradient, momentum, forward, inverse]
    specs = [VMEM, HBM, HBM, HBM, VMEM]
    aliases = {}
    if before is not None:
        aliases = {len(operands): 0}
        operands.append(before)
        specs.append(HBM)
    return pl.pallas_call(
        kernel,
        out_shape=jax.ShapeDtypeStruct(momentum.shape, jnp.float32),
        in_specs=specs,
        out_specs=HBM,
        scratch_shapes=[
            pltpu.VMEM((2, UNIT, ROWS_HERE, HALF), jnp.bfloat16),
            pltpu.VMEM((2, UNIT, ROWS_HERE, HALF), jnp.float32),
            pltpu.VMEM((2, WIDE, WIDE), jnp.bfloat16),
            pltpu.SemaphoreType.DMA((7,)),
        ],
        input_output_aliases=aliases,
        compiler_params=pltpu.CompilerParams(vmem_limit_bytes=VMEM_LIMIT),
        cost_estimate=cost(12 * UNIT * ROWS_HERE * WIDTH * WIDE, 3000000),
    )(*operands)


def decode(sums, params, inverse):
    def kernel(first, second, third, fourth, params_ref, inverse_ref, out_ref):
        total = first[...].astype(jnp.float32) + second[...].astype(jnp.float32)
        total += third[...].astype(jnp.float32) + fourth[...].astype(jnp.float32)
        total = total * (1.0 / REPS)
        restored = jnp.concatenate([stacked(total[i]) for i in range(UNIT)], axis=0)
        decoded = dot3(restored, inverse_ref)
        for i in range(UNIT):
            for at in range(HALF // WIDE):
                columns = slice(at * WIDE, (at + 1) * WIDE)
                row = (i * (HALF // WIDE) + at) * ROWS_HERE
                after = params_ref[i, :, columns].astype(jnp.float32) - step_size * decoded[row : row + ROWS_HERE]
                out_ref[i, :, columns] = after.astype(jnp.bfloat16)

    return pl.pallas_call(
        kernel,
        out_shape=HALF_UNIT,
        in_specs=[VMEM] * 6,
        out_specs=VMEM,
        compiler_params=pltpu.CompilerParams(vmem_limit_bytes=VMEM_LIMIT),
        cost_estimate=cost(6 * UNIT * ROWS_HERE * HALF * WIDE, 1500000),
    )(*sums, params, inverse)


def first_place(place_ref):
    return jnp.where(place_ref[3] == 0, place_ref[2], place_ref[1])


def second_place(place_ref):
    return jnp.where(place_ref[3] == 0, place_ref[1], place_ref[2])


def bring_together(place, blocks):
    def kernel(place_ref, *refs):
        here = first_place(place_ref)
        for (_, steps), block in zip(blocks, refs):
            refs[-1][:, lax.rem(here + (4 - steps), 4)] = block[...]

    return pl.pallas_call(
        kernel,
        out_shape=jax.ShapeDtypeStruct((UNIT, 4, ROWS_HERE, HALF), jnp.bfloat16),
        in_specs=[SMEM] + [VMEM] * len(blocks),
        out_specs=VMEM,
        compiler_params=pltpu.CompilerParams(vmem_limit_bytes=VMEM_LIMIT),
        cost_estimate=cost(0, 1800000),
    )(place, *[block for block, _ in blocks])


def write_blocks(place, whole, items):
    blocks = [item[0] for item in items]

    def kernel(place_ref, *refs):
        ins, out, sems = refs[: len(blocks)], refs[-2], refs[-1]
        y, x, core = place_ref[1], place_ref[2], place_ref[3]
        copies = []
        for block, (_, unit, steps, other) in zip(ins, items):
            side = core if other == 0 else 1 - core
            here = lax.rem(jnp.where(side == 0, y, x) + (4 - steps), 4)
            columns = pl.ds(pl.multiple_of(side * HALF, LANES), HALF)
            for i in range(4):
                rows = jnp.where(side == 0, 4 * here + i, 4 * i + here)
                target = out.at[pl.ds(unit * UNIT, UNIT), rows, :, columns]
                copies.append(pltpu.make_async_copy(block.at[:, i], target, sems.at[len(copies)]))
        for copy in copies:
            copy.start()
        for copy in copies:
            copy.wait()

    operands = [place] + blocks
    specs = [SMEM] + [VMEM] * len(blocks)
    aliases = {}
    if whole is not None:
        aliases = {len(operands): 0}
        operands.append(whole)
        specs.append(HBM)
    return pl.pallas_call(
        kernel,
        out_shape=jax.ShapeDtypeStruct((LAYERS, 16, ROWS_HERE, WIDTH), jnp.bfloat16),
        in_specs=specs,
        out_specs=HBM,
        scratch_shapes=[pltpu.SemaphoreType.DMA((4 * len(blocks),))],
        input_output_aliases=aliases,
        compiler_params=pltpu.CompilerParams(vmem_limit_bytes=VMEM_LIMIT),
        cost_estimate=cost(0, 2 * sum(b.size * 2 for b in blocks)),
    )(*operands)


def move(x, step):
    pairs = []
    for device in range(128):
        z, core, y, u = device // 32, device // 16 % 2, device // 4 % 4, device % 4
        z, core, y, u = step(z, core, y, u)
        pairs.append((device, (z % 4 * 2 + core) * 16 + y % 4 * 4 + u % 4))
    return lax.ppermute(x, ("rep", "fsdp"), pairs)


def swap(x):
    return move(x, lambda z, core, y, u: (z, 1 - core, y, u))


def ring_z(x):
    return move(x, lambda z, core, y, u: (z + 1 - 2 * core, core, y, u))


def along_first(x, by):
    return move(x, lambda z, core, y, u: (z, core, y, u + by) if core == 0 else (z, core, y + by, u))


def along_second(x, by):
    return move(x, lambda z, core, y, u: (z, core, y + by, u) if core == 0 else (z, core, y, u + by))


def spread(x, along, unit):
    ahead, behind = along(x, 1), along(x, -1)
    across = along(ahead, 1) if unit == 0 else along(behind, -1)
    return [(ahead, 1), (behind, 3), (across, 2)]


def shards(gradient, momentum, params, bands):
    rep, fsdp = lax.axis_index("rep"), lax.axis_index("fsdp")
    place = jnp.stack(
        [lax.shift_right_logical(rep, 1), lax.shift_right_logical(fsdp, 2), fsdp & 3, rep & 1]
    ).astype(jnp.int32)
    table = cosine_table()
    forward = split_table(np.kron(np.eye(WIDE // GROUP), table.T))
    inverse = split_table(np.kron(np.eye(WIDE // GROUP), table))
    blocks = HALF // GROUP
    by_layer = jnp.transpose(bands[0], (0, 3, 1, 2)).reshape(LAYERS, 2, ROWS_HERE, 2, blocks)
    by_layer = jnp.pad(jnp.transpose(by_layer, (0, 1, 3, 2, 4)), ((0, 0),) * 4 + ((0, LANES - blocks),))
    common = (place, by_layer, gradient, momentum, forward)

    theirs = pick(*common, range(UNITS), False)
    inverse_here = None
    updated, own = [], []
    for unit in range(UNITS):
        received = swap(theirs[unit])
        first = unit == 0
        picked = pick(*common, [unit], True, received, params, inverse if first else None)
        if first:
            inverse_here = picked[2]
        sums = [picked[0]]
        for _ in range(3):
            sums.append(ring_z(sums[-1]))
        updated.append(decode(sums, picked[1], inverse_here))
    near, far = [], []
    for unit in range(UNITS):
        block = updated[unit]
        block = bring_together(place, [(block, 0)] + spread(block, along_first, unit))
        ahead, behind, across = spread(block, along_second, unit)
        own.append((block, unit, 0))
        near += [(ahead[0], unit, 1), (behind[0], unit, 3)]
        far.append((across[0], unit, 2))

    new_momentum = None
    for unit in range(UNITS):
        new_momentum = keep_rest(*common, inverse_here, unit, new_momentum)

    whole = None
    for group in (own, near, far):
        items = [item + (0,) for item in group] + [(swap(item[0]),) + item[1:] + (1,) for item in group]
        whole = write_blocks(place, whole, items)
    return new_momentum, whole.reshape(LAYERS, 16 * ROWS_HERE, WIDTH)


def solution(mesh):
    in_specs = (
        P("rep", None, "fsdp", None),
        P("rep", None, "fsdp", None),
        P(None, "fsdp", None),
        P("rep", None, "fsdp", None, None),
    )
    out_specs = (P("rep", None, "fsdp", None), P())
    return jax.shard_map(shards, mesh=mesh, in_specs=in_specs, out_specs=out_specs, check_vma=False)
```

time: 557 us -> 106 us (0.19)
  waiting for transfers between devices: 190 us -> 31.6 us
  blocking collectives: 114 us -> 0 us
  matrix products: 105 us -> 0 us
  local copies, waits for them, and re-layouts: 108 us -> 7.92 us
  starting transfers between devices: 0.33 us -> 41.6 us
  Pallas kernels: 0 us -> 23 us
  other arithmetic: 21.3 us -> 0.08 us
  between operations: 14.3 us -> 0.99 us
    all_gather x4 -> x0, waiting for transfers between devices: 188 us -> none  [update_layers(): gathered = lax.all_gather(updated, 'fsdp', axis=1, tiled=True)]
    all_gather x8 -> x0, blocking collectives: 114 us -> none  [the longest x4 57.4 us: update_layers(): lax.all_gather(picked[None].astype(jnp.bfloat16), 'rep', axis=0, tiled=True)]
    dot_general x20 -> x0, matrix products: 105 us -> none  [the longest x4 36.4 us: update_layers(): picked = jnp.einsum('lrcsb,lrcbj->lrcsj', chosen, banded, precision=highest)]
    another operation x8 -> x0, local copies, waits for them, and re-layouts: 44.9 us -> none
    ppermute x0 -> x28, starting transfers between devices: none -> 41.6 us  [move(): return lax.ppermute(x, ('rep', 'fsdp'), pairs)]
    ppermute x0 -> x28, waiting for transfers between devices: none -> 31.6 us  [move(): return lax.ppermute(x, ('rep', 'fsdp'), pairs)]
    pallas_call x0 -> x12, Pallas kernels: none -> 23 us  [the longest x3 8.65 us: write_blocks(): pl.pallas_call(kernel, out_shape=jax.ShapeDtypeStruct((LAYERS, 16, ROWS_H...]
    div x4 -> x0, local copies, waits for them, and re-layouts: 22.1 us -> none  [decode_update(): jnp.einsum('alrcsb,alrcsj->lrcbj', chosen, values, precision=highest)]
  transfers between devices with their start and end apart: 4 -> 28, of which waited for: 4 -> 12; matrix products, arithmetic and copies ran while one was open for 2% -> 0% of each run, Pallas kernels for 0% -> 17%
where the time goes in v3:
time: 106 us; the launch traced here: 105 us
  starting transfers between devices  41.6 us (39%)
  waiting for transfers between devices  31.6 us (30%)
  Pallas kernels  23 us (22%)
  local copies, waits for them, and re-layouts  7.92 us (7%)
    ppermute x28, starting transfers between devices, move(): return lax.ppermute(x, ('rep', 'fsdp'), pairs)  41.6 us
    ppermute x28, waiting for transfers between devices, move(): return lax.ppermute(x, ('rep', 'fsdp'), pairs)  31.6 us
    pallas_call x3, Pallas kernels, write_blocks(): pl.pallas_call(kernel, out_shape=jax.ShapeDtypeStruct((LAYERS, 16, ROWS_H...  8.65 us
    unnamed x18, local copies, waits for them, and re-layouts  6.89 us
    pallas_call x2, Pallas kernels, keep_rest(): pl.pallas_call(kernel, out_shape=jax.ShapeDtypeStruct(momentum.shape, jnp...  6.65 us
    pallas_call x3, Pallas kernels, pick(): pl.pallas_call(kernel, out_shape=out_shapes, in_specs=[SMEM, VMEM, HBM, H...  5.7 us
  transfers between devices with their start and end apart: 28, of which 12 were waited for; matrix products, arithmetic and copies ran while one was open for 0% of the time, Pallas kernels for 17%

profile of v3, /device:TPU:1, one launch (start us, length us, event | category | flops | bytes accessed | tf_op | source)
XLA Modules:
  0.0 105.2 jit_solution(15842016740603155065)
XLA Ops:
  0.6 1.0 reshape.12
  1.8 1.5 %copy-done = f32[1,4,8,13824]{3,2,1,0:T(8,128)S(1)} copy-done((f32[1,4,8,13824]{3,2,1,0:T(8,128)S(1)}, f32[1,4,8,13824]{3,2,1,0:T(8,128)}, u32[]{:S(2)}) %copy-start) | copy-done | bytes 1769496
  3.3 1.2 %copy-done.2 = bf16[1,4,8,13824]{3,2,1,0:T(8,128)(2,1)S(1)} copy-done((bf16[1,4,8,13824]{3,2,1,0:T(8,128)(2,1)S(1)}, bf16[1,4,8,13824]{3,2,1,0:T(8,128)(2,1)}, u32[]{:S(2)}) %copy-start.2) | copy-done | bytes 884760
  4.4 0.9 copy-done.4
  5.4 2.4 %shard_map.95 = (bf16[2,8,6912]{2,1,0:T(8,128)(2,1)S(1)}, bf16[2,8,6912]{2,1,0:T(8,128)(2,1)S(1)}) custom-call(s32[4]{0:T(128)S(1)} %pad_add_fusion.place_ref, s32[4,2,2,8,128]{4,3,2,1,0:T(8,128)S(1)} %pad.4.bands_ref, bf16[1,4,8,13824]{3,2,1,0:T(8,128)(2,1)S(1)} %copy-done.2, f32[1,4,8,13824]{3,2,1,0:T(8,128)S(1)} %copy-done, bf16[2,256,256]{2,1,0:T(8,128)(2,1)S(1)} %copy-done.4), custom_call_target="tpu_custom_call" | custom-call | flops 339738624 | bytes 3000000 | tf_op jit(solution)/shard_map/pallas_call | solution.py:132
  7.8 1.5 %collective-permute-start.9 = (bf16[2,8,6912]{2,1,0:T(8,128)(2,1)S(1)}, bf16[2,8,6912]{2,1,0:T(8,128)(2,1)S(1)}, u32[]{:S(2)}, u32[]{:S(2)}) collective-permute-start(bf16[2,8,6912]{2,1,0:T(8,128)(2,1)S(1)} %get-tuple-element.13), channel_id=1, source_target_pairs={{0,16},{1,17},{2,18},{3,19},{4,20},{5,21},{6,22},{7,23},{8,24},{9,... | collective-permute-start | bytes 663560 | tf_op jit(solution)/shard_map/ppermute | solution.py:300
  9.4 1.0 collective-permute-done.9.refs_0_
  10.4 1.2 %copy-done.6 = bf16[4,8,13824]{2,1,0:T(8,128)(2,1)S(1)} copy-done((bf16[4,8,13824]{2,1,0:T(8,128)(2,1)S(1)}, bf16[4,8,13824]{2,1,0:T(8,128)(2,1)}, u32[]{:S(2)}) %copy-start.6) | copy-done | bytes 884760
  11.5 1.6 %shard_map.101 = (bf16[2,8,6912]{2,1,0:T(8,128)(2,1)S(1)}, bf16[2,8,6912]{2,1,0:T(8,128)(2,1)S(1)}) custom-call(s32[4]{0:T(128)S(1)} %pad_add_fusion.place_ref, s32[4,2,2,8,128]{4,3,2,1,0:T(8,128)S(1)} %pad.4.bands_ref, bf16[1,4,8,13824]{3,2,1,0:T(8,128)(2,1)S(1)} %copy-done.2, f32[1,4,8,13824]{3,2,1,0:T(8,128)S(1)} %copy-done, ...), custom_call_target="tpu_custom_call" | custom-call | flops 169869312 | bytes 1500000 | tf_op jit(solution)/shard_map/pallas_call | solution.py:132
  13.2 3.9 %collective-permute-start.10 = (bf16[2,8,6912]{2,1,0:T(8,128)(2,1)S(1)}, bf16[2,8,6912]{2,1,0:T(8,128)(2,1)S(1)}, u32[]{:S(2)}, u32[]{:S(2)}) collective-permute-start(bf16[2,8,6912]{2,1,0:T(8,128)(2,1)S(1)} %get-tuple-element.14.first), channel_id=1, source_target_pairs={{0,32},{1,33},{2,34},{3,35},{4,36},{5,37},{6,38},{7,39},{8,40},{9,... | collective-permute-start | bytes 663560 | tf_op jit(solution)/shard_map/ppermute | solution.py:300
  17.1 1.2 %copy-done.7 = bf16[4,8,13824]{2,1,0:T(8,128)(2,1)S(1)} copy-done((bf16[4,8,13824]{2,1,0:T(8,128)(2,1)S(1)}, bf16[4,8,13824]{2,1,0:T(8,128)(2,1)}, u32[]{:S(2)}) %copy-start.7) | copy-done | bytes 884760
  18.3 0.9 copy-done.8
  19.2 1.7 %shard_map.96 = (bf16[2,8,6912]{2,1,0:T(8,128)(2,1)S(1)}, bf16[2,8,6912]{2,1,0:T(8,128)(2,1)S(1)}, bf16[2,256,256]{2,1,0:T(8,128)(2,1)S(1)}) custom-call(s32[4]{0:T(128)S(1)} %pad_add_fusion.place_ref, s32[4,2,2,8,128]{4,3,2,1,0:T(8,128)S(1)} %pad.4.bands_ref, bf16[1,4,8,13824]{3,2,1,0:T(8,128)(2,1)S(1)} %copy-done.2, f32[1,4,8,13824]{3,2,1,0:T(8,128)S(1)} %copy-done, ...), custom_call_target="tpu_custom_call" | custom-call | flops 169869312 | bytes 1500000 | tf_op jit(solution)/shard_map/pallas_call | solution.py:132
  21.1 2.0 %collective-permute-start.11 = (bf16[2,8,6912]{2,1,0:T(8,128)(2,1)S(1)}, bf16[2,8,6912]{2,1,0:T(8,128)(2,1)S(1)}, u32[]{:S(2)}, u32[]{:S(2)}) collective-permute-start(bf16[2,8,6912]{2,1,0:T(8,128)(2,1)S(1)} %collective-permute-done.10.second), channel_id=1, source_target_pairs={{0,32},{1,33},{2,34},{3,35},{4,36},{5,37},{6,38},{7,39},{8,40},{9,... | collective-permute-start | bytes 663560 | tf_op jit(solution)/shard_map/ppermute | solution.py:300
  23.1 2.9 %collective-permute-done.1.second = bf16[2,8,6912]{2,1,0:T(8,128)(2,1)S(1)} collective-permute-done((bf16[2,8,6912]{2,1,0:T(8,128)(2,1)S(1)}, bf16[2,8,6912]{2,1,0:T(8,128)(2,1)S(1)}, u32[]{:S(2)}, u32[]{:S(2)}) %collective-permute-start.1) | collective-permute-done | bytes 221216 | tf_op jit(solution)/shard_map/ppermute | solution.py:300
  26.1 1.0 collective-permute-start.2
  27.1 1.3 %collective-permute-done.11.third = bf16[2,8,6912]{2,1,0:T(8,128)(2,1)S(1)} collective-permute-done((bf16[2,8,6912]{2,1,0:T(8,128)(2,1)S(1)}, bf16[2,8,6912]{2,1,0:T(8,128)(2,1)S(1)}, u32[]{:S(2)}, u32[]{:S(2)}) %collective-permute-start.11) | collective-permute-done | bytes 221216 | tf_op jit(solution)/shard_map/ppermute | solution.py:300
  28.4 1.0 collective-permute-start.12
  29.5 1.7 %collective-permute-done.2.third = bf16[2,8,6912]{2,1,0:T(8,128)(2,1)S(1)} collective-permute-done((bf16[2,8,6912]{2,1,0:T(8,128)(2,1)S(1)}, bf16[2,8,6912]{2,1,0:T(8,128)(2,1)S(1)}, u32[]{:S(2)}, u32[]{:S(2)}) %collective-permute-start.2) | collective-permute-done | bytes 221216 | tf_op jit(solution)/shard_map/ppermute | solution.py:300
  31.1 2.0 %collective-permute-start.3 = (bf16[2,8,6912]{2,1,0:T(8,128)(2,1)S(1)}, bf16[2,8,6912]{2,1,0:T(8,128)(2,1)S(1)}, u32[]{:S(2)}, u32[]{:S(2)}) collective-permute-start(bf16[2,8,6912]{2,1,0:T(8,128)(2,1)S(1)} %collective-permute-done.2.third), channel_id=1, source_target_pairs={{0,32},{1,33},{2,34},{3,35},{4,36},{5,37},{6,38},{7,39},{8,40},{9,... | collective-permute-start | bytes 663560 | tf_op jit(solution)/shard_map/ppermute | solution.py:300
  33.9 2.8 %collective-permute-start.14 = (bf16[2,8,6912]{2,1,0:T(8,128)(2,1)S(1)}, bf16[2,8,6912]{2,1,0:T(8,128)(2,1)S(1)}, u32[]{:S(2)}, u32[]{:S(2)}) collective-permute-start(bf16[2,8,6912]{2,1,0:T(8,128)(2,1)S(1)} %shard_map.102.refs_0_), channel_id=1, source_target_pairs={{0,3},{1,0},{2,1},{3,2},{4,7},{5,4},{6,5},{7,6},{8,11},{9,8},{10,9... | collective-permute-start | bytes 663560 | tf_op jit(solution)/shard_map/ppermute | solution.py:300
  37.1 0.6 collective-permute-start.4
  37.7 1.3 %collective-permute-start.13 = (bf16[2,8,6912]{2,1,0:T(8,128)(2,1)S(1)}, bf16[2,8,6912]{2,1,0:T(8,128)(2,1)S(1)}, u32[]{:S(2)}, u32[]{:S(2)}) collective-permute-start(bf16[2,8,6912]{2,1,0:T(8,128)(2,1)S(1)} %shard_map.102.refs_0_), channel_id=1, source_target_pairs={{0,1},{1,2},{2,3},{3,0},{4,5},{5,6},{6,7},{7,4},{8,9},{9,10},{10,1... | collective-permute-start | bytes 663560 | tf_op jit(solution)/shard_map/ppermute | solution.py:300
  39.0 0.6 collective-permute-done.14.refs_2_
  39.6 3.4 %collective-permute-start.15 = (bf16[2,8,6912]{2,1,0:T(8,128)(2,1)S(1)}, bf16[2,8,6912]{2,1,0:T(8,128)(2,1)S(1)}, u32[]{:S(2)}, u32[]{:S(2)}) collective-permute-start(bf16[2,8,6912]{2,1,0:T(8,128)(2,1)S(1)} %collective-permute-done.14.refs_2_), channel_id=1, source_target_pairs={{0,3},{1,0},{2,1},{3,2},{4,7},{5,4},{6,5},{7,6},{8,11},{9,8},{10,9... | collective-permute-start | bytes 663560 | tf_op jit(solution)/shard_map/ppermute | solution.py:300
  43.1 1.3 %collective-permute-start.6 = (bf16[2,8,6912]{2,1,0:T(8,128)(2,1)S(1)}, bf16[2,8,6912]{2,1,0:T(8,128)(2,1)S(1)}, u32[]{:S(2)}, u32[]{:S(2)}) collective-permute-start(bf16[2,8,6912]{2,1,0:T(8,128)(2,1)S(1)} %collective-permute-done.4.refs_1_), channel_id=1, source_target_pairs={{0,1},{1,2},{2,3},{3,0},{4,5},{5,6},{6,7},{7,4},{8,9},{9,10},{10,1... | collective-permute-start | bytes 663560 | tf_op jit(solution)/shard_map/ppermute | solution.py:300
  44.4 1.4 %collective-permute-done.13.refs_1_ = bf16[2,8,6912]{2,1,0:T(8,128)(2,1)S(1)} collective-permute-done((bf16[2,8,6912]{2,1,0:T(8,128)(2,1)S(1)}, bf16[2,8,6912]{2,1,0:T(8,128)(2,1)S(1)}, u32[]{:S(2)}, u32[]{:S(2)}) %collective-permute-start.13) | collective-permute-done | bytes 221216 | tf_op jit(solution)/shard_map/ppermute | solution.py:300
  45.9 0.6 shard_map.103.refs_1_
  46.5 5.1 %collective-permute-start.27 = (bf16[2,4,8,6912]{3,2,1,0:T(8,128)(2,1)S(1)}, bf16[2,4,8,6912]{3,2,1,0:T(8,128)(2,1)S(1)}, u32[]{:S(2)}, u32[]{:S(2)}) collective-permute-start(bf16[2,4,8,6912]{3,2,1,0:T(8,128)(2,1)S(1)} %shard_map.103.refs_1_), channel_id=1, source_target_pairs={{0,16},{1,17},{2,18},{3,19},{4,20},{5,21},{6,22},{7,23},{8,24},{9,... | collective-permute-start | bytes 2654216 | tf_op jit(solution)/shard_map/ppermute | solution.py:300
  51.9 2.4 %collective-permute-start.16 = (bf16[2,4,8,6912]{3,2,1,0:T(8,128)(2,1)S(1)}, bf16[2,4,8,6912]{3,2,1,0:T(8,128)(2,1)S(1)}, u32[]{:S(2)}, u32[]{:S(2)}) collective-permute-start(bf16[2,4,8,6912]{3,2,1,0:T(8,128)(2,1)S(1)} %shard_map.103.refs_1_), channel_id=1, source_target_pairs={{0,12},{1,13},{2,14},{3,15},{4,0},{5,1},{6,2},{7,3},{8,4},{9,5},{1... | collective-permute-start | bytes 2654216 | tf_op jit(solution)/shard_map/ppermute | solution.py:300
  54.3 0.6 shard_map.100.refs_0_
  55.0 3.0 %collective-permute-start.26 = (bf16[2,4,8,6912]{3,2,1,0:T(8,128)(2,1)S(1)}, bf16[2,4,8,6912]{3,2,1,0:T(8,128)(2,1)S(1)}, u32[]{:S(2)}, u32[]{:S(2)}) collective-permute-start(bf16[2,4,8,6912]{3,2,1,0:T(8,128)(2,1)S(1)} %shard_map.100.refs_0_), channel_id=1, source_target_pairs={{0,16},{1,17},{2,18},{3,19},{4,20},{5,21},{6,22},{7,23},{8,24},{9,... | collective-permute-start | bytes 2654216 | tf_op jit(solution)/shard_map/ppermute | solution.py:300
  57.9 0.5 collective-permute-start.20
  58.5 6.5 %collective-permute-done.21.refs_2_ = bf16[2,4,8,6912]{3,2,1,0:T(8,128)(2,1)S(1)} collective-permute-done((bf16[2,4,8,6912]{3,2,1,0:T(8,128)(2,1)S(1)}, bf16[2,4,8,6912]{3,2,1,0:T(8,128)(2,1)S(1)}, u32[]{:S(2)}, u32[]{:S(2)}) %collective-permute-start.21) | collective-permute-done | bytes 884768 | tf_op jit(solution)/shard_map/ppermute | solution.py:300
  65.0 0.9 collective-permute-start.24
  65.9 2.5 %collective-permute-start.17 = (bf16[2,4,8,6912]{3,2,1,0:T(8,128)(2,1)S(1)}, bf16[2,4,8,6912]{3,2,1,0:T(8,128)(2,1)S(1)}, u32[]{:S(2)}, u32[]{:S(2)}) collective-permute-start(bf16[2,4,8,6912]{3,2,1,0:T(8,128)(2,1)S(1)} %collective-permute-done.16.refs_3_), channel_id=1, source_target_pairs={{0,12},{1,13},{2,14},{3,15},{4,0},{5,1},{6,2},{7,3},{8,4},{9,5},{1... | collective-permute-start | bytes 2654216 | tf_op jit(solution)/shard_map/ppermute | solution.py:300
  68.4 6.1 %collective-permute-done.7.refs_0_ = bf16[2,4,8,6912]{3,2,1,0:T(8,128)(2,1)S(1)} collective-permute-done((bf16[2,4,8,6912]{3,2,1,0:T(8,128)(2,1)S(1)}, bf16[2,4,8,6912]{3,2,1,0:T(8,128)(2,1)S(1)}, u32[]{:S(2)}, u32[]{:S(2)}) %collective-permute-start.7) | collective-permute-done | bytes 884768 | tf_op jit(solution)/shard_map/ppermute | solution.py:300
  74.5 1.3 %collective-permute-start.25 = (bf16[2,4,8,6912]{3,2,1,0:T(8,128)(2,1)S(1)}, bf16[2,4,8,6912]{3,2,1,0:T(8,128)(2,1)S(1)}, u32[]{:S(2)}, u32[]{:S(2)}) collective-permute-start(bf16[2,4,8,6912]{3,2,1,0:T(8,128)(2,1)S(1)} %collective-permute-done.16.refs_3_), channel_id=1, source_target_pairs={{0,16},{1,17},{2,18},{3,19},{4,20},{5,21},{6,22},{7,23},{8,24},{9,... | collective-permute-start | bytes 2654216 | tf_op jit(solution)/shard_map/ppermute | solution.py:300
  75.9 0.4 collective-permute-start.23
  76.3 6.9 %collective-permute-done.17.refs_1_ = bf16[2,4,8,6912]{3,2,1,0:T(8,128)(2,1)S(1)} collective-permute-done((bf16[2,4,8,6912]{3,2,1,0:T(8,128)(2,1)S(1)}, bf16[2,4,8,6912]{3,2,1,0:T(8,128)(2,1)S(1)}, u32[]{:S(2)}, u32[]{:S(2)}) %collective-permute-start.17) | collective-permute-done | bytes 884768 | tf_op jit(solution)/shard_map/ppermute | solution.py:300
  83.2 2.0 %collective-permute-start.19 = (bf16[2,4,8,6912]{3,2,1,0:T(8,128)(2,1)S(1)}, bf16[2,4,8,6912]{3,2,1,0:T(8,128)(2,1)S(1)}, u32[]{:S(2)}, u32[]{:S(2)}) collective-permute-start(bf16[2,4,8,6912]{3,2,1,0:T(8,128)(2,1)S(1)} %collective-permute-done.17.refs_1_), channel_id=1, source_target_pairs={{0,16},{1,17},{2,18},{3,19},{4,20},{5,21},{6,22},{7,23},{8,24},{9,... | collective-permute-start | bytes 2654216 | tf_op jit(solution)/shard_map/ppermute | solution.py:300
  85.3 2.6 %collective-permute-done.8.refs_0_ = bf16[2,4,8,6912]{3,2,1,0:T(8,128)(2,1)S(1)} collective-permute-done((bf16[2,4,8,6912]{3,2,1,0:T(8,128)(2,1)S(1)}, bf16[2,4,8,6912]{3,2,1,0:T(8,128)(2,1)S(1)}, u32[]{:S(2)}, u32[]{:S(2)}) %collective-permute-start.8) | collective-permute-done | bytes 884768 | tf_op jit(solution)/shard_map/ppermute | solution.py:300
  87.9 1.8 %collective-permute-start.18 = (bf16[2,4,8,6912]{3,2,1,0:T(8,128)(2,1)S(1)}, bf16[2,4,8,6912]{3,2,1,0:T(8,128)(2,1)S(1)}, u32[]{:S(2)}, u32[]{:S(2)}) collective-permute-start(bf16[2,4,8,6912]{3,2,1,0:T(8,128)(2,1)S(1)} %collective-permute-done.8.refs_0_), channel_id=1, source_target_pairs={{0,16},{1,17},{2,18},{3,19},{4,20},{5,21},{6,22},{7,23},{8,24},{9,... | collective-permute-start | bytes 2654216 | tf_op jit(solution)/shard_map/ppermute | solution.py:300
  89.7 3.3 %shard_map.97.refs_0_ = f32[1,4,8,13824]{3,2,1,0:T(8,128)} custom-call(s32[4,2,2,8,128]{4,3,2,1,0:T(8,128)S(1)} %pad.4.bands_ref, bf16[1,4,8,13824]{3,2,1,0:T(8,128)(2,1)S(1)} %copy-done.3, f32[1,4,8,13824]{3,2,1,0:T(8,128)S(1)} %copy-done.1, bf16[2,256,256]{2,1,0:T(8,128)(2,1)S(1)} %copy-done.5, bf16[2,256,256]{2,1,0:T(8,128)(2,1)S(1)} %get-tuple-element.10.inverse_ref), custom_call_target="tpu_custom_call" | custom-call | flops 679477248 | bytes 3000000 | tf_op jit(solution)/shard_map/pallas_call | solution.py:190
  93.0 3.3 %shard_map.98 = f32[1,4,8,13824]{3,2,1,0:T(8,128)} custom-call(s32[4,2,2,8,128]{4,3,2,1,0:T(8,128)S(1)} %pad.4.bands_ref, bf16[1,4,8,13824]{3,2,1,0:T(8,128)(2,1)S(1)} %copy-done.3, f32[1,4,8,13824]{3,2,1,0:T(8,128)S(1)} %copy-done.1, bf16[2,256,256]{2,1,0:T(8,128)(2,1)S(1)} %copy-done.5, ...), custom_call_target="tpu_custom_call", output_to_operand_aliasing={{}: (5, {})} | custom-call | flops 679477248 | bytes 3000000 | tf_op jit(solution)/shard_map/pallas_call | solution.py:190
  96.4 2.5 %shard_map.104.refs_8_ = bf16[4,16,8,13824]{3,2,1,0:T(8,128)(2,1)} custom-call(s32[4]{0:T(128)S(1)} %pad_add_fusion.place_ref, bf16[2,4,8,6912]{3,2,1,0:T(8,128)(2,1)S(1)} %shard_map.100.refs_0_, bf16[2,4,8,6912]{3,2,1,0:T(8,128)(2,1)S(1)} %shard_map.103.refs_1_, bf16[2,4,8,6912]{3,2,1,0:T(8,128)(2,1)S(1)} %collective-permute-done.26.refs_2_, ...), custom_call_target="tpu_custom_call" | custom-call | bytes 7077888 | tf_op jit(solution)/shard_map/pallas_call | solution.py:282
  98.9 3.7 %shard_map.105.refs_4_ = bf16[4,16,8,13824]{3,2,1,0:T(8,128)(2,1)} custom-call(s32[4]{0:T(128)S(1)} %pad_add_fusion.place_ref, bf16[2,4,8,6912]{3,2,1,0:T(8,128)(2,1)S(1)} %collective-permute-done.7.refs_0_, bf16[2,4,8,6912]{3,2,1,0:T(8,128)(2,1)S(1)} %collective-permute-done.20.refs_1_, ...), custom_call_target="tpu_custom_call", output_to_operand_aliasing={{}: (9, {})} | custom-call | bytes 14155776 | tf_op jit(solution)/shard_map/pallas_call | solution.py:282
  102.6 2.5 %shard_map.106 = bf16[4,16,8,13824]{3,2,1,0:T(8,128)(2,1)} custom-call(s32[4]{0:T(128)S(1)} %pad_add_fusion.place_ref, bf16[2,4,8,6912]{3,2,1,0:T(8,128)(2,1)S(1)} %collective-permute-done.8.refs_0_, bf16[2,4,8,6912]{3,2,1,0:T(8,128)(2,1)S(1)} %collective-permute-done.17.refs_1_, ...), custom_call_target="tpu_custom_call", output_to_operand_aliasing={{}: (5, {})} | custom-call | bytes 7077888 | tf_op jit(solution)/shard_map/pallas_call | solution.py:282
  (42 shorter events, 2.3 us)
Async XLA Ops:
  0.6 89.1 %copy-start.5 = (bf16[2,256,256]{2,1,0:T(8,128)(2,1)S(1)}, bf16[2,256,256]{2,1,0:T(8,128)(2,1)}, u32[]{:S(2)}) copy-start(bf16[2,256,256]{2,1,0:T(8,128)(2,1)} %constant.35.forward_ref) | copy-start | bytes 786436
  1.8 1.5 %copy-start = (f32[1,4,8,13824]{3,2,1,0:T(8,128)S(1)}, f32[1,4,8,13824]{3,2,1,0:T(8,128)}, u32[]{:S(2)}) copy-start(f32[1,4,8,13824]{3,2,1,0:T(8,128)} %momentum_ref.9) | copy-start | bytes 5308420
  3.3 1.2 %copy-start.2 = (bf16[1,4,8,13824]{3,2,1,0:T(8,128)(2,1)S(1)}, bf16[1,4,8,13824]{3,2,1,0:T(8,128)(2,1)}, u32[]{:S(2)}) copy-start(bf16[1,4,8,13824]{3,2,1,0:T(8,128)(2,1)} %gradient_ref.9) | copy-start | bytes 2654212
  4.4 0.9 copy-start.4
  5.4 84.3 %copy-start.1 = (f32[1,4,8,13824]{3,2,1,0:T(8,128)S(1)}, f32[1,4,8,13824]{3,2,1,0:T(8,128)}, u32[]{:S(2)}) copy-start(f32[1,4,8,13824]{3,2,1,0:T(8,128)} %momentum_ref.9) | copy-start | bytes 5308420
  5.4 84.3 %copy-start.3 = (bf16[1,4,8,13824]{3,2,1,0:T(8,128)(2,1)S(1)}, bf16[1,4,8,13824]{3,2,1,0:T(8,128)(2,1)}, u32[]{:S(2)}) copy-start(bf16[1,4,8,13824]{3,2,1,0:T(8,128)(2,1)} %gradient_ref.9) | copy-start | bytes 2654212
  7.8 2.6 %collective-permute-start.9 = (bf16[2,8,6912]{2,1,0:T(8,128)(2,1)S(1)}, bf16[2,8,6912]{2,1,0:T(8,128)(2,1)S(1)}, u32[]{:S(2)}, u32[]{:S(2)}) collective-permute-start(bf16[2,8,6912]{2,1,0:T(8,128)(2,1)S(1)} %get-tuple-element.13), channel_id=1, source_target_pairs={{0,16},{1,17},{2,18},{3,19},{4,20},{5,21},{6,22},{7,23},{8,24},{9,... | collective-permute-start | bytes 663560 | tf_op jit(solution)/shard_map/ppermute | solution.py:300
  9.3 7.8 %collective-permute-start = (bf16[2,8,6912]{2,1,0:T(8,128)(2,1)S(1)}, bf16[2,8,6912]{2,1,0:T(8,128)(2,1)S(1)}, u32[]{:S(2)}, u32[]{:S(2)}) collective-permute-start(bf16[2,8,6912]{2,1,0:T(8,128)(2,1)S(1)} %get-tuple-element.9), channel_id=1, source_target_pairs={{0,16},{1,17},{2,18},{3,19},{4,20},{5,21},{6,22},{7,23},{8,24},{9,... | collective-permute-start | bytes 663560 | tf_op jit(solution)/shard_map/ppermute | solution.py:300
  10.4 1.2 %copy-start.6 = (bf16[4,8,13824]{2,1,0:T(8,128)(2,1)S(1)}, bf16[4,8,13824]{2,1,0:T(8,128)(2,1)}, u32[]{:S(2)}) copy-start(bf16[4,8,13824]{2,1,0:T(8,128)(2,1)} %refs_1_.3) | copy-start | bytes 2654212
  13.2 7.9 %collective-permute-start.10 = (bf16[2,8,6912]{2,1,0:T(8,128)(2,1)S(1)}, bf16[2,8,6912]{2,1,0:T(8,128)(2,1)S(1)}, u32[]{:S(2)}, u32[]{:S(2)}) collective-permute-start(bf16[2,8,6912]{2,1,0:T(8,128)(2,1)S(1)} %get-tuple-element.14.first), channel_id=1, source_target_pairs={{0,32},{1,33},{2,34},{3,35},{4,36},{5,37},{6,38},{7,39},{8,40},{9,... | collective-permute-start | bytes 663560 | tf_op jit(solution)/shard_map/ppermute | solution.py:300
  17.1 1.2 %copy-start.7 = (bf16[4,8,13824]{2,1,0:T(8,128)(2,1)S(1)}, bf16[4,8,13824]{2,1,0:T(8,128)(2,1)}, u32[]{:S(2)}) copy-start(bf16[4,8,13824]{2,1,0:T(8,128)(2,1)} %refs_1_.3) | copy-start | bytes 2654212
  18.3 0.9 copy-start.8
  20.9 5.1 %collective-permute-start.1 = (bf16[2,8,6912]{2,1,0:T(8,128)(2,1)S(1)}, bf16[2,8,6912]{2,1,0:T(8,128)(2,1)S(1)}, u32[]{:S(2)}, u32[]{:S(2)}) collective-permute-start(bf16[2,8,6912]{2,1,0:T(8,128)(2,1)S(1)} %get-tuple-element.11.first), channel_id=1, source_target_pairs={{0,32},{1,33},{2,34},{3,35},{4,36},{5,37},{6,38},{7,39},{8,40},{9,... | collective-permute-start | bytes 663560 | tf_op jit(solution)/shard_map/ppermute | solution.py:300
  21.1 7.3 %collective-permute-start.11 = (bf16[2,8,6912]{2,1,0:T(8,128)(2,1)S(1)}, bf16[2,8,6912]{2,1,0:T(8,128)(2,1)S(1)}, u32[]{:S(2)}, u32[]{:S(2)}) collective-permute-start(bf16[2,8,6912]{2,1,0:T(8,128)(2,1)S(1)} %collective-permute-done.10.second), channel_id=1, source_target_pairs={{0,32},{1,33},{2,34},{3,35},{4,36},{5,37},{6,38},{7,39},{8,40},{9,... | collective-permute-start | bytes 663560 | tf_op jit(solution)/shard_map/ppermute | solution.py:300
  26.1 5.1 %collective-permute-start.2 = (bf16[2,8,6912]{2,1,0:T(8,128)(2,1)S(1)}, bf16[2,8,6912]{2,1,0:T(8,128)(2,1)S(1)}, u32[]{:S(2)}, u32[]{:S(2)}) collective-permute-start(bf16[2,8,6912]{2,1,0:T(8,128)(2,1)S(1)} %collective-permute-done.1.second), channel_id=1, source_target_pairs={{0,32},{1,33},{2,34},{3,35},{4,36},{5,37},{6,38},{7,39},{8,40},{9,... | collective-permute-start | bytes 663560 | tf_op jit(solution)/shard_map/ppermute | solution.py:300
  28.4 5.1 %collective-permute-start.12 = (bf16[2,8,6912]{2,1,0:T(8,128)(2,1)S(1)}, bf16[2,8,6912]{2,1,0:T(8,128)(2,1)S(1)}, u32[]{:S(2)}, u32[]{:S(2)}) collective-permute-start(bf16[2,8,6912]{2,1,0:T(8,128)(2,1)S(1)} %collective-permute-done.11.third), channel_id=1, source_target_pairs={{0,32},{1,33},{2,34},{3,35},{4,36},{5,37},{6,38},{7,39},{8,40},{9,... | collective-permute-start | bytes 663560 | tf_op jit(solution)/shard_map/ppermute | solution.py:300
  31.1 5.6 %collective-permute-start.3 = (bf16[2,8,6912]{2,1,0:T(8,128)(2,1)S(1)}, bf16[2,8,6912]{2,1,0:T(8,128)(2,1)S(1)}, u32[]{:S(2)}, u32[]{:S(2)}) collective-permute-start(bf16[2,8,6912]{2,1,0:T(8,128)(2,1)S(1)} %collective-permute-done.2.third), channel_id=1, source_target_pairs={{0,32},{1,33},{2,34},{3,35},{4,36},{5,37},{6,38},{7,39},{8,40},{9,... | collective-permute-start | bytes 663560 | tf_op jit(solution)/shard_map/ppermute | solution.py:300
  33.9 5.7 %collective-permute-start.14 = (bf16[2,8,6912]{2,1,0:T(8,128)(2,1)S(1)}, bf16[2,8,6912]{2,1,0:T(8,128)(2,1)S(1)}, u32[]{:S(2)}, u32[]{:S(2)}) collective-permute-start(bf16[2,8,6912]{2,1,0:T(8,128)(2,1)S(1)} %shard_map.102.refs_0_), channel_id=1, source_target_pairs={{0,3},{1,0},{2,1},{3,2},{4,7},{5,4},{6,5},{7,6},{8,11},{9,8},{10,9... | collective-permute-start | bytes 663560 | tf_op jit(solution)/shard_map/ppermute | solution.py:300
  37.1 6.1 %collective-permute-start.4 = (bf16[2,8,6912]{2,1,0:T(8,128)(2,1)S(1)}, bf16[2,8,6912]{2,1,0:T(8,128)(2,1)S(1)}, u32[]{:S(2)}, u32[]{:S(2)}) collective-permute-start(bf16[2,8,6912]{2,1,0:T(8,128)(2,1)S(1)} %shard_map.99.refs_0_), channel_id=1, source_target_pairs={{0,1},{1,2},{2,3},{3,0},{4,5},{5,6},{6,7},{7,4},{8,9},{9,10},{10,1... | collective-permute-start | bytes 663560 | tf_op jit(solution)/shard_map/ppermute | solution.py:300
  37.7 8.1 %collective-permute-start.13 = (bf16[2,8,6912]{2,1,0:T(8,128)(2,1)S(1)}, bf16[2,8,6912]{2,1,0:T(8,128)(2,1)S(1)}, u32[]{:S(2)}, u32[]{:S(2)}) collective-permute-start(bf16[2,8,6912]{2,1,0:T(8,128)(2,1)S(1)} %shard_map.102.refs_0_), channel_id=1, source_target_pairs={{0,1},{1,2},{2,3},{3,0},{4,5},{5,6},{6,7},{7,4},{8,9},{9,10},{10,1... | collective-permute-start | bytes 663560 | tf_op jit(solution)/shard_map/ppermute | solution.py:300
  39.6 6.3 %collective-permute-start.15 = (bf16[2,8,6912]{2,1,0:T(8,128)(2,1)S(1)}, bf16[2,8,6912]{2,1,0:T(8,128)(2,1)S(1)}, u32[]{:S(2)}, u32[]{:S(2)}) collective-permute-start(bf16[2,8,6912]{2,1,0:T(8,128)(2,1)S(1)} %collective-permute-done.14.refs_2_), channel_id=1, source_target_pairs={{0,3},{1,0},{2,1},{3,2},{4,7},{5,4},{6,5},{7,6},{8,11},{9,8},{10,9... | collective-permute-start | bytes 663560 | tf_op jit(solution)/shard_map/ppermute | solution.py:300
  43.0 11.3 %collective-permute-start.5 = (bf16[2,8,6912]{2,1,0:T(8,128)(2,1)S(1)}, bf16[2,8,6912]{2,1,0:T(8,128)(2,1)S(1)}, u32[]{:S(2)}, u32[]{:S(2)}) collective-permute-start(bf16[2,8,6912]{2,1,0:T(8,128)(2,1)S(1)} %shard_map.99.refs_0_), channel_id=1, source_target_pairs={{0,3},{1,0},{2,1},{3,2},{4,7},{5,4},{6,5},{7,6},{8,11},{9,8},{10,9... | collective-permute-start | bytes 663560 | tf_op jit(solution)/shard_map/ppermute | solution.py:300
  43.1 11.2 %collective-permute-start.6 = (bf16[2,8,6912]{2,1,0:T(8,128)(2,1)S(1)}, bf16[2,8,6912]{2,1,0:T(8,128)(2,1)S(1)}, u32[]{:S(2)}, u32[]{:S(2)}) collective-permute-start(bf16[2,8,6912]{2,1,0:T(8,128)(2,1)S(1)} %collective-permute-done.4.refs_1_), channel_id=1, source_target_pairs={{0,1},{1,2},{2,3},{3,0},{4,5},{5,6},{6,7},{7,4},{8,9},{9,10},{10,1... | collective-permute-start | bytes 663560 | tf_op jit(solution)/shard_map/ppermute | solution.py:300
  46.5 11.5 %collective-permute-start.27 = (bf16[2,4,8,6912]{3,2,1,0:T(8,128)(2,1)S(1)}, bf16[2,4,8,6912]{3,2,1,0:T(8,128)(2,1)S(1)}, u32[]{:S(2)}, u32[]{:S(2)}) collective-permute-start(bf16[2,4,8,6912]{3,2,1,0:T(8,128)(2,1)S(1)} %shard_map.103.refs_1_), channel_id=1, source_target_pairs={{0,16},{1,17},{2,18},{3,19},{4,20},{5,21},{6,22},{7,23},{8,24},{9,... | collective-permute-start | bytes 2654216 | tf_op jit(solution)/shard_map/ppermute | solution.py:300
  51.6 13.4 %collective-permute-start.21 = (bf16[2,4,8,6912]{3,2,1,0:T(8,128)(2,1)S(1)}, bf16[2,4,8,6912]{3,2,1,0:T(8,128)(2,1)S(1)}, u32[]{:S(2)}, u32[]{:S(2)}) collective-permute-start(bf16[2,4,8,6912]{3,2,1,0:T(8,128)(2,1)S(1)} %shard_map.103.refs_1_), channel_id=1, source_target_pairs={{0,4},{1,5},{2,6},{3,7},{4,8},{5,9},{6,10},{7,11},{8,12},{9,13},{1... | collective-permute-start | bytes 2654216 | tf_op jit(solution)/shard_map/ppermute | solution.py:300
  51.9 14.0 %collective-permute-start.16 = (bf16[2,4,8,6912]{3,2,1,0:T(8,128)(2,1)S(1)}, bf16[2,4,8,6912]{3,2,1,0:T(8,128)(2,1)S(1)}, u32[]{:S(2)}, u32[]{:S(2)}) collective-permute-start(bf16[2,4,8,6912]{3,2,1,0:T(8,128)(2,1)S(1)} %shard_map.103.refs_1_), channel_id=1, source_target_pairs={{0,12},{1,13},{2,14},{3,15},{4,0},{5,1},{6,2},{7,3},{8,4},{9,5},{1... | collective-permute-start | bytes 2654216 | tf_op jit(solution)/shard_map/ppermute | solution.py:300
  54.9 19.6 %collective-permute-start.7 = (bf16[2,4,8,6912]{3,2,1,0:T(8,128)(2,1)S(1)}, bf16[2,4,8,6912]{3,2,1,0:T(8,128)(2,1)S(1)}, u32[]{:S(2)}, u32[]{:S(2)}) collective-permute-start(bf16[2,4,8,6912]{3,2,1,0:T(8,128)(2,1)S(1)} %shard_map.100.refs_0_), channel_id=1, source_target_pairs={{0,4},{1,5},{2,6},{3,7},{4,8},{5,9},{6,10},{7,11},{8,12},{9,13},{1... | collective-permute-start | bytes 2654216 | tf_op jit(solution)/shard_map/ppermute | solution.py:300
  55.0 19.5 %collective-permute-start.26 = (bf16[2,4,8,6912]{3,2,1,0:T(8,128)(2,1)S(1)}, bf16[2,4,8,6912]{3,2,1,0:T(8,128)(2,1)S(1)}, u32[]{:S(2)}, u32[]{:S(2)}) collective-permute-start(bf16[2,4,8,6912]{3,2,1,0:T(8,128)(2,1)S(1)} %shard_map.100.refs_0_), channel_id=1, source_target_pairs={{0,16},{1,17},{2,18},{3,19},{4,20},{5,21},{6,22},{7,23},{8,24},{9,... | collective-permute-start | bytes 2654216 | tf_op jit(solution)/shard_map/ppermute | solution.py:300
  57.9 17.9 %collective-permute-start.20 = (bf16[2,4,8,6912]{3,2,1,0:T(8,128)(2,1)S(1)}, bf16[2,4,8,6912]{3,2,1,0:T(8,128)(2,1)S(1)}, u32[]{:S(2)}, u32[]{:S(2)}) collective-permute-start(bf16[2,4,8,6912]{3,2,1,0:T(8,128)(2,1)S(1)} %shard_map.100.refs_0_), channel_id=1, source_target_pairs={{0,12},{1,13},{2,14},{3,15},{4,0},{5,1},{6,2},{7,3},{8,4},{9,5},{1... | collective-permute-start | bytes 2654216 | tf_op jit(solution)/shard_map/ppermute | solution.py:300
  65.0 10.9 %collective-permute-start.24 = (bf16[2,4,8,6912]{3,2,1,0:T(8,128)(2,1)S(1)}, bf16[2,4,8,6912]{3,2,1,0:T(8,128)(2,1)S(1)}, u32[]{:S(2)}, u32[]{:S(2)}) collective-permute-start(bf16[2,4,8,6912]{3,2,1,0:T(8,128)(2,1)S(1)} %collective-permute-done.21.refs_2_), channel_id=1, source_target_pairs={{0,16},{1,17},{2,18},{3,19},{4,20},{5,21},{6,22},{7,23},{8,24},{9,... | collective-permute-start | bytes 2654216 | tf_op jit(solution)/shard_map/ppermute | solution.py:300
  65.9 17.3 %collective-permute-start.17 = (bf16[2,4,8,6912]{3,2,1,0:T(8,128)(2,1)S(1)}, bf16[2,4,8,6912]{3,2,1,0:T(8,128)(2,1)S(1)}, u32[]{:S(2)}, u32[]{:S(2)}) collective-permute-start(bf16[2,4,8,6912]{3,2,1,0:T(8,128)(2,1)S(1)} %collective-permute-done.16.refs_3_), channel_id=1, source_target_pairs={{0,12},{1,13},{2,14},{3,15},{4,0},{5,1},{6,2},{7,3},{8,4},{9,5},{1... | collective-permute-start | bytes 2654216 | tf_op jit(solution)/shard_map/ppermute | solution.py:300
  74.5 13.4 %collective-permute-start.8 = (bf16[2,4,8,6912]{3,2,1,0:T(8,128)(2,1)S(1)}, bf16[2,4,8,6912]{3,2,1,0:T(8,128)(2,1)S(1)}, u32[]{:S(2)}, u32[]{:S(2)}) collective-permute-start(bf16[2,4,8,6912]{3,2,1,0:T(8,128)(2,1)S(1)} %collective-permute-done.7.refs_0_), channel_id=1, source_target_pairs={{0,4},{1,5},{2,6},{3,7},{4,8},{5,9},{6,10},{7,11},{8,12},{9,13},{1... | collective-permute-start | bytes 2654216 | tf_op jit(solution)/shard_map/ppermute | solution.py:300
  74.5 24.3 %collective-permute-start.25 = (bf16[2,4,8,6912]{3,2,1,0:T(8,128)(2,1)S(1)}, bf16[2,4,8,6912]{3,2,1,0:T(8,128)(2,1)S(1)}, u32[]{:S(2)}, u32[]{:S(2)}) collective-permute-start(bf16[2,4,8,6912]{3,2,1,0:T(8,128)(2,1)S(1)} %collective-permute-done.16.refs_3_), channel_id=1, source_target_pairs={{0,16},{1,17},{2,18},{3,19},{4,20},{5,21},{6,22},{7,23},{8,24},{9,... | collective-permute-start | bytes 2654216 | tf_op jit(solution)/shard_map/ppermute | solution.py:300
  75.8 23.1 %collective-permute-start.22 = (bf16[2,4,8,6912]{3,2,1,0:T(8,128)(2,1)S(1)}, bf16[2,4,8,6912]{3,2,1,0:T(8,128)(2,1)S(1)}, u32[]{:S(2)}, u32[]{:S(2)}) collective-permute-start(bf16[2,4,8,6912]{3,2,1,0:T(8,128)(2,1)S(1)} %collective-permute-done.7.refs_0_), channel_id=1, source_target_pairs={{0,16},{1,17},{2,18},{3,19},{4,20},{5,21},{6,22},{7,23},{8,24},{9,... | collective-permute-start | bytes 2654216 | tf_op jit(solution)/shard_map/ppermute | solution.py:300
  75.9 23.0 %collective-permute-start.23 = (bf16[2,4,8,6912]{3,2,1,0:T(8,128)(2,1)S(1)}, bf16[2,4,8,6912]{3,2,1,0:T(8,128)(2,1)S(1)}, u32[]{:S(2)}, u32[]{:S(2)}) collective-permute-start(bf16[2,4,8,6912]{3,2,1,0:T(8,128)(2,1)S(1)} %collective-permute-done.20.refs_1_), channel_id=1, source_target_pairs={{0,16},{1,17},{2,18},{3,19},{4,20},{5,21},{6,22},{7,23},{8,24},{9,... | collective-permute-start | bytes 2654216 | tf_op jit(solution)/shard_map/ppermute | solution.py:300
  83.2 19.4 %collective-permute-start.19 = (bf16[2,4,8,6912]{3,2,1,0:T(8,128)(2,1)S(1)}, bf16[2,4,8,6912]{3,2,1,0:T(8,128)(2,1)S(1)}, u32[]{:S(2)}, u32[]{:S(2)}) collective-permute-start(bf16[2,4,8,6912]{3,2,1,0:T(8,128)(2,1)S(1)} %collective-permute-done.17.refs_1_), channel_id=1, source_target_pairs={{0,16},{1,17},{2,18},{3,19},{4,20},{5,21},{6,22},{7,23},{8,24},{9,... | collective-permute-start | bytes 2654216 | tf_op jit(solution)/shard_map/ppermute | solution.py:300
  87.9 14.7 %collective-permute-start.18 = (bf16[2,4,8,6912]{3,2,1,0:T(8,128)(2,1)S(1)}, bf16[2,4,8,6912]{3,2,1,0:T(8,128)(2,1)S(1)}, u32[]{:S(2)}, u32[]{:S(2)}) collective-permute-start(bf16[2,4,8,6912]{3,2,1,0:T(8,128)(2,1)S(1)} %collective-permute-done.8.refs_0_), channel_id=1, source_target_pairs={{0,16},{1,17},{2,18},{3,19},{4,20},{5,21},{6,22},{7,23},{8,24},{9,... | collective-permute-start | bytes 2654216 | tf_op jit(solution)/shard_map/ppermute | solution.py:300

commit v4 on v3

v4 whole, which is shorter than its diff:
```python
import math

import jax
import jax.numpy as jnp
import numpy as np
from jax import lax
from jax.experimental import pallas as pl
from jax.experimental.pallas import tpu as pltpu
from jax.sharding import PartitionSpec as P

GROUP = 64
BANDS = 8
LAYERS = 4
ROWS_HERE = 8
WIDTH = 13824
HALF = WIDTH // 2
WIDE = 256
LANES = 128
REPS = 8
UNIT = 2
UNITS = LAYERS // UNIT

decay_rate = 0.9
step_size = 1.0
VMEM_LIMIT = 16 * 1024 * 1024
VMEM_FIRST = 16 * 1024 * 1024


def cosine_table():
    k = np.arange(GROUP, dtype=np.float64)
    n = np.arange(GROUP, dtype=np.float64)
    scale = np.where(k == 0, math.sqrt(1.0 / GROUP), math.sqrt(2.0 / GROUP))
    return scale[:, None] * np.cos(math.pi * (2.0 * n[None, :] + 1.0) * k[:, None] / (2.0 * GROUP))


def split_table(table):
    high = jnp.asarray(table, jnp.float32).astype(jnp.bfloat16)
    low = (jnp.asarray(table, jnp.float32) - high.astype(jnp.float32)).astype(jnp.bfloat16)
    return jnp.stack([high, low])


def dot3(x, table_ref):
    high = x.astype(jnp.bfloat16)
    low = (x - high.astype(jnp.float32)).astype(jnp.bfloat16)
    total = jnp.dot(high, table_ref[1], preferred_element_type=jnp.float32)
    total += jnp.dot(low, table_ref[0], preferred_element_type=jnp.float32)
    return total + jnp.dot(high, table_ref[0], preferred_element_type=jnp.float32)


def stacked(x):
    return jnp.concatenate([x[:, at : at + WIDE] for at in range(0, x.shape[1], WIDE)], axis=0)


def pick_tiles(bands_ref, side, layers, spectra):
    lane = lax.broadcasted_iota(jnp.int32, (ROWS_HERE, LANES), 1)
    upper = lax.shift_right_logical(lane, 6)
    band = lax.bitwise_and(lax.shift_right_logical(lane, 3), 7)
    tiles = {}
    for i, layer in enumerate(layers):
        first_bands = bands_ref[layer, 0, side]
        second_bands = bands_ref[layer, 1, side]
        for tile in range(HALF // LANES):
            index = upper + 2 * tile
            first = jnp.take_along_axis(first_bands, index, axis=1)
            second = jnp.take_along_axis(second_bands, index, axis=1)
            row = (i * (HALF // WIDE) + tile // 2) * ROWS_HERE
            column = (tile % 2) * LANES
            values = spectra[row : row + ROWS_HERE, column : column + LANES]
            tiles[i, tile] = jnp.where((first == band) | (second == band), values, 0.0)
    return tiles


def merged_rows(gradient, momentum):
    merged = decay_rate * momentum + gradient.astype(jnp.float32)
    return jnp.concatenate([stacked(merged[i]) for i in range(merged.shape[0])], axis=0)


HBM = pl.BlockSpec(memory_space=pl.ANY)
VMEM = pl.BlockSpec(memory_space=pltpu.VMEM)
SMEM = pl.BlockSpec(memory_space=pltpu.SMEM)
HALF_UNIT = jax.ShapeDtypeStruct((UNIT, ROWS_HERE, HALF), jnp.bfloat16)
HALF_LAYERS = jax.ShapeDtypeStruct((LAYERS, ROWS_HERE, HALF), jnp.bfloat16)
HALF_MOMENTUM = jax.ShapeDtypeStruct((LAYERS, ROWS_HERE, HALF), jnp.float32)
TABLE = jax.ShapeDtypeStruct((2, WIDE, WIDE), jnp.bfloat16)
TOKEN = jax.ShapeDtypeStruct((8, 128), jnp.float32)


def cost(flops, size):
    return pl.CostEstimate(flops=flops, bytes_accessed=size, transcendentals=0)


def store_picked(bands_ref, side, unit, spectra, out_ref):
    layers = range(unit * UNIT, unit * UNIT + UNIT)
    for (layer, tile), values in pick_tiles(bands_ref, side, layers, spectra).items():
        out_ref[unit * UNIT + layer, :, tile * LANES : (tile + 1) * LANES] = values.astype(jnp.bfloat16)


def pick_theirs(place, by_layer, gradient, momentum, params, forward, inverse):
    out_shapes = [HALF_LAYERS, HALF_LAYERS, HALF_MOMENTUM, HALF_LAYERS, TABLE, TABLE]

    def kernel(place_ref, bands_ref, gradient_ref, momentum_ref, params_ref, forward_ref, inverse_ref, *refs):
        picked, own_gradient, own_momentum, own_params, table, back_table, gradients, momenta, sems = refs
        core = place_ref[3]
        own = pl.ds(pl.multiple_of(core * HALF, LANES), HALF)
        theirs = pl.ds(pl.multiple_of((1 - core) * HALF, LANES), HALF)
        pairs = [(forward_ref, table)]
        for unit in range(UNITS):
            layers = pl.ds(unit * UNIT, UNIT)
            pairs.append((gradient_ref.at[0, layers, :, theirs], gradients.at[layers]))
            pairs.append((momentum_ref.at[0, layers, :, theirs], momenta.at[layers]))
        pairs.append((gradient_ref.at[0, :, :, own], own_gradient))
        pairs.append((momentum_ref.at[0, :, :, own], own_momentum))
        pairs.append((params_ref.at[:, :, own], own_params))
        pairs.append((inverse_ref, back_table))
        copies = [pltpu.make_async_copy(src, dst, sems.at[i]) for i, (src, dst) in enumerate(pairs)]
        for copy in copies:
            copy.start()
        copies[0].wait()
        for unit in range(UNITS):
            copies[1 + 2 * unit].wait()
            copies[2 + 2 * unit].wait()
            layers = slice(unit * UNIT, unit * UNIT + UNIT)
            spectra = dot3(merged_rows(gradients[layers], momenta[layers]), table)
            store_picked(bands_ref, 1 - core, unit, spectra, picked)
        for copy in copies[1 + 2 * UNITS :]:
            copy.wait()

    return pl.pallas_call(
        kernel,
        out_shape=out_shapes,
        in_specs=[SMEM, VMEM] + [HBM] * 5,
        out_specs=[VMEM] * len(out_shapes),
        scratch_shapes=[
            pltpu.VMEM((LAYERS, ROWS_HERE, HALF), jnp.bfloat16),
            pltpu.VMEM((LAYERS, ROWS_HERE, HALF), jnp.float32),
            pltpu.SemaphoreType.DMA((5 + 2 * UNITS,)),
        ],
        compiler_params=pltpu.CompilerParams(vmem_limit_bytes=VMEM_FIRST),
        cost_estimate=cost(6 * LAYERS * ROWS_HERE * HALF * WIDE, 6000000),
    )(place, by_layer, gradient, momentum, params, forward, inverse)


def pick_own(place, by_layer, gradient, momentum, forward):
    def kernel(place_ref, bands_ref, gradient_ref, momentum_ref, table_ref, picked):
        for unit in range(UNITS):
            layers = slice(unit * UNIT, unit * UNIT + UNIT)
            spectra = dot3(merged_rows(gradient_ref[layers], momentum_ref[layers]), table_ref)
            store_picked(bands_ref, place_ref[3], unit, spectra, picked)

    return pl.pallas_call(
        kernel,
        out_shape=HALF_LAYERS,
        in_specs=[SMEM] + [VMEM] * 4,
        out_specs=VMEM,
        compiler_params=pltpu.CompilerParams(vmem_limit_bytes=VMEM_LIMIT),
        cost_estimate=cost(6 * LAYERS * ROWS_HERE * HALF * WIDE, 2000000),
    )(place, by_layer, gradient, momentum, forward)


def pair_sum(mine, received, tokens=()):
    def kernel(mine_ref, received_ref, *refs):
        total = mine_ref[...].astype(jnp.float32) + received_ref[...].astype(jnp.float32)
        refs[-1][...] = total.astype(jnp.bfloat16)

    return pl.pallas_call(
        kernel,
        out_shape=HALF_LAYERS,
        in_specs=[VMEM] * (2 + len(tokens)),
        out_specs=VMEM,
        compiler_params=pltpu.CompilerParams(vmem_limit_bytes=VMEM_LIMIT),
        cost_estimate=cost(0, 1400000),
    )(mine, received, *tokens)


def keep_rest(place, by_layer, gradient, momentum, forward, inverse, unit, before):
    def kernel(bands_ref, gradient_ref, momentum_ref, forward_ref, inverse_ref, *refs):
        out_ref, token_ref, gradients, momenta, table, sems = refs[-6:]
        token_ref[...] = jnp.zeros_like(token_ref)
        layers = pl.ds(unit * UNIT, UNIT)
        pairs = [(forward_ref, table)]
        for side in range(2):
            columns = pl.ds(side * HALF, HALF)
            pairs.append((gradient_ref.at[0, layers, :, columns], gradients.at[side]))
            pairs.append((momentum_ref.at[0, layers, :, columns], momenta.at[side]))
        copies = [pltpu.make_async_copy(src, dst, sems.at[i]) for i, (src, dst) in enumerate(pairs)]
        for copy in copies:
            copy.start()
        copies[0].wait()
        for side in range(2):
            copies[1 + 2 * side].wait()
            copies[2 + 2 * side].wait()
            merged = merged_rows(gradients[side], momenta[side])
            spectra = dot3(merged, table)
            tiles = pick_tiles(bands_ref, side, range(unit * UNIT, unit * UNIT + UNIT), spectra)
            wide = [
                jnp.concatenate([tiles[i, at], tiles[i, at + 1]], axis=1)
                for i in range(UNIT)
                for at in range(0, HALF // LANES, 2)
            ]
            kept = merged - dot3(jnp.concatenate(wide, axis=0), inverse_ref)
            for i in range(UNIT):
                for at in range(HALF // WIDE):
                    row = (i * (HALF // WIDE) + at) * ROWS_HERE
                    momenta[side, i, :, at * WIDE : (at + 1) * WIDE] = kept[row : row + ROWS_HERE]
            target = out_ref.at[0, layers, :, pl.ds(side * HALF, HALF)]
            copies.append(pltpu.make_async_copy(momenta.at[side], target, sems.at[5 + side]))
            copies[-1].start()
        copies[-2].wait()
        copies[-1].wait()

    operands = [by_layer, gradient, momentum, forward, inverse]
    specs = [VMEM, HBM, HBM, HBM, VMEM]
    aliases = {}
    if before is not None:
        aliases = {len(operands): 0}
        operands.append(before)
        specs.append(HBM)
    return pl.pallas_call(
        kernel,
        out_shape=[jax.ShapeDtypeStruct(momentum.shape, jnp.float32), TOKEN],
        in_specs=specs,
        out_specs=[HBM, VMEM],
        scratch_shapes=[
            pltpu.VMEM((2, UNIT, ROWS_HERE, HALF), jnp.bfloat16),
            pltpu.VMEM((2, UNIT, ROWS_HERE, HALF), jnp.float32),
            pltpu.VMEM((2, WIDE, WIDE), jnp.bfloat16),
            pltpu.SemaphoreType.DMA((7,)),
        ],
        input_output_aliases=aliases,
        compiler_params=pltpu.CompilerParams(vmem_limit_bytes=VMEM_LIMIT),
        cost_estimate=cost(12 * UNIT * ROWS_HERE * WIDTH * WIDE, 3000000),
    )(*operands)


def decode(mine, received, params, inverse, tokens):
    def kernel(mine_ref, received_ref, params_ref, inverse_ref, *refs):
        for layer in range(LAYERS):
            total = mine_ref[layer].astype(jnp.float32) + received_ref[layer].astype(jnp.float32)
            restored = stacked(total * (1.0 / REPS))
            restored = jnp.concatenate([restored, jnp.zeros((ROWS_HERE, WIDE), jnp.float32)], axis=0)
            decoded = dot3(restored, inverse_ref)
            for at in range(HALF // WIDE):
                columns = slice(at * WIDE, (at + 1) * WIDE)
                change = step_size * decoded[at * ROWS_HERE : (at + 1) * ROWS_HERE]
                updated = params_ref[layer, :, columns].astype(jnp.float32) - change
                refs[-1][layer, :, columns] = updated.astype(jnp.bfloat16)

    return pl.pallas_call(
        kernel,
        out_shape=HALF_LAYERS,
        in_specs=[VMEM] * (4 + len(tokens)),
        out_specs=VMEM,
        compiler_params=pltpu.CompilerParams(vmem_limit_bytes=VMEM_LIMIT),
        cost_estimate=cost(6 * LAYERS * ROWS_HERE * HALF * WIDE, 3000000),
    )(mine, received, params, inverse, *tokens)


def first_place(place_ref):
    return jnp.where(place_ref[3] == 0, place_ref[2], place_ref[1])


def second_place(place_ref):
    return jnp.where(place_ref[3] == 0, place_ref[1], place_ref[2])


def bring_together(place, blocks):
    def kernel(place_ref, *refs):
        here = first_place(place_ref)
        for (_, steps), block in zip(blocks, refs):
            for unit in range(UNITS):
                source = lax.rem(here + (4 - steps), 4)
                refs[len(blocks) + unit][:, source] = block[unit * UNIT : (unit + 1) * UNIT]

    return pl.pallas_call(
        kernel,
        out_shape=[jax.ShapeDtypeStruct((UNIT, 4, ROWS_HERE, HALF), jnp.bfloat16)] * UNITS,
        in_specs=[SMEM] + [VMEM] * len(blocks),
        out_specs=[VMEM] * UNITS,
        compiler_params=pltpu.CompilerParams(vmem_limit_bytes=VMEM_LIMIT),
        cost_estimate=cost(0, 3600000),
    )(place, *[block for block, _ in blocks])


def write_blocks(place, whole, items):
    blocks = [item[0] for item in items]

    def kernel(place_ref, *refs):
        ins, (out, token_ref, sems) = refs[: len(blocks)], refs[-3:]
        token_ref[...] = jnp.zeros_like(token_ref)
        y, x, core = place_ref[1], place_ref[2], place_ref[3]
        copies = []
        for block, (_, unit, steps, other) in zip(ins, items):
            side = core if other == 0 else 1 - core
            here = lax.rem(jnp.where(side == 0, y, x) + (4 - steps), 4)
            columns = pl.ds(pl.multiple_of(side * HALF, LANES), HALF)
            for i in range(4):
                rows = jnp.where(side == 0, 4 * here + i, 4 * i + here)
                for layer in range(UNIT):
                    target = out.at[unit * UNIT + layer, rows, :, columns]
                    copies.append(pltpu.make_async_copy(block.at[layer, i], target, sems.at[len(copies)]))
        for copy in copies:
            copy.start()
        for copy in copies:
            copy.wait()

    operands = [place] + blocks
    specs = [SMEM] + [VMEM] * len(blocks)
    aliases = {}
    if whole is not None:
        aliases = {len(operands): 0}
        operands.append(whole)
        specs.append(HBM)
    return pl.pallas_call(
        kernel,
        out_shape=[jax.ShapeDtypeStruct((LAYERS, 16, ROWS_HERE, WIDTH), jnp.bfloat16), TOKEN],
        in_specs=specs,
        out_specs=[HBM, VMEM],
        scratch_shapes=[pltpu.SemaphoreType.DMA((4 * UNIT * len(blocks),))],
        input_output_aliases=aliases,
        compiler_params=pltpu.CompilerParams(vmem_limit_bytes=VMEM_LIMIT),
        cost_estimate=cost(0, 2 * sum(b.size * 2 for b in blocks)),
    )(*operands)


def move(x, step):
    pairs = []
    for device in range(128):
        z, core, y, u = device // 32, device // 16 % 2, device // 4 % 4, device % 4
        z, core, y, u = step(z, core, y, u)
        pairs.append((device, (z % 4 * 2 + core) * 16 + y % 4 * 4 + u % 4))
    return lax.ppermute(x, ("rep", "fsdp"), pairs)


def swap(x):
    return move(x, lambda z, core, y, u: (z, 1 - core, y, u))


def along_first(x, by):
    return move(x, lambda z, core, y, u: (z, core, y, u + by) if core == 0 else (z, core, y + by, u))


def along_second(x, by):
    return move(x, lambda z, core, y, u: (z, core, y + by, u) if core == 0 else (z, core, y, u + by))


def after(x, *tokens):
    def kernel(x_ref, *refs):
        pass

    return pl.pallas_call(
        kernel,
        out_shape=jax.ShapeDtypeStruct(x.shape, x.dtype),
        in_specs=[VMEM] * (1 + len(tokens)),
        out_specs=VMEM,
        input_output_aliases={0: 0},
        compiler_params=pltpu.CompilerParams(vmem_limit_bytes=VMEM_LIMIT),
        cost_estimate=cost(0, 4096),
    )(x, *tokens)


def spread(x, along, unit, tokens=()):
    ahead, behind = along(x, 1), along(x, -1)
    if tokens and unit == 0:
        ahead = after(ahead, *tokens)
    elif tokens:
        behind = after(behind, *tokens)
    across = along(ahead, 1) if unit == 0 else along(behind, -1)
    return [(ahead, 1), (behind, 3), (across, 2)]


def exchange_z(x, step):
    return move(x, lambda z, core, y, u: (z ^ 1 if core == step else 3 - z, core, y, u))


def shards(gradient, momentum, params, bands):
    rep, fsdp = lax.axis_index("rep"), lax.axis_index("fsdp")
    place = jnp.stack(
        [lax.shift_right_logical(rep, 1), lax.shift_right_logical(fsdp, 2), fsdp & 3, rep & 1]
    ).astype(jnp.int32)
    table = cosine_table()
    forward = split_table(np.kron(np.eye(WIDE // GROUP), table.T))
    inverse = split_table(np.kron(np.eye(WIDE // GROUP), table))
    blocks = HALF // GROUP
    by_layer = jnp.transpose(bands[0], (0, 3, 1, 2)).reshape(LAYERS, 2, ROWS_HERE, 2, blocks)
    by_layer = jnp.pad(jnp.transpose(by_layer, (0, 1, 3, 2, 4)), ((0, 0),) * 4 + ((0, LANES - blocks),))

    gradient, momentum, params, forward, inverse = (
        pltpu.with_memory_space_constraint(x, pltpu.HBM) for x in (gradient, momentum, params, forward, inverse)
    )
    theirs, own_gradient, own_momentum, own_params, forward_here, inverse_here = pick_theirs(
        place, by_layer, gradient, momentum, params, forward, inverse
    )
    received = swap(theirs)
    mine = pick_own(place, by_layer, own_gradient, own_momentum, forward_here)
    new_momentum, tokens = None, []
    for unit in range(UNITS):
        new_momentum, token = keep_rest(place, by_layer, gradient, momentum, forward_here, inverse_here, unit, new_momentum)
        tokens.append(token)
    chip = pair_sum(mine, received)
    two_chips = pair_sum(chip, exchange_z(chip, 0), tokens[:1])
    block = decode(two_chips, exchange_z(two_chips, 1), own_params, inverse_here, tokens[1:])
    own = bring_together(place, [(block, 0)] + spread(block, along_first, 0))

    items = []
    for unit, block in enumerate(own):
        items += [(block, unit, 0, 0), (swap(block), unit, 0, 1)]
    whole, token = write_blocks(place, None, items)
    far, tokens = [], [token]
    for unit, block in enumerate(own):
        ahead, behind, across = spread(block, along_second, unit, tokens)
        near = []
        for moved, steps in (ahead, behind):
            near += [(moved, unit, steps, 0), (swap(moved), unit, steps, 1)]
        whole, token = write_blocks(place, whole, near)
        tokens.append(token)
        far.append(across[0])
    far[1] = after(far[1], *tokens)
    for unit, block in enumerate(far):
        whole, token = write_blocks(place, whole, [(block, unit, 2, 0), (swap(block), unit, 2, 1)])
    return new_momentum, whole.reshape(LAYERS, 16 * ROWS_HERE, WIDTH)


def solution(mesh):
    in_specs = (
        P("rep", None, "fsdp", None),
        P("rep", None, "fsdp", None),
        P(None, "fsdp", None),
        P("rep", None, "fsdp", None, None),
    )
    out_specs = (P("rep", None, "fsdp", None), P())
    return jax.shard_map(shards, mesh=mesh, in_specs=in_specs, out_specs=out_specs, check_vma=False)
```

time: 106 us -> 95.6 us (0.902)
  starting transfers between devices: 41.6 us -> 25.1 us
  waiting for transfers between devices: 31.6 us -> 41.7 us
  local copies, waits for them, and re-layouts: 7.92 us -> 0.98 us
  Pallas kernels: 23 us -> 26.7 us
    ppermute x28 -> x20, starting transfers between devices: 41.6 us -> 25.1 us  [move(): return lax.ppermute(x, ('rep', 'fsdp'), pairs)]
    ppermute x28 -> x20, waiting for transfers between devices: 31.6 us -> 41.7 us  [move(): return lax.ppermute(x, ('rep', 'fsdp'), pairs)]
    unnamed x18 -> x0, local copies, waits for them, and re-layouts: 6.89 us -> none
    pallas_call x12 -> x16, Pallas kernels: 23 us -> 26.7 us  [the longest x5 12.8 us: write_blocks(): pl.pallas_call(kernel, out_shape=[jax.ShapeDtypeStruct((LAYERS, 16, ROWS_...]
  transfers between devices with their start and end apart: 28 -> 20, of which waited for: 12 -> 10; matrix products, arithmetic and copies ran while one was open for 0% -> 0% of each run, Pallas kernels for 17% -> 21%
where the time goes in v4:
time: 95.6 us; the launch traced here: 95.4 us
  waiting for transfers between devices  41.7 us (44%)
  Pallas kernels  26.7 us (28%)
  starting transfers between devices  25.1 us (26%)
  local copies, waits for them, and re-layouts  0.98 us (1%)
    ppermute x20, waiting for transfers between devices, move(): return lax.ppermute(x, ('rep', 'fsdp'), pairs)  41.7 us
    ppermute x20, starting transfers between devices, move(): return lax.ppermute(x, ('rep', 'fsdp'), pairs)  25.1 us
    pallas_call x5, Pallas kernels, write_blocks(): pl.pallas_call(kernel, out_shape=[jax.ShapeDtypeStruct((LAYERS, 16, ROWS_...  12.8 us
    pallas_call x2, Pallas kernels, keep_rest(): pl.pallas_call(kernel, out_shape=[jax.ShapeDtypeStruct(momentum.shape, jn...  7.8 us
    pallas_call x1, Pallas kernels, pick_theirs(): pl.pallas_call(kernel, out_shape=out_shapes, in_specs=[SMEM, VMEM] + [HBM...  3.05 us
  transfers between devices with their start and end apart: 20, of which 10 were waited for; matrix products, arithmetic and copies ran while one was open for 0% of the time, Pallas kernels for 21%

profile of v4, /device:TPU:1, one launch (start us, length us, event | category | flops | bytes accessed | tf_op | source)
XLA Modules:
  0.0 95.4 jit_solution(3849526540011557395)
XLA Ops:
  0.6 1.0 %reshape.12 = s32[4,2,8,2,108]{4,3,1,2,0:T(2,128)S(1)} reshape(s32[4,2,8,216]{3,1,2,0:T(2,128)} %bitcast.15) | data formatting | bytes 110592 | tf_op jit(solution)/shard_map/reshape | solution.py:384
  1.6 0.1 pad_add_fusion.place_ref
  1.7 3.0 %shard_map.95 = (bf16[4,8,6912]{2,1,0:T(8,128)(2,1)S(1)}, bf16[4,8,6912]{2,1,0:T(8,128)(2,1)S(1)}, f32[4,8,6912]{2,1,0:T(8,128)S(1)}, bf16[4,8,6912]{2,1,0:T(8,1...) custom-call(s32[4]{0:T(128)S(1)} %pad_add_fusion.place_ref, ...), custom_call_target="tpu_custom_call" | custom-call | flops 339738624 | bytes 6000000 | tf_op jit(solution)/shard_map/pallas_call | solution.py:128
  4.8 1.5 %collective-permute-start = (bf16[4,8,6912]{2,1,0:T(8,128)(2,1)S(1)}, bf16[4,8,6912]{2,1,0:T(8,128)(2,1)S(1)}, u32[]{:S(2)}, u32[]{:S(2)}) collective-permute-start(bf16[4,8,6912]{2,1,0:T(8,128)(2,1)S(1)} %get-tuple-element.28), channel_id=1, source_target_pairs={{0,16},{1,17},{2,18},{3,19},{4,20},{5,21},{6,22},{7,23},{8,24},{9,... | collective-permute-start | bytes 1327112 | tf_op jit(solution)/shard_map/ppermute | solution.py:331
  6.3 1.7 %shard_map.98.mine_ref = bf16[4,8,6912]{2,1,0:T(8,128)(2,1)S(1)} custom-call(s32[4]{0:T(128)S(1)} %pad_add_fusion.place_ref, s32[4,2,2,8,128]{4,3,2,1,0:T(8,128)S(1)} %pad.4.bands_ref, bf16[4,8,6912]{2,1,0:T(8,128)(2,1)S(1)} %get-tuple-element.26.gradient_ref, f32[4,8,6912]{2,1,0:T(8,128)S(1)} %get-tuple-element.27.momentum_ref, ...), custom_call_target="tpu_custom_call" | custom-call | flops 339738624 | bytes 2000000 | tf_op jit(solution)/shard_map/pallas_call | solution.py:150
  8.0 0.0 collective-permute-done.received_ref
  8.0 0.1 shard_map.99.mine_ref
  8.1 3.9 %collective-permute-start.1 = (bf16[4,8,6912]{2,1,0:T(8,128)(2,1)S(1)}, bf16[4,8,6912]{2,1,0:T(8,128)(2,1)S(1)}, u32[]{:S(2)}, u32[]{:S(2)}) collective-permute-start(bf16[4,8,6912]{2,1,0:T(8,128)(2,1)S(1)} %shard_map.99.mine_ref), channel_id=1, source_target_pairs={{0,32},{1,33},{2,34},{3,35},{4,36},{5,37},{6,38},{7,39},{8,40},{9,... | collective-permute-start | bytes 1327112 | tf_op jit(solution)/shard_map/ppermute | solution.py:331
  12.0 3.9 %shard_map.96 = (f32[1,4,8,13824]{3,2,1,0:T(8,128)}, f32[8,128]{1,0:T(8,128)S(1)}) custom-call(s32[4,2,2,8,128]{4,3,2,1,0:T(8,128)S(1)} %pad.4.bands_ref, bf16[1,4,8,13824]{3,2,1,0:T(8,128)(2,1)} %gradient_ref.5, f32[1,4,8,13824]{3,2,1,0:T(8,128)} %momentum_ref.5, bf16[2,256,256]{2,1,0:T(8,128)(2,1)S(1)} %get-tuple-element.22.forward_ref.table_ref, ...), custom_call_target="tpu_custom_call" | custom-call | flops 679477248 | bytes 3000000 | tf_op jit(solution)/shard_map/pallas_call | solution.py:218
  15.9 1.8 %collective-permute-done.1.received_ref = bf16[4,8,6912]{2,1,0:T(8,128)(2,1)S(1)} collective-permute-done((bf16[4,8,6912]{2,1,0:T(8,128)(2,1)S(1)}, bf16[4,8,6912]{2,1,0:T(8,128)(2,1)S(1)}, u32[]{:S(2)}, u32[]{:S(2)}) %collective-permute-start.1) | collective-permute-done | bytes 442400 | tf_op jit(solution)/shard_map/ppermute | solution.py:331
  17.7 0.1 shard_map.100.mine_ref
  17.8 0.1 collective-permute-start.2
  17.9 3.9 %shard_map.97 = (f32[1,4,8,13824]{3,2,1,0:T(8,128)}, f32[8,128]{1,0:T(8,128)S(1)}) custom-call(s32[4,2,2,8,128]{4,3,2,1,0:T(8,128)S(1)} %pad.4.bands_ref, bf16[1,4,8,13824]{3,2,1,0:T(8,128)(2,1)} %gradient_ref.5, f32[1,4,8,13824]{3,2,1,0:T(8,128)} %momentum_ref.5, ...), custom_call_target="tpu_custom_call", output_to_operand_aliasing={{0}: (5, {})} | custom-call | flops 679477248 | bytes 3000000 | tf_op jit(solution)/shard_map/pallas_call | solution.py:218
  21.8 3.5 %collective-permute-done.2.received_ref = bf16[4,8,6912]{2,1,0:T(8,128)(2,1)S(1)} collective-permute-done((bf16[4,8,6912]{2,1,0:T(8,128)(2,1)S(1)}, bf16[4,8,6912]{2,1,0:T(8,128)(2,1)S(1)}, u32[]{:S(2)}, u32[]{:S(2)}) %collective-permute-start.2) | collective-permute-done | bytes 442400 | tf_op jit(solution)/shard_map/ppermute | solution.py:331
  25.3 0.6 shard_map.101.refs_0_
  25.9 1.4 %collective-permute-start.3 = (bf16[4,8,6912]{2,1,0:T(8,128)(2,1)S(1)}, bf16[4,8,6912]{2,1,0:T(8,128)(2,1)S(1)}, u32[]{:S(2)}, u32[]{:S(2)}) collective-permute-start(bf16[4,8,6912]{2,1,0:T(8,128)(2,1)S(1)} %shard_map.101.refs_0_), channel_id=1, source_target_pairs={{0,1},{1,2},{2,3},{3,0},{4,5},{5,6},{6,7},{7,4},{8,9},{9,10},{10,1... | collective-permute-start | bytes 1327112 | tf_op jit(solution)/shard_map/ppermute | solution.py:331
  27.3 1.5 %collective-permute-start.4 = (bf16[4,8,6912]{2,1,0:T(8,128)(2,1)S(1)}, bf16[4,8,6912]{2,1,0:T(8,128)(2,1)S(1)}, u32[]{:S(2)}, u32[]{:S(2)}) collective-permute-start(bf16[4,8,6912]{2,1,0:T(8,128)(2,1)S(1)} %shard_map.101.refs_0_), channel_id=1, source_target_pairs={{0,3},{1,0},{2,1},{3,2},{4,7},{5,4},{6,5},{7,6},{8,11},{9,8},{10,9... | collective-permute-start | bytes 1327112 | tf_op jit(solution)/shard_map/ppermute | solution.py:331
  28.8 5.9 %collective-permute-done.3.refs_1_ = bf16[4,8,6912]{2,1,0:T(8,128)(2,1)S(1)} collective-permute-done((bf16[4,8,6912]{2,1,0:T(8,128)(2,1)S(1)}, bf16[4,8,6912]{2,1,0:T(8,128)(2,1)S(1)}, u32[]{:S(2)}, u32[]{:S(2)}) %collective-permute-start.3) | collective-permute-done | bytes 442400 | tf_op jit(solution)/shard_map/ppermute | solution.py:331
  34.7 0.0 collective-permute-start.5
  34.7 0.0 collective-permute-done.4.refs_2_
  34.7 8.6 %collective-permute-done.5.refs_3_ = bf16[4,8,6912]{2,1,0:T(8,128)(2,1)S(1)} collective-permute-done((bf16[4,8,6912]{2,1,0:T(8,128)(2,1)S(1)}, bf16[4,8,6912]{2,1,0:T(8,128)(2,1)S(1)}, u32[]{:S(2)}, u32[]{:S(2)}) %collective-permute-start.5) | collective-permute-done | bytes 442400 | tf_op jit(solution)/shard_map/ppermute | solution.py:331
  43.4 0.7 shard_map.102
  44.0 3.5 %collective-permute-start.7 = (bf16[2,4,8,6912]{3,2,1,0:T(8,128)(2,1)S(1)}, bf16[2,4,8,6912]{3,2,1,0:T(8,128)(2,1)S(1)}, u32[]{:S(2)}, u32[]{:S(2)}) collective-permute-start(bf16[2,4,8,6912]{3,2,1,0:T(8,128)(2,1)S(1)} %get-tuple-element.33.refs_0_), channel_id=1, source_target_pairs={{0,16},{1,17},{2,18},{3,19},{4,20},{5,21},{6,22},{7,23},{8,24},{9,... | collective-permute-start | bytes 2654216 | tf_op jit(solution)/shard_map/ppermute | solution.py:331
  47.6 0.1 collective-permute-start.8
  47.7 0.0 collective-permute-start.9
  47.7 2.7 %collective-permute-start.11 = (bf16[2,4,8,6912]{3,2,1,0:T(8,128)(2,1)S(1)}, bf16[2,4,8,6912]{3,2,1,0:T(8,128)(2,1)S(1)}, u32[]{:S(2)}, u32[]{:S(2)}) collective-permute-start(bf16[2,4,8,6912]{3,2,1,0:T(8,128)(2,1)S(1)} %get-tuple-element.33.refs_0_), channel_id=1, source_target_pairs={{0,12},{1,13},{2,14},{3,15},{4,0},{5,1},{6,2},{7,3},{8,4},{9,5},{1... | collective-permute-start | bytes 2654216 | tf_op jit(solution)/shard_map/ppermute | solution.py:331
  50.3 0.5 collective-permute-done.8.refs_3_
  50.9 2.6 %shard_map.103 = (bf16[4,16,8,13824]{3,2,1,0:T(8,128)(2,1)}, f32[8,128]{1,0:T(8,128)S(1)}) custom-call(s32[4]{0:T(128)S(1)} %pad_add_fusion.place_ref, bf16[2,4,8,6912]{3,2,1,0:T(8,128)(2,1)S(1)} %get-tuple-element.33.refs_0_, bf16[2,4,8,6912]{3,2,1,0:T(8,128)(2,1)S(1)} %collective-permute-done.7.refs_1_, ...), custom_call_target="tpu_custom_call" | custom-call | bytes 7077888 | tf_op jit(solution)/shard_map/pallas_call | solution.py:313
  53.5 7.6 %collective-permute-done.9.x_ref = bf16[2,4,8,6912]{3,2,1,0:T(8,128)(2,1)S(1)} collective-permute-done((bf16[2,4,8,6912]{3,2,1,0:T(8,128)(2,1)S(1)}, bf16[2,4,8,6912]{3,2,1,0:T(8,128)(2,1)S(1)}, u32[]{:S(2)}, u32[]{:S(2)}) %collective-permute-start.9) | collective-permute-done | bytes 884768 | tf_op jit(solution)/shard_map/ppermute | solution.py:331
  61.1 1.3 %collective-permute-start.10 = (bf16[2,4,8,6912]{3,2,1,0:T(8,128)(2,1)S(1)}, bf16[2,4,8,6912]{3,2,1,0:T(8,128)(2,1)S(1)}, u32[]{:S(2)}, u32[]{:S(2)}) collective-permute-start(bf16[2,4,8,6912]{3,2,1,0:T(8,128)(2,1)S(1)} %shard_map.104.refs_0_), channel_id=1, source_target_pairs={{0,16},{1,17},{2,18},{3,19},{4,20},{5,21},{6,22},{7,23},{8,24},{9,... | collective-permute-start | bytes 2654216 | tf_op jit(solution)/shard_map/ppermute | solution.py:331
  62.3 0.0 collective-permute-done.11.refs_2_
  62.3 0.4 collective-permute-start.12
  62.7 1.0 %collective-permute-start.6 = (bf16[2,4,8,6912]{3,2,1,0:T(8,128)(2,1)S(1)}, bf16[2,4,8,6912]{3,2,1,0:T(8,128)(2,1)S(1)}, u32[]{:S(2)}, u32[]{:S(2)}) collective-permute-start(bf16[2,4,8,6912]{3,2,1,0:T(8,128)(2,1)S(1)} %get-tuple-element.32.refs_2_), channel_id=1, source_target_pairs={{0,12},{1,13},{2,14},{3,15},{4,0},{5,1},{6,2},{7,3},{8,4},{9,5},{1... | collective-permute-start | bytes 2654216 | tf_op jit(solution)/shard_map/ppermute | solution.py:331
  63.7 0.4 collective-permute-start.18
  64.2 6.4 %collective-permute-done.14.refs_0_ = bf16[2,4,8,6912]{3,2,1,0:T(8,128)(2,1)S(1)} collective-permute-done((bf16[2,4,8,6912]{3,2,1,0:T(8,128)(2,1)S(1)}, bf16[2,4,8,6912]{3,2,1,0:T(8,128)(2,1)S(1)}, u32[]{:S(2)}, u32[]{:S(2)}) %collective-permute-start.14) | collective-permute-done | bytes 884768 | tf_op jit(solution)/shard_map/ppermute | solution.py:331
  70.5 1.3 %collective-permute-start.15 = (bf16[2,4,8,6912]{3,2,1,0:T(8,128)(2,1)S(1)}, bf16[2,4,8,6912]{3,2,1,0:T(8,128)(2,1)S(1)}, u32[]{:S(2)}, u32[]{:S(2)}) collective-permute-start(bf16[2,4,8,6912]{3,2,1,0:T(8,128)(2,1)S(1)} %collective-permute-done.14.refs_0_), channel_id=1, source_target_pairs={{0,16},{1,17},{2,18},{3,19},{4,20},{5,21},{6,22},{7,23},{8,24},{9,... | collective-permute-start | bytes 2654216 | tf_op jit(solution)/shard_map/ppermute | solution.py:331
  71.8 0.0 collective-permute-done.12.refs_3_
  71.8 2.6 %shard_map.105 = (bf16[4,16,8,13824]{3,2,1,0:T(8,128)(2,1)}, f32[8,128]{1,0:T(8,128)S(1)}) custom-call(s32[4]{0:T(128)S(1)} %pad_add_fusion.place_ref, bf16[2,4,8,6912]{3,2,1,0:T(8,128)(2,1)S(1)} %shard_map.104.refs_0_, bf16[2,4,8,6912]{3,2,1,0:T(8,128)(2,1)S(1)} %collective-permute-done.10.refs_1_, ...), custom_call_target="tpu_custom_call", output_to_operand_aliasing={{0}: (5, {})} | custom-call | bytes 7077888 | tf_op jit(solution)/shard_map/pallas_call | solution.py:313
  74.4 0.5 collective-permute-done.6.x_ref
  74.9 1.2 %collective-permute-start.16 = (bf16[2,4,8,6912]{3,2,1,0:T(8,128)(2,1)S(1)}, bf16[2,4,8,6912]{3,2,1,0:T(8,128)(2,1)S(1)}, u32[]{:S(2)}, u32[]{:S(2)}) collective-permute-start(bf16[2,4,8,6912]{3,2,1,0:T(8,128)(2,1)S(1)} %shard_map.106.refs_2_), channel_id=1, source_target_pairs={{0,16},{1,17},{2,18},{3,19},{4,20},{5,21},{6,22},{7,23},{8,24},{9,... | collective-permute-start | bytes 2654216 | tf_op jit(solution)/shard_map/ppermute | solution.py:331
  76.1 1.4 %collective-permute-start.13 = (bf16[2,4,8,6912]{3,2,1,0:T(8,128)(2,1)S(1)}, bf16[2,4,8,6912]{3,2,1,0:T(8,128)(2,1)S(1)}, u32[]{:S(2)}, u32[]{:S(2)}) collective-permute-start(bf16[2,4,8,6912]{3,2,1,0:T(8,128)(2,1)S(1)} %shard_map.106.refs_2_), channel_id=1, source_target_pairs={{0,12},{1,13},{2,14},{3,15},{4,0},{5,1},{6,2},{7,3},{8,4},{9,5},{1... | collective-permute-start | bytes 2654216 | tf_op jit(solution)/shard_map/ppermute | solution.py:331
  77.5 2.5 %collective-permute-done.18.refs_0_ = bf16[2,4,8,6912]{3,2,1,0:T(8,128)(2,1)S(1)} collective-permute-done((bf16[2,4,8,6912]{3,2,1,0:T(8,128)(2,1)S(1)}, bf16[2,4,8,6912]{3,2,1,0:T(8,128)(2,1)S(1)}, u32[]{:S(2)}, u32[]{:S(2)}) %collective-permute-start.18) | collective-permute-done | bytes 884768 | tf_op jit(solution)/shard_map/ppermute | solution.py:331
  80.0 1.3 %collective-permute-start.19 = (bf16[2,4,8,6912]{3,2,1,0:T(8,128)(2,1)S(1)}, bf16[2,4,8,6912]{3,2,1,0:T(8,128)(2,1)S(1)}, u32[]{:S(2)}, u32[]{:S(2)}) collective-permute-start(bf16[2,4,8,6912]{3,2,1,0:T(8,128)(2,1)S(1)} %collective-permute-done.18.refs_0_), channel_id=1, source_target_pairs={{0,16},{1,17},{2,18},{3,19},{4,20},{5,21},{6,22},{7,23},{8,24},{9,... | collective-permute-start | bytes 2654216 | tf_op jit(solution)/shard_map/ppermute | solution.py:331
  81.3 2.6 %shard_map.107 = (bf16[4,16,8,13824]{3,2,1,0:T(8,128)(2,1)}, f32[8,128]{1,0:T(8,128)S(1)}) custom-call(s32[4]{0:T(128)S(1)} %pad_add_fusion.place_ref, bf16[2,4,8,6912]{3,2,1,0:T(8,128)(2,1)S(1)} %collective-permute-done.14.refs_0_, bf16[2,4,8,6912]{3,2,1,0:T(8,128)(2,1)S(1)} %collective-permute-done.15.refs_1_, ...), custom_call_target="tpu_custom_call", output_to_operand_aliasing={{0}: (5, {})} | custom-call | bytes 7077888 | tf_op jit(solution)/shard_map/pallas_call | solution.py:313
  83.9 4.4 %collective-permute-done.13.x_ref = bf16[2,4,8,6912]{3,2,1,0:T(8,128)(2,1)S(1)} collective-permute-done((bf16[2,4,8,6912]{3,2,1,0:T(8,128)(2,1)S(1)}, bf16[2,4,8,6912]{3,2,1,0:T(8,128)(2,1)S(1)}, u32[]{:S(2)}, u32[]{:S(2)}) %collective-permute-start.13) | collective-permute-done | bytes 884768 | tf_op jit(solution)/shard_map/ppermute | solution.py:331
  88.3 2.1 %collective-permute-start.17 = (bf16[2,4,8,6912]{3,2,1,0:T(8,128)(2,1)S(1)}, bf16[2,4,8,6912]{3,2,1,0:T(8,128)(2,1)S(1)}, u32[]{:S(2)}, u32[]{:S(2)}) collective-permute-start(bf16[2,4,8,6912]{3,2,1,0:T(8,128)(2,1)S(1)} %shard_map.108.refs_0_), channel_id=1, source_target_pairs={{0,16},{1,17},{2,18},{3,19},{4,20},{5,21},{6,22},{7,23},{8,24},{9,... | collective-permute-start | bytes 2654216 | tf_op jit(solution)/shard_map/ppermute | solution.py:331
  90.4 2.5 %shard_map.109 = (bf16[4,16,8,13824]{3,2,1,0:T(8,128)(2,1)}, f32[8,128]{1,0:T(8,128)}) custom-call(s32[4]{0:T(128)S(1)} %pad_add_fusion.place_ref, bf16[2,4,8,6912]{3,2,1,0:T(8,128)(2,1)S(1)} %collective-permute-done.18.refs_0_, bf16[2,4,8,6912]{3,2,1,0:T(8,128)(2,1)S(1)} %collective-permute-done.19.refs_1_, ...), custom_call_target="tpu_custom_call", output_to_operand_aliasing={{0}: (3, {})} | custom-call | bytes 3538944 | tf_op jit(solution)/shard_map/pallas_call | solution.py:313
  92.9 2.5 %shard_map.110 = (bf16[4,16,8,13824]{3,2,1,0:T(8,128)(2,1)}, f32[8,128]{1,0:T(8,128)}) custom-call(s32[4]{0:T(128)S(1)} %pad_add_fusion.place_ref, bf16[2,4,8,6912]{3,2,1,0:T(8,128)(2,1)S(1)} %shard_map.108.refs_0_, bf16[2,4,8,6912]{3,2,1,0:T(8,128)(2,1)S(1)} %collective-permute-done.17.refs_1_, ...), custom_call_target="tpu_custom_call", output_to_operand_aliasing={{0}: (3, {})} | custom-call | bytes 3538944 | tf_op jit(solution)/shard_map/pallas_call | solution.py:313
  (12 shorter events, 0.0 us)
Async XLA Ops:
  4.8 3.2 %collective-permute-start = (bf16[4,8,6912]{2,1,0:T(8,128)(2,1)S(1)}, bf16[4,8,6912]{2,1,0:T(8,128)(2,1)S(1)}, u32[]{:S(2)}, u32[]{:S(2)}) collective-permute-start(bf16[4,8,6912]{2,1,0:T(8,128)(2,1)S(1)} %get-tuple-element.28), channel_id=1, source_target_pairs={{0,16},{1,17},{2,18},{3,19},{4,20},{5,21},{6,22},{7,23},{8,24},{9,... | collective-permute-start | bytes 1327112 | tf_op jit(solution)/shard_map/ppermute | solution.py:331
  8.1 9.6 %collective-permute-start.1 = (bf16[4,8,6912]{2,1,0:T(8,128)(2,1)S(1)}, bf16[4,8,6912]{2,1,0:T(8,128)(2,1)S(1)}, u32[]{:S(2)}, u32[]{:S(2)}) collective-permute-start(bf16[4,8,6912]{2,1,0:T(8,128)(2,1)S(1)} %shard_map.99.mine_ref), channel_id=1, source_target_pairs={{0,32},{1,33},{2,34},{3,35},{4,36},{5,37},{6,38},{7,39},{8,40},{9,... | collective-permute-start | bytes 1327112 | tf_op jit(solution)/shard_map/ppermute | solution.py:331
  17.8 7.5 %collective-permute-start.2 = (bf16[4,8,6912]{2,1,0:T(8,128)(2,1)S(1)}, bf16[4,8,6912]{2,1,0:T(8,128)(2,1)S(1)}, u32[]{:S(2)}, u32[]{:S(2)}) collective-permute-start(bf16[4,8,6912]{2,1,0:T(8,128)(2,1)S(1)} %shard_map.100.mine_ref), channel_id=1, source_target_pairs={{0,96},{1,97},{2,98},{3,99},{4,100},{5,101},{6,102},{7,103},{8,104... | collective-permute-start | bytes 1327112 | tf_op jit(solution)/shard_map/ppermute | solution.py:331
  25.9 8.8 %collective-permute-start.3 = (bf16[4,8,6912]{2,1,0:T(8,128)(2,1)S(1)}, bf16[4,8,6912]{2,1,0:T(8,128)(2,1)S(1)}, u32[]{:S(2)}, u32[]{:S(2)}) collective-permute-start(bf16[4,8,6912]{2,1,0:T(8,128)(2,1)S(1)} %shard_map.101.refs_0_), channel_id=1, source_target_pairs={{0,1},{1,2},{2,3},{3,0},{4,5},{5,6},{6,7},{7,4},{8,9},{9,10},{10,1... | collective-permute-start | bytes 1327112 | tf_op jit(solution)/shard_map/ppermute | solution.py:331
  27.3 7.5 %collective-permute-start.4 = (bf16[4,8,6912]{2,1,0:T(8,128)(2,1)S(1)}, bf16[4,8,6912]{2,1,0:T(8,128)(2,1)S(1)}, u32[]{:S(2)}, u32[]{:S(2)}) collective-permute-start(bf16[4,8,6912]{2,1,0:T(8,128)(2,1)S(1)} %shard_map.101.refs_0_), channel_id=1, source_target_pairs={{0,3},{1,0},{2,1},{3,2},{4,7},{5,4},{6,5},{7,6},{8,11},{9,8},{10,9... | collective-permute-start | bytes 1327112 | tf_op jit(solution)/shard_map/ppermute | solution.py:331
  34.7 8.7 %collective-permute-start.5 = (bf16[4,8,6912]{2,1,0:T(8,128)(2,1)S(1)}, bf16[4,8,6912]{2,1,0:T(8,128)(2,1)S(1)}, u32[]{:S(2)}, u32[]{:S(2)}) collective-permute-start(bf16[4,8,6912]{2,1,0:T(8,128)(2,1)S(1)} %collective-permute-done.3.refs_1_), channel_id=1, source_target_pairs={{0,1},{1,2},{2,3},{3,0},{4,5},{5,6},{6,7},{7,4},{8,9},{9,10},{10,1... | collective-permute-start | bytes 1327112 | tf_op jit(solution)/shard_map/ppermute | solution.py:331
  44.0 6.3 %collective-permute-start.7 = (bf16[2,4,8,6912]{3,2,1,0:T(8,128)(2,1)S(1)}, bf16[2,4,8,6912]{3,2,1,0:T(8,128)(2,1)S(1)}, u32[]{:S(2)}, u32[]{:S(2)}) collective-permute-start(bf16[2,4,8,6912]{3,2,1,0:T(8,128)(2,1)S(1)} %get-tuple-element.33.refs_0_), channel_id=1, source_target_pairs={{0,16},{1,17},{2,18},{3,19},{4,20},{5,21},{6,22},{7,23},{8,24},{9,... | collective-permute-start | bytes 2654216 | tf_op jit(solution)/shard_map/ppermute | solution.py:331
  47.6 3.3 %collective-permute-start.8 = (bf16[2,4,8,6912]{3,2,1,0:T(8,128)(2,1)S(1)}, bf16[2,4,8,6912]{3,2,1,0:T(8,128)(2,1)S(1)}, u32[]{:S(2)}, u32[]{:S(2)}) collective-permute-start(bf16[2,4,8,6912]{3,2,1,0:T(8,128)(2,1)S(1)} %get-tuple-element.32.refs_2_), channel_id=1, source_target_pairs={{0,16},{1,17},{2,18},{3,19},{4,20},{5,21},{6,22},{7,23},{8,24},{9,... | collective-permute-start | bytes 2654216 | tf_op jit(solution)/shard_map/ppermute | solution.py:331
  47.7 13.4 %collective-permute-start.9 = (bf16[2,4,8,6912]{3,2,1,0:T(8,128)(2,1)S(1)}, bf16[2,4,8,6912]{3,2,1,0:T(8,128)(2,1)S(1)}, u32[]{:S(2)}, u32[]{:S(2)}) collective-permute-start(bf16[2,4,8,6912]{3,2,1,0:T(8,128)(2,1)S(1)} %get-tuple-element.33.refs_0_), channel_id=1, source_target_pairs={{0,4},{1,5},{2,6},{3,7},{4,8},{5,9},{6,10},{7,11},{8,12},{9,13},{1... | collective-permute-start | bytes 2654216 | tf_op jit(solution)/shard_map/ppermute | solution.py:331
  47.7 14.7 %collective-permute-start.11 = (bf16[2,4,8,6912]{3,2,1,0:T(8,128)(2,1)S(1)}, bf16[2,4,8,6912]{3,2,1,0:T(8,128)(2,1)S(1)}, u32[]{:S(2)}, u32[]{:S(2)}) collective-permute-start(bf16[2,4,8,6912]{3,2,1,0:T(8,128)(2,1)S(1)} %get-tuple-element.33.refs_0_), channel_id=1, source_target_pairs={{0,12},{1,13},{2,14},{3,15},{4,0},{5,1},{6,2},{7,3},{8,4},{9,5},{1... | collective-permute-start | bytes 2654216 | tf_op jit(solution)/shard_map/ppermute | solution.py:331
  50.3 20.2 %collective-permute-start.14 = (bf16[2,4,8,6912]{3,2,1,0:T(8,128)(2,1)S(1)}, bf16[2,4,8,6912]{3,2,1,0:T(8,128)(2,1)S(1)}, u32[]{:S(2)}, u32[]{:S(2)}) collective-permute-start(bf16[2,4,8,6912]{3,2,1,0:T(8,128)(2,1)S(1)} %get-tuple-element.32.refs_2_), channel_id=1, source_target_pairs={{0,4},{1,5},{2,6},{3,7},{4,8},{5,9},{6,10},{7,11},{8,12},{9,13},{1... | collective-permute-start | bytes 2654216 | tf_op jit(solution)/shard_map/ppermute | solution.py:331
  61.1 10.8 %collective-permute-start.10 = (bf16[2,4,8,6912]{3,2,1,0:T(8,128)(2,1)S(1)}, bf16[2,4,8,6912]{3,2,1,0:T(8,128)(2,1)S(1)}, u32[]{:S(2)}, u32[]{:S(2)}) collective-permute-start(bf16[2,4,8,6912]{3,2,1,0:T(8,128)(2,1)S(1)} %shard_map.104.refs_0_), channel_id=1, source_target_pairs={{0,16},{1,17},{2,18},{3,19},{4,20},{5,21},{6,22},{7,23},{8,24},{9,... | collective-permute-start | bytes 2654216 | tf_op jit(solution)/shard_map/ppermute | solution.py:331
  62.3 9.5 %collective-permute-start.12 = (bf16[2,4,8,6912]{3,2,1,0:T(8,128)(2,1)S(1)}, bf16[2,4,8,6912]{3,2,1,0:T(8,128)(2,1)S(1)}, u32[]{:S(2)}, u32[]{:S(2)}) collective-permute-start(bf16[2,4,8,6912]{3,2,1,0:T(8,128)(2,1)S(1)} %collective-permute-done.11.refs_2_), channel_id=1, source_target_pairs={{0,16},{1,17},{2,18},{3,19},{4,20},{5,21},{6,22},{7,23},{8,24},{9,... | collective-permute-start | bytes 2654216 | tf_op jit(solution)/shard_map/ppermute | solution.py:331
  62.7 12.2 %collective-permute-start.6 = (bf16[2,4,8,6912]{3,2,1,0:T(8,128)(2,1)S(1)}, bf16[2,4,8,6912]{3,2,1,0:T(8,128)(2,1)S(1)}, u32[]{:S(2)}, u32[]{:S(2)}) collective-permute-start(bf16[2,4,8,6912]{3,2,1,0:T(8,128)(2,1)S(1)} %get-tuple-element.32.refs_2_), channel_id=1, source_target_pairs={{0,12},{1,13},{2,14},{3,15},{4,0},{5,1},{6,2},{7,3},{8,4},{9,5},{1... | collective-permute-start | bytes 2654216 | tf_op jit(solution)/shard_map/ppermute | solution.py:331
  63.7 16.3 %collective-permute-start.18 = (bf16[2,4,8,6912]{3,2,1,0:T(8,128)(2,1)S(1)}, bf16[2,4,8,6912]{3,2,1,0:T(8,128)(2,1)S(1)}, u32[]{:S(2)}, u32[]{:S(2)}) collective-permute-start(bf16[2,4,8,6912]{3,2,1,0:T(8,128)(2,1)S(1)} %shard_map.104.refs_0_), channel_id=1, source_target_pairs={{0,4},{1,5},{2,6},{3,7},{4,8},{5,9},{6,10},{7,11},{8,12},{9,13},{1... | collective-permute-start | bytes 2654216 | tf_op jit(solution)/shard_map/ppermute | solution.py:331
  70.5 10.8 %collective-permute-start.15 = (bf16[2,4,8,6912]{3,2,1,0:T(8,128)(2,1)S(1)}, bf16[2,4,8,6912]{3,2,1,0:T(8,128)(2,1)S(1)}, u32[]{:S(2)}, u32[]{:S(2)}) collective-permute-start(bf16[2,4,8,6912]{3,2,1,0:T(8,128)(2,1)S(1)} %collective-permute-done.14.refs_0_), channel_id=1, source_target_pairs={{0,16},{1,17},{2,18},{3,19},{4,20},{5,21},{6,22},{7,23},{8,24},{9,... | collective-permute-start | bytes 2654216 | tf_op jit(solution)/shard_map/ppermute | solution.py:331
  74.9 6.4 %collective-permute-start.16 = (bf16[2,4,8,6912]{3,2,1,0:T(8,128)(2,1)S(1)}, bf16[2,4,8,6912]{3,2,1,0:T(8,128)(2,1)S(1)}, u32[]{:S(2)}, u32[]{:S(2)}) collective-permute-start(bf16[2,4,8,6912]{3,2,1,0:T(8,128)(2,1)S(1)} %shard_map.106.refs_2_), channel_id=1, source_target_pairs={{0,16},{1,17},{2,18},{3,19},{4,20},{5,21},{6,22},{7,23},{8,24},{9,... | collective-permute-start | bytes 2654216 | tf_op jit(solution)/shard_map/ppermute | solution.py:331
  76.1 12.2 %collective-permute-start.13 = (bf16[2,4,8,6912]{3,2,1,0:T(8,128)(2,1)S(1)}, bf16[2,4,8,6912]{3,2,1,0:T(8,128)(2,1)S(1)}, u32[]{:S(2)}, u32[]{:S(2)}) collective-permute-start(bf16[2,4,8,6912]{3,2,1,0:T(8,128)(2,1)S(1)} %shard_map.106.refs_2_), channel_id=1, source_target_pairs={{0,12},{1,13},{2,14},{3,15},{4,0},{5,1},{6,2},{7,3},{8,4},{9,5},{1... | collective-permute-start | bytes 2654216 | tf_op jit(solution)/shard_map/ppermute | solution.py:331
  80.0 10.4 %collective-permute-start.19 = (bf16[2,4,8,6912]{3,2,1,0:T(8,128)(2,1)S(1)}, bf16[2,4,8,6912]{3,2,1,0:T(8,128)(2,1)S(1)}, u32[]{:S(2)}, u32[]{:S(2)}) collective-permute-start(bf16[2,4,8,6912]{3,2,1,0:T(8,128)(2,1)S(1)} %collective-permute-done.18.refs_0_), channel_id=1, source_target_pairs={{0,16},{1,17},{2,18},{3,19},{4,20},{5,21},{6,22},{7,23},{8,24},{9,... | collective-permute-start | bytes 2654216 | tf_op jit(solution)/shard_map/ppermute | solution.py:331
  88.3 4.6 %collective-permute-start.17 = (bf16[2,4,8,6912]{3,2,1,0:T(8,128)(2,1)S(1)}, bf16[2,4,8,6912]{3,2,1,0:T(8,128)(2,1)S(1)}, u32[]{:S(2)}, u32[]{:S(2)}) collective-permute-start(bf16[2,4,8,6912]{3,2,1,0:T(8,128)(2,1)S(1)} %shard_map.108.refs_0_), channel_id=1, source_target_pairs={{0,16},{1,17},{2,18},{3,19},{4,20},{5,21},{6,22},{7,23},{8,24},{9,... | collective-permute-start | bytes 2654216 | tf_op jit(solution)/shard_map/ppermute | solution.py:331

commit v5 on v4

--- a/solution.py
+++ b/solution.py
@@ -157,6 +157,23 @@
     )(place, by_layer, gradient, momentum, forward)
 
 
+def chip_sums(mine, received):
+    def kernel(mine_ref, received_ref, *outs):
+        for unit, out_ref in enumerate(outs):
+            layers = slice(unit * UNIT, (unit + 1) * UNIT)
+            total = mine_ref[layers].astype(jnp.float32) + received_ref[layers].astype(jnp.float32)
+            out_ref[...] = total.astype(jnp.bfloat16)
+
+    return pl.pallas_call(
+        kernel,
+        out_shape=[HALF_UNIT] * UNITS,
+        in_specs=[VMEM] * 2,
+        out_specs=[VMEM] * UNITS,
+        compiler_params=pltpu.CompilerParams(vmem_limit_bytes=VMEM_LIMIT),
+        cost_estimate=cost(0, 1400000),
+    )(mine, received)
+
+
 def pair_sum(mine, received, tokens=()):
     def kernel(mine_ref, received_ref, *refs):
         total = mine_ref[...].astype(jnp.float32) + received_ref[...].astype(jnp.float32)
@@ -164,15 +181,15 @@
 
     return pl.pallas_call(
         kernel,
-        out_shape=HALF_LAYERS,
+        out_shape=HALF_UNIT,
         in_specs=[VMEM] * (2 + len(tokens)),
         out_specs=VMEM,
         compiler_params=pltpu.CompilerParams(vmem_limit_bytes=VMEM_LIMIT),
-        cost_estimate=cost(0, 1400000),
+        cost_estimate=cost(0, 700000),
     )(mine, received, *tokens)
 
 
-def keep_rest(place, by_layer, gradient, momentum, forward, inverse, unit, before):
+def keep_rest(place, by_layer, gradient, momentum, forward, inverse, unit, before, tokens=()):
     def kernel(bands_ref, gradient_ref, momentum_ref, forward_ref, inverse_ref, *refs):
         out_ref, token_ref, gradients, momenta, table, sems = refs[-6:]
         token_ref[...] = jnp.zeros_like(token_ref)
@@ -208,8 +225,8 @@
         copies[-2].wait()
         copies[-1].wait()
 
-    operands = [by_layer, gradient, momentum, forward, inverse]
-    specs = [VMEM, HBM, HBM, HBM, VMEM]
+    operands = [by_layer, gradient, momentum, forward, inverse, *tokens]
+    specs = [VMEM, HBM, HBM, HBM, VMEM] + [VMEM] * len(tokens)
     aliases = {}
     if before is not None:
         aliases = {len(operands): 0}
@@ -232,26 +249,27 @@
     )(*operands)
 
 
-def decode(mine, received, params, inverse, tokens):
+def decode(mine, received, params, inverse, unit, tokens=()):
     def kernel(mine_ref, received_ref, params_ref, inverse_ref, *refs):
-        for layer in range(LAYERS):
-            total = mine_ref[layer].astype(jnp.float32) + received_ref[layer].astype(jnp.float32)
-            restored = stacked(total * (1.0 / REPS))
-            restored = jnp.concatenate([restored, jnp.zeros((ROWS_HERE, WIDE), jnp.float32)], axis=0)
-            decoded = dot3(restored, inverse_ref)
+        total = mine_ref[...].astype(jnp.float32) + received_ref[...].astype(jnp.float32)
+        total = total * (1.0 / REPS)
+        restored = jnp.concatenate([stacked(total[i]) for i in range(UNIT)], axis=0)
+        decoded = dot3(restored, inverse_ref)
+        for i in range(UNIT):
             for at in range(HALF // WIDE):
                 columns = slice(at * WIDE, (at + 1) * WIDE)
-                change = step_size * decoded[at * ROWS_HERE : (at + 1) * ROWS_HERE]
-                updated = params_ref[layer, :, columns].astype(jnp.float32) - change
-                refs[-1][layer, :, columns] = updated.astype(jnp.bfloat16)
-
-    return pl.pallas_call(
-        kernel,
-        out_shape=HALF_LAYERS,
+                row = (i * (HALF // WIDE) + at) * ROWS_HERE
+                change = step_size * decoded[row : row + ROWS_HERE]
+                updated = params_ref[unit * UNIT + i, :, columns].astype(jnp.float32) - change
+                refs[-1][i, :, columns] = updated.astype(jnp.bfloat16)
+
+    return pl.pallas_call(
+        kernel,
+        out_shape=HALF_UNIT,
         in_specs=[VMEM] * (4 + len(tokens)),
         out_specs=VMEM,
         compiler_params=pltpu.CompilerParams(vmem_limit_bytes=VMEM_LIMIT),
-        cost_estimate=cost(6 * LAYERS * ROWS_HERE * HALF * WIDE, 3000000),
+        cost_estimate=cost(6 * UNIT * ROWS_HERE * HALF * WIDE, 1500000),
     )(mine, received, params, inverse, *tokens)
 
 
@@ -263,22 +281,24 @@
     return jnp.where(place_ref[3] == 0, place_ref[1], place_ref[2])
 
 
-def bring_together(place, blocks):
+def bring_together(place, units):
+    blocks = [block for unit in units for block, _ in unit]
+
     def kernel(place_ref, *refs):
         here = first_place(place_ref)
-        for (_, steps), block in zip(blocks, refs):
-            for unit in range(UNITS):
-                source = lax.rem(here + (4 - steps), 4)
-                refs[len(blocks) + unit][:, source] = block[unit * UNIT : (unit + 1) * UNIT]
-
-    return pl.pallas_call(
-        kernel,
-        out_shape=[jax.ShapeDtypeStruct((UNIT, 4, ROWS_HERE, HALF), jnp.bfloat16)] * UNITS,
+        ins = iter(refs)
+        for at, unit in enumerate(units):
+            for _, steps in unit:
+                refs[-1][at * UNIT : (at + 1) * UNIT, lax.rem(here + (4 - steps), 4)] = next(ins)[...]
+
+    return pl.pallas_call(
+        kernel,
+        out_shape=jax.ShapeDtypeStruct((LAYERS, 4, ROWS_HERE, HALF), jnp.bfloat16),
         in_specs=[SMEM] + [VMEM] * len(blocks),
-        out_specs=[VMEM] * UNITS,
+        out_specs=VMEM,
         compiler_params=pltpu.CompilerParams(vmem_limit_bytes=VMEM_LIMIT),
         cost_estimate=cost(0, 3600000),
-    )(place, *[block for block, _ in blocks])
+    )(place, *blocks)
 
 
 def write_blocks(place, whole, items):
@@ -289,14 +309,14 @@
         token_ref[...] = jnp.zeros_like(token_ref)
         y, x, core = place_ref[1], place_ref[2], place_ref[3]
         copies = []
-        for block, (_, unit, steps, other) in zip(ins, items):
+        for block, (_, first_layer, steps, other) in zip(ins, items):
             side = core if other == 0 else 1 - core
+            columns = pl.ds(pl.multiple_of(side * HALF, LANES), HALF)
             here = lax.rem(jnp.where(side == 0, y, x) + (4 - steps), 4)
-            columns = pl.ds(pl.multiple_of(side * HALF, LANES), HALF)
             for i in range(4):
                 rows = jnp.where(side == 0, 4 * here + i, 4 * i + here)
-                for layer in range(UNIT):
-                    target = out.at[unit * UNIT + layer, rows, :, columns]
+                for layer in range(block.shape[0]):
+                    target = out.at[first_layer + layer, rows, :, columns]
                     copies.append(pltpu.make_async_copy(block.at[layer, i], target, sems.at[len(copies)]))
         for copy in copies:
             copy.start()
@@ -315,7 +335,7 @@
         out_shape=[jax.ShapeDtypeStruct((LAYERS, 16, ROWS_HERE, WIDTH), jnp.bfloat16), TOKEN],
         in_specs=specs,
         out_specs=[HBM, VMEM],
-        scratch_shapes=[pltpu.SemaphoreType.DMA((4 * UNIT * len(blocks),))],
+        scratch_shapes=[pltpu.SemaphoreType.DMA((4 * sum(block.shape[0] for block in blocks),))],
         input_output_aliases=aliases,
         compiler_params=pltpu.CompilerParams(vmem_limit_bytes=VMEM_LIMIT),
         cost_estimate=cost(0, 2 * sum(b.size * 2 for b in blocks)),
@@ -356,6 +376,34 @@
         compiler_params=pltpu.CompilerParams(vmem_limit_bytes=VMEM_LIMIT),
         cost_estimate=cost(0, 4096),
     )(x, *tokens)
+
+
+def copied(x, token):
+    def kernel(x_ref, token_ref, out_ref):
+        out_ref[...] = x_ref[...]
+
+    return pl.pallas_call(
+        kernel,
+        out_shape=jax.ShapeDtypeStruct(x.shape, x.dtype),
+        in_specs=[VMEM] * 2,
+        out_specs=VMEM,
+        compiler_params=pltpu.CompilerParams(vmem_limit_bytes=VMEM_LIMIT),
+        cost_estimate=cost(0, 2 * x.size * 2),
+    )(x, token)
+
+
+def part(x, unit):
+    def kernel(x_ref, *refs):
+        refs[-1][...] = x_ref[unit * UNIT : (unit + 1) * UNIT]
+
+    return pl.pallas_call(
+        kernel,
+        out_shape=jax.ShapeDtypeStruct((UNIT, *x.shape[1:]), x.dtype),
+        in_specs=[VMEM],
+        out_specs=VMEM,
+        compiler_params=pltpu.CompilerParams(vmem_limit_bytes=VMEM_LIMIT),
+        cost_estimate=cost(0, 2 * x.size),
+    )(x)
 
 
 def spread(x, along, unit, tokens=()):
@@ -392,31 +440,36 @@
     )
     received = swap(theirs)
     mine = pick_own(place, by_layer, own_gradient, own_momentum, forward_here)
+    chips = chip_sums(mine, received)
+    two_chips = [pair_sum(chip, exchange_z(chip, 0)) for chip in chips]
+    everyone = [exchange_z(block, 1) for block in two_chips]
+    updated = []
+    for unit in range(UNITS):
+        updated.append(decode(two_chips[unit], everyone[unit], own_params, inverse_here, unit, two_chips[unit + 1 :]))
+
+    first = []
+    for unit, block in enumerate(updated):
+        first.append([(block, 0)] + spread(block, along_first, unit, updated[unit + 1 :]))
+    own = bring_together(place, first)
+
     new_momentum, tokens = None, []
     for unit in range(UNITS):
-        new_momentum, token = keep_rest(place, by_layer, gradient, momentum, forward_here, inverse_here, unit, new_momentum)
+        new_momentum, token = keep_rest(
+            place, by_layer, gradient, momentum, forward_here, inverse_here, unit, new_momentum, [own]
+        )
         tokens.append(token)
-    chip = pair_sum(mine, received)
-    two_chips = pair_sum(chip, exchange_z(chip, 0), tokens[:1])
-    block = decode(two_chips, exchange_z(two_chips, 1), own_params, inverse_here, tokens[1:])
-    own = bring_together(place, [(block, 0)] + spread(block, along_first, 0))
-
-    items = []
-    for unit, block in enumerate(own):
-        items += [(block, unit, 0, 0), (swap(block), unit, 0, 1)]
+
+    ahead, behind = along_second(own, 1), along_second(own, -1)
+    ahead, behind = after(ahead, *tokens), after(behind, *tokens)
+    across = [along_second(part(ahead, 0), 1), along_second(part(behind, 1), -1)]
+    near = [(own, 0), (ahead, 1), (behind, 3)]
+    others = [(swap(copied(own, behind)), 0), (swap(ahead), 1), (swap(behind), 3)]
+    items = [(block, 0, steps, 0) for block, steps in near] + [(block, 0, steps, 1) for block, steps in others]
     whole, token = write_blocks(place, None, items)
-    far, tokens = [], [token]
-    for unit, block in enumerate(own):
-        ahead, behind, across = spread(block, along_second, unit, tokens)
-        near = []
-        for moved, steps in (ahead, behind):
-            near += [(moved, unit, steps, 0), (swap(moved), unit, steps, 1)]
-        whole, token = write_blocks(place, whole, near)
-        tokens.append(token)
-        far.append(across[0])
-    far[1] = after(far[1], *tokens)
-    for unit, block in enumerate(far):
-        whole, token = write_blocks(place, whole, [(block, unit, 2, 0), (swap(block), unit, 2, 1)])
+    across = [after(block, token) for block in across]
+    others = [swap(block) for block in across]
+    for other, blocks in enumerate((across, others)):
+        whole, _ = write_blocks(place, whole, [(block, unit * UNIT, 2, other) for unit, block in enumerate(blocks)])
     return new_momentum, whole.reshape(LAYERS, 16 * ROWS_HERE, WIDTH)
 
 

time: 95.6 us -> 87.5 us (0.915)
  waiting for transfers between devices: 41.7 us -> 31 us
  starting transfers between devices: 25.1 us -> 29.7 us
  Pallas kernels: 26.7 us -> 24.6 us
    ppermute x20, waiting for transfers between devices: 41.7 us -> 31 us  [move(): return lax.ppermute(x, ('rep', 'fsdp'), pairs)]
    ppermute x20, starting transfers between devices: 25.1 us -> 29.7 us  [move(): return lax.ppermute(x, ('rep', 'fsdp'), pairs)]
    pallas_call x5 -> x3, Pallas kernels: 12.8 us -> 10.3 us  [write_blocks(): pl.pallas_call(kernel, out_shape=[jax.ShapeDtypeStruct((LAYERS, 16, ROWS_...]
  transfers between devices with their start and end apart: 20 -> 20, of which waited for: 10 -> 11; matrix products, arithmetic and copies ran while one was open for 0% -> 0% of each run, Pallas kernels for 21% -> 21%
where the time goes in v5:
time: 87.5 us; the launch traced here: 87.2 us
  waiting for transfers between devices  31 us (35%)
  starting transfers between devices  29.7 us (34%)
  Pallas kernels  24.6 us (28%)
  local copies, waits for them, and re-layouts  0.98 us (1%)
    ppermute x20, waiting for transfers between devices, move(): return lax.ppermute(x, ('rep', 'fsdp'), pairs)  31 us
    ppermute x20, starting transfers between devices, move(): return lax.ppermute(x, ('rep', 'fsdp'), pairs)  29.7 us
    pallas_call x3, Pallas kernels, write_blocks(): pl.pallas_call(kernel, out_shape=[jax.ShapeDtypeStruct((LAYERS, 16, ROWS_...  10.3 us
    pallas_call x2, Pallas kernels, keep_rest(): pl.pallas_call(kernel, out_shape=[jax.ShapeDtypeStruct(momentum.shape, jn...  7.8 us
    pallas_call x1, Pallas kernels, pick_theirs(): pl.pallas_call(kernel, out_shape=out_shapes, in_specs=[SMEM, VMEM] + [HBM...  3.05 us
  transfers between devices with their start and end apart: 20, of which 11 were waited for; matrix products, arithmetic and copies ran while one was open for 0% of the time, Pallas kernels for 21%

profile of v5, /device:TPU:1, one launch (start us, length us, event | category | flops | bytes accessed | tf_op | source)
XLA Modules:
  0.0 87.2 jit_solution(5349977180819717335)
XLA Ops:
  0.6 1.0 %reshape.12 = s32[4,2,8,2,108]{4,3,1,2,0:T(2,128)S(1)} reshape(s32[4,2,8,216]{3,1,2,0:T(2,128)} %bitcast.15) | data formatting | bytes 110592 | tf_op jit(solution)/shard_map/reshape | solution.py:432
  1.6 0.1 pad_add_fusion.place_ref
  1.7 3.0 %shard_map.95 = (bf16[4,8,6912]{2,1,0:T(8,128)(2,1)S(1)}, bf16[4,8,6912]{2,1,0:T(8,128)(2,1)S(1)}, f32[4,8,6912]{2,1,0:T(8,128)S(1)}, bf16[4,8,6912]{2,1,0:T(8,1...) custom-call(s32[4]{0:T(128)S(1)} %pad_add_fusion.place_ref, ...), custom_call_target="tpu_custom_call" | custom-call | flops 339738624 | bytes 6000000 | tf_op jit(solution)/shard_map/pallas_call | solution.py:128
  4.8 1.5 %collective-permute-start = (bf16[4,8,6912]{2,1,0:T(8,128)(2,1)S(1)}, bf16[4,8,6912]{2,1,0:T(8,128)(2,1)S(1)}, u32[]{:S(2)}, u32[]{:S(2)}) collective-permute-start(bf16[4,8,6912]{2,1,0:T(8,128)(2,1)S(1)} %get-tuple-element.22), channel_id=1, source_target_pairs={{0,16},{1,17},{2,18},{3,19},{4,20},{5,21},{6,22},{7,23},{8,24},{9,... | collective-permute-start | bytes 1327112 | tf_op jit(solution)/shard_map/ppermute | solution.py:351
  6.3 1.7 %shard_map.96.mine_ref = bf16[4,8,6912]{2,1,0:T(8,128)(2,1)S(1)} custom-call(s32[4]{0:T(128)S(1)} %pad_add_fusion.place_ref, s32[4,2,2,8,128]{4,3,2,1,0:T(8,128)S(1)} %pad.4.bands_ref, bf16[4,8,6912]{2,1,0:T(8,128)(2,1)S(1)} %get-tuple-element.20.gradient_ref, f32[4,8,6912]{2,1,0:T(8,128)S(1)} %get-tuple-element.21.momentum_ref, ...), custom_call_target="tpu_custom_call" | custom-call | flops 339738624 | bytes 2000000 | tf_op jit(solution)/shard_map/pallas_call | solution.py:150
  8.0 0.1 shard_map.97
  8.1 3.9 %collective-permute-start.1 = (bf16[2,8,6912]{2,1,0:T(8,128)(2,1)S(1)}, bf16[2,8,6912]{2,1,0:T(8,128)(2,1)S(1)}, u32[]{:S(2)}, u32[]{:S(2)}) collective-permute-start(bf16[2,8,6912]{2,1,0:T(8,128)(2,1)S(1)} %get-tuple-element.23.mine_ref), channel_id=1, source_target_pairs={{0,32},{1,33},{2,34},{3,35},{4,36},{5,37},{6,38},{7,39},{8,40},{9,... | collective-permute-start | bytes 663560 | tf_op jit(solution)/shard_map/ppermute | solution.py:351
  12.0 0.1 collective-permute-start.3
  12.1 3.2 %collective-permute-done.1.received_ref = bf16[2,8,6912]{2,1,0:T(8,128)(2,1)S(1)} collective-permute-done((bf16[2,8,6912]{2,1,0:T(8,128)(2,1)S(1)}, bf16[2,8,6912]{2,1,0:T(8,128)(2,1)S(1)}, u32[]{:S(2)}, u32[]{:S(2)}) %collective-permute-start.1) | collective-permute-done | bytes 221216 | tf_op jit(solution)/shard_map/ppermute | solution.py:351
  15.3 0.1 shard_map.98.mine_ref
  15.4 0.1 collective-permute-start.2
  15.5 2.5 %collective-permute-done.3.received_ref = bf16[2,8,6912]{2,1,0:T(8,128)(2,1)S(1)} collective-permute-done((bf16[2,8,6912]{2,1,0:T(8,128)(2,1)S(1)}, bf16[2,8,6912]{2,1,0:T(8,128)(2,1)S(1)}, u32[]{:S(2)}, u32[]{:S(2)}) %collective-permute-start.3) | collective-permute-done | bytes 221216 | tf_op jit(solution)/shard_map/ppermute | solution.py:351
  18.0 0.1 shard_map.99.refs_0_.mine_ref
  18.1 0.1 collective-permute-start.5
  18.2 2.4 %collective-permute-done.2.received_ref = bf16[2,8,6912]{2,1,0:T(8,128)(2,1)S(1)} collective-permute-done((bf16[2,8,6912]{2,1,0:T(8,128)(2,1)S(1)}, bf16[2,8,6912]{2,1,0:T(8,128)(2,1)S(1)}, u32[]{:S(2)}, u32[]{:S(2)}) %collective-permute-start.2) | collective-permute-done | bytes 221216 | tf_op jit(solution)/shard_map/ppermute | solution.py:351
  20.6 0.4 shard_map.100.refs_0_
  20.9 1.4 %collective-permute-start.4 = (bf16[2,8,6912]{2,1,0:T(8,128)(2,1)S(1)}, bf16[2,8,6912]{2,1,0:T(8,128)(2,1)S(1)}, u32[]{:S(2)}, u32[]{:S(2)}) collective-permute-start(bf16[2,8,6912]{2,1,0:T(8,128)(2,1)S(1)} %shard_map.100.refs_0_), channel_id=1, source_target_pairs={{0,1},{1,2},{2,3},{3,0},{4,5},{5,6},{6,7},{7,4},{8,9},{9,10},{10,1... | collective-permute-start | bytes 663560 | tf_op jit(solution)/shard_map/ppermute | solution.py:351
  22.3 0.9 %collective-permute-done.5.received_ref = bf16[2,8,6912]{2,1,0:T(8,128)(2,1)S(1)} collective-permute-done((bf16[2,8,6912]{2,1,0:T(8,128)(2,1)S(1)}, bf16[2,8,6912]{2,1,0:T(8,128)(2,1)S(1)}, u32[]{:S(2)}, u32[]{:S(2)}) %collective-permute-start.5) | collective-permute-done | bytes 221216 | tf_op jit(solution)/shard_map/ppermute | solution.py:351
  23.2 0.3 shard_map.101.refs_0_.refs_4_
  23.6 2.8 %collective-permute-start.9 = (bf16[2,8,6912]{2,1,0:T(8,128)(2,1)S(1)}, bf16[2,8,6912]{2,1,0:T(8,128)(2,1)S(1)}, u32[]{:S(2)}, u32[]{:S(2)}) collective-permute-start(bf16[2,8,6912]{2,1,0:T(8,128)(2,1)S(1)} %shard_map.101.refs_0_.refs_4_), channel_id=1, source_target_pairs={{0,3},{1,0},{2,1},{3,2},{4,7},{5,4},{6,5},{7,6},{8,11},{9,8},{10,9... | collective-permute-start | bytes 663560 | tf_op jit(solution)/shard_map/ppermute | solution.py:351
  26.4 0.5 collective-permute-start.6
  26.8 1.0 %collective-permute-start.8 = (bf16[2,8,6912]{2,1,0:T(8,128)(2,1)S(1)}, bf16[2,8,6912]{2,1,0:T(8,128)(2,1)S(1)}, u32[]{:S(2)}, u32[]{:S(2)}) collective-permute-start(bf16[2,8,6912]{2,1,0:T(8,128)(2,1)S(1)} %shard_map.101.refs_0_.refs_4_), channel_id=1, source_target_pairs={{0,1},{1,2},{2,3},{3,0},{4,5},{5,6},{6,7},{7,4},{8,9},{9,10},{10,1... | collective-permute-start | bytes 663560 | tf_op jit(solution)/shard_map/ppermute | solution.py:351
  27.9 0.0 collective-permute-start.7
  27.9 1.4 %collective-permute-done.9.refs_6_ = bf16[2,8,6912]{2,1,0:T(8,128)(2,1)S(1)} collective-permute-done((bf16[2,8,6912]{2,1,0:T(8,128)(2,1)S(1)}, bf16[2,8,6912]{2,1,0:T(8,128)(2,1)S(1)}, u32[]{:S(2)}, u32[]{:S(2)}) %collective-permute-start.9) | collective-permute-done | bytes 221216 | tf_op jit(solution)/shard_map/ppermute | solution.py:351
  29.3 3.1 %collective-permute-start.10 = (bf16[2,8,6912]{2,1,0:T(8,128)(2,1)S(1)}, bf16[2,8,6912]{2,1,0:T(8,128)(2,1)S(1)}, u32[]{:S(2)}, u32[]{:S(2)}) collective-permute-start(bf16[2,8,6912]{2,1,0:T(8,128)(2,1)S(1)} %collective-permute-done.9.refs_6_), channel_id=1, source_target_pairs={{0,3},{1,0},{2,1},{3,2},{4,7},{5,4},{6,5},{7,6},{8,11},{9,8},{10,9... | collective-permute-start | bytes 663560 | tf_op jit(solution)/shard_map/ppermute | solution.py:351
  32.4 0.5 collective-permute-done.8.refs_5_
  32.8 2.7 %collective-permute-done.7.refs_3_ = bf16[2,8,6912]{2,1,0:T(8,128)(2,1)S(1)} collective-permute-done((bf16[2,8,6912]{2,1,0:T(8,128)(2,1)S(1)}, bf16[2,8,6912]{2,1,0:T(8,128)(2,1)S(1)}, u32[]{:S(2)}, u32[]{:S(2)}) %collective-permute-start.7) | collective-permute-done | bytes 221216 | tf_op jit(solution)/shard_map/ppermute | solution.py:351
  35.5 0.7 shard_map.103.refs_0_.x_ref
  36.2 2.3 %collective-permute-start.13 = (bf16[4,4,8,6912]{3,2,1,0:T(8,128)(2,1)S(1)}, bf16[4,4,8,6912]{3,2,1,0:T(8,128)(2,1)S(1)}, u32[]{:S(2)}, u32[]{:S(2)}) collective-permute-start(bf16[4,4,8,6912]{3,2,1,0:T(8,128)(2,1)S(1)} %shard_map.103.refs_0_.x_ref), channel_id=1, source_target_pairs={{0,12},{1,13},{2,14},{3,15},{4,0},{5,1},{6,2},{7,3},{8,4},{9,5},{1... | collective-permute-start | bytes 5308424 | tf_op jit(solution)/shard_map/ppermute | solution.py:351
  38.5 3.9 %shard_map.104 = (f32[1,4,8,13824]{3,2,1,0:T(8,128)}, f32[8,128]{1,0:T(8,128)S(1)}) custom-call(s32[4,2,2,8,128]{4,3,2,1,0:T(8,128)S(1)} %pad.4.bands_ref, bf16[1,4,8,13824]{3,2,1,0:T(8,128)(2,1)} %gradient_ref.5, f32[1,4,8,13824]{3,2,1,0:T(8,128)} %momentum_ref.5, bf16[2,256,256]{2,1,0:T(8,128)(2,1)S(1)} %get-tuple-element.18.table_ref.forward_ref, ...), custom_call_target="tpu_custom_call" | custom-call | flops 679477248 | bytes 3000000 | tf_op jit(solution)/shard_map/pallas_call | solution.py:235
  42.4 3.9 %shard_map.105 = (f32[1,4,8,13824]{3,2,1,0:T(8,128)}, f32[8,128]{1,0:T(8,128)S(1)}) custom-call(s32[4,2,2,8,128]{4,3,2,1,0:T(8,128)S(1)} %pad.4.bands_ref, bf16[1,4,8,13824]{3,2,1,0:T(8,128)(2,1)} %gradient_ref.5, f32[1,4,8,13824]{3,2,1,0:T(8,128)} %momentum_ref.5, ...), custom_call_target="tpu_custom_call", output_to_operand_aliasing={{0}: (6, {})} | custom-call | flops 679477248 | bytes 3000000 | tf_op jit(solution)/shard_map/pallas_call | solution.py:235
  46.3 11.8 %collective-permute-done.13.x_ref = bf16[4,4,8,6912]{3,2,1,0:T(8,128)(2,1)S(1)} collective-permute-done((bf16[4,4,8,6912]{3,2,1,0:T(8,128)(2,1)S(1)}, bf16[4,4,8,6912]{3,2,1,0:T(8,128)(2,1)S(1)}, u32[]{:S(2)}, u32[]{:S(2)}) %collective-permute-start.13) | collective-permute-done | bytes 1769504 | tf_op jit(solution)/shard_map/ppermute | solution.py:351
  58.1 0.1 shard_map.109
  58.2 5.7 %collective-permute-start.16 = (bf16[4,4,8,6912]{3,2,1,0:T(8,128)(2,1)S(1)}, bf16[4,4,8,6912]{3,2,1,0:T(8,128)(2,1)S(1)}, u32[]{:S(2)}, u32[]{:S(2)}) collective-permute-start(bf16[4,4,8,6912]{3,2,1,0:T(8,128)(2,1)S(1)} %shard_map.108.token_ref.refs_2_.x_ref), channel_id=1, source_target_pairs={{0,16},{1,17},{2,18},{3,19},{4,20},{5,21},{6,22},{7,23},{8,24},{9,... | collective-permute-start | bytes 5308424 | tf_op jit(solution)/shard_map/ppermute | solution.py:351
  63.9 0.1 collective-permute-start.14
  64.0 3.0 %collective-permute-start.15 = (bf16[4,4,8,6912]{3,2,1,0:T(8,128)(2,1)S(1)}, bf16[4,4,8,6912]{3,2,1,0:T(8,128)(2,1)S(1)}, u32[]{:S(2)}, u32[]{:S(2)}) collective-permute-start(bf16[4,4,8,6912]{3,2,1,0:T(8,128)(2,1)S(1)} %shard_map.106.x_ref.refs_1_), channel_id=1, source_target_pairs={{0,16},{1,17},{2,18},{3,19},{4,20},{5,21},{6,22},{7,23},{8,24},{9,... | collective-permute-start | bytes 5308424 | tf_op jit(solution)/shard_map/ppermute | solution.py:351
  67.0 0.1 shard_map.107
  67.1 0.1 collective-permute-start.12
  67.1 0.1 shard_map.112
  67.2 3.5 %collective-permute-start.18 = (bf16[2,4,8,6912]{3,2,1,0:T(8,128)(2,1)S(1)}, bf16[2,4,8,6912]{3,2,1,0:T(8,128)(2,1)S(1)}, u32[]{:S(2)}, u32[]{:S(2)}) collective-permute-start(bf16[2,4,8,6912]{3,2,1,0:T(8,128)(2,1)S(1)} %shard_map.112), channel_id=1, source_target_pairs={{0,12},{1,13},{2,14},{3,15},{4,0},{5,1},{6,2},{7,3},{8,4},{9,5},{1... | collective-permute-start | bytes 2654216 | tf_op jit(solution)/shard_map/ppermute | solution.py:351
  70.7 1.6 %collective-permute-done.15.refs_4_ = bf16[4,4,8,6912]{3,2,1,0:T(8,128)(2,1)S(1)} collective-permute-done((bf16[4,4,8,6912]{3,2,1,0:T(8,128)(2,1)S(1)}, bf16[4,4,8,6912]{3,2,1,0:T(8,128)(2,1)S(1)}, u32[]{:S(2)}, u32[]{:S(2)}) %collective-permute-start.15) | collective-permute-done | bytes 1769504 | tf_op jit(solution)/shard_map/ppermute | solution.py:351
  72.3 5.3 %shard_map.110 = (bf16[4,16,8,13824]{3,2,1,0:T(8,128)(2,1)}, f32[8,128]{1,0:T(8,128)S(1)}) custom-call(s32[4]{0:T(128)S(1)} %pad_add_fusion.place_ref, bf16[4,4,8,6912]{3,2,1,0:T(8,128)(2,1)S(1)} %shard_map.103.refs_0_.x_ref, bf16[4,4,8,6912]{3,2,1,0:T(8,128)(2,1)S(1)} %shard_map.106.x_ref.refs_1_, ...), custom_call_target="tpu_custom_call" | custom-call | bytes 21233664 | tf_op jit(solution)/shard_map/pallas_call | solution.py:333
  77.6 3.4 %collective-permute-done.12.x_ref = bf16[2,4,8,6912]{3,2,1,0:T(8,128)(2,1)S(1)} collective-permute-done((bf16[2,4,8,6912]{3,2,1,0:T(8,128)(2,1)S(1)}, bf16[2,4,8,6912]{3,2,1,0:T(8,128)(2,1)S(1)}, u32[]{:S(2)}, u32[]{:S(2)}) %collective-permute-start.12) | collective-permute-done | bytes 884768 | tf_op jit(solution)/shard_map/ppermute | solution.py:351
  81.0 0.4 collective-permute-start.17
  81.4 0.1 collective-permute-start.19
  81.5 2.5 %shard_map.114 = (bf16[4,16,8,13824]{3,2,1,0:T(8,128)(2,1)}, f32[8,128]{1,0:T(8,128)}) custom-call(s32[4]{0:T(128)S(1)} %pad_add_fusion.place_ref, bf16[2,4,8,6912]{3,2,1,0:T(8,128)(2,1)S(1)} %shard_map.111.refs_0_, bf16[2,4,8,6912]{3,2,1,0:T(8,128)(2,1)S(1)} %shard_map.113.refs_1_, ...), custom_call_target="tpu_custom_call", output_to_operand_aliasing={{0}: (3, {})} | custom-call | bytes 3538944 | tf_op jit(solution)/shard_map/pallas_call | solution.py:333
  84.0 0.7 collective-permute-done.19.refs_1_
  84.7 2.5 %shard_map.115 = (bf16[4,16,8,13824]{3,2,1,0:T(8,128)(2,1)}, f32[8,128]{1,0:T(8,128)}) custom-call(s32[4]{0:T(128)S(1)} %pad_add_fusion.place_ref, bf16[2,4,8,6912]{3,2,1,0:T(8,128)(2,1)S(1)} %collective-permute-done.17.refs_0_, bf16[2,4,8,6912]{3,2,1,0:T(8,128)(2,1)S(1)} %collective-permute-done.19.refs_1_, ...), custom_call_target="tpu_custom_call", output_to_operand_aliasing={{0}: (3, {})} | custom-call | bytes 3538944 | tf_op jit(solution)/shard_map/pallas_call | solution.py:333
  (17 shorter events, 0.0 us)
Async XLA Ops:
  4.8 3.2 %collective-permute-start = (bf16[4,8,6912]{2,1,0:T(8,128)(2,1)S(1)}, bf16[4,8,6912]{2,1,0:T(8,128)(2,1)S(1)}, u32[]{:S(2)}, u32[]{:S(2)}) collective-permute-start(bf16[4,8,6912]{2,1,0:T(8,128)(2,1)S(1)} %get-tuple-element.22), channel_id=1, source_target_pairs={{0,16},{1,17},{2,18},{3,19},{4,20},{5,21},{6,22},{7,23},{8,24},{9,... | collective-permute-start | bytes 1327112 | tf_op jit(solution)/shard_map/ppermute | solution.py:351
  8.1 7.2 %collective-permute-start.1 = (bf16[2,8,6912]{2,1,0:T(8,128)(2,1)S(1)}, bf16[2,8,6912]{2,1,0:T(8,128)(2,1)S(1)}, u32[]{:S(2)}, u32[]{:S(2)}) collective-permute-start(bf16[2,8,6912]{2,1,0:T(8,128)(2,1)S(1)} %get-tuple-element.23.mine_ref), channel_id=1, source_target_pairs={{0,32},{1,33},{2,34},{3,35},{4,36},{5,37},{6,38},{7,39},{8,40},{9,... | collective-permute-start | bytes 663560 | tf_op jit(solution)/shard_map/ppermute | solution.py:351
  12.0 6.0 %collective-permute-start.3 = (bf16[2,8,6912]{2,1,0:T(8,128)(2,1)S(1)}, bf16[2,8,6912]{2,1,0:T(8,128)(2,1)S(1)}, u32[]{:S(2)}, u32[]{:S(2)}) collective-permute-start(bf16[2,8,6912]{2,1,0:T(8,128)(2,1)S(1)} %get-tuple-element.25.mine_ref), channel_id=1, source_target_pairs={{0,32},{1,33},{2,34},{3,35},{4,36},{5,37},{6,38},{7,39},{8,40},{9,... | collective-permute-start | bytes 663560 | tf_op jit(solution)/shard_map/ppermute | solution.py:351
  15.4 5.2 %collective-permute-start.2 = (bf16[2,8,6912]{2,1,0:T(8,128)(2,1)S(1)}, bf16[2,8,6912]{2,1,0:T(8,128)(2,1)S(1)}, u32[]{:S(2)}, u32[]{:S(2)}) collective-permute-start(bf16[2,8,6912]{2,1,0:T(8,128)(2,1)S(1)} %shard_map.98.mine_ref), channel_id=1, source_target_pairs={{0,96},{1,97},{2,98},{3,99},{4,100},{5,101},{6,102},{7,103},{8,104... | collective-permute-start | bytes 663560 | tf_op jit(solution)/shard_map/ppermute | solution.py:351
  18.1 5.2 %collective-permute-start.5 = (bf16[2,8,6912]{2,1,0:T(8,128)(2,1)S(1)}, bf16[2,8,6912]{2,1,0:T(8,128)(2,1)S(1)}, u32[]{:S(2)}, u32[]{:S(2)}) collective-permute-start(bf16[2,8,6912]{2,1,0:T(8,128)(2,1)S(1)} %shard_map.99.refs_0_.mine_ref), channel_id=1, source_target_pairs={{0,96},{1,97},{2,98},{3,99},{4,100},{5,101},{6,102},{7,103},{8,104... | collective-permute-start | bytes 663560 | tf_op jit(solution)/shard_map/ppermute | solution.py:351
  20.9 6.9 %collective-permute-start.4 = (bf16[2,8,6912]{2,1,0:T(8,128)(2,1)S(1)}, bf16[2,8,6912]{2,1,0:T(8,128)(2,1)S(1)}, u32[]{:S(2)}, u32[]{:S(2)}) collective-permute-start(bf16[2,8,6912]{2,1,0:T(8,128)(2,1)S(1)} %shard_map.100.refs_0_), channel_id=1, source_target_pairs={{0,1},{1,2},{2,3},{3,0},{4,5},{5,6},{6,7},{7,4},{8,9},{9,10},{10,1... | collective-permute-start | bytes 663560 | tf_op jit(solution)/shard_map/ppermute | solution.py:351
  23.6 5.7 %collective-permute-start.9 = (bf16[2,8,6912]{2,1,0:T(8,128)(2,1)S(1)}, bf16[2,8,6912]{2,1,0:T(8,128)(2,1)S(1)}, u32[]{:S(2)}, u32[]{:S(2)}) collective-permute-start(bf16[2,8,6912]{2,1,0:T(8,128)(2,1)S(1)} %shard_map.101.refs_0_.refs_4_), channel_id=1, source_target_pairs={{0,3},{1,0},{2,1},{3,2},{4,7},{5,4},{6,5},{7,6},{8,11},{9,8},{10,9... | collective-permute-start | bytes 663560 | tf_op jit(solution)/shard_map/ppermute | solution.py:351
  26.4 6.0 %collective-permute-start.6 = (bf16[2,8,6912]{2,1,0:T(8,128)(2,1)S(1)}, bf16[2,8,6912]{2,1,0:T(8,128)(2,1)S(1)}, u32[]{:S(2)}, u32[]{:S(2)}) collective-permute-start(bf16[2,8,6912]{2,1,0:T(8,128)(2,1)S(1)} %shard_map.100.refs_0_), channel_id=1, source_target_pairs={{0,3},{1,0},{2,1},{3,2},{4,7},{5,4},{6,5},{7,6},{8,11},{9,8},{10,9... | collective-permute-start | bytes 663560 | tf_op jit(solution)/shard_map/ppermute | solution.py:351
  26.8 6.0 %collective-permute-start.8 = (bf16[2,8,6912]{2,1,0:T(8,128)(2,1)S(1)}, bf16[2,8,6912]{2,1,0:T(8,128)(2,1)S(1)}, u32[]{:S(2)}, u32[]{:S(2)}) collective-permute-start(bf16[2,8,6912]{2,1,0:T(8,128)(2,1)S(1)} %shard_map.101.refs_0_.refs_4_), channel_id=1, source_target_pairs={{0,1},{1,2},{2,3},{3,0},{4,5},{5,6},{6,7},{7,4},{8,9},{9,10},{10,1... | collective-permute-start | bytes 663560 | tf_op jit(solution)/shard_map/ppermute | solution.py:351
  27.9 7.7 %collective-permute-start.7 = (bf16[2,8,6912]{2,1,0:T(8,128)(2,1)S(1)}, bf16[2,8,6912]{2,1,0:T(8,128)(2,1)S(1)}, u32[]{:S(2)}, u32[]{:S(2)}) collective-permute-start(bf16[2,8,6912]{2,1,0:T(8,128)(2,1)S(1)} %shard_map.102.refs_1_), channel_id=1, source_target_pairs={{0,1},{1,2},{2,3},{3,0},{4,5},{5,6},{6,7},{7,4},{8,9},{9,10},{10,1... | collective-permute-start | bytes 663560 | tf_op jit(solution)/shard_map/ppermute | solution.py:351
  29.3 6.2 %collective-permute-start.10 = (bf16[2,8,6912]{2,1,0:T(8,128)(2,1)S(1)}, bf16[2,8,6912]{2,1,0:T(8,128)(2,1)S(1)}, u32[]{:S(2)}, u32[]{:S(2)}) collective-permute-start(bf16[2,8,6912]{2,1,0:T(8,128)(2,1)S(1)} %collective-permute-done.9.refs_6_), channel_id=1, source_target_pairs={{0,3},{1,0},{2,1},{3,2},{4,7},{5,4},{6,5},{7,6},{8,11},{9,8},{10,9... | collective-permute-start | bytes 663560 | tf_op jit(solution)/shard_map/ppermute | solution.py:351
  36.2 21.9 %collective-permute-start.13 = (bf16[4,4,8,6912]{3,2,1,0:T(8,128)(2,1)S(1)}, bf16[4,4,8,6912]{3,2,1,0:T(8,128)(2,1)S(1)}, u32[]{:S(2)}, u32[]{:S(2)}) collective-permute-start(bf16[4,4,8,6912]{3,2,1,0:T(8,128)(2,1)S(1)} %shard_map.103.refs_0_.x_ref), channel_id=1, source_target_pairs={{0,12},{1,13},{2,14},{3,15},{4,0},{5,1},{6,2},{7,3},{8,4},{9,5},{1... | collective-permute-start | bytes 5308424 | tf_op jit(solution)/shard_map/ppermute | solution.py:351
  38.5 25.5 %collective-permute-start.11 = (bf16[4,4,8,6912]{3,2,1,0:T(8,128)(2,1)S(1)}, bf16[4,4,8,6912]{3,2,1,0:T(8,128)(2,1)S(1)}, u32[]{:S(2)}, u32[]{:S(2)}) collective-permute-start(bf16[4,4,8,6912]{3,2,1,0:T(8,128)(2,1)S(1)} %shard_map.103.refs_0_.x_ref), channel_id=1, source_target_pairs={{0,4},{1,5},{2,6},{3,7},{4,8},{5,9},{6,10},{7,11},{8,12},{9,13},{1... | collective-permute-start | bytes 5308424 | tf_op jit(solution)/shard_map/ppermute | solution.py:351
  58.2 12.5 %collective-permute-start.16 = (bf16[4,4,8,6912]{3,2,1,0:T(8,128)(2,1)S(1)}, bf16[4,4,8,6912]{3,2,1,0:T(8,128)(2,1)S(1)}, u32[]{:S(2)}, u32[]{:S(2)}) collective-permute-start(bf16[4,4,8,6912]{3,2,1,0:T(8,128)(2,1)S(1)} %shard_map.108.token_ref.refs_2_.x_ref), channel_id=1, source_target_pairs={{0,16},{1,17},{2,18},{3,19},{4,20},{5,21},{6,22},{7,23},{8,24},{9,... | collective-permute-start | bytes 5308424 | tf_op jit(solution)/shard_map/ppermute | solution.py:351
  63.9 6.8 %collective-permute-start.14 = (bf16[4,4,8,6912]{3,2,1,0:T(8,128)(2,1)S(1)}, bf16[4,4,8,6912]{3,2,1,0:T(8,128)(2,1)S(1)}, u32[]{:S(2)}, u32[]{:S(2)}) collective-permute-start(bf16[4,4,8,6912]{3,2,1,0:T(8,128)(2,1)S(1)} %shard_map.109), channel_id=1, source_target_pairs={{0,16},{1,17},{2,18},{3,19},{4,20},{5,21},{6,22},{7,23},{8,24},{9,... | collective-permute-start | bytes 5308424 | tf_op jit(solution)/shard_map/ppermute | solution.py:351
  64.0 8.3 %collective-permute-start.15 = (bf16[4,4,8,6912]{3,2,1,0:T(8,128)(2,1)S(1)}, bf16[4,4,8,6912]{3,2,1,0:T(8,128)(2,1)S(1)}, u32[]{:S(2)}, u32[]{:S(2)}) collective-permute-start(bf16[4,4,8,6912]{3,2,1,0:T(8,128)(2,1)S(1)} %shard_map.106.x_ref.refs_1_), channel_id=1, source_target_pairs={{0,16},{1,17},{2,18},{3,19},{4,20},{5,21},{6,22},{7,23},{8,24},{9,... | collective-permute-start | bytes 5308424 | tf_op jit(solution)/shard_map/ppermute | solution.py:351
  67.1 13.9 %collective-permute-start.12 = (bf16[2,4,8,6912]{3,2,1,0:T(8,128)(2,1)S(1)}, bf16[2,4,8,6912]{3,2,1,0:T(8,128)(2,1)S(1)}, u32[]{:S(2)}, u32[]{:S(2)}) collective-permute-start(bf16[2,4,8,6912]{3,2,1,0:T(8,128)(2,1)S(1)} %shard_map.107), channel_id=1, source_target_pairs={{0,4},{1,5},{2,6},{3,7},{4,8},{5,9},{6,10},{7,11},{8,12},{9,13},{1... | collective-permute-start | bytes 2654216 | tf_op jit(solution)/shard_map/ppermute | solution.py:351
  67.2 14.2 %collective-permute-start.18 = (bf16[2,4,8,6912]{3,2,1,0:T(8,128)(2,1)S(1)}, bf16[2,4,8,6912]{3,2,1,0:T(8,128)(2,1)S(1)}, u32[]{:S(2)}, u32[]{:S(2)}) collective-permute-start(bf16[2,4,8,6912]{3,2,1,0:T(8,128)(2,1)S(1)} %shard_map.112), channel_id=1, source_target_pairs={{0,12},{1,13},{2,14},{3,15},{4,0},{5,1},{6,2},{7,3},{8,4},{9,5},{1... | collective-permute-start | bytes 2654216 | tf_op jit(solution)/shard_map/ppermute | solution.py:351
  81.0 3.0 %collective-permute-start.17 = (bf16[2,4,8,6912]{3,2,1,0:T(8,128)(2,1)S(1)}, bf16[2,4,8,6912]{3,2,1,0:T(8,128)(2,1)S(1)}, u32[]{:S(2)}, u32[]{:S(2)}) collective-permute-start(bf16[2,4,8,6912]{3,2,1,0:T(8,128)(2,1)S(1)} %shard_map.111.refs_0_), channel_id=1, source_target_pairs={{0,16},{1,17},{2,18},{3,19},{4,20},{5,21},{6,22},{7,23},{8,24},{9,... | collective-permute-start | bytes 2654216 | tf_op jit(solution)/shard_map/ppermute | solution.py:351
  81.4 3.3 %collective-permute-start.19 = (bf16[2,4,8,6912]{3,2,1,0:T(8,128)(2,1)S(1)}, bf16[2,4,8,6912]{3,2,1,0:T(8,128)(2,1)S(1)}, u32[]{:S(2)}, u32[]{:S(2)}) collective-permute-start(bf16[2,4,8,6912]{3,2,1,0:T(8,128)(2,1)S(1)} %shard_map.113.refs_1_), channel_id=1, source_target_pairs={{0,16},{1,17},{2,18},{3,19},{4,20},{5,21},{6,22},{7,23},{8,24},{9,... | collective-permute-start | bytes 2654216 | tf_op jit(solution)/shard_map/ppermute | solution.py:351

commit v6 on v5

--- a/solution.py
+++ b/solution.py
@@ -17,6 +17,7 @@
 WIDE = 256
 LANES = 128
 REPS = 8
+BLOCKS = WIDTH // GROUP
 UNIT = 2
 UNITS = LAYERS // UNIT
 
@@ -60,7 +61,7 @@
         first_bands = bands_ref[layer, 0, side]
         second_bands = bands_ref[layer, 1, side]
         for tile in range(HALF // LANES):
-            index = upper + 2 * tile
+            index = upper + (2 * tile + jnp.where(side == 0, 0, LANES - BLOCKS // 2))
             first = jnp.take_along_axis(first_bands, index, axis=1)
             second = jnp.take_along_axis(second_bands, index, axis=1)
             row = (i * (HALF // WIDE) + tile // 2) * ROWS_HERE
@@ -82,6 +83,7 @@
 HALF_LAYERS = jax.ShapeDtypeStruct((LAYERS, ROWS_HERE, HALF), jnp.bfloat16)
 HALF_MOMENTUM = jax.ShapeDtypeStruct((LAYERS, ROWS_HERE, HALF), jnp.float32)
 TABLE = jax.ShapeDtypeStruct((2, WIDE, WIDE), jnp.bfloat16)
+SIDE_BANDS = jax.ShapeDtypeStruct((LAYERS, 2, 2, ROWS_HERE, LANES), jnp.int32)
 TOKEN = jax.ShapeDtypeStruct((8, 128), jnp.float32)
 
 
@@ -96,10 +98,11 @@
 
 
 def pick_theirs(place, by_layer, gradient, momentum, params, forward, inverse):
-    out_shapes = [HALF_LAYERS, HALF_LAYERS, HALF_MOMENTUM, HALF_LAYERS, TABLE, TABLE]
-
-    def kernel(place_ref, bands_ref, gradient_ref, momentum_ref, params_ref, forward_ref, inverse_ref, *refs):
-        picked, own_gradient, own_momentum, own_params, table, back_table, gradients, momenta, sems = refs
+    out_shapes = [HALF_LAYERS, HALF_LAYERS, HALF_MOMENTUM, HALF_LAYERS, TABLE, TABLE, SIDE_BANDS]
+
+    def kernel(place_ref, raw_ref, gradient_ref, momentum_ref, params_ref, forward_ref, inverse_ref, *refs):
+        picked, own_gradient, own_momentum, own_params, table, back_table, bands_ref = refs[:7]
+        gradients, momenta, raw, sems = refs[7:]
         core = place_ref[3]
         own = pl.ds(pl.multiple_of(core * HALF, LANES), HALF)
         theirs = pl.ds(pl.multiple_of((1 - core) * HALF, LANES), HALF)
@@ -112,9 +115,17 @@
         pairs.append((momentum_ref.at[0, :, :, own], own_momentum))
         pairs.append((params_ref.at[:, :, own], own_params))
         pairs.append((inverse_ref, back_table))
+        pairs.insert(0, (raw_ref, raw))
         copies = [pltpu.make_async_copy(src, dst, sems.at[i]) for i, (src, dst) in enumerate(pairs)]
         for copy in copies:
             copy.start()
+        copies[0].wait()
+        for layer in range(LAYERS):
+            both = raw[layer]
+            for i in range(2):
+                bands_ref[layer, i, 0] = both[:, i, :LANES]
+                bands_ref[layer, i, 1] = both[:, i, BLOCKS - LANES :]
+        copies.pop(0)
         copies[0].wait()
         for unit in range(UNITS):
             copies[1 + 2 * unit].wait()
@@ -128,12 +139,13 @@
     return pl.pallas_call(
         kernel,
         out_shape=out_shapes,
-        in_specs=[SMEM, VMEM] + [HBM] * 5,
+        in_specs=[SMEM] + [HBM] * 6,
         out_specs=[VMEM] * len(out_shapes),
         scratch_shapes=[
             pltpu.VMEM((LAYERS, ROWS_HERE, HALF), jnp.bfloat16),
             pltpu.VMEM((LAYERS, ROWS_HERE, HALF), jnp.float32),
-            pltpu.SemaphoreType.DMA((5 + 2 * UNITS,)),
+            pltpu.VMEM((LAYERS, ROWS_HERE, 2, BLOCKS), jnp.int32),
+            pltpu.SemaphoreType.DMA((6 + 2 * UNITS,)),
         ],
         compiler_params=pltpu.CompilerParams(vmem_limit_bytes=VMEM_FIRST),
         cost_estimate=cost(6 * LAYERS * ROWS_HERE * HALF * WIDE, 6000000),
@@ -406,14 +418,8 @@
     )(x)
 
 
-def spread(x, along, unit, tokens=()):
-    ahead, behind = along(x, 1), along(x, -1)
-    if tokens and unit == 0:
-        ahead = after(ahead, *tokens)
-    elif tokens:
-        behind = after(behind, *tokens)
-    across = along(ahead, 1) if unit == 0 else along(behind, -1)
-    return [(ahead, 1), (behind, 3), (across, 2)]
+def spread(x, along):
+    return [(along(x, 1), 1), (along(x, -1), 3), (along(x, 2), 2)]
 
 
 def exchange_z(x, step):
@@ -428,14 +434,12 @@
     table = cosine_table()
     forward = split_table(np.kron(np.eye(WIDE // GROUP), table.T))
     inverse = split_table(np.kron(np.eye(WIDE // GROUP), table))
-    blocks = HALF // GROUP
-    by_layer = jnp.transpose(bands[0], (0, 3, 1, 2)).reshape(LAYERS, 2, ROWS_HERE, 2, blocks)
-    by_layer = jnp.pad(jnp.transpose(by_layer, (0, 1, 3, 2, 4)), ((0, 0),) * 4 + ((0, LANES - blocks),))
-
-    gradient, momentum, params, forward, inverse = (
-        pltpu.with_memory_space_constraint(x, pltpu.HBM) for x in (gradient, momentum, params, forward, inverse)
+    by_layer = jnp.transpose(bands[0], (0, 1, 3, 2))
+    gradient, momentum, params, forward, inverse, by_layer = (
+        pltpu.with_memory_space_constraint(x, pltpu.HBM)
+        for x in (gradient, momentum, params, forward, inverse, by_layer)
     )
-    theirs, own_gradient, own_momentum, own_params, forward_here, inverse_here = pick_theirs(
+    theirs, own_gradient, own_momentum, own_params, forward_here, inverse_here, by_layer = pick_theirs(
         place, by_layer, gradient, momentum, params, forward, inverse
     )
     received = swap(theirs)
@@ -449,7 +453,7 @@
 
     first = []
     for unit, block in enumerate(updated):
-        first.append([(block, 0)] + spread(block, along_first, unit, updated[unit + 1 :]))
+        first.append([(block, 0)] + spread(block, along_first))
     own = bring_together(place, first)
 
     new_momentum, tokens = None, []
@@ -460,16 +464,17 @@
         tokens.append(token)
 
     ahead, behind = along_second(own, 1), along_second(own, -1)
+    whole, token = write_blocks(place, None, [(own, 0, 0, 0)])
+    tokens.append(token)
     ahead, behind = after(ahead, *tokens), after(behind, *tokens)
     across = [along_second(part(ahead, 0), 1), along_second(part(behind, 1), -1)]
-    near = [(own, 0), (ahead, 1), (behind, 3)]
-    others = [(swap(copied(own, behind)), 0), (swap(ahead), 1), (swap(behind), 3)]
-    items = [(block, 0, steps, 0) for block, steps in near] + [(block, 0, steps, 1) for block, steps in others]
-    whole, token = write_blocks(place, None, items)
-    across = [after(block, token) for block in across]
-    others = [swap(block) for block in across]
-    for other, blocks in enumerate((across, others)):
-        whole, _ = write_blocks(place, whole, [(block, unit * UNIT, 2, other) for unit, block in enumerate(blocks)])
+    items = [(ahead, 0, 1, 0), (behind, 0, 3, 0), (swap(ahead), 0, 1, 1), (swap(behind), 0, 3, 1)]
+    whole, token = write_blocks(place, whole, items)
+    items = [(swap(copied(own, token)), 0, 0, 1)]
+    for unit, block in enumerate(across):
+        block = after(block, token)
+        items += [(block, unit * UNIT, 2, 0), (swap(block), unit * UNIT, 2, 1)]
+    whole, _ = write_blocks(place, whole, items)
     return new_momentum, whole.reshape(LAYERS, 16 * ROWS_HERE, WIDTH)
 
 

time: 87.5 us -> 84.8 us (0.969)
  starting transfers between devices: 29.7 us -> 25.2 us
  waiting for transfers between devices: 31 us -> 34.5 us
  local copies, waits for them, and re-layouts: 0.98 us -> 0 us
    ppermute x20, starting transfers between devices: 29.7 us -> 25.2 us  [move(): return lax.ppermute(x, ('rep', 'fsdp'), pairs)]
    ppermute x20, waiting for transfers between devices: 31 us -> 34.5 us  [move(): return lax.ppermute(x, ('rep', 'fsdp'), pairs)]
    reshape x2 -> x0, local copies, waits for them, and re-layouts: 0.98 us -> none  [shards(): jnp.transpose(bands[0], (0, 3, 1, 2))]
  transfers between devices with their start and end apart: 20 -> 20, of which waited for: 11 -> 13; matrix products, arithmetic and copies ran while one was open for 0% -> 0% of each run, Pallas kernels for 21% -> 19%
where the time goes in v6:
time: 84.8 us; the launch traced here: 84.7 us
  waiting for transfers between devices  34.5 us (41%)
  starting transfers between devices  25.2 us (30%)
  Pallas kernels  24.2 us (29%)
    ppermute x20, waiting for transfers between devices, move(): return lax.ppermute(x, ('rep', 'fsdp'), pairs)  34.5 us
    ppermute x20, starting transfers between devices, move(): return lax.ppermute(x, ('rep', 'fsdp'), pairs)  25.2 us
    pallas_call x3, Pallas kernels, write_blocks(): pl.pallas_call(kernel, out_shape=[jax.ShapeDtypeStruct((LAYERS, 16, ROWS_...  9.76 us
    pallas_call x2, Pallas kernels, keep_rest(): pl.pallas_call(kernel, out_shape=[jax.ShapeDtypeStruct(momentum.shape, jn...  7.81 us
    pallas_call x1, Pallas kernels, pick_theirs(): pl.pallas_call(kernel, out_shape=out_shapes, in_specs=[SMEM] + [HBM] * 6,...  3.1 us
  transfers between devices with their start and end apart: 20, of which 13 were waited for; matrix products, arithmetic and copies ran while one was open for 0% of the time, Pallas kernels for 19%

profile of v6, /device:TPU:1, one launch (start us, length us, event | category | flops | bytes accessed | tf_op | source)
XLA Modules:
  0.0 84.7 jit_solution(17144276424046028004)
XLA Ops:
  0.6 0.1 pad_add_fusion.place_ref
  0.7 3.1 %shard_map.95 = (bf16[4,8,6912]{2,1,0:T(8,128)(2,1)S(1)}, bf16[4,8,6912]{2,1,0:T(8,128)(2,1)S(1)}, f32[4,8,6912]{2,1,0:T(8,128)S(1)}, bf16[4,8,6912]{2,1,0:T(8,1...) custom-call(s32[4]{0:T(128)S(1)} %pad_add_fusion.place_ref, ...), custom_call_target="tpu_custom_call" | custom-call | flops 339738624 | bytes 6000000 | tf_op jit(solution)/shard_map/pallas_call | solution.py:139
  3.8 1.5 %collective-permute-start = (bf16[4,8,6912]{2,1,0:T(8,128)(2,1)S(1)}, bf16[4,8,6912]{2,1,0:T(8,128)(2,1)S(1)}, u32[]{:S(2)}, u32[]{:S(2)}) collective-permute-start(bf16[4,8,6912]{2,1,0:T(8,128)(2,1)S(1)} %get-tuple-element.25), channel_id=1, source_target_pairs={{0,16},{1,17},{2,18},{3,19},{4,20},{5,21},{6,22},{7,23},{8,24},{9,... | collective-permute-start | bytes 1327112 | tf_op jit(solution)/shard_map/ppermute | solution.py:363
  5.3 1.7 %shard_map.96.mine_ref = bf16[4,8,6912]{2,1,0:T(8,128)(2,1)S(1)} custom-call(s32[4]{0:T(128)S(1)} %pad_add_fusion.place_ref, s32[4,2,2,8,128]{4,3,2,1,0:T(8,128)S(1)} %get-tuple-element.20.bands_ref, bf16[4,8,6912]{2,1,0:T(8,128)(2,1)S(1)} %get-tuple-element.23.gradient_ref, f32[4,8,6912]{2,1,0:T(8,128)S(1)} %get-tuple-element.24.momentum_ref, ...), custom_call_target="tpu_custom_call" | custom-call | flops 339738624 | bytes 2000000 | tf_op jit(solution)/shard_map/pallas_call | solution.py:162
  7.0 0.1 shard_map.97
  7.1 3.9 %collective-permute-start.1 = (bf16[2,8,6912]{2,1,0:T(8,128)(2,1)S(1)}, bf16[2,8,6912]{2,1,0:T(8,128)(2,1)S(1)}, u32[]{:S(2)}, u32[]{:S(2)}) collective-permute-start(bf16[2,8,6912]{2,1,0:T(8,128)(2,1)S(1)} %get-tuple-element.26.mine_ref), channel_id=1, source_target_pairs={{0,32},{1,33},{2,34},{3,35},{4,36},{5,37},{6,38},{7,39},{8,40},{9,... | collective-permute-start | bytes 663560 | tf_op jit(solution)/shard_map/ppermute | solution.py:363
  11.1 0.1 collective-permute-start.3
  11.1 3.2 %collective-permute-done.1.received_ref = bf16[2,8,6912]{2,1,0:T(8,128)(2,1)S(1)} collective-permute-done((bf16[2,8,6912]{2,1,0:T(8,128)(2,1)S(1)}, bf16[2,8,6912]{2,1,0:T(8,128)(2,1)S(1)}, u32[]{:S(2)}, u32[]{:S(2)}) %collective-permute-start.1) | collective-permute-done | bytes 221216 | tf_op jit(solution)/shard_map/ppermute | solution.py:363
  14.4 0.1 collective-permute-start.2
  14.5 2.5 %collective-permute-done.3.received_ref = bf16[2,8,6912]{2,1,0:T(8,128)(2,1)S(1)} collective-permute-done((bf16[2,8,6912]{2,1,0:T(8,128)(2,1)S(1)}, bf16[2,8,6912]{2,1,0:T(8,128)(2,1)S(1)}, u32[]{:S(2)}, u32[]{:S(2)}) %collective-permute-start.3) | collective-permute-done | bytes 221216 | tf_op jit(solution)/shard_map/ppermute | solution.py:363
  17.1 0.1 collective-permute-start.7
  17.2 2.4 %collective-permute-done.2.received_ref = bf16[2,8,6912]{2,1,0:T(8,128)(2,1)S(1)} collective-permute-done((bf16[2,8,6912]{2,1,0:T(8,128)(2,1)S(1)}, bf16[2,8,6912]{2,1,0:T(8,128)(2,1)S(1)}, u32[]{:S(2)}, u32[]{:S(2)}) %collective-permute-start.2) | collective-permute-done | bytes 221216 | tf_op jit(solution)/shard_map/ppermute | solution.py:363
  19.6 0.3 shard_map.100.refs_0_
  19.9 1.4 %collective-permute-start.4 = (bf16[2,8,6912]{2,1,0:T(8,128)(2,1)S(1)}, bf16[2,8,6912]{2,1,0:T(8,128)(2,1)S(1)}, u32[]{:S(2)}, u32[]{:S(2)}) collective-permute-start(bf16[2,8,6912]{2,1,0:T(8,128)(2,1)S(1)} %shard_map.100.refs_0_), channel_id=1, source_target_pairs={{0,1},{1,2},{2,3},{3,0},{4,5},{5,6},{6,7},{7,4},{8,9},{9,10},{10,1... | collective-permute-start | bytes 663560 | tf_op jit(solution)/shard_map/ppermute | solution.py:363
  21.3 1.5 %collective-permute-start.5 = (bf16[2,8,6912]{2,1,0:T(8,128)(2,1)S(1)}, bf16[2,8,6912]{2,1,0:T(8,128)(2,1)S(1)}, u32[]{:S(2)}, u32[]{:S(2)}) collective-permute-start(bf16[2,8,6912]{2,1,0:T(8,128)(2,1)S(1)} %shard_map.100.refs_0_), channel_id=1, source_target_pairs={{0,3},{1,0},{2,1},{3,2},{4,7},{5,4},{6,5},{7,6},{8,11},{9,8},{10,9... | collective-permute-start | bytes 663560 | tf_op jit(solution)/shard_map/ppermute | solution.py:363
  22.8 1.6 %collective-permute-start.6 = (bf16[2,8,6912]{2,1,0:T(8,128)(2,1)S(1)}, bf16[2,8,6912]{2,1,0:T(8,128)(2,1)S(1)}, u32[]{:S(2)}, u32[]{:S(2)}) collective-permute-start(bf16[2,8,6912]{2,1,0:T(8,128)(2,1)S(1)} %shard_map.100.refs_0_), channel_id=1, source_target_pairs={{0,2},{1,3},{2,0},{3,1},{4,6},{5,7},{6,4},{7,5},{8,10},{9,11},{10,... | collective-permute-start | bytes 663560 | tf_op jit(solution)/shard_map/ppermute | solution.py:363
  24.4 0.3 shard_map.101.refs_4_
  24.8 0.5 collective-permute-start.8
  25.2 2.3 %collective-permute-start.9 = (bf16[2,8,6912]{2,1,0:T(8,128)(2,1)S(1)}, bf16[2,8,6912]{2,1,0:T(8,128)(2,1)S(1)}, u32[]{:S(2)}, u32[]{:S(2)}) collective-permute-start(bf16[2,8,6912]{2,1,0:T(8,128)(2,1)S(1)} %shard_map.101.refs_4_), channel_id=1, source_target_pairs={{0,3},{1,0},{2,1},{3,2},{4,7},{5,4},{6,5},{7,6},{8,11},{9,8},{10,9... | collective-permute-start | bytes 663560 | tf_op jit(solution)/shard_map/ppermute | solution.py:363
  27.5 0.2 collective-permute-start.10
  27.7 0.4 collective-permute-done.5.refs_2_
  28.1 1.8 %collective-permute-done.6.refs_3_ = bf16[2,8,6912]{2,1,0:T(8,128)(2,1)S(1)} collective-permute-done((bf16[2,8,6912]{2,1,0:T(8,128)(2,1)S(1)}, bf16[2,8,6912]{2,1,0:T(8,128)(2,1)S(1)}, u32[]{:S(2)}, u32[]{:S(2)}) %collective-permute-start.6) | collective-permute-done | bytes 221216 | tf_op jit(solution)/shard_map/ppermute | solution.py:363
  29.9 2.4 %collective-permute-done.8.refs_5_ = bf16[2,8,6912]{2,1,0:T(8,128)(2,1)S(1)} collective-permute-done((bf16[2,8,6912]{2,1,0:T(8,128)(2,1)S(1)}, bf16[2,8,6912]{2,1,0:T(8,128)(2,1)S(1)}, u32[]{:S(2)}, u32[]{:S(2)}) %collective-permute-start.8) | collective-permute-done | bytes 221216 | tf_op jit(solution)/shard_map/ppermute | solution.py:363
  32.3 2.1 %collective-permute-done.10.refs_7_ = bf16[2,8,6912]{2,1,0:T(8,128)(2,1)S(1)} collective-permute-done((bf16[2,8,6912]{2,1,0:T(8,128)(2,1)S(1)}, bf16[2,8,6912]{2,1,0:T(8,128)(2,1)S(1)}, u32[]{:S(2)}, u32[]{:S(2)}) %collective-permute-start.10) | collective-permute-done | bytes 221216 | tf_op jit(solution)/shard_map/ppermute | solution.py:363
  34.4 0.7 shard_map.102.refs_0_.x_ref
  35.0 1.3 %collective-permute-start.11 = (bf16[4,4,8,6912]{3,2,1,0:T(8,128)(2,1)S(1)}, bf16[4,4,8,6912]{3,2,1,0:T(8,128)(2,1)S(1)}, u32[]{:S(2)}, u32[]{:S(2)}) collective-permute-start(bf16[4,4,8,6912]{3,2,1,0:T(8,128)(2,1)S(1)} %shard_map.102.refs_0_.x_ref), channel_id=1, source_target_pairs={{0,4},{1,5},{2,6},{3,7},{4,8},{5,9},{6,10},{7,11},{8,12},{9,13},{1... | collective-permute-start | bytes 5308424 | tf_op jit(solution)/shard_map/ppermute | solution.py:363
  36.3 1.7 %collective-permute-start.12 = (bf16[4,4,8,6912]{3,2,1,0:T(8,128)(2,1)S(1)}, bf16[4,4,8,6912]{3,2,1,0:T(8,128)(2,1)S(1)}, u32[]{:S(2)}, u32[]{:S(2)}) collective-permute-start(bf16[4,4,8,6912]{3,2,1,0:T(8,128)(2,1)S(1)} %shard_map.102.refs_0_.x_ref), channel_id=1, source_target_pairs={{0,12},{1,13},{2,14},{3,15},{4,0},{5,1},{6,2},{7,3},{8,4},{9,5},{1... | collective-permute-start | bytes 5308424 | tf_op jit(solution)/shard_map/ppermute | solution.py:363
  38.0 1.9 %shard_map.105 = (bf16[4,16,8,13824]{3,2,1,0:T(8,128)(2,1)}, f32[8,128]{1,0:T(8,128)S(1)}) custom-call(s32[4]{0:T(128)S(1)} %pad_add_fusion.place_ref, bf16[4,4,8,6912]{3,2,1,0:T(8,128)(2,1)S(1)} %shard_map.102.refs_0_.x_ref), custom_call_target="tpu_custom_call" | custom-call | bytes 3538944 | tf_op jit(solution)/shard_map/pallas_call | solution.py:345
  39.9 3.9 %shard_map.103 = (f32[1,4,8,13824]{3,2,1,0:T(8,128)}, f32[8,128]{1,0:T(8,128)S(1)}) custom-call(s32[4,2,2,8,128]{4,3,2,1,0:T(8,128)S(1)} %get-tuple-element.20.bands_ref, bf16[1,4,8,13824]{3,2,1,0:T(8,128)(2,1)} %gradient_ref.5, f32[1,4,8,13824]{3,2,1,0:T(8,128)} %momentum_ref.5, bf16[2,256,256]{2,1,0:T(8,128)(2,1)S(1)} %get-tuple-element.21.table_ref.forward_ref, ...), custom_call_target="tpu_custom_call" | custom-call | flops 679477248 | bytes 3000000 | tf_op jit(solution)/shard_map/pallas_call | solution.py:247
  43.8 3.9 %shard_map.104 = (f32[1,4,8,13824]{3,2,1,0:T(8,128)}, f32[8,128]{1,0:T(8,128)S(1)}) custom-call(s32[4,2,2,8,128]{4,3,2,1,0:T(8,128)S(1)} %get-tuple-element.20.bands_ref, bf16[1,4,8,13824]{3,2,1,0:T(8,128)(2,1)} %gradient_ref.5, f32[1,4,8,13824]{3,2,1,0:T(8,128)} %momentum_ref.5, ...), custom_call_target="tpu_custom_call", output_to_operand_aliasing={{0}: (6, {})} | custom-call | flops 679477248 | bytes 3000000 | tf_op jit(solution)/shard_map/pallas_call | solution.py:247
  47.7 10.4 %collective-permute-done.11.x_ref = bf16[4,4,8,6912]{3,2,1,0:T(8,128)(2,1)S(1)} collective-permute-done((bf16[4,4,8,6912]{3,2,1,0:T(8,128)(2,1)S(1)}, bf16[4,4,8,6912]{3,2,1,0:T(8,128)(2,1)S(1)}, u32[]{:S(2)}, u32[]{:S(2)}) %collective-permute-start.11) | collective-permute-done | bytes 1769504 | tf_op jit(solution)/shard_map/ppermute | solution.py:363
  58.1 4.4 %collective-permute-start.13 = (bf16[4,4,8,6912]{3,2,1,0:T(8,128)(2,1)S(1)}, bf16[4,4,8,6912]{3,2,1,0:T(8,128)(2,1)S(1)}, u32[]{:S(2)}, u32[]{:S(2)}) collective-permute-start(bf16[4,4,8,6912]{3,2,1,0:T(8,128)(2,1)S(1)} %shard_map.106.refs_0_.x_ref), channel_id=1, source_target_pairs={{0,16},{1,17},{2,18},{3,19},{4,20},{5,21},{6,22},{7,23},{8,24},{9,... | collective-permute-start | bytes 5308424 | tf_op jit(solution)/shard_map/ppermute | solution.py:363
  62.5 0.4 collective-permute-start.14
  62.8 0.1 shard_map.110
  62.9 0.1 shard_map.112
  63.0 0.3 collective-permute-start.16
  63.2 2.5 %collective-permute-start.18 = (bf16[2,4,8,6912]{3,2,1,0:T(8,128)(2,1)S(1)}, bf16[2,4,8,6912]{3,2,1,0:T(8,128)(2,1)S(1)}, u32[]{:S(2)}, u32[]{:S(2)}) collective-permute-start(bf16[2,4,8,6912]{3,2,1,0:T(8,128)(2,1)S(1)} %shard_map.112), channel_id=1, source_target_pairs={{0,12},{1,13},{2,14},{3,15},{4,0},{5,1},{6,2},{7,3},{8,4},{9,5},{1... | collective-permute-start | bytes 2654216 | tf_op jit(solution)/shard_map/ppermute | solution.py:363
  65.7 0.1 collective-permute-done.13.refs_2_
  65.8 2.5 %collective-permute-done.14.refs_3_ = bf16[4,4,8,6912]{3,2,1,0:T(8,128)(2,1)S(1)} collective-permute-done((bf16[4,4,8,6912]{3,2,1,0:T(8,128)(2,1)S(1)}, bf16[4,4,8,6912]{3,2,1,0:T(8,128)(2,1)S(1)}, u32[]{:S(2)}, u32[]{:S(2)}) %collective-permute-start.14) | collective-permute-done | bytes 1769504 | tf_op jit(solution)/shard_map/ppermute | solution.py:363
  68.3 4.0 %shard_map.108 = (bf16[4,16,8,13824]{3,2,1,0:T(8,128)(2,1)}, f32[8,128]{1,0:T(8,128)S(1)}) custom-call(s32[4]{0:T(128)S(1)} %pad_add_fusion.place_ref, bf16[4,4,8,6912]{3,2,1,0:T(8,128)(2,1)S(1)} %shard_map.106.refs_0_.x_ref, bf16[4,4,8,6912]{3,2,1,0:T(8,128)(2,1)S(1)} %shard_map.107.refs_1_.x_ref, ...), custom_call_target="tpu_custom_call", output_to_operand_aliasing={{0}: (5, {})} | custom-call | bytes 14155776 | tf_op jit(solution)/shard_map/pallas_call | solution.py:345
  72.3 0.1 shard_map.109
  72.4 0.5 collective-permute-start.15
  72.9 3.6 %collective-permute-done.16.x_ref = bf16[2,4,8,6912]{3,2,1,0:T(8,128)(2,1)S(1)} collective-permute-done((bf16[2,4,8,6912]{3,2,1,0:T(8,128)(2,1)S(1)}, bf16[2,4,8,6912]{3,2,1,0:T(8,128)(2,1)S(1)}, u32[]{:S(2)}, u32[]{:S(2)}) %collective-permute-start.16) | collective-permute-done | bytes 884768 | tf_op jit(solution)/shard_map/ppermute | solution.py:363
  76.4 1.0 %collective-permute-start.17 = (bf16[2,4,8,6912]{3,2,1,0:T(8,128)(2,1)S(1)}, bf16[2,4,8,6912]{3,2,1,0:T(8,128)(2,1)S(1)}, u32[]{:S(2)}, u32[]{:S(2)}) collective-permute-start(bf16[2,4,8,6912]{3,2,1,0:T(8,128)(2,1)S(1)} %shard_map.111.refs_1_), channel_id=1, source_target_pairs={{0,16},{1,17},{2,18},{3,19},{4,20},{5,21},{6,22},{7,23},{8,24},{9,... | collective-permute-start | bytes 2654216 | tf_op jit(solution)/shard_map/ppermute | solution.py:363
  77.4 0.2 collective-permute-start.19
  77.7 1.8 %collective-permute-done.17.refs_2_ = bf16[2,4,8,6912]{3,2,1,0:T(8,128)(2,1)S(1)} collective-permute-done((bf16[2,4,8,6912]{3,2,1,0:T(8,128)(2,1)S(1)}, bf16[2,4,8,6912]{3,2,1,0:T(8,128)(2,1)S(1)}, u32[]{:S(2)}, u32[]{:S(2)}) %collective-permute-start.17) | collective-permute-done | bytes 884768 | tf_op jit(solution)/shard_map/ppermute | solution.py:363
  79.5 1.3 %collective-permute-done.19.refs_4_ = bf16[2,4,8,6912]{3,2,1,0:T(8,128)(2,1)S(1)} collective-permute-done((bf16[2,4,8,6912]{3,2,1,0:T(8,128)(2,1)S(1)}, bf16[2,4,8,6912]{3,2,1,0:T(8,128)(2,1)S(1)}, u32[]{:S(2)}, u32[]{:S(2)}) %collective-permute-start.19) | collective-permute-done | bytes 884768 | tf_op jit(solution)/shard_map/ppermute | solution.py:363
  80.8 3.9 %shard_map.114 = (bf16[4,16,8,13824]{3,2,1,0:T(8,128)(2,1)}, f32[8,128]{1,0:T(8,128)}) custom-call(s32[4]{0:T(128)S(1)} %pad_add_fusion.place_ref, bf16[4,4,8,6912]{3,2,1,0:T(8,128)(2,1)S(1)} %collective-permute-done.15.refs_0_, bf16[2,4,8,6912]{3,2,1,0:T(8,128)(2,1)S(1)} %shard_map.111.refs_1_, ...), custom_call_target="tpu_custom_call", output_to_operand_aliasing={{0}: (6, {})} | custom-call | bytes 10616832 | tf_op jit(solution)/shard_map/pallas_call | solution.py:345
  (13 shorter events, 0.1 us)
Async XLA Ops:
  3.8 3.2 %collective-permute-start = (bf16[4,8,6912]{2,1,0:T(8,128)(2,1)S(1)}, bf16[4,8,6912]{2,1,0:T(8,128)(2,1)S(1)}, u32[]{:S(2)}, u32[]{:S(2)}) collective-permute-start(bf16[4,8,6912]{2,1,0:T(8,128)(2,1)S(1)} %get-tuple-element.25), channel_id=1, source_target_pairs={{0,16},{1,17},{2,18},{3,19},{4,20},{5,21},{6,22},{7,23},{8,24},{9,... | collective-permute-start | bytes 1327112 | tf_op jit(solution)/shard_map/ppermute | solution.py:363
  7.1 7.2 %collective-permute-start.1 = (bf16[2,8,6912]{2,1,0:T(8,128)(2,1)S(1)}, bf16[2,8,6912]{2,1,0:T(8,128)(2,1)S(1)}, u32[]{:S(2)}, u32[]{:S(2)}) collective-permute-start(bf16[2,8,6912]{2,1,0:T(8,128)(2,1)S(1)} %get-tuple-element.26.mine_ref), channel_id=1, source_target_pairs={{0,32},{1,33},{2,34},{3,35},{4,36},{5,37},{6,38},{7,39},{8,40},{9,... | collective-permute-start | bytes 663560 | tf_op jit(solution)/shard_map/ppermute | solution.py:363
  11.1 6.0 %collective-permute-start.3 = (bf16[2,8,6912]{2,1,0:T(8,128)(2,1)S(1)}, bf16[2,8,6912]{2,1,0:T(8,128)(2,1)S(1)}, u32[]{:S(2)}, u32[]{:S(2)}) collective-permute-start(bf16[2,8,6912]{2,1,0:T(8,128)(2,1)S(1)} %get-tuple-element.28.mine_ref), channel_id=1, source_target_pairs={{0,32},{1,33},{2,34},{3,35},{4,36},{5,37},{6,38},{7,39},{8,40},{9,... | collective-permute-start | bytes 663560 | tf_op jit(solution)/shard_map/ppermute | solution.py:363
  14.4 5.2 %collective-permute-start.2 = (bf16[2,8,6912]{2,1,0:T(8,128)(2,1)S(1)}, bf16[2,8,6912]{2,1,0:T(8,128)(2,1)S(1)}, u32[]{:S(2)}, u32[]{:S(2)}) collective-permute-start(bf16[2,8,6912]{2,1,0:T(8,128)(2,1)S(1)} %shard_map.98.mine_ref), channel_id=1, source_target_pairs={{0,96},{1,97},{2,98},{3,99},{4,100},{5,101},{6,102},{7,103},{8,104... | collective-permute-start | bytes 663560 | tf_op jit(solution)/shard_map/ppermute | solution.py:363
  17.1 7.3 %collective-permute-start.7 = (bf16[2,8,6912]{2,1,0:T(8,128)(2,1)S(1)}, bf16[2,8,6912]{2,1,0:T(8,128)(2,1)S(1)}, u32[]{:S(2)}, u32[]{:S(2)}) collective-permute-start(bf16[2,8,6912]{2,1,0:T(8,128)(2,1)S(1)} %shard_map.99.refs_0_.mine_ref), channel_id=1, source_target_pairs={{0,96},{1,97},{2,98},{3,99},{4,100},{5,101},{6,102},{7,103},{8,104... | collective-permute-start | bytes 663560 | tf_op jit(solution)/shard_map/ppermute | solution.py:363
  19.9 7.6 %collective-permute-start.4 = (bf16[2,8,6912]{2,1,0:T(8,128)(2,1)S(1)}, bf16[2,8,6912]{2,1,0:T(8,128)(2,1)S(1)}, u32[]{:S(2)}, u32[]{:S(2)}) collective-permute-start(bf16[2,8,6912]{2,1,0:T(8,128)(2,1)S(1)} %shard_map.100.refs_0_), channel_id=1, source_target_pairs={{0,1},{1,2},{2,3},{3,0},{4,5},{5,6},{6,7},{7,4},{8,9},{9,10},{10,1... | collective-permute-start | bytes 663560 | tf_op jit(solution)/shard_map/ppermute | solution.py:363
  21.3 6.8 %collective-permute-start.5 = (bf16[2,8,6912]{2,1,0:T(8,128)(2,1)S(1)}, bf16[2,8,6912]{2,1,0:T(8,128)(2,1)S(1)}, u32[]{:S(2)}, u32[]{:S(2)}) collective-permute-start(bf16[2,8,6912]{2,1,0:T(8,128)(2,1)S(1)} %shard_map.100.refs_0_), channel_id=1, source_target_pairs={{0,3},{1,0},{2,1},{3,2},{4,7},{5,4},{6,5},{7,6},{8,11},{9,8},{10,9... | collective-permute-start | bytes 663560 | tf_op jit(solution)/shard_map/ppermute | solution.py:363
  22.8 7.1 %collective-permute-start.6 = (bf16[2,8,6912]{2,1,0:T(8,128)(2,1)S(1)}, bf16[2,8,6912]{2,1,0:T(8,128)(2,1)S(1)}, u32[]{:S(2)}, u32[]{:S(2)}) collective-permute-start(bf16[2,8,6912]{2,1,0:T(8,128)(2,1)S(1)} %shard_map.100.refs_0_), channel_id=1, source_target_pairs={{0,2},{1,3},{2,0},{3,1},{4,6},{5,7},{6,4},{7,5},{8,10},{9,11},{10,... | collective-permute-start | bytes 663560 | tf_op jit(solution)/shard_map/ppermute | solution.py:363
  24.8 7.5 %collective-permute-start.8 = (bf16[2,8,6912]{2,1,0:T(8,128)(2,1)S(1)}, bf16[2,8,6912]{2,1,0:T(8,128)(2,1)S(1)}, u32[]{:S(2)}, u32[]{:S(2)}) collective-permute-start(bf16[2,8,6912]{2,1,0:T(8,128)(2,1)S(1)} %shard_map.101.refs_4_), channel_id=1, source_target_pairs={{0,1},{1,2},{2,3},{3,0},{4,5},{5,6},{6,7},{7,4},{8,9},{9,10},{10,1... | collective-permute-start | bytes 663560 | tf_op jit(solution)/shard_map/ppermute | solution.py:363
  25.2 7.1 %collective-permute-start.9 = (bf16[2,8,6912]{2,1,0:T(8,128)(2,1)S(1)}, bf16[2,8,6912]{2,1,0:T(8,128)(2,1)S(1)}, u32[]{:S(2)}, u32[]{:S(2)}) collective-permute-start(bf16[2,8,6912]{2,1,0:T(8,128)(2,1)S(1)} %shard_map.101.refs_4_), channel_id=1, source_target_pairs={{0,3},{1,0},{2,1},{3,2},{4,7},{5,4},{6,5},{7,6},{8,11},{9,8},{10,9... | collective-permute-start | bytes 663560 | tf_op jit(solution)/shard_map/ppermute | solution.py:363
  27.5 6.9 %collective-permute-start.10 = (bf16[2,8,6912]{2,1,0:T(8,128)(2,1)S(1)}, bf16[2,8,6912]{2,1,0:T(8,128)(2,1)S(1)}, u32[]{:S(2)}, u32[]{:S(2)}) collective-permute-start(bf16[2,8,6912]{2,1,0:T(8,128)(2,1)S(1)} %shard_map.101.refs_4_), channel_id=1, source_target_pairs={{0,2},{1,3},{2,0},{3,1},{4,6},{5,7},{6,4},{7,5},{8,10},{9,11},{10,... | collective-permute-start | bytes 663560 | tf_op jit(solution)/shard_map/ppermute | solution.py:363
  35.0 23.0 %collective-permute-start.11 = (bf16[4,4,8,6912]{3,2,1,0:T(8,128)(2,1)S(1)}, bf16[4,4,8,6912]{3,2,1,0:T(8,128)(2,1)S(1)}, u32[]{:S(2)}, u32[]{:S(2)}) collective-permute-start(bf16[4,4,8,6912]{3,2,1,0:T(8,128)(2,1)S(1)} %shard_map.102.refs_0_.x_ref), channel_id=1, source_target_pairs={{0,4},{1,5},{2,6},{3,7},{4,8},{5,9},{6,10},{7,11},{8,12},{9,13},{1... | collective-permute-start | bytes 5308424 | tf_op jit(solution)/shard_map/ppermute | solution.py:363
  36.3 26.2 %collective-permute-start.12 = (bf16[4,4,8,6912]{3,2,1,0:T(8,128)(2,1)S(1)}, bf16[4,4,8,6912]{3,2,1,0:T(8,128)(2,1)S(1)}, u32[]{:S(2)}, u32[]{:S(2)}) collective-permute-start(bf16[4,4,8,6912]{3,2,1,0:T(8,128)(2,1)S(1)} %shard_map.102.refs_0_.x_ref), channel_id=1, source_target_pairs={{0,12},{1,13},{2,14},{3,15},{4,0},{5,1},{6,2},{7,3},{8,4},{9,5},{1... | collective-permute-start | bytes 5308424 | tf_op jit(solution)/shard_map/ppermute | solution.py:363
  58.1 7.7 %collective-permute-start.13 = (bf16[4,4,8,6912]{3,2,1,0:T(8,128)(2,1)S(1)}, bf16[4,4,8,6912]{3,2,1,0:T(8,128)(2,1)S(1)}, u32[]{:S(2)}, u32[]{:S(2)}) collective-permute-start(bf16[4,4,8,6912]{3,2,1,0:T(8,128)(2,1)S(1)} %shard_map.106.refs_0_.x_ref), channel_id=1, source_target_pairs={{0,16},{1,17},{2,18},{3,19},{4,20},{5,21},{6,22},{7,23},{8,24},{9,... | collective-permute-start | bytes 5308424 | tf_op jit(solution)/shard_map/ppermute | solution.py:363
  62.5 5.8 %collective-permute-start.14 = (bf16[4,4,8,6912]{3,2,1,0:T(8,128)(2,1)S(1)}, bf16[4,4,8,6912]{3,2,1,0:T(8,128)(2,1)S(1)}, u32[]{:S(2)}, u32[]{:S(2)}) collective-permute-start(bf16[4,4,8,6912]{3,2,1,0:T(8,128)(2,1)S(1)} %shard_map.107.refs_1_.x_ref), channel_id=1, source_target_pairs={{0,16},{1,17},{2,18},{3,19},{4,20},{5,21},{6,22},{7,23},{8,24},{9,... | collective-permute-start | bytes 5308424 | tf_op jit(solution)/shard_map/ppermute | solution.py:363
  63.0 13.5 %collective-permute-start.16 = (bf16[2,4,8,6912]{3,2,1,0:T(8,128)(2,1)S(1)}, bf16[2,4,8,6912]{3,2,1,0:T(8,128)(2,1)S(1)}, u32[]{:S(2)}, u32[]{:S(2)}) collective-permute-start(bf16[2,4,8,6912]{3,2,1,0:T(8,128)(2,1)S(1)} %shard_map.110), channel_id=1, source_target_pairs={{0,4},{1,5},{2,6},{3,7},{4,8},{5,9},{6,10},{7,11},{8,12},{9,13},{1... | collective-permute-start | bytes 2654216 | tf_op jit(solution)/shard_map/ppermute | solution.py:363
  63.2 14.2 %collective-permute-start.18 = (bf16[2,4,8,6912]{3,2,1,0:T(8,128)(2,1)S(1)}, bf16[2,4,8,6912]{3,2,1,0:T(8,128)(2,1)S(1)}, u32[]{:S(2)}, u32[]{:S(2)}) collective-permute-start(bf16[2,4,8,6912]{3,2,1,0:T(8,128)(2,1)S(1)} %shard_map.112), channel_id=1, source_target_pairs={{0,12},{1,13},{2,14},{3,15},{4,0},{5,1},{6,2},{7,3},{8,4},{9,5},{1... | collective-permute-start | bytes 2654216 | tf_op jit(solution)/shard_map/ppermute | solution.py:363
  72.4 8.3 %collective-permute-start.15 = (bf16[4,4,8,6912]{3,2,1,0:T(8,128)(2,1)S(1)}, bf16[4,4,8,6912]{3,2,1,0:T(8,128)(2,1)S(1)}, u32[]{:S(2)}, u32[]{:S(2)}) collective-permute-start(bf16[4,4,8,6912]{3,2,1,0:T(8,128)(2,1)S(1)} %shard_map.109), channel_id=1, source_target_pairs={{0,16},{1,17},{2,18},{3,19},{4,20},{5,21},{6,22},{7,23},{8,24},{9,... | collective-permute-start | bytes 5308424 | tf_op jit(solution)/shard_map/ppermute | solution.py:363
  76.4 3.1 %collective-permute-start.17 = (bf16[2,4,8,6912]{3,2,1,0:T(8,128)(2,1)S(1)}, bf16[2,4,8,6912]{3,2,1,0:T(8,128)(2,1)S(1)}, u32[]{:S(2)}, u32[]{:S(2)}) collective-permute-start(bf16[2,4,8,6912]{3,2,1,0:T(8,128)(2,1)S(1)} %shard_map.111.refs_1_), channel_id=1, source_target_pairs={{0,16},{1,17},{2,18},{3,19},{4,20},{5,21},{6,22},{7,23},{8,24},{9,... | collective-permute-start | bytes 2654216 | tf_op jit(solution)/shard_map/ppermute | solution.py:363
  77.4 3.3 %collective-permute-start.19 = (bf16[2,4,8,6912]{3,2,1,0:T(8,128)(2,1)S(1)}, bf16[2,4,8,6912]{3,2,1,0:T(8,128)(2,1)S(1)}, u32[]{:S(2)}, u32[]{:S(2)}) collective-permute-start(bf16[2,4,8,6912]{3,2,1,0:T(8,128)(2,1)S(1)} %shard_map.113.refs_3_), channel_id=1, source_target_pairs={{0,16},{1,17},{2,18},{3,19},{4,20},{5,21},{6,22},{7,23},{8,24},{9,... | collective-permute-start | bytes 2654216 | tf_op jit(solution)/shard_map/ppermute | solution.py:363

commit v7 on v6

--- a/solution.py
+++ b/solution.py
@@ -55,19 +55,17 @@
 def pick_tiles(bands_ref, side, layers, spectra):
     lane = lax.broadcasted_iota(jnp.int32, (ROWS_HERE, LANES), 1)
     upper = lax.shift_right_logical(lane, 6)
-    band = lax.bitwise_and(lax.shift_right_logical(lane, 3), 7)
+    bit = lax.shift_left(jnp.ones_like(lane), lax.bitwise_and(lax.shift_right_logical(lane, 3), 7))
     tiles = {}
     for i, layer in enumerate(layers):
-        first_bands = bands_ref[layer, 0, side]
-        second_bands = bands_ref[layer, 1, side]
+        chosen = bands_ref[layer, side]
         for tile in range(HALF // LANES):
             index = upper + (2 * tile + jnp.where(side == 0, 0, LANES - BLOCKS // 2))
-            first = jnp.take_along_axis(first_bands, index, axis=1)
-            second = jnp.take_along_axis(second_bands, index, axis=1)
+            here = jnp.take_along_axis(chosen, index, axis=1)
             row = (i * (HALF // WIDE) + tile // 2) * ROWS_HERE
             column = (tile % 2) * LANES
             values = spectra[row : row + ROWS_HERE, column : column + LANES]
-            tiles[i, tile] = jnp.where((first == band) | (second == band), values, 0.0)
+            tiles[i, tile] = jnp.where(lax.bitwise_and(here, bit) != 0, values, 0.0)
     return tiles
 
 
@@ -83,7 +81,7 @@
 HALF_LAYERS = jax.ShapeDtypeStruct((LAYERS, ROWS_HERE, HALF), jnp.bfloat16)
 HALF_MOMENTUM = jax.ShapeDtypeStruct((LAYERS, ROWS_HERE, HALF), jnp.float32)
 TABLE = jax.ShapeDtypeStruct((2, WIDE, WIDE), jnp.bfloat16)
-SIDE_BANDS = jax.ShapeDtypeStruct((LAYERS, 2, 2, ROWS_HERE, LANES), jnp.int32)
+SIDE_BANDS = jax.ShapeDtypeStruct((LAYERS, 2, ROWS_HERE, LANES), jnp.int32)
 TOKEN = jax.ShapeDtypeStruct((8, 128), jnp.float32)
 
 
@@ -122,9 +120,10 @@
         copies[0].wait()
         for layer in range(LAYERS):
             both = raw[layer]
-            for i in range(2):
-                bands_ref[layer, i, 0] = both[:, i, :LANES]
-                bands_ref[layer, i, 1] = both[:, i, BLOCKS - LANES :]
+            bits = lax.shift_left(jnp.ones_like(both), both)
+            bits = lax.bitwise_or(bits[:, 0], bits[:, 1])
+            bands_ref[layer, 0] = bits[:, :LANES]
+            bands_ref[layer, 1] = bits[:, BLOCKS - LANES :]
         copies.pop(0)
         copies[0].wait()
         for unit in range(UNITS):

time: 84.8 us -> 84.6 us (level)
  Pallas kernels: 24.2 us -> 23.1 us
  transfers between devices with their start and end apart: 20 -> 20, of which waited for: 13 -> 14; matrix products, arithmetic and copies ran while one was open for 0% -> 0% of each run, Pallas kernels for 19% -> 18%
where the time goes in v7:
time: 84.6 us; the launch traced here: 84.4 us
  waiting for transfers between devices  35 us (41%)
  starting transfers between devices  25.5 us (30%)
  Pallas kernels  23.1 us (27%)
    ppermute x20, waiting for transfers between devices, move(): return lax.ppermute(x, ('rep', 'fsdp'), pairs)  35 us
    ppermute x20, starting transfers between devices, move(): return lax.ppermute(x, ('rep', 'fsdp'), pairs)  25.5 us
    pallas_call x3, Pallas kernels, write_blocks(): pl.pallas_call(kernel, out_shape=[jax.ShapeDtypeStruct((LAYERS, 16, ROWS_...  9.76 us
    pallas_call x2, Pallas kernels, keep_rest(): pl.pallas_call(kernel, out_shape=[jax.ShapeDtypeStruct(momentum.shape, jn...  7.36 us
    pallas_call x1, Pallas kernels, pick_theirs(): pl.pallas_call(kernel, out_shape=out_shapes, in_specs=[SMEM] + [HBM] * 6,...  2.87 us
  transfers between devices with their start and end apart: 20, of which 14 were waited for; matrix products, arithmetic and copies ran while one was open for 0% of the time, Pallas kernels for 18%

profile of v7, /device:TPU:1, one launch (start us, length us, event | category | flops | bytes accessed | tf_op | source)
XLA Modules:
  0.0 84.4 jit_solution(15957444014077176508)
XLA Ops:
  0.6 0.1 pad_add_fusion.place_ref
  0.7 2.9 %shard_map.95 = (bf16[4,8,6912]{2,1,0:T(8,128)(2,1)S(1)}, bf16[4,8,6912]{2,1,0:T(8,128)(2,1)S(1)}, f32[4,8,6912]{2,1,0:T(8,128)S(1)}, bf16[4,8,6912]{2,1,0:T(8,1...) custom-call(s32[4]{0:T(128)S(1)} %pad_add_fusion.place_ref, ...), custom_call_target="tpu_custom_call" | custom-call | flops 339738624 | bytes 6000000 | tf_op jit(solution)/shard_map/pallas_call | solution.py:138
  3.6 1.5 %collective-permute-start = (bf16[4,8,6912]{2,1,0:T(8,128)(2,1)S(1)}, bf16[4,8,6912]{2,1,0:T(8,128)(2,1)S(1)}, u32[]{:S(2)}, u32[]{:S(2)}) collective-permute-start(bf16[4,8,6912]{2,1,0:T(8,128)(2,1)S(1)} %get-tuple-element.25), channel_id=1, source_target_pairs={{0,16},{1,17},{2,18},{3,19},{4,20},{5,21},{6,22},{7,23},{8,24},{9,... | collective-permute-start | bytes 1327112 | tf_op jit(solution)/shard_map/ppermute | solution.py:362
  5.1 1.3 %shard_map.96.mine_ref = bf16[4,8,6912]{2,1,0:T(8,128)(2,1)S(1)} custom-call(s32[4]{0:T(128)S(1)} %pad_add_fusion.place_ref, s32[4,2,8,128]{3,2,1,0:T(8,128)S(1)} %get-tuple-element.20.bands_ref, bf16[4,8,6912]{2,1,0:T(8,128)(2,1)S(1)} %get-tuple-element.23.gradient_ref, f32[4,8,6912]{2,1,0:T(8,128)S(1)} %get-tuple-element.24.momentum_ref, ...), custom_call_target="tpu_custom_call" | custom-call | flops 339738624 | bytes 2000000 | tf_op jit(solution)/shard_map/pallas_call | solution.py:161
  6.4 0.1 collective-permute-done.received_ref
  6.5 0.1 shard_map.97
  6.6 3.9 %collective-permute-start.1 = (bf16[2,8,6912]{2,1,0:T(8,128)(2,1)S(1)}, bf16[2,8,6912]{2,1,0:T(8,128)(2,1)S(1)}, u32[]{:S(2)}, u32[]{:S(2)}) collective-permute-start(bf16[2,8,6912]{2,1,0:T(8,128)(2,1)S(1)} %get-tuple-element.26.mine_ref), channel_id=1, source_target_pairs={{0,32},{1,33},{2,34},{3,35},{4,36},{5,37},{6,38},{7,39},{8,40},{9,... | collective-permute-start | bytes 663560 | tf_op jit(solution)/shard_map/ppermute | solution.py:362
  10.5 0.1 collective-permute-start.3
  10.6 3.2 %collective-permute-done.1.received_ref = bf16[2,8,6912]{2,1,0:T(8,128)(2,1)S(1)} collective-permute-done((bf16[2,8,6912]{2,1,0:T(8,128)(2,1)S(1)}, bf16[2,8,6912]{2,1,0:T(8,128)(2,1)S(1)}, u32[]{:S(2)}, u32[]{:S(2)}) %collective-permute-start.1) | collective-permute-done | bytes 221216 | tf_op jit(solution)/shard_map/ppermute | solution.py:362
  13.9 0.1 collective-permute-start.2
  14.0 2.5 %collective-permute-done.3.received_ref = bf16[2,8,6912]{2,1,0:T(8,128)(2,1)S(1)} collective-permute-done((bf16[2,8,6912]{2,1,0:T(8,128)(2,1)S(1)}, bf16[2,8,6912]{2,1,0:T(8,128)(2,1)S(1)}, u32[]{:S(2)}, u32[]{:S(2)}) %collective-permute-start.3) | collective-permute-done | bytes 221216 | tf_op jit(solution)/shard_map/ppermute | solution.py:362
  16.6 0.1 collective-permute-start.7
  16.7 2.4 %collective-permute-done.2.received_ref = bf16[2,8,6912]{2,1,0:T(8,128)(2,1)S(1)} collective-permute-done((bf16[2,8,6912]{2,1,0:T(8,128)(2,1)S(1)}, bf16[2,8,6912]{2,1,0:T(8,128)(2,1)S(1)}, u32[]{:S(2)}, u32[]{:S(2)}) %collective-permute-start.2) | collective-permute-done | bytes 221216 | tf_op jit(solution)/shard_map/ppermute | solution.py:362
  19.1 0.3 shard_map.100.refs_0_
  19.4 1.4 %collective-permute-start.4 = (bf16[2,8,6912]{2,1,0:T(8,128)(2,1)S(1)}, bf16[2,8,6912]{2,1,0:T(8,128)(2,1)S(1)}, u32[]{:S(2)}, u32[]{:S(2)}) collective-permute-start(bf16[2,8,6912]{2,1,0:T(8,128)(2,1)S(1)} %shard_map.100.refs_0_), channel_id=1, source_target_pairs={{0,1},{1,2},{2,3},{3,0},{4,5},{5,6},{6,7},{7,4},{8,9},{9,10},{10,1... | collective-permute-start | bytes 663560 | tf_op jit(solution)/shard_map/ppermute | solution.py:362
  20.8 1.5 %collective-permute-start.5 = (bf16[2,8,6912]{2,1,0:T(8,128)(2,1)S(1)}, bf16[2,8,6912]{2,1,0:T(8,128)(2,1)S(1)}, u32[]{:S(2)}, u32[]{:S(2)}) collective-permute-start(bf16[2,8,6912]{2,1,0:T(8,128)(2,1)S(1)} %shard_map.100.refs_0_), channel_id=1, source_target_pairs={{0,3},{1,0},{2,1},{3,2},{4,7},{5,4},{6,5},{7,6},{8,11},{9,8},{10,9... | collective-permute-start | bytes 663560 | tf_op jit(solution)/shard_map/ppermute | solution.py:362
  22.3 1.6 %collective-permute-start.6 = (bf16[2,8,6912]{2,1,0:T(8,128)(2,1)S(1)}, bf16[2,8,6912]{2,1,0:T(8,128)(2,1)S(1)}, u32[]{:S(2)}, u32[]{:S(2)}) collective-permute-start(bf16[2,8,6912]{2,1,0:T(8,128)(2,1)S(1)} %shard_map.100.refs_0_), channel_id=1, source_target_pairs={{0,2},{1,3},{2,0},{3,1},{4,6},{5,7},{6,4},{7,5},{8,10},{9,11},{10,... | collective-permute-start | bytes 663560 | tf_op jit(solution)/shard_map/ppermute | solution.py:362
  23.9 0.3 shard_map.101.refs_4_
  24.2 0.5 collective-permute-start.8
  24.7 2.3 %collective-permute-start.9 = (bf16[2,8,6912]{2,1,0:T(8,128)(2,1)S(1)}, bf16[2,8,6912]{2,1,0:T(8,128)(2,1)S(1)}, u32[]{:S(2)}, u32[]{:S(2)}) collective-permute-start(bf16[2,8,6912]{2,1,0:T(8,128)(2,1)S(1)} %shard_map.101.refs_4_), channel_id=1, source_target_pairs={{0,3},{1,0},{2,1},{3,2},{4,7},{5,4},{6,5},{7,6},{8,11},{9,8},{10,9... | collective-permute-start | bytes 663560 | tf_op jit(solution)/shard_map/ppermute | solution.py:362
  27.0 0.2 collective-permute-start.10
  27.2 0.4 collective-permute-done.5.refs_2_
  27.6 1.6 %collective-permute-done.6.refs_3_ = bf16[2,8,6912]{2,1,0:T(8,128)(2,1)S(1)} collective-permute-done((bf16[2,8,6912]{2,1,0:T(8,128)(2,1)S(1)}, bf16[2,8,6912]{2,1,0:T(8,128)(2,1)S(1)}, u32[]{:S(2)}, u32[]{:S(2)}) %collective-permute-start.6) | collective-permute-done | bytes 221216 | tf_op jit(solution)/shard_map/ppermute | solution.py:362
  29.2 2.6 %collective-permute-done.8.refs_5_ = bf16[2,8,6912]{2,1,0:T(8,128)(2,1)S(1)} collective-permute-done((bf16[2,8,6912]{2,1,0:T(8,128)(2,1)S(1)}, bf16[2,8,6912]{2,1,0:T(8,128)(2,1)S(1)}, u32[]{:S(2)}, u32[]{:S(2)}) %collective-permute-start.8) | collective-permute-done | bytes 221216 | tf_op jit(solution)/shard_map/ppermute | solution.py:362
  31.8 2.1 %collective-permute-done.10.refs_7_ = bf16[2,8,6912]{2,1,0:T(8,128)(2,1)S(1)} collective-permute-done((bf16[2,8,6912]{2,1,0:T(8,128)(2,1)S(1)}, bf16[2,8,6912]{2,1,0:T(8,128)(2,1)S(1)}, u32[]{:S(2)}, u32[]{:S(2)}) %collective-permute-start.10) | collective-permute-done | bytes 221216 | tf_op jit(solution)/shard_map/ppermute | solution.py:362
  33.9 0.7 shard_map.102.refs_0_.x_ref
  34.5 1.3 %collective-permute-start.11 = (bf16[4,4,8,6912]{3,2,1,0:T(8,128)(2,1)S(1)}, bf16[4,4,8,6912]{3,2,1,0:T(8,128)(2,1)S(1)}, u32[]{:S(2)}, u32[]{:S(2)}) collective-permute-start(bf16[4,4,8,6912]{3,2,1,0:T(8,128)(2,1)S(1)} %shard_map.102.refs_0_.x_ref), channel_id=1, source_target_pairs={{0,4},{1,5},{2,6},{3,7},{4,8},{5,9},{6,10},{7,11},{8,12},{9,13},{1... | collective-permute-start | bytes 5308424 | tf_op jit(solution)/shard_map/ppermute | solution.py:362
  35.8 1.7 %collective-permute-start.12 = (bf16[4,4,8,6912]{3,2,1,0:T(8,128)(2,1)S(1)}, bf16[4,4,8,6912]{3,2,1,0:T(8,128)(2,1)S(1)}, u32[]{:S(2)}, u32[]{:S(2)}) collective-permute-start(bf16[4,4,8,6912]{3,2,1,0:T(8,128)(2,1)S(1)} %shard_map.102.refs_0_.x_ref), channel_id=1, source_target_pairs={{0,12},{1,13},{2,14},{3,15},{4,0},{5,1},{6,2},{7,3},{8,4},{9,5},{1... | collective-permute-start | bytes 5308424 | tf_op jit(solution)/shard_map/ppermute | solution.py:362
  37.4 1.9 %shard_map.105 = (bf16[4,16,8,13824]{3,2,1,0:T(8,128)(2,1)}, f32[8,128]{1,0:T(8,128)S(1)}) custom-call(s32[4]{0:T(128)S(1)} %pad_add_fusion.place_ref, bf16[4,4,8,6912]{3,2,1,0:T(8,128)(2,1)S(1)} %shard_map.102.refs_0_.x_ref), custom_call_target="tpu_custom_call" | custom-call | bytes 3538944 | tf_op jit(solution)/shard_map/pallas_call | solution.py:344
  39.3 3.7 %shard_map.103 = (f32[1,4,8,13824]{3,2,1,0:T(8,128)}, f32[8,128]{1,0:T(8,128)S(1)}) custom-call(s32[4,2,8,128]{3,2,1,0:T(8,128)S(1)} %get-tuple-element.20.bands_ref, bf16[1,4,8,13824]{3,2,1,0:T(8,128)(2,1)} %gradient_ref.5, f32[1,4,8,13824]{3,2,1,0:T(8,128)} %momentum_ref.5, bf16[2,256,256]{2,1,0:T(8,128)(2,1)S(1)} %get-tuple-element.21.table_ref.forward_ref, ...), custom_call_target="tpu_custom_call" | custom-call | flops 679477248 | bytes 3000000 | tf_op jit(solution)/shard_map/pallas_call | solution.py:246
  43.0 3.7 %shard_map.104 = (f32[1,4,8,13824]{3,2,1,0:T(8,128)}, f32[8,128]{1,0:T(8,128)S(1)}) custom-call(s32[4,2,8,128]{3,2,1,0:T(8,128)S(1)} %get-tuple-element.20.bands_ref, bf16[1,4,8,13824]{3,2,1,0:T(8,128)(2,1)} %gradient_ref.5, f32[1,4,8,13824]{3,2,1,0:T(8,128)} %momentum_ref.5, ...), custom_call_target="tpu_custom_call", output_to_operand_aliasing={{0}: (6, {})} | custom-call | flops 679477248 | bytes 3000000 | tf_op jit(solution)/shard_map/pallas_call | solution.py:246
  46.7 10.9 %collective-permute-done.11.x_ref = bf16[4,4,8,6912]{3,2,1,0:T(8,128)(2,1)S(1)} collective-permute-done((bf16[4,4,8,6912]{3,2,1,0:T(8,128)(2,1)S(1)}, bf16[4,4,8,6912]{3,2,1,0:T(8,128)(2,1)S(1)}, u32[]{:S(2)}, u32[]{:S(2)}) %collective-permute-start.11) | collective-permute-done | bytes 1769504 | tf_op jit(solution)/shard_map/ppermute | solution.py:362
  57.6 4.7 %collective-permute-start.13 = (bf16[4,4,8,6912]{3,2,1,0:T(8,128)(2,1)S(1)}, bf16[4,4,8,6912]{3,2,1,0:T(8,128)(2,1)S(1)}, u32[]{:S(2)}, u32[]{:S(2)}) collective-permute-start(bf16[4,4,8,6912]{3,2,1,0:T(8,128)(2,1)S(1)} %shard_map.106.refs_0_.x_ref), channel_id=1, source_target_pairs={{0,16},{1,17},{2,18},{3,19},{4,20},{5,21},{6,22},{7,23},{8,24},{9,... | collective-permute-start | bytes 5308424 | tf_op jit(solution)/shard_map/ppermute | solution.py:362
  62.2 0.4 collective-permute-start.14
  62.7 0.1 shard_map.112
  62.7 0.3 collective-permute-start.16
  63.0 2.5 %collective-permute-start.18 = (bf16[2,4,8,6912]{3,2,1,0:T(8,128)(2,1)S(1)}, bf16[2,4,8,6912]{3,2,1,0:T(8,128)(2,1)S(1)}, u32[]{:S(2)}, u32[]{:S(2)}) collective-permute-start(bf16[2,4,8,6912]{3,2,1,0:T(8,128)(2,1)S(1)} %shard_map.112), channel_id=1, source_target_pairs={{0,12},{1,13},{2,14},{3,15},{4,0},{5,1},{6,2},{7,3},{8,4},{9,5},{1... | collective-permute-start | bytes 2654216 | tf_op jit(solution)/shard_map/ppermute | solution.py:362
  65.5 0.1 collective-permute-done.13.refs_2_
  65.6 2.5 %collective-permute-done.14.refs_3_ = bf16[4,4,8,6912]{3,2,1,0:T(8,128)(2,1)S(1)} collective-permute-done((bf16[4,4,8,6912]{3,2,1,0:T(8,128)(2,1)S(1)}, bf16[4,4,8,6912]{3,2,1,0:T(8,128)(2,1)S(1)}, u32[]{:S(2)}, u32[]{:S(2)}) %collective-permute-start.14) | collective-permute-done | bytes 1769504 | tf_op jit(solution)/shard_map/ppermute | solution.py:362
  68.1 4.0 %shard_map.108 = (bf16[4,16,8,13824]{3,2,1,0:T(8,128)(2,1)}, f32[8,128]{1,0:T(8,128)S(1)}) custom-call(s32[4]{0:T(128)S(1)} %pad_add_fusion.place_ref, bf16[4,4,8,6912]{3,2,1,0:T(8,128)(2,1)S(1)} %shard_map.106.refs_0_.x_ref, bf16[4,4,8,6912]{3,2,1,0:T(8,128)(2,1)S(1)} %shard_map.107.refs_1_.x_ref, ...), custom_call_target="tpu_custom_call", output_to_operand_aliasing={{0}: (5, {})} | custom-call | bytes 14155776 | tf_op jit(solution)/shard_map/pallas_call | solution.py:344
  72.1 0.1 shard_map.109
  72.2 0.5 collective-permute-start.15
  72.7 3.6 %collective-permute-done.16.x_ref = bf16[2,4,8,6912]{3,2,1,0:T(8,128)(2,1)S(1)} collective-permute-done((bf16[2,4,8,6912]{3,2,1,0:T(8,128)(2,1)S(1)}, bf16[2,4,8,6912]{3,2,1,0:T(8,128)(2,1)S(1)}, u32[]{:S(2)}, u32[]{:S(2)}) %collective-permute-start.16) | collective-permute-done | bytes 884768 | tf_op jit(solution)/shard_map/ppermute | solution.py:362
  76.2 1.0 %collective-permute-start.17 = (bf16[2,4,8,6912]{3,2,1,0:T(8,128)(2,1)S(1)}, bf16[2,4,8,6912]{3,2,1,0:T(8,128)(2,1)S(1)}, u32[]{:S(2)}, u32[]{:S(2)}) collective-permute-start(bf16[2,4,8,6912]{3,2,1,0:T(8,128)(2,1)S(1)} %shard_map.111.refs_1_), channel_id=1, source_target_pairs={{0,16},{1,17},{2,18},{3,19},{4,20},{5,21},{6,22},{7,23},{8,24},{9,... | collective-permute-start | bytes 2654216 | tf_op jit(solution)/shard_map/ppermute | solution.py:362
  77.2 0.3 collective-permute-start.19
  77.5 1.8 %collective-permute-done.17.refs_2_ = bf16[2,4,8,6912]{3,2,1,0:T(8,128)(2,1)S(1)} collective-permute-done((bf16[2,4,8,6912]{3,2,1,0:T(8,128)(2,1)S(1)}, bf16[2,4,8,6912]{3,2,1,0:T(8,128)(2,1)S(1)}, u32[]{:S(2)}, u32[]{:S(2)}) %collective-permute-start.17) | collective-permute-done | bytes 884768 | tf_op jit(solution)/shard_map/ppermute | solution.py:362
  79.3 1.3 %collective-permute-done.19.refs_4_ = bf16[2,4,8,6912]{3,2,1,0:T(8,128)(2,1)S(1)} collective-permute-done((bf16[2,4,8,6912]{3,2,1,0:T(8,128)(2,1)S(1)}, bf16[2,4,8,6912]{3,2,1,0:T(8,128)(2,1)S(1)}, u32[]{:S(2)}, u32[]{:S(2)}) %collective-permute-start.19) | collective-permute-done | bytes 884768 | tf_op jit(solution)/shard_map/ppermute | solution.py:362
  80.5 3.9 %shard_map.114 = (bf16[4,16,8,13824]{3,2,1,0:T(8,128)(2,1)}, f32[8,128]{1,0:T(8,128)}) custom-call(s32[4]{0:T(128)S(1)} %pad_add_fusion.place_ref, bf16[4,4,8,6912]{3,2,1,0:T(8,128)(2,1)S(1)} %collective-permute-done.15.refs_0_, bf16[2,4,8,6912]{3,2,1,0:T(8,128)(2,1)S(1)} %shard_map.111.refs_1_, ...), custom_call_target="tpu_custom_call", output_to_operand_aliasing={{0}: (6, {})} | custom-call | bytes 10616832 | tf_op jit(solution)/shard_map/pallas_call | solution.py:344
  (13 shorter events, 0.2 us)
Async XLA Ops:
  3.6 2.9 %collective-permute-start = (bf16[4,8,6912]{2,1,0:T(8,128)(2,1)S(1)}, bf16[4,8,6912]{2,1,0:T(8,128)(2,1)S(1)}, u32[]{:S(2)}, u32[]{:S(2)}) collective-permute-start(bf16[4,8,6912]{2,1,0:T(8,128)(2,1)S(1)} %get-tuple-element.25), channel_id=1, source_target_pairs={{0,16},{1,17},{2,18},{3,19},{4,20},{5,21},{6,22},{7,23},{8,24},{9,... | collective-permute-start | bytes 1327112 | tf_op jit(solution)/shard_map/ppermute | solution.py:362
  6.6 7.2 %collective-permute-start.1 = (bf16[2,8,6912]{2,1,0:T(8,128)(2,1)S(1)}, bf16[2,8,6912]{2,1,0:T(8,128)(2,1)S(1)}, u32[]{:S(2)}, u32[]{:S(2)}) collective-permute-start(bf16[2,8,6912]{2,1,0:T(8,128)(2,1)S(1)} %get-tuple-element.26.mine_ref), channel_id=1, source_target_pairs={{0,32},{1,33},{2,34},{3,35},{4,36},{5,37},{6,38},{7,39},{8,40},{9,... | collective-permute-start | bytes 663560 | tf_op jit(solution)/shard_map/ppermute | solution.py:362
  10.5 6.0 %collective-permute-start.3 = (bf16[2,8,6912]{2,1,0:T(8,128)(2,1)S(1)}, bf16[2,8,6912]{2,1,0:T(8,128)(2,1)S(1)}, u32[]{:S(2)}, u32[]{:S(2)}) collective-permute-start(bf16[2,8,6912]{2,1,0:T(8,128)(2,1)S(1)} %get-tuple-element.28.mine_ref), channel_id=1, source_target_pairs={{0,32},{1,33},{2,34},{3,35},{4,36},{5,37},{6,38},{7,39},{8,40},{9,... | collective-permute-start | bytes 663560 | tf_op jit(solution)/shard_map/ppermute | solution.py:362
  13.9 5.2 %collective-permute-start.2 = (bf16[2,8,6912]{2,1,0:T(8,128)(2,1)S(1)}, bf16[2,8,6912]{2,1,0:T(8,128)(2,1)S(1)}, u32[]{:S(2)}, u32[]{:S(2)}) collective-permute-start(bf16[2,8,6912]{2,1,0:T(8,128)(2,1)S(1)} %shard_map.98.mine_ref), channel_id=1, source_target_pairs={{0,96},{1,97},{2,98},{3,99},{4,100},{5,101},{6,102},{7,103},{8,104... | collective-permute-start | bytes 663560 | tf_op jit(solution)/shard_map/ppermute | solution.py:362
  16.6 7.3 %collective-permute-start.7 = (bf16[2,8,6912]{2,1,0:T(8,128)(2,1)S(1)}, bf16[2,8,6912]{2,1,0:T(8,128)(2,1)S(1)}, u32[]{:S(2)}, u32[]{:S(2)}) collective-permute-start(bf16[2,8,6912]{2,1,0:T(8,128)(2,1)S(1)} %shard_map.99.refs_0_.mine_ref), channel_id=1, source_target_pairs={{0,96},{1,97},{2,98},{3,99},{4,100},{5,101},{6,102},{7,103},{8,104... | collective-permute-start | bytes 663560 | tf_op jit(solution)/shard_map/ppermute | solution.py:362
  19.4 7.6 %collective-permute-start.4 = (bf16[2,8,6912]{2,1,0:T(8,128)(2,1)S(1)}, bf16[2,8,6912]{2,1,0:T(8,128)(2,1)S(1)}, u32[]{:S(2)}, u32[]{:S(2)}) collective-permute-start(bf16[2,8,6912]{2,1,0:T(8,128)(2,1)S(1)} %shard_map.100.refs_0_), channel_id=1, source_target_pairs={{0,1},{1,2},{2,3},{3,0},{4,5},{5,6},{6,7},{7,4},{8,9},{9,10},{10,1... | collective-permute-start | bytes 663560 | tf_op jit(solution)/shard_map/ppermute | solution.py:362
  20.8 6.8 %collective-permute-start.5 = (bf16[2,8,6912]{2,1,0:T(8,128)(2,1)S(1)}, bf16[2,8,6912]{2,1,0:T(8,128)(2,1)S(1)}, u32[]{:S(2)}, u32[]{:S(2)}) collective-permute-start(bf16[2,8,6912]{2,1,0:T(8,128)(2,1)S(1)} %shard_map.100.refs_0_), channel_id=1, source_target_pairs={{0,3},{1,0},{2,1},{3,2},{4,7},{5,4},{6,5},{7,6},{8,11},{9,8},{10,9... | collective-permute-start | bytes 663560 | tf_op jit(solution)/shard_map/ppermute | solution.py:362
  22.3 6.9 %collective-permute-start.6 = (bf16[2,8,6912]{2,1,0:T(8,128)(2,1)S(1)}, bf16[2,8,6912]{2,1,0:T(8,128)(2,1)S(1)}, u32[]{:S(2)}, u32[]{:S(2)}) collective-permute-start(bf16[2,8,6912]{2,1,0:T(8,128)(2,1)S(1)} %shard_map.100.refs_0_), channel_id=1, source_target_pairs={{0,2},{1,3},{2,0},{3,1},{4,6},{5,7},{6,4},{7,5},{8,10},{9,11},{10,... | collective-permute-start | bytes 663560 | tf_op jit(solution)/shard_map/ppermute | solution.py:362
  24.2 7.5 %collective-permute-start.8 = (bf16[2,8,6912]{2,1,0:T(8,128)(2,1)S(1)}, bf16[2,8,6912]{2,1,0:T(8,128)(2,1)S(1)}, u32[]{:S(2)}, u32[]{:S(2)}) collective-permute-start(bf16[2,8,6912]{2,1,0:T(8,128)(2,1)S(1)} %shard_map.101.refs_4_), channel_id=1, source_target_pairs={{0,1},{1,2},{2,3},{3,0},{4,5},{5,6},{6,7},{7,4},{8,9},{9,10},{10,1... | collective-permute-start | bytes 663560 | tf_op jit(solution)/shard_map/ppermute | solution.py:362
  24.7 7.1 %collective-permute-start.9 = (bf16[2,8,6912]{2,1,0:T(8,128)(2,1)S(1)}, bf16[2,8,6912]{2,1,0:T(8,128)(2,1)S(1)}, u32[]{:S(2)}, u32[]{:S(2)}) collective-permute-start(bf16[2,8,6912]{2,1,0:T(8,128)(2,1)S(1)} %shard_map.101.refs_4_), channel_id=1, source_target_pairs={{0,3},{1,0},{2,1},{3,2},{4,7},{5,4},{6,5},{7,6},{8,11},{9,8},{10,9... | collective-permute-start | bytes 663560 | tf_op jit(solution)/shard_map/ppermute | solution.py:362
  27.0 6.9 %collective-permute-start.10 = (bf16[2,8,6912]{2,1,0:T(8,128)(2,1)S(1)}, bf16[2,8,6912]{2,1,0:T(8,128)(2,1)S(1)}, u32[]{:S(2)}, u32[]{:S(2)}) collective-permute-start(bf16[2,8,6912]{2,1,0:T(8,128)(2,1)S(1)} %shard_map.101.refs_4_), channel_id=1, source_target_pairs={{0,2},{1,3},{2,0},{3,1},{4,6},{5,7},{6,4},{7,5},{8,10},{9,11},{10,... | collective-permute-start | bytes 663560 | tf_op jit(solution)/shard_map/ppermute | solution.py:362
  34.5 23.0 %collective-permute-start.11 = (bf16[4,4,8,6912]{3,2,1,0:T(8,128)(2,1)S(1)}, bf16[4,4,8,6912]{3,2,1,0:T(8,128)(2,1)S(1)}, u32[]{:S(2)}, u32[]{:S(2)}) collective-permute-start(bf16[4,4,8,6912]{3,2,1,0:T(8,128)(2,1)S(1)} %shard_map.102.refs_0_.x_ref), channel_id=1, source_target_pairs={{0,4},{1,5},{2,6},{3,7},{4,8},{5,9},{6,10},{7,11},{8,12},{9,13},{1... | collective-permute-start | bytes 5308424 | tf_op jit(solution)/shard_map/ppermute | solution.py:362
  35.8 26.4 %collective-permute-start.12 = (bf16[4,4,8,6912]{3,2,1,0:T(8,128)(2,1)S(1)}, bf16[4,4,8,6912]{3,2,1,0:T(8,128)(2,1)S(1)}, u32[]{:S(2)}, u32[]{:S(2)}) collective-permute-start(bf16[4,4,8,6912]{3,2,1,0:T(8,128)(2,1)S(1)} %shard_map.102.refs_0_.x_ref), channel_id=1, source_target_pairs={{0,12},{1,13},{2,14},{3,15},{4,0},{5,1},{6,2},{7,3},{8,4},{9,5},{1... | collective-permute-start | bytes 5308424 | tf_op jit(solution)/shard_map/ppermute | solution.py:362
  57.6 8.0 %collective-permute-start.13 = (bf16[4,4,8,6912]{3,2,1,0:T(8,128)(2,1)S(1)}, bf16[4,4,8,6912]{3,2,1,0:T(8,128)(2,1)S(1)}, u32[]{:S(2)}, u32[]{:S(2)}) collective-permute-start(bf16[4,4,8,6912]{3,2,1,0:T(8,128)(2,1)S(1)} %shard_map.106.refs_0_.x_ref), channel_id=1, source_target_pairs={{0,16},{1,17},{2,18},{3,19},{4,20},{5,21},{6,22},{7,23},{8,24},{9,... | collective-permute-start | bytes 5308424 | tf_op jit(solution)/shard_map/ppermute | solution.py:362
  62.2 5.8 %collective-permute-start.14 = (bf16[4,4,8,6912]{3,2,1,0:T(8,128)(2,1)S(1)}, bf16[4,4,8,6912]{3,2,1,0:T(8,128)(2,1)S(1)}, u32[]{:S(2)}, u32[]{:S(2)}) collective-permute-start(bf16[4,4,8,6912]{3,2,1,0:T(8,128)(2,1)S(1)} %shard_map.107.refs_1_.x_ref), channel_id=1, source_target_pairs={{0,16},{1,17},{2,18},{3,19},{4,20},{5,21},{6,22},{7,23},{8,24},{9,... | collective-permute-start | bytes 5308424 | tf_op jit(solution)/shard_map/ppermute | solution.py:362
  62.7 13.5 %collective-permute-start.16 = (bf16[2,4,8,6912]{3,2,1,0:T(8,128)(2,1)S(1)}, bf16[2,4,8,6912]{3,2,1,0:T(8,128)(2,1)S(1)}, u32[]{:S(2)}, u32[]{:S(2)}) collective-permute-start(bf16[2,4,8,6912]{3,2,1,0:T(8,128)(2,1)S(1)} %shard_map.110), channel_id=1, source_target_pairs={{0,4},{1,5},{2,6},{3,7},{4,8},{5,9},{6,10},{7,11},{8,12},{9,13},{1... | collective-permute-start | bytes 2654216 | tf_op jit(solution)/shard_map/ppermute | solution.py:362
  63.0 14.2 %collective-permute-start.18 = (bf16[2,4,8,6912]{3,2,1,0:T(8,128)(2,1)S(1)}, bf16[2,4,8,6912]{3,2,1,0:T(8,128)(2,1)S(1)}, u32[]{:S(2)}, u32[]{:S(2)}) collective-permute-start(bf16[2,4,8,6912]{3,2,1,0:T(8,128)(2,1)S(1)} %shard_map.112), channel_id=1, source_target_pairs={{0,12},{1,13},{2,14},{3,15},{4,0},{5,1},{6,2},{7,3},{8,4},{9,5},{1... | collective-permute-start | bytes 2654216 | tf_op jit(solution)/shard_map/ppermute | solution.py:362
  72.2 8.3 %collective-permute-start.15 = (bf16[4,4,8,6912]{3,2,1,0:T(8,128)(2,1)S(1)}, bf16[4,4,8,6912]{3,2,1,0:T(8,128)(2,1)S(1)}, u32[]{:S(2)}, u32[]{:S(2)}) collective-permute-start(bf16[4,4,8,6912]{3,2,1,0:T(8,128)(2,1)S(1)} %shard_map.109), channel_id=1, source_target_pairs={{0,16},{1,17},{2,18},{3,19},{4,20},{5,21},{6,22},{7,23},{8,24},{9,... | collective-permute-start | bytes 5308424 | tf_op jit(solution)/shard_map/ppermute | solution.py:362
  76.2 3.1 %collective-permute-start.17 = (bf16[2,4,8,6912]{3,2,1,0:T(8,128)(2,1)S(1)}, bf16[2,4,8,6912]{3,2,1,0:T(8,128)(2,1)S(1)}, u32[]{:S(2)}, u32[]{:S(2)}) collective-permute-start(bf16[2,4,8,6912]{3,2,1,0:T(8,128)(2,1)S(1)} %shard_map.111.refs_1_), channel_id=1, source_target_pairs={{0,16},{1,17},{2,18},{3,19},{4,20},{5,21},{6,22},{7,23},{8,24},{9,... | collective-permute-start | bytes 2654216 | tf_op jit(solution)/shard_map/ppermute | solution.py:362
  77.2 3.3 %collective-permute-start.19 = (bf16[2,4,8,6912]{3,2,1,0:T(8,128)(2,1)S(1)}, bf16[2,4,8,6912]{3,2,1,0:T(8,128)(2,1)S(1)}, u32[]{:S(2)}, u32[]{:S(2)}) collective-permute-start(bf16[2,4,8,6912]{3,2,1,0:T(8,128)(2,1)S(1)} %shard_map.113.refs_3_), channel_id=1, source_target_pairs={{0,16},{1,17},{2,18},{3,19},{4,20},{5,21},{6,22},{7,23},{8,24},{9,... | collective-permute-start | bytes 2654216 | tf_op jit(solution)/shard_map/ppermute | solution.py:362

commit v8 on v7

--- a/solution.py
+++ b/solution.py
@@ -323,12 +323,17 @@
         for block, (_, first_layer, steps, other) in zip(ins, items):
             side = core if other == 0 else 1 - core
             columns = pl.ds(pl.multiple_of(side * HALF, LANES), HALF)
-            here = lax.rem(jnp.where(side == 0, y, x) + (4 - steps), 4)
-            for i in range(4):
-                rows = jnp.where(side == 0, 4 * here + i, 4 * i + here)
-                for layer in range(block.shape[0]):
-                    target = out.at[first_layer + layer, rows, :, columns]
-                    copies.append(pltpu.make_async_copy(block.at[layer, i], target, sems.at[len(copies)]))
+            along, across = jnp.where(side == 0, x, y), jnp.where(side == 0, y, x)
+            if len(block.shape) == 4:
+                across = lax.rem(across + (4 - steps), 4)
+                parts = [(i, layer, block.at[layer, i]) for i in range(4) for layer in range(block.shape[0])]
+            else:
+                along = lax.rem(along + (4 - steps), 4)
+                parts = [(along, layer, block.at[layer]) for layer in range(block.shape[0])]
+            for i, layer, source in parts:
+                rows = jnp.where(side == 0, 4 * across + i, 4 * i + across)
+                target = out.at[first_layer + layer, rows, :, columns]
+                copies.append(pltpu.make_async_copy(source, target, sems.at[len(copies)]))
         for copy in copies:
             copy.start()
         for copy in copies:
@@ -463,17 +468,21 @@
         tokens.append(token)
 
     ahead, behind = along_second(own, 1), along_second(own, -1)
-    whole, token = write_blocks(place, None, [(own, 0, 0, 0)])
+    items = [(own, 0, 0, 0)]
+    for unit, blocks in enumerate(first):
+        items += [(swap(block), unit * UNIT, steps, 1) for block, steps in blocks]
+    whole, token = write_blocks(place, None, items)
     tokens.append(token)
     ahead, behind = after(ahead, *tokens), after(behind, *tokens)
-    across = [along_second(part(ahead, 0), 1), along_second(part(behind, 1), -1)]
-    items = [(ahead, 0, 1, 0), (behind, 0, 3, 0), (swap(ahead), 0, 1, 1), (swap(behind), 0, 3, 1)]
+    across = [along_second(part(behind, 0), -1), along_second(part(ahead, 1), 1)]
+    items = [(ahead, 0, 1, 0), (behind, 0, 3, 0)]
+    for unit in range(UNITS):
+        items += [(swap(part(block, unit)), unit * UNIT, steps, 1) for block, steps in ((ahead, 1), (behind, 3))]
     whole, token = write_blocks(place, whole, items)
-    items = [(swap(copied(own, token)), 0, 0, 1)]
-    for unit, block in enumerate(across):
-        block = after(block, token)
-        items += [(block, unit * UNIT, 2, 0), (swap(block), unit * UNIT, 2, 1)]
-    whole, _ = write_blocks(place, whole, items)
+    across = [after(block, token) for block in across]
+    others = [swap(block) for block in across]
+    for other, blocks in enumerate((across, others)):
+        whole, _ = write_blocks(place, whole, [(block, unit * UNIT, 2, other) for unit, block in enumerate(blocks)])
     return new_momentum, whole.reshape(LAYERS, 16 * ROWS_HERE, WIDTH)
 
 

time: 84.6 us -> 84 us (level)
  waiting for transfers between devices: 35 us -> 27.4 us
  starting transfers between devices: 25.5 us -> 30 us
  Pallas kernels: 23.1 us -> 25.3 us
    ppermute x20 -> x29, waiting for transfers between devices: 35 us -> 27.4 us  [move(): return lax.ppermute(x, ('rep', 'fsdp'), pairs)]
    ppermute x20 -> x29, starting transfers between devices: 25.5 us -> 30 us  [move(): return lax.ppermute(x, ('rep', 'fsdp'), pairs)]
    pallas_call x3 -> x4, Pallas kernels: 9.76 us -> 12 us  [write_blocks(): pl.pallas_call(kernel, out_shape=[jax.ShapeDtypeStruct((LAYERS, 16, ROWS_...]
  transfers between devices with their start and end apart: 20 -> 29, of which waited for: 14 -> 16; matrix products, arithmetic and copies ran while one was open for 0% -> 0% of each run, Pallas kernels for 18% -> 23%
where the time goes in v8:
time: 84 us; the launch traced here: 83.8 us
  starting transfers between devices  30 us (36%)
  waiting for transfers between devices  27.4 us (33%)
  Pallas kernels  25.3 us (30%)
  between operations  1 us (1%)
    ppermute x29, starting transfers between devices, move(): return lax.ppermute(x, ('rep', 'fsdp'), pairs)  30 us
    ppermute x29, waiting for transfers between devices, move(): return lax.ppermute(x, ('rep', 'fsdp'), pairs)  27.4 us
    pallas_call x4, Pallas kernels, write_blocks(): pl.pallas_call(kernel, out_shape=[jax.ShapeDtypeStruct((LAYERS, 16, ROWS_...  12 us
    pallas_call x2, Pallas kernels, keep_rest(): pl.pallas_call(kernel, out_shape=[jax.ShapeDtypeStruct(momentum.shape, jn...  7.35 us
    pallas_call x1, Pallas kernels, pick_theirs(): pl.pallas_call(kernel, out_shape=out_shapes, in_specs=[SMEM] + [HBM] * 6,...  2.87 us
  transfers between devices with their start and end apart: 29, of which 16 were waited for; matrix products, arithmetic and copies ran while one was open for 0% of the time, Pallas kernels for 23%

profile of v8, /device:TPU:1, one launch (start us, length us, event | category | flops | bytes accessed | tf_op | source)
XLA Modules:
  0.0 83.8 jit_solution(15900661972337737661)
XLA Ops:
  0.7 2.9 %shard_map.95 = (bf16[4,8,6912]{2,1,0:T(8,128)(2,1)S(1)}, bf16[4,8,6912]{2,1,0:T(8,128)(2,1)S(1)}, f32[4,8,6912]{2,1,0:T(8,128)S(1)}, bf16[4,8,6912]{2,1,0:T(8,1...) custom-call(s32[4]{0:T(128)S(1)} %pad_add_fusion.place_ref, ...), custom_call_target="tpu_custom_call" | custom-call | flops 339738624 | bytes 6000000 | tf_op jit(solution)/shard_map/pallas_call | solution.py:138
  3.6 1.5 %collective-permute-start = (bf16[4,8,6912]{2,1,0:T(8,128)(2,1)S(1)}, bf16[4,8,6912]{2,1,0:T(8,128)(2,1)S(1)}, u32[]{:S(2)}, u32[]{:S(2)}) collective-permute-start(bf16[4,8,6912]{2,1,0:T(8,128)(2,1)S(1)} %get-tuple-element.26), channel_id=1, source_target_pairs={{0,16},{1,17},{2,18},{3,19},{4,20},{5,21},{6,22},{7,23},{8,24},{9,... | collective-permute-start | bytes 1327112 | tf_op jit(solution)/shard_map/ppermute | solution.py:367
  5.1 1.3 %shard_map.96.mine_ref = bf16[4,8,6912]{2,1,0:T(8,128)(2,1)S(1)} custom-call(s32[4]{0:T(128)S(1)} %pad_add_fusion.place_ref, s32[4,2,8,128]{3,2,1,0:T(8,128)S(1)} %get-tuple-element.21.bands_ref, bf16[4,8,6912]{2,1,0:T(8,128)(2,1)S(1)} %get-tuple-element.24.gradient_ref, f32[4,8,6912]{2,1,0:T(8,128)S(1)} %get-tuple-element.25.momentum_ref, ...), custom_call_target="tpu_custom_call" | custom-call | flops 339738624 | bytes 2000000 | tf_op jit(solution)/shard_map/pallas_call | solution.py:161
  6.6 3.9 %collective-permute-start.1 = (bf16[2,8,6912]{2,1,0:T(8,128)(2,1)S(1)}, bf16[2,8,6912]{2,1,0:T(8,128)(2,1)S(1)}, u32[]{:S(2)}, u32[]{:S(2)}) collective-permute-start(bf16[2,8,6912]{2,1,0:T(8,128)(2,1)S(1)} %get-tuple-element.27.mine_ref), channel_id=1, source_target_pairs={{0,32},{1,33},{2,34},{3,35},{4,36},{5,37},{6,38},{7,39},{8,40},{9,... | collective-permute-start | bytes 663560 | tf_op jit(solution)/shard_map/ppermute | solution.py:367
  10.6 3.2 %collective-permute-done.1.received_ref = bf16[2,8,6912]{2,1,0:T(8,128)(2,1)S(1)} collective-permute-done((bf16[2,8,6912]{2,1,0:T(8,128)(2,1)S(1)}, bf16[2,8,6912]{2,1,0:T(8,128)(2,1)S(1)}, u32[]{:S(2)}, u32[]{:S(2)}) %collective-permute-start.1) | collective-permute-done | bytes 221216 | tf_op jit(solution)/shard_map/ppermute | solution.py:367
  14.0 2.5 %collective-permute-done.3.received_ref = bf16[2,8,6912]{2,1,0:T(8,128)(2,1)S(1)} collective-permute-done((bf16[2,8,6912]{2,1,0:T(8,128)(2,1)S(1)}, bf16[2,8,6912]{2,1,0:T(8,128)(2,1)S(1)}, u32[]{:S(2)}, u32[]{:S(2)}) %collective-permute-start.3) | collective-permute-done | bytes 221216 | tf_op jit(solution)/shard_map/ppermute | solution.py:367
  16.7 2.4 %collective-permute-done.2.received_ref = bf16[2,8,6912]{2,1,0:T(8,128)(2,1)S(1)} collective-permute-done((bf16[2,8,6912]{2,1,0:T(8,128)(2,1)S(1)}, bf16[2,8,6912]{2,1,0:T(8,128)(2,1)S(1)}, u32[]{:S(2)}, u32[]{:S(2)}) %collective-permute-start.2) | collective-permute-done | bytes 221216 | tf_op jit(solution)/shard_map/ppermute | solution.py:367
  19.1 0.4 shard_map.100.refs_0_
  19.4 3.0 %collective-permute-start.6 = (bf16[2,8,6912]{2,1,0:T(8,128)(2,1)S(1)}, bf16[2,8,6912]{2,1,0:T(8,128)(2,1)S(1)}, u32[]{:S(2)}, u32[]{:S(2)}) collective-permute-start(bf16[2,8,6912]{2,1,0:T(8,128)(2,1)S(1)} %shard_map.100.refs_0_), channel_id=1, source_target_pairs={{0,2},{1,3},{2,0},{3,1},{4,6},{5,7},{6,4},{7,5},{8,10},{9,11},{10,... | collective-permute-start | bytes 663560 | tf_op jit(solution)/shard_map/ppermute | solution.py:367
  22.4 0.8 collective-permute-start.5
  23.2 0.7 collective-permute-start.4
  23.9 0.4 shard_map.101.refs_4_
  24.3 0.8 collective-permute-start.10
  25.1 2.1 %collective-permute-start.9 = (bf16[2,8,6912]{2,1,0:T(8,128)(2,1)S(1)}, bf16[2,8,6912]{2,1,0:T(8,128)(2,1)S(1)}, u32[]{:S(2)}, u32[]{:S(2)}) collective-permute-start(bf16[2,8,6912]{2,1,0:T(8,128)(2,1)S(1)} %shard_map.101.refs_4_), channel_id=1, source_target_pairs={{0,3},{1,0},{2,1},{3,2},{4,7},{5,4},{6,5},{7,6},{8,11},{9,8},{10,9... | collective-permute-start | bytes 663560 | tf_op jit(solution)/shard_map/ppermute | solution.py:367
  27.2 1.6 %collective-permute-done.5.refs_2_ = bf16[2,8,6912]{2,1,0:T(8,128)(2,1)S(1)} collective-permute-done((bf16[2,8,6912]{2,1,0:T(8,128)(2,1)S(1)}, bf16[2,8,6912]{2,1,0:T(8,128)(2,1)S(1)}, u32[]{:S(2)}, u32[]{:S(2)}) %collective-permute-start.5) | collective-permute-done | bytes 221216 | tf_op jit(solution)/shard_map/ppermute | solution.py:367
  28.8 3.0 %collective-permute-done.4.refs_1_ = bf16[2,8,6912]{2,1,0:T(8,128)(2,1)S(1)} collective-permute-done((bf16[2,8,6912]{2,1,0:T(8,128)(2,1)S(1)}, bf16[2,8,6912]{2,1,0:T(8,128)(2,1)S(1)}, u32[]{:S(2)}, u32[]{:S(2)}) %collective-permute-start.4) | collective-permute-done | bytes 221216 | tf_op jit(solution)/shard_map/ppermute | solution.py:367
  31.9 1.8 %collective-permute-done.9.refs_6_ = bf16[2,8,6912]{2,1,0:T(8,128)(2,1)S(1)} collective-permute-done((bf16[2,8,6912]{2,1,0:T(8,128)(2,1)S(1)}, bf16[2,8,6912]{2,1,0:T(8,128)(2,1)S(1)}, u32[]{:S(2)}, u32[]{:S(2)}) %collective-permute-start.9) | collective-permute-done | bytes 221216 | tf_op jit(solution)/shard_map/ppermute | solution.py:367
  33.6 0.6 collective-permute-done.8.refs_5_
  34.2 0.7 shard_map.102.refs_0_
  34.9 1.0 %collective-permute-start.21 = (bf16[4,4,8,6912]{3,2,1,0:T(8,128)(2,1)S(1)}, bf16[4,4,8,6912]{3,2,1,0:T(8,128)(2,1)S(1)}, u32[]{:S(2)}, u32[]{:S(2)}) collective-permute-start(bf16[4,4,8,6912]{3,2,1,0:T(8,128)(2,1)S(1)} %shard_map.102.refs_0_), channel_id=1, source_target_pairs={{0,4},{1,5},{2,6},{3,7},{4,8},{5,9},{6,10},{7,11},{8,12},{9,13},{1... | collective-permute-start | bytes 5308424 | tf_op jit(solution)/shard_map/ppermute | solution.py:367
  35.9 1.8 %collective-permute-start.11 = (bf16[4,4,8,6912]{3,2,1,0:T(8,128)(2,1)S(1)}, bf16[4,4,8,6912]{3,2,1,0:T(8,128)(2,1)S(1)}, u32[]{:S(2)}, u32[]{:S(2)}) collective-permute-start(bf16[4,4,8,6912]{3,2,1,0:T(8,128)(2,1)S(1)} %shard_map.102.refs_0_), channel_id=1, source_target_pairs={{0,12},{1,13},{2,14},{3,15},{4,0},{5,1},{6,2},{7,3},{8,4},{9,5},{1... | collective-permute-start | bytes 5308424 | tf_op jit(solution)/shard_map/ppermute | solution.py:367
  37.6 4.0 %collective-permute-start.12 = (bf16[2,8,6912]{2,1,0:T(8,128)(2,1)S(1)}, bf16[2,8,6912]{2,1,0:T(8,128)(2,1)S(1)}, u32[]{:S(2)}, u32[]{:S(2)}) collective-permute-start(bf16[2,8,6912]{2,1,0:T(8,128)(2,1)S(1)} %shard_map.100.refs_0_), channel_id=1, source_target_pairs={{0,16},{1,17},{2,18},{3,19},{4,20},{5,21},{6,22},{7,23},{8,24},{9,... | collective-permute-start | bytes 663560 | tf_op jit(solution)/shard_map/ppermute | solution.py:367
  41.6 0.5 collective-permute-start.15
  42.2 0.6 collective-permute-done.12.refs_1_
  42.7 0.4 collective-permute-start.14
  43.1 0.3 collective-permute-start.13
  43.4 0.3 collective-permute-start.19
  43.8 0.5 collective-permute-done.14.refs_3_
  44.2 0.4 collective-permute-start.18
  44.6 0.3 collective-permute-start.17
  44.9 3.7 %shard_map.103 = (f32[1,4,8,13824]{3,2,1,0:T(8,128)}, f32[8,128]{1,0:T(8,128)S(1)}) custom-call(s32[4,2,8,128]{3,2,1,0:T(8,128)S(1)} %get-tuple-element.21.bands_ref, bf16[1,4,8,13824]{3,2,1,0:T(8,128)(2,1)} %gradient_ref.5, f32[1,4,8,13824]{3,2,1,0:T(8,128)} %momentum_ref.5, bf16[2,256,256]{2,1,0:T(8,128)(2,1)S(1)} %get-tuple-element.22.table_ref.forward_ref, ...), custom_call_target="tpu_custom_call" | custom-call | flops 679477248 | bytes 3000000 | tf_op jit(solution)/shard_map/pallas_call | solution.py:246
  48.6 3.7 %shard_map.104 = (f32[1,4,8,13824]{3,2,1,0:T(8,128)}, f32[8,128]{1,0:T(8,128)S(1)}) custom-call(s32[4,2,8,128]{3,2,1,0:T(8,128)S(1)} %get-tuple-element.21.bands_ref, bf16[1,4,8,13824]{3,2,1,0:T(8,128)(2,1)} %gradient_ref.5, f32[1,4,8,13824]{3,2,1,0:T(8,128)} %momentum_ref.5, ...), custom_call_target="tpu_custom_call", output_to_operand_aliasing={{0}: (6, {})} | custom-call | flops 679477248 | bytes 3000000 | tf_op jit(solution)/shard_map/pallas_call | solution.py:246
  52.3 3.0 %shard_map.105 = (bf16[4,16,8,13824]{3,2,1,0:T(8,128)(2,1)}, f32[8,128]{1,0:T(8,128)S(1)}) custom-call(s32[4]{0:T(128)S(1)} %pad_add_fusion.place_ref, bf16[4,4,8,6912]{3,2,1,0:T(8,128)(2,1)S(1)} %shard_map.102.refs_0_, bf16[2,8,6912]{2,1,0:T(8,128)(2,1)S(1)} %collective-permute-done.12.refs_1_, bf16[2,8,6912]{2,1,0:T(8,128)(2,1)S(1)} %collective-permute-done.13.refs_2_, ...), custom_call_target="tpu_custom_call" | custom-call | bytes 7077888 | tf_op jit(solution)/shard_map/pallas_call | solution.py:349
  55.4 2.5 %collective-permute-done.21.x_ref = bf16[4,4,8,6912]{3,2,1,0:T(8,128)(2,1)S(1)} collective-permute-done((bf16[4,4,8,6912]{3,2,1,0:T(8,128)(2,1)S(1)}, bf16[4,4,8,6912]{3,2,1,0:T(8,128)(2,1)S(1)}, u32[]{:S(2)}, u32[]{:S(2)}) %collective-permute-start.21) | collective-permute-done | bytes 1769504 | tf_op jit(solution)/shard_map/ppermute | solution.py:367
  57.9 4.4 %collective-permute-start.22 = (bf16[2,4,8,6912]{3,2,1,0:T(8,128)(2,1)S(1)}, bf16[2,4,8,6912]{3,2,1,0:T(8,128)(2,1)S(1)}, u32[]{:S(2)}, u32[]{:S(2)}) collective-permute-start(bf16[2,4,8,6912]{3,2,1,0:T(8,128)(2,1)S(1)} %shard_map.109), channel_id=1, source_target_pairs={{0,16},{1,17},{2,18},{3,19},{4,20},{5,21},{6,22},{7,23},{8,24},{9,... | collective-permute-start | bytes 2654216 | tf_op jit(solution)/shard_map/ppermute | solution.py:367
  62.5 0.2 collective-permute-start.25
  62.7 0.4 collective-permute-start.24
  63.1 0.1 collective-permute-start.23
  63.2 1.1 %collective-permute-done.22.refs_2_ = bf16[2,4,8,6912]{3,2,1,0:T(8,128)(2,1)S(1)} collective-permute-done((bf16[2,4,8,6912]{3,2,1,0:T(8,128)(2,1)S(1)}, bf16[2,4,8,6912]{3,2,1,0:T(8,128)(2,1)S(1)}, u32[]{:S(2)}, u32[]{:S(2)}) %collective-permute-start.22) | collective-permute-done | bytes 884768 | tf_op jit(solution)/shard_map/ppermute | solution.py:367
  64.3 1.6 %collective-permute-start.20 = (bf16[2,4,8,6912]{3,2,1,0:T(8,128)(2,1)S(1)}, bf16[2,4,8,6912]{3,2,1,0:T(8,128)(2,1)S(1)}, u32[]{:S(2)}, u32[]{:S(2)}) collective-permute-start(bf16[2,4,8,6912]{3,2,1,0:T(8,128)(2,1)S(1)} %shard_map.107), channel_id=1, source_target_pairs={{0,12},{1,13},{2,14},{3,15},{4,0},{5,1},{6,2},{7,3},{8,4},{9,5},{1... | collective-permute-start | bytes 2654216 | tf_op jit(solution)/shard_map/ppermute | solution.py:367
  65.9 1.0 %collective-permute-done.24.refs_4_ = bf16[2,4,8,6912]{3,2,1,0:T(8,128)(2,1)S(1)} collective-permute-done((bf16[2,4,8,6912]{3,2,1,0:T(8,128)(2,1)S(1)}, bf16[2,4,8,6912]{3,2,1,0:T(8,128)(2,1)S(1)}, u32[]{:S(2)}, u32[]{:S(2)}) %collective-permute-start.24) | collective-permute-done | bytes 884768 | tf_op jit(solution)/shard_map/ppermute | solution.py:367
  66.9 1.3 %collective-permute-done.23.refs_3_ = bf16[2,4,8,6912]{3,2,1,0:T(8,128)(2,1)S(1)} collective-permute-done((bf16[2,4,8,6912]{3,2,1,0:T(8,128)(2,1)S(1)}, bf16[2,4,8,6912]{3,2,1,0:T(8,128)(2,1)S(1)}, u32[]{:S(2)}, u32[]{:S(2)}) %collective-permute-start.23) | collective-permute-done | bytes 884768 | tf_op jit(solution)/shard_map/ppermute | solution.py:367
  68.1 4.0 %shard_map.112 = (bf16[4,16,8,13824]{3,2,1,0:T(8,128)(2,1)}, f32[8,128]{1,0:T(8,128)S(1)}) custom-call(s32[4]{0:T(128)S(1)} %pad_add_fusion.place_ref, bf16[4,4,8,6912]{3,2,1,0:T(8,128)(2,1)S(1)} %shard_map.108.x_ref.refs_0_, bf16[4,4,8,6912]{3,2,1,0:T(8,128)(2,1)S(1)} %shard_map.106.x_ref.refs_1_, ...), custom_call_target="tpu_custom_call", output_to_operand_aliasing={{0}: (7, {})} | custom-call | bytes 14155776 | tf_op jit(solution)/shard_map/pallas_call | solution.py:349
  72.1 4.5 %collective-permute-done.27.x_ref = bf16[2,4,8,6912]{3,2,1,0:T(8,128)(2,1)S(1)} collective-permute-done((bf16[2,4,8,6912]{3,2,1,0:T(8,128)(2,1)S(1)}, bf16[2,4,8,6912]{3,2,1,0:T(8,128)(2,1)S(1)}, u32[]{:S(2)}, u32[]{:S(2)}) %collective-permute-start.27) | collective-permute-done | bytes 884768 | tf_op jit(solution)/shard_map/ppermute | solution.py:367
  76.6 1.2 %collective-permute-start.28 = (bf16[2,4,8,6912]{3,2,1,0:T(8,128)(2,1)S(1)}, bf16[2,4,8,6912]{3,2,1,0:T(8,128)(2,1)S(1)}, u32[]{:S(2)}, u32[]{:S(2)}) collective-permute-start(bf16[2,4,8,6912]{3,2,1,0:T(8,128)(2,1)S(1)} %shard_map.114.refs_1_), channel_id=1, source_target_pairs={{0,16},{1,17},{2,18},{3,19},{4,20},{5,21},{6,22},{7,23},{8,24},{9,... | collective-permute-start | bytes 2654216 | tf_op jit(solution)/shard_map/ppermute | solution.py:367
  77.9 2.5 %shard_map.115 = (bf16[4,16,8,13824]{3,2,1,0:T(8,128)(2,1)}, f32[8,128]{1,0:T(8,128)}) custom-call(s32[4]{0:T(128)S(1)} %pad_add_fusion.place_ref, bf16[2,4,8,6912]{3,2,1,0:T(8,128)(2,1)S(1)} %shard_map.113.refs_0_, bf16[2,4,8,6912]{3,2,1,0:T(8,128)(2,1)S(1)} %shard_map.114.refs_1_, ...), custom_call_target="tpu_custom_call", output_to_operand_aliasing={{0}: (3, {})} | custom-call | bytes 3538944 | tf_op jit(solution)/shard_map/pallas_call | solution.py:349
  80.4 0.7 collective-permute-done.26.refs_0_
  81.2 2.5 %shard_map.116 = (bf16[4,16,8,13824]{3,2,1,0:T(8,128)(2,1)}, f32[8,128]{1,0:T(8,128)}) custom-call(s32[4]{0:T(128)S(1)} %pad_add_fusion.place_ref, bf16[2,4,8,6912]{3,2,1,0:T(8,128)(2,1)S(1)} %collective-permute-done.26.refs_0_, bf16[2,4,8,6912]{3,2,1,0:T(8,128)(2,1)S(1)} %collective-permute-done.28.refs_1_, ...), custom_call_target="tpu_custom_call", output_to_operand_aliasing={{0}: (3, {})} | custom-call | bytes 3538944 | tf_op jit(solution)/shard_map/pallas_call | solution.py:349
  (33 shorter events, 1.1 us)
Async XLA Ops:
  3.6 2.9 %collective-permute-start = (bf16[4,8,6912]{2,1,0:T(8,128)(2,1)S(1)}, bf16[4,8,6912]{2,1,0:T(8,128)(2,1)S(1)}, u32[]{:S(2)}, u32[]{:S(2)}) collective-permute-start(bf16[4,8,6912]{2,1,0:T(8,128)(2,1)S(1)} %get-tuple-element.26), channel_id=1, source_target_pairs={{0,16},{1,17},{2,18},{3,19},{4,20},{5,21},{6,22},{7,23},{8,24},{9,... | collective-permute-start | bytes 1327112 | tf_op jit(solution)/shard_map/ppermute | solution.py:367
  6.6 7.2 %collective-permute-start.1 = (bf16[2,8,6912]{2,1,0:T(8,128)(2,1)S(1)}, bf16[2,8,6912]{2,1,0:T(8,128)(2,1)S(1)}, u32[]{:S(2)}, u32[]{:S(2)}) collective-permute-start(bf16[2,8,6912]{2,1,0:T(8,128)(2,1)S(1)} %get-tuple-element.27.mine_ref), channel_id=1, source_target_pairs={{0,32},{1,33},{2,34},{3,35},{4,36},{5,37},{6,38},{7,39},{8,40},{9,... | collective-permute-start | bytes 663560 | tf_op jit(solution)/shard_map/ppermute | solution.py:367
  10.5 6.0 %collective-permute-start.3 = (bf16[2,8,6912]{2,1,0:T(8,128)(2,1)S(1)}, bf16[2,8,6912]{2,1,0:T(8,128)(2,1)S(1)}, u32[]{:S(2)}, u32[]{:S(2)}) collective-permute-start(bf16[2,8,6912]{2,1,0:T(8,128)(2,1)S(1)} %get-tuple-element.29.mine_ref), channel_id=1, source_target_pairs={{0,32},{1,33},{2,34},{3,35},{4,36},{5,37},{6,38},{7,39},{8,40},{9,... | collective-permute-start | bytes 663560 | tf_op jit(solution)/shard_map/ppermute | solution.py:367
  13.9 5.2 %collective-permute-start.2 = (bf16[2,8,6912]{2,1,0:T(8,128)(2,1)S(1)}, bf16[2,8,6912]{2,1,0:T(8,128)(2,1)S(1)}, u32[]{:S(2)}, u32[]{:S(2)}) collective-permute-start(bf16[2,8,6912]{2,1,0:T(8,128)(2,1)S(1)} %shard_map.98.mine_ref), channel_id=1, source_target_pairs={{0,96},{1,97},{2,98},{3,99},{4,100},{5,101},{6,102},{7,103},{8,104... | collective-permute-start | bytes 663560 | tf_op jit(solution)/shard_map/ppermute | solution.py:367
  16.6 7.3 %collective-permute-start.7 = (bf16[2,8,6912]{2,1,0:T(8,128)(2,1)S(1)}, bf16[2,8,6912]{2,1,0:T(8,128)(2,1)S(1)}, u32[]{:S(2)}, u32[]{:S(2)}) collective-permute-start(bf16[2,8,6912]{2,1,0:T(8,128)(2,1)S(1)} %shard_map.99.refs_0_.mine_ref), channel_id=1, source_target_pairs={{0,96},{1,97},{2,98},{3,99},{4,100},{5,101},{6,102},{7,103},{8,104... | collective-permute-start | bytes 663560 | tf_op jit(solution)/shard_map/ppermute | solution.py:367
  19.4 7.7 %collective-permute-start.6 = (bf16[2,8,6912]{2,1,0:T(8,128)(2,1)S(1)}, bf16[2,8,6912]{2,1,0:T(8,128)(2,1)S(1)}, u32[]{:S(2)}, u32[]{:S(2)}) collective-permute-start(bf16[2,8,6912]{2,1,0:T(8,128)(2,1)S(1)} %shard_map.100.refs_0_), channel_id=1, source_target_pairs={{0,2},{1,3},{2,0},{3,1},{4,6},{5,7},{6,4},{7,5},{8,10},{9,11},{10,... | collective-permute-start | bytes 663560 | tf_op jit(solution)/shard_map/ppermute | solution.py:367
  22.4 6.4 %collective-permute-start.5 = (bf16[2,8,6912]{2,1,0:T(8,128)(2,1)S(1)}, bf16[2,8,6912]{2,1,0:T(8,128)(2,1)S(1)}, u32[]{:S(2)}, u32[]{:S(2)}) collective-permute-start(bf16[2,8,6912]{2,1,0:T(8,128)(2,1)S(1)} %shard_map.100.refs_0_), channel_id=1, source_target_pairs={{0,3},{1,0},{2,1},{3,2},{4,7},{5,4},{6,5},{7,6},{8,11},{9,8},{10,9... | collective-permute-start | bytes 663560 | tf_op jit(solution)/shard_map/ppermute | solution.py:367
  23.2 8.7 %collective-permute-start.4 = (bf16[2,8,6912]{2,1,0:T(8,128)(2,1)S(1)}, bf16[2,8,6912]{2,1,0:T(8,128)(2,1)S(1)}, u32[]{:S(2)}, u32[]{:S(2)}) collective-permute-start(bf16[2,8,6912]{2,1,0:T(8,128)(2,1)S(1)} %shard_map.100.refs_0_), channel_id=1, source_target_pairs={{0,1},{1,2},{2,3},{3,0},{4,5},{5,6},{6,7},{7,4},{8,9},{9,10},{10,1... | collective-permute-start | bytes 663560 | tf_op jit(solution)/shard_map/ppermute | solution.py:367
  24.3 7.6 %collective-permute-start.10 = (bf16[2,8,6912]{2,1,0:T(8,128)(2,1)S(1)}, bf16[2,8,6912]{2,1,0:T(8,128)(2,1)S(1)}, u32[]{:S(2)}, u32[]{:S(2)}) collective-permute-start(bf16[2,8,6912]{2,1,0:T(8,128)(2,1)S(1)} %shard_map.101.refs_4_), channel_id=1, source_target_pairs={{0,2},{1,3},{2,0},{3,1},{4,6},{5,7},{6,4},{7,5},{8,10},{9,11},{10,... | collective-permute-start | bytes 663560 | tf_op jit(solution)/shard_map/ppermute | solution.py:367
  25.1 8.6 %collective-permute-start.9 = (bf16[2,8,6912]{2,1,0:T(8,128)(2,1)S(1)}, bf16[2,8,6912]{2,1,0:T(8,128)(2,1)S(1)}, u32[]{:S(2)}, u32[]{:S(2)}) collective-permute-start(bf16[2,8,6912]{2,1,0:T(8,128)(2,1)S(1)} %shard_map.101.refs_4_), channel_id=1, source_target_pairs={{0,3},{1,0},{2,1},{3,2},{4,7},{5,4},{6,5},{7,6},{8,11},{9,8},{10,9... | collective-permute-start | bytes 663560 | tf_op jit(solution)/shard_map/ppermute | solution.py:367
  27.1 7.1 %collective-permute-start.8 = (bf16[2,8,6912]{2,1,0:T(8,128)(2,1)S(1)}, bf16[2,8,6912]{2,1,0:T(8,128)(2,1)S(1)}, u32[]{:S(2)}, u32[]{:S(2)}) collective-permute-start(bf16[2,8,6912]{2,1,0:T(8,128)(2,1)S(1)} %shard_map.101.refs_4_), channel_id=1, source_target_pairs={{0,1},{1,2},{2,3},{3,0},{4,5},{5,6},{6,7},{7,4},{8,9},{9,10},{10,1... | collective-permute-start | bytes 663560 | tf_op jit(solution)/shard_map/ppermute | solution.py:367
  34.9 22.9 %collective-permute-start.21 = (bf16[4,4,8,6912]{3,2,1,0:T(8,128)(2,1)S(1)}, bf16[4,4,8,6912]{3,2,1,0:T(8,128)(2,1)S(1)}, u32[]{:S(2)}, u32[]{:S(2)}) collective-permute-start(bf16[4,4,8,6912]{3,2,1,0:T(8,128)(2,1)S(1)} %shard_map.102.refs_0_), channel_id=1, source_target_pairs={{0,4},{1,5},{2,6},{3,7},{4,8},{5,9},{6,10},{7,11},{8,12},{9,13},{1... | collective-permute-start | bytes 5308424 | tf_op jit(solution)/shard_map/ppermute | solution.py:367
  35.9 26.5 %collective-permute-start.11 = (bf16[4,4,8,6912]{3,2,1,0:T(8,128)(2,1)S(1)}, bf16[4,4,8,6912]{3,2,1,0:T(8,128)(2,1)S(1)}, u32[]{:S(2)}, u32[]{:S(2)}) collective-permute-start(bf16[4,4,8,6912]{3,2,1,0:T(8,128)(2,1)S(1)} %shard_map.102.refs_0_), channel_id=1, source_target_pairs={{0,12},{1,13},{2,14},{3,15},{4,0},{5,1},{6,2},{7,3},{8,4},{9,5},{1... | collective-permute-start | bytes 5308424 | tf_op jit(solution)/shard_map/ppermute | solution.py:367
  37.6 5.1 %collective-permute-start.12 = (bf16[2,8,6912]{2,1,0:T(8,128)(2,1)S(1)}, bf16[2,8,6912]{2,1,0:T(8,128)(2,1)S(1)}, u32[]{:S(2)}, u32[]{:S(2)}) collective-permute-start(bf16[2,8,6912]{2,1,0:T(8,128)(2,1)S(1)} %shard_map.100.refs_0_), channel_id=1, source_target_pairs={{0,16},{1,17},{2,18},{3,19},{4,20},{5,21},{6,22},{7,23},{8,24},{9,... | collective-permute-start | bytes 663560 | tf_op jit(solution)/shard_map/ppermute | solution.py:367
  41.6 1.5 %collective-permute-start.16 = (bf16[2,8,6912]{2,1,0:T(8,128)(2,1)S(1)}, bf16[2,8,6912]{2,1,0:T(8,128)(2,1)S(1)}, u32[]{:S(2)}, u32[]{:S(2)}) collective-permute-start(bf16[2,8,6912]{2,1,0:T(8,128)(2,1)S(1)} %shard_map.101.refs_4_), channel_id=1, source_target_pairs={{0,16},{1,17},{2,18},{3,19},{4,20},{5,21},{6,22},{7,23},{8,24},{9,... | collective-permute-start | bytes 663560 | tf_op jit(solution)/shard_map/ppermute | solution.py:367
  41.6 1.8 %collective-permute-start.15 = (bf16[2,8,6912]{2,1,0:T(8,128)(2,1)S(1)}, bf16[2,8,6912]{2,1,0:T(8,128)(2,1)S(1)}, u32[]{:S(2)}, u32[]{:S(2)}) collective-permute-start(bf16[2,8,6912]{2,1,0:T(8,128)(2,1)S(1)} %collective-permute-done.6.refs_3_), channel_id=1, source_target_pairs={{0,16},{1,17},{2,18},{3,19},{4,20},{5,21},{6,22},{7,23},{8,24},{9,... | collective-permute-start | bytes 663560 | tf_op jit(solution)/shard_map/ppermute | solution.py:367
  42.7 1.5 %collective-permute-start.14 = (bf16[2,8,6912]{2,1,0:T(8,128)(2,1)S(1)}, bf16[2,8,6912]{2,1,0:T(8,128)(2,1)S(1)}, u32[]{:S(2)}, u32[]{:S(2)}) collective-permute-start(bf16[2,8,6912]{2,1,0:T(8,128)(2,1)S(1)} %collective-permute-done.5.refs_2_), channel_id=1, source_target_pairs={{0,16},{1,17},{2,18},{3,19},{4,20},{5,21},{6,22},{7,23},{8,24},{9,... | collective-permute-start | bytes 663560 | tf_op jit(solution)/shard_map/ppermute | solution.py:367
  43.1 1.5 %collective-permute-start.13 = (bf16[2,8,6912]{2,1,0:T(8,128)(2,1)S(1)}, bf16[2,8,6912]{2,1,0:T(8,128)(2,1)S(1)}, u32[]{:S(2)}, u32[]{:S(2)}) collective-permute-start(bf16[2,8,6912]{2,1,0:T(8,128)(2,1)S(1)} %collective-permute-done.4.refs_1_), channel_id=1, source_target_pairs={{0,16},{1,17},{2,18},{3,19},{4,20},{5,21},{6,22},{7,23},{8,24},{9,... | collective-permute-start | bytes 663560 | tf_op jit(solution)/shard_map/ppermute | solution.py:367
  43.4 8.8 %collective-permute-start.19 = (bf16[2,8,6912]{2,1,0:T(8,128)(2,1)S(1)}, bf16[2,8,6912]{2,1,0:T(8,128)(2,1)S(1)}, u32[]{:S(2)}, u32[]{:S(2)}) collective-permute-start(bf16[2,8,6912]{2,1,0:T(8,128)(2,1)S(1)} %collective-permute-done.10.refs_7_), channel_id=1, source_target_pairs={{0,16},{1,17},{2,18},{3,19},{4,20},{5,21},{6,22},{7,23},{8,24},{9,... | collective-permute-start | bytes 663560 | tf_op jit(solution)/shard_map/ppermute | solution.py:367
  44.2 8.1 %collective-permute-start.18 = (bf16[2,8,6912]{2,1,0:T(8,128)(2,1)S(1)}, bf16[2,8,6912]{2,1,0:T(8,128)(2,1)S(1)}, u32[]{:S(2)}, u32[]{:S(2)}) collective-permute-start(bf16[2,8,6912]{2,1,0:T(8,128)(2,1)S(1)} %collective-permute-done.9.refs_6_), channel_id=1, source_target_pairs={{0,16},{1,17},{2,18},{3,19},{4,20},{5,21},{6,22},{7,23},{8,24},{9,... | collective-permute-start | bytes 663560 | tf_op jit(solution)/shard_map/ppermute | solution.py:367
  44.6 7.7 %collective-permute-start.17 = (bf16[2,8,6912]{2,1,0:T(8,128)(2,1)S(1)}, bf16[2,8,6912]{2,1,0:T(8,128)(2,1)S(1)}, u32[]{:S(2)}, u32[]{:S(2)}) collective-permute-start(bf16[2,8,6912]{2,1,0:T(8,128)(2,1)S(1)} %collective-permute-done.8.refs_5_), channel_id=1, source_target_pairs={{0,16},{1,17},{2,18},{3,19},{4,20},{5,21},{6,22},{7,23},{8,24},{9,... | collective-permute-start | bytes 663560 | tf_op jit(solution)/shard_map/ppermute | solution.py:367
  57.9 6.4 %collective-permute-start.22 = (bf16[2,4,8,6912]{3,2,1,0:T(8,128)(2,1)S(1)}, bf16[2,4,8,6912]{3,2,1,0:T(8,128)(2,1)S(1)}, u32[]{:S(2)}, u32[]{:S(2)}) collective-permute-start(bf16[2,4,8,6912]{3,2,1,0:T(8,128)(2,1)S(1)} %shard_map.109), channel_id=1, source_target_pairs={{0,16},{1,17},{2,18},{3,19},{4,20},{5,21},{6,22},{7,23},{8,24},{9,... | collective-permute-start | bytes 2654216 | tf_op jit(solution)/shard_map/ppermute | solution.py:367
  62.5 3.4 %collective-permute-start.25 = (bf16[2,4,8,6912]{3,2,1,0:T(8,128)(2,1)S(1)}, bf16[2,4,8,6912]{3,2,1,0:T(8,128)(2,1)S(1)}, u32[]{:S(2)}, u32[]{:S(2)}) collective-permute-start(bf16[2,4,8,6912]{3,2,1,0:T(8,128)(2,1)S(1)} %shard_map.111), channel_id=1, source_target_pairs={{0,16},{1,17},{2,18},{3,19},{4,20},{5,21},{6,22},{7,23},{8,24},{9,... | collective-permute-start | bytes 2654216 | tf_op jit(solution)/shard_map/ppermute | solution.py:367
  62.7 4.2 %collective-permute-start.24 = (bf16[2,4,8,6912]{3,2,1,0:T(8,128)(2,1)S(1)}, bf16[2,4,8,6912]{3,2,1,0:T(8,128)(2,1)S(1)}, u32[]{:S(2)}, u32[]{:S(2)}) collective-permute-start(bf16[2,4,8,6912]{3,2,1,0:T(8,128)(2,1)S(1)} %shard_map.110), channel_id=1, source_target_pairs={{0,16},{1,17},{2,18},{3,19},{4,20},{5,21},{6,22},{7,23},{8,24},{9,... | collective-permute-start | bytes 2654216 | tf_op jit(solution)/shard_map/ppermute | solution.py:367
  63.1 5.0 %collective-permute-start.23 = (bf16[2,4,8,6912]{3,2,1,0:T(8,128)(2,1)S(1)}, bf16[2,4,8,6912]{3,2,1,0:T(8,128)(2,1)S(1)}, u32[]{:S(2)}, u32[]{:S(2)}) collective-permute-start(bf16[2,4,8,6912]{3,2,1,0:T(8,128)(2,1)S(1)} %shard_map.107), channel_id=1, source_target_pairs={{0,16},{1,17},{2,18},{3,19},{4,20},{5,21},{6,22},{7,23},{8,24},{9,... | collective-permute-start | bytes 2654216 | tf_op jit(solution)/shard_map/ppermute | solution.py:367
  63.2 13.4 %collective-permute-start.27 = (bf16[2,4,8,6912]{3,2,1,0:T(8,128)(2,1)S(1)}, bf16[2,4,8,6912]{3,2,1,0:T(8,128)(2,1)S(1)}, u32[]{:S(2)}, u32[]{:S(2)}) collective-permute-start(bf16[2,4,8,6912]{3,2,1,0:T(8,128)(2,1)S(1)} %shard_map.110), channel_id=1, source_target_pairs={{0,4},{1,5},{2,6},{3,7},{4,8},{5,9},{6,10},{7,11},{8,12},{9,13},{1... | collective-permute-start | bytes 2654216 | tf_op jit(solution)/shard_map/ppermute | solution.py:367
  64.3 13.5 %collective-permute-start.20 = (bf16[2,4,8,6912]{3,2,1,0:T(8,128)(2,1)S(1)}, bf16[2,4,8,6912]{3,2,1,0:T(8,128)(2,1)S(1)}, u32[]{:S(2)}, u32[]{:S(2)}) collective-permute-start(bf16[2,4,8,6912]{3,2,1,0:T(8,128)(2,1)S(1)} %shard_map.107), channel_id=1, source_target_pairs={{0,12},{1,13},{2,14},{3,15},{4,0},{5,1},{6,2},{7,3},{8,4},{9,5},{1... | collective-permute-start | bytes 2654216 | tf_op jit(solution)/shard_map/ppermute | solution.py:367
  76.6 3.8 %collective-permute-start.28 = (bf16[2,4,8,6912]{3,2,1,0:T(8,128)(2,1)S(1)}, bf16[2,4,8,6912]{3,2,1,0:T(8,128)(2,1)S(1)}, u32[]{:S(2)}, u32[]{:S(2)}) collective-permute-start(bf16[2,4,8,6912]{3,2,1,0:T(8,128)(2,1)S(1)} %shard_map.114.refs_1_), channel_id=1, source_target_pairs={{0,16},{1,17},{2,18},{3,19},{4,20},{5,21},{6,22},{7,23},{8,24},{9,... | collective-permute-start | bytes 2654216 | tf_op jit(solution)/shard_map/ppermute | solution.py:367
  77.9 3.3 %collective-permute-start.26 = (bf16[2,4,8,6912]{3,2,1,0:T(8,128)(2,1)S(1)}, bf16[2,4,8,6912]{3,2,1,0:T(8,128)(2,1)S(1)}, u32[]{:S(2)}, u32[]{:S(2)}) collective-permute-start(bf16[2,4,8,6912]{3,2,1,0:T(8,128)(2,1)S(1)} %shard_map.113.refs_0_), channel_id=1, source_target_pairs={{0,16},{1,17},{2,18},{3,19},{4,20},{5,21},{6,22},{7,23},{8,24},{9,... | collective-permute-start | bytes 2654216 | tf_op jit(solution)/shard_map/ppermute | solution.py:367

commit v9 on v8

--- a/solution.py
+++ b/solution.py
@@ -95,12 +95,12 @@
         out_ref[unit * UNIT + layer, :, tile * LANES : (tile + 1) * LANES] = values.astype(jnp.bfloat16)
 
 
-def pick_theirs(place, by_layer, gradient, momentum, params, forward, inverse):
-    out_shapes = [HALF_LAYERS, HALF_LAYERS, HALF_MOMENTUM, HALF_LAYERS, TABLE, TABLE, SIDE_BANDS]
-
-    def kernel(place_ref, raw_ref, gradient_ref, momentum_ref, params_ref, forward_ref, inverse_ref, *refs):
-        picked, own_gradient, own_momentum, own_params, table, back_table, bands_ref = refs[:7]
-        gradients, momenta, raw, sems = refs[7:]
+def pick_theirs(place, by_layer, gradient, momentum, forward):
+    out_shapes = [HALF_LAYERS, HALF_LAYERS, HALF_MOMENTUM, TABLE, SIDE_BANDS]
+
+    def kernel(place_ref, raw_ref, gradient_ref, momentum_ref, forward_ref, *refs):
+        picked, own_gradient, own_momentum, table, bands_ref = refs[:5]
+        gradients, momenta, raw, sems = refs[5:]
         core = place_ref[3]
         own = pl.ds(pl.multiple_of(core * HALF, LANES), HALF)
         theirs = pl.ds(pl.multiple_of((1 - core) * HALF, LANES), HALF)
@@ -111,8 +111,6 @@
             pairs.append((momentum_ref.at[0, layers, :, theirs], momenta.at[layers]))
         pairs.append((gradient_ref.at[0, :, :, own], own_gradient))
         pairs.append((momentum_ref.at[0, :, :, own], own_momentum))
-        pairs.append((params_ref.at[:, :, own], own_params))
-        pairs.append((inverse_ref, back_table))
         pairs.insert(0, (raw_ref, raw))
         copies = [pltpu.make_async_copy(src, dst, sems.at[i]) for i, (src, dst) in enumerate(pairs)]
         for copy in copies:
@@ -138,34 +136,45 @@
     return pl.pallas_call(
         kernel,
         out_shape=out_shapes,
-        in_specs=[SMEM] + [HBM] * 6,
+        in_specs=[SMEM] + [HBM] * 4,
         out_specs=[VMEM] * len(out_shapes),
         scratch_shapes=[
             pltpu.VMEM((LAYERS, ROWS_HERE, HALF), jnp.bfloat16),
             pltpu.VMEM((LAYERS, ROWS_HERE, HALF), jnp.float32),
             pltpu.VMEM((LAYERS, ROWS_HERE, 2, BLOCKS), jnp.int32),
-            pltpu.SemaphoreType.DMA((6 + 2 * UNITS,)),
+            pltpu.SemaphoreType.DMA((4 + 2 * UNITS,)),
         ],
         compiler_params=pltpu.CompilerParams(vmem_limit_bytes=VMEM_FIRST),
         cost_estimate=cost(6 * LAYERS * ROWS_HERE * HALF * WIDE, 6000000),
-    )(place, by_layer, gradient, momentum, params, forward, inverse)
-
-
-def pick_own(place, by_layer, gradient, momentum, forward):
-    def kernel(place_ref, bands_ref, gradient_ref, momentum_ref, table_ref, picked):
+    )(place, by_layer, gradient, momentum, forward)
+
+
+def pick_own(place, by_layer, gradient, momentum, forward, params, inverse):
+    def kernel(place_ref, bands_ref, gradient_ref, momentum_ref, table_ref, params_ref, inverse_ref, *refs):
+        picked, own_params, back_table, sems = refs
+        own = pl.ds(pl.multiple_of(place_ref[3] * HALF, LANES), HALF)
+        copies = [
+            pltpu.make_async_copy(params_ref.at[:, :, own], own_params, sems.at[0]),
+            pltpu.make_async_copy(inverse_ref, back_table, sems.at[1]),
+        ]
+        for copy in copies:
+            copy.start()
         for unit in range(UNITS):
             layers = slice(unit * UNIT, unit * UNIT + UNIT)
             spectra = dot3(merged_rows(gradient_ref[layers], momentum_ref[layers]), table_ref)
             store_picked(bands_ref, place_ref[3], unit, spectra, picked)
-
-    return pl.pallas_call(
-        kernel,
-        out_shape=HALF_LAYERS,
-        in_specs=[SMEM] + [VMEM] * 4,
-        out_specs=VMEM,
+        for copy in copies:
+            copy.wait()
+
+    return pl.pallas_call(
+        kernel,
+        out_shape=[HALF_LAYERS, HALF_LAYERS, TABLE],
+        in_specs=[SMEM] + [VMEM] * 4 + [HBM] * 2,
+        out_specs=[VMEM] * 3,
+        scratch_shapes=[pltpu.SemaphoreType.DMA((2,))],
         compiler_params=pltpu.CompilerParams(vmem_limit_bytes=VMEM_LIMIT),
         cost_estimate=cost(6 * LAYERS * ROWS_HERE * HALF * WIDE, 2000000),
-    )(place, by_layer, gradient, momentum, forward)
+    )(place, by_layer, gradient, momentum, forward, params, inverse)
 
 
 def chip_sums(mine, received):
@@ -443,11 +452,13 @@
         pltpu.with_memory_space_constraint(x, pltpu.HBM)
         for x in (gradient, momentum, params, forward, inverse, by_layer)
     )
-    theirs, own_gradient, own_momentum, own_params, forward_here, inverse_here, by_layer = pick_theirs(
-        place, by_layer, gradient, momentum, params, forward, inverse
+    theirs, own_gradient, own_momentum, forward_here, by_layer = pick_theirs(
+        place, by_layer, gradient, momentum, forward
     )
     received = swap(theirs)
-    mine = pick_own(place, by_layer, own_gradient, own_momentum, forward_here)
+    mine, own_params, inverse_here = pick_own(
+        place, by_layer, own_gradient, own_momentum, forward_here, params, inverse
+    )
     chips = chip_sums(mine, received)
     two_chips = [pair_sum(chip, exchange_z(chip, 0)) for chip in chips]
     everyone = [exchange_z(block, 1) for block in two_chips]

time: 84 us -> 84.4 us (level)
  transfers between devices with their start and end apart: 29 -> 29, of which waited for: 16 -> 15; matrix products, arithmetic and copies ran while one was open for 0% -> 0% of each run, Pallas kernels for 23% -> 24%
where the time goes in v9:
time: 84.4 us; the launch traced here: 84.2 us
  starting transfers between devices  29.5 us (35%)
  waiting for transfers between devices  27.5 us (33%)
  Pallas kernels  26.1 us (31%)
  between operations  1.01 us (1%)
    ppermute x29, starting transfers between devices, move(): return lax.ppermute(x, ('rep', 'fsdp'), pairs)  29.5 us
    ppermute x29, waiting for transfers between devices, move(): return lax.ppermute(x, ('rep', 'fsdp'), pairs)  27.5 us
    pallas_call x4, Pallas kernels, write_blocks(): pl.pallas_call(kernel, out_shape=[jax.ShapeDtypeStruct((LAYERS, 16, ROWS_...  11.9 us
    pallas_call x2, Pallas kernels, keep_rest(): pl.pallas_call(kernel, out_shape=[jax.ShapeDtypeStruct(momentum.shape, jn...  7.35 us
    pallas_call x1, Pallas kernels, pick_theirs(): pl.pallas_call(kernel, out_shape=out_shapes, in_specs=[SMEM] + [HBM] * 4,...  2.85 us
    pallas_call x1, Pallas kernels, pick_own(): pl.pallas_call(kernel, out_shape=[HALF_LAYERS, HALF_LAYERS, TABLE], in_sp...  2.16 us
  transfers between devices with their start and end apart: 29, of which 15 were waited for; matrix products, arithmetic and copies ran while one was open for 0% of the time, Pallas kernels for 24%

profile of v9, /device:TPU:1, one launch (start us, length us, event | category | flops | bytes accessed | tf_op | source)
XLA Modules:
  0.0 84.2 jit_solution(17648551754313445110)
XLA Ops:
  0.7 2.8 %shard_map.95 = (bf16[4,8,6912]{2,1,0:T(8,128)(2,1)S(1)}, bf16[4,8,6912]{2,1,0:T(8,128)(2,1)S(1)}, f32[4,8,6912]{2,1,0:T(8,128)S(1)}, bf16[2,256,256]{2,1,0:T(8,128)(2,1)S(1)}, s32[4,2,8,128]{3,2,1,0:T(8,128)S(1)}) custom-call(s32[4]{0:T(128)S(1)} %pad_add_fusion.place_ref, s32[4,8,2,216]{3,2,1,0:T(2,128)} %bitcast.9, bf16[1,4,8,13824]{3,2,1,0:T(8,128)(2,1)} %gradient_ref.5, ...), custom_call_target="tpu_custom_call" | custom-call | flops 339738624 | bytes 6000000 | tf_op jit(solution)/shard_map/pallas_call | solution.py:136
  3.6 1.5 %collective-permute-start = (bf16[4,8,6912]{2,1,0:T(8,128)(2,1)S(1)}, bf16[4,8,6912]{2,1,0:T(8,128)(2,1)S(1)}, u32[]{:S(2)}, u32[]{:S(2)}) collective-permute-start(bf16[4,8,6912]{2,1,0:T(8,128)(2,1)S(1)} %get-tuple-element.28), channel_id=1, source_target_pairs={{0,16},{1,17},{2,18},{3,19},{4,20},{5,21},{6,22},{7,23},{8,24},{9,... | collective-permute-start | bytes 1327112 | tf_op jit(solution)/shard_map/ppermute | solution.py:376
  5.1 2.2 %shard_map.96 = (bf16[4,8,6912]{2,1,0:T(8,128)(2,1)S(1)}, bf16[4,8,6912]{2,1,0:T(8,128)(2,1)S(1)}, bf16[2,256,256]{2,1,0:T(8,128)(2,1)S(1)}) custom-call(s32[4]{0:T(128)S(1)} %pad_add_fusion.place_ref, s32[4,2,8,128]{3,2,1,0:T(8,128)S(1)} %get-tuple-element.22.bands_ref, bf16[4,8,6912]{2,1,0:T(8,128)(2,1)S(1)} %get-tuple-element.24.gradient_ref, ...), custom_call_target="tpu_custom_call" | custom-call | flops 339738624 | bytes 2000000 | tf_op jit(solution)/shard_map/pallas_call | solution.py:169
  7.4 3.9 %collective-permute-start.1 = (bf16[2,8,6912]{2,1,0:T(8,128)(2,1)S(1)}, bf16[2,8,6912]{2,1,0:T(8,128)(2,1)S(1)}, u32[]{:S(2)}, u32[]{:S(2)}) collective-permute-start(bf16[2,8,6912]{2,1,0:T(8,128)(2,1)S(1)} %get-tuple-element.29.mine_ref), channel_id=1, source_target_pairs={{0,32},{1,33},{2,34},{3,35},{4,36},{5,37},{6,38},{7,39},{8,40},{9,... | collective-permute-start | bytes 663560 | tf_op jit(solution)/shard_map/ppermute | solution.py:376
  11.4 3.2 %collective-permute-done.1.received_ref = bf16[2,8,6912]{2,1,0:T(8,128)(2,1)S(1)} collective-permute-done((bf16[2,8,6912]{2,1,0:T(8,128)(2,1)S(1)}, bf16[2,8,6912]{2,1,0:T(8,128)(2,1)S(1)}, u32[]{:S(2)}, u32[]{:S(2)}) %collective-permute-start.1) | collective-permute-done | bytes 221216 | tf_op jit(solution)/shard_map/ppermute | solution.py:376
  14.8 2.5 %collective-permute-done.3.received_ref = bf16[2,8,6912]{2,1,0:T(8,128)(2,1)S(1)} collective-permute-done((bf16[2,8,6912]{2,1,0:T(8,128)(2,1)S(1)}, bf16[2,8,6912]{2,1,0:T(8,128)(2,1)S(1)}, u32[]{:S(2)}, u32[]{:S(2)}) %collective-permute-start.3) | collective-permute-done | bytes 221216 | tf_op jit(solution)/shard_map/ppermute | solution.py:376
  17.4 2.4 %collective-permute-done.2.received_ref = bf16[2,8,6912]{2,1,0:T(8,128)(2,1)S(1)} collective-permute-done((bf16[2,8,6912]{2,1,0:T(8,128)(2,1)S(1)}, bf16[2,8,6912]{2,1,0:T(8,128)(2,1)S(1)}, u32[]{:S(2)}, u32[]{:S(2)}) %collective-permute-start.2) | collective-permute-done | bytes 221216 | tf_op jit(solution)/shard_map/ppermute | solution.py:376
  19.8 0.3 shard_map.100.refs_0_
  20.2 3.0 %collective-permute-start.6 = (bf16[2,8,6912]{2,1,0:T(8,128)(2,1)S(1)}, bf16[2,8,6912]{2,1,0:T(8,128)(2,1)S(1)}, u32[]{:S(2)}, u32[]{:S(2)}) collective-permute-start(bf16[2,8,6912]{2,1,0:T(8,128)(2,1)S(1)} %shard_map.100.refs_0_), channel_id=1, source_target_pairs={{0,2},{1,3},{2,0},{3,1},{4,6},{5,7},{6,4},{7,5},{8,10},{9,11},{10,... | collective-permute-start | bytes 663560 | tf_op jit(solution)/shard_map/ppermute | solution.py:376
  23.2 0.8 collective-permute-start.5
  23.9 0.7 collective-permute-start.4
  24.6 0.3 shard_map.101.refs_4_
  25.0 0.8 collective-permute-start.10
  25.8 2.0 %collective-permute-start.9 = (bf16[2,8,6912]{2,1,0:T(8,128)(2,1)S(1)}, bf16[2,8,6912]{2,1,0:T(8,128)(2,1)S(1)}, u32[]{:S(2)}, u32[]{:S(2)}) collective-permute-start(bf16[2,8,6912]{2,1,0:T(8,128)(2,1)S(1)} %shard_map.101.refs_4_), channel_id=1, source_target_pairs={{0,3},{1,0},{2,1},{3,2},{4,7},{5,4},{6,5},{7,6},{8,11},{9,8},{10,9... | collective-permute-start | bytes 663560 | tf_op jit(solution)/shard_map/ppermute | solution.py:376
  27.9 0.3 collective-permute-start.8
  28.2 1.4 %collective-permute-done.5.refs_2_ = bf16[2,8,6912]{2,1,0:T(8,128)(2,1)S(1)} collective-permute-done((bf16[2,8,6912]{2,1,0:T(8,128)(2,1)S(1)}, bf16[2,8,6912]{2,1,0:T(8,128)(2,1)S(1)}, u32[]{:S(2)}, u32[]{:S(2)}) %collective-permute-start.5) | collective-permute-done | bytes 221216 | tf_op jit(solution)/shard_map/ppermute | solution.py:376
  29.6 3.0 %collective-permute-done.4.refs_1_ = bf16[2,8,6912]{2,1,0:T(8,128)(2,1)S(1)} collective-permute-done((bf16[2,8,6912]{2,1,0:T(8,128)(2,1)S(1)}, bf16[2,8,6912]{2,1,0:T(8,128)(2,1)S(1)}, u32[]{:S(2)}, u32[]{:S(2)}) %collective-permute-start.4) | collective-permute-done | bytes 221216 | tf_op jit(solution)/shard_map/ppermute | solution.py:376
  32.6 1.8 %collective-permute-done.9.refs_6_ = bf16[2,8,6912]{2,1,0:T(8,128)(2,1)S(1)} collective-permute-done((bf16[2,8,6912]{2,1,0:T(8,128)(2,1)S(1)}, bf16[2,8,6912]{2,1,0:T(8,128)(2,1)S(1)}, u32[]{:S(2)}, u32[]{:S(2)}) %collective-permute-start.9) | collective-permute-done | bytes 221216 | tf_op jit(solution)/shard_map/ppermute | solution.py:376
  34.4 0.6 collective-permute-done.8.refs_5_
  35.0 0.7 shard_map.102.refs_0_
  35.6 1.0 %collective-permute-start.21 = (bf16[4,4,8,6912]{3,2,1,0:T(8,128)(2,1)S(1)}, bf16[4,4,8,6912]{3,2,1,0:T(8,128)(2,1)S(1)}, u32[]{:S(2)}, u32[]{:S(2)}) collective-permute-start(bf16[4,4,8,6912]{3,2,1,0:T(8,128)(2,1)S(1)} %shard_map.102.refs_0_), channel_id=1, source_target_pairs={{0,4},{1,5},{2,6},{3,7},{4,8},{5,9},{6,10},{7,11},{8,12},{9,13},{1... | collective-permute-start | bytes 5308424 | tf_op jit(solution)/shard_map/ppermute | solution.py:376
  36.6 1.8 %collective-permute-start.11 = (bf16[4,4,8,6912]{3,2,1,0:T(8,128)(2,1)S(1)}, bf16[4,4,8,6912]{3,2,1,0:T(8,128)(2,1)S(1)}, u32[]{:S(2)}, u32[]{:S(2)}) collective-permute-start(bf16[4,4,8,6912]{3,2,1,0:T(8,128)(2,1)S(1)} %shard_map.102.refs_0_), channel_id=1, source_target_pairs={{0,12},{1,13},{2,14},{3,15},{4,0},{5,1},{6,2},{7,3},{8,4},{9,5},{1... | collective-permute-start | bytes 5308424 | tf_op jit(solution)/shard_map/ppermute | solution.py:376
  38.4 3.6 %collective-permute-start.12 = (bf16[2,8,6912]{2,1,0:T(8,128)(2,1)S(1)}, bf16[2,8,6912]{2,1,0:T(8,128)(2,1)S(1)}, u32[]{:S(2)}, u32[]{:S(2)}) collective-permute-start(bf16[2,8,6912]{2,1,0:T(8,128)(2,1)S(1)} %shard_map.100.refs_0_), channel_id=1, source_target_pairs={{0,16},{1,17},{2,18},{3,19},{4,20},{5,21},{6,22},{7,23},{8,24},{9,... | collective-permute-start | bytes 663560 | tf_op jit(solution)/shard_map/ppermute | solution.py:376
  42.0 0.5 collective-permute-start.15
  42.5 0.6 collective-permute-done.12.refs_1_
  43.1 0.4 collective-permute-start.14
  43.5 0.3 collective-permute-start.13
  43.8 0.3 collective-permute-start.19
  44.1 0.5 collective-permute-done.14.refs_3_
  44.6 0.4 collective-permute-start.18
  45.0 0.3 collective-permute-start.17
  45.3 3.7 %shard_map.103 = (f32[1,4,8,13824]{3,2,1,0:T(8,128)}, f32[8,128]{1,0:T(8,128)S(1)}) custom-call(s32[4,2,8,128]{3,2,1,0:T(8,128)S(1)} %get-tuple-element.22.bands_ref, bf16[1,4,8,13824]{3,2,1,0:T(8,128)(2,1)} %gradient_ref.5, f32[1,4,8,13824]{3,2,1,0:T(8,128)} %momentum_ref.5, bf16[2,256,256]{2,1,0:T(8,128)(2,1)S(1)} %get-tuple-element.23.table_ref.forward_ref, ...), custom_call_target="tpu_custom_call" | custom-call | flops 679477248 | bytes 3000000 | tf_op jit(solution)/shard_map/pallas_call | solution.py:255
  49.0 3.7 %shard_map.104 = (f32[1,4,8,13824]{3,2,1,0:T(8,128)}, f32[8,128]{1,0:T(8,128)S(1)}) custom-call(s32[4,2,8,128]{3,2,1,0:T(8,128)S(1)} %get-tuple-element.22.bands_ref, bf16[1,4,8,13824]{3,2,1,0:T(8,128)(2,1)} %gradient_ref.5, f32[1,4,8,13824]{3,2,1,0:T(8,128)} %momentum_ref.5, ...), custom_call_target="tpu_custom_call", output_to_operand_aliasing={{0}: (6, {})} | custom-call | flops 679477248 | bytes 3000000 | tf_op jit(solution)/shard_map/pallas_call | solution.py:255
  52.7 3.0 %shard_map.105 = (bf16[4,16,8,13824]{3,2,1,0:T(8,128)(2,1)}, f32[8,128]{1,0:T(8,128)S(1)}) custom-call(s32[4]{0:T(128)S(1)} %pad_add_fusion.place_ref, bf16[4,4,8,6912]{3,2,1,0:T(8,128)(2,1)S(1)} %shard_map.102.refs_0_, bf16[2,8,6912]{2,1,0:T(8,128)(2,1)S(1)} %collective-permute-done.12.refs_1_, bf16[2,8,6912]{2,1,0:T(8,128)(2,1)S(1)} %collective-permute-done.13.refs_2_, ...), custom_call_target="tpu_custom_call" | custom-call | bytes 7077888 | tf_op jit(solution)/shard_map/pallas_call | solution.py:358
  55.7 2.8 %collective-permute-done.21.x_ref = bf16[4,4,8,6912]{3,2,1,0:T(8,128)(2,1)S(1)} collective-permute-done((bf16[4,4,8,6912]{3,2,1,0:T(8,128)(2,1)S(1)}, bf16[4,4,8,6912]{3,2,1,0:T(8,128)(2,1)S(1)}, u32[]{:S(2)}, u32[]{:S(2)}) %collective-permute-start.21) | collective-permute-done | bytes 1769504 | tf_op jit(solution)/shard_map/ppermute | solution.py:376
  58.7 4.0 %collective-permute-start.22 = (bf16[2,4,8,6912]{3,2,1,0:T(8,128)(2,1)S(1)}, bf16[2,4,8,6912]{3,2,1,0:T(8,128)(2,1)S(1)}, u32[]{:S(2)}, u32[]{:S(2)}) collective-permute-start(bf16[2,4,8,6912]{3,2,1,0:T(8,128)(2,1)S(1)} %shard_map.109), channel_id=1, source_target_pairs={{0,16},{1,17},{2,18},{3,19},{4,20},{5,21},{6,22},{7,23},{8,24},{9,... | collective-permute-start | bytes 2654216 | tf_op jit(solution)/shard_map/ppermute | solution.py:376
  62.9 0.2 collective-permute-start.25
  63.1 0.4 collective-permute-start.24
  63.6 1.1 %collective-permute-done.22.refs_2_ = bf16[2,4,8,6912]{3,2,1,0:T(8,128)(2,1)S(1)} collective-permute-done((bf16[2,4,8,6912]{3,2,1,0:T(8,128)(2,1)S(1)}, bf16[2,4,8,6912]{3,2,1,0:T(8,128)(2,1)S(1)}, u32[]{:S(2)}, u32[]{:S(2)}) %collective-permute-start.22) | collective-permute-done | bytes 884768 | tf_op jit(solution)/shard_map/ppermute | solution.py:376
  64.7 1.6 %collective-permute-start.20 = (bf16[2,4,8,6912]{3,2,1,0:T(8,128)(2,1)S(1)}, bf16[2,4,8,6912]{3,2,1,0:T(8,128)(2,1)S(1)}, u32[]{:S(2)}, u32[]{:S(2)}) collective-permute-start(bf16[2,4,8,6912]{3,2,1,0:T(8,128)(2,1)S(1)} %shard_map.107), channel_id=1, source_target_pairs={{0,12},{1,13},{2,14},{3,15},{4,0},{5,1},{6,2},{7,3},{8,4},{9,5},{1... | collective-permute-start | bytes 2654216 | tf_op jit(solution)/shard_map/ppermute | solution.py:376
  66.3 1.0 %collective-permute-done.24.refs_4_ = bf16[2,4,8,6912]{3,2,1,0:T(8,128)(2,1)S(1)} collective-permute-done((bf16[2,4,8,6912]{3,2,1,0:T(8,128)(2,1)S(1)}, bf16[2,4,8,6912]{3,2,1,0:T(8,128)(2,1)S(1)}, u32[]{:S(2)}, u32[]{:S(2)}) %collective-permute-start.24) | collective-permute-done | bytes 884768 | tf_op jit(solution)/shard_map/ppermute | solution.py:376
  67.2 1.3 %collective-permute-done.23.refs_3_ = bf16[2,4,8,6912]{3,2,1,0:T(8,128)(2,1)S(1)} collective-permute-done((bf16[2,4,8,6912]{3,2,1,0:T(8,128)(2,1)S(1)}, bf16[2,4,8,6912]{3,2,1,0:T(8,128)(2,1)S(1)}, u32[]{:S(2)}, u32[]{:S(2)}) %collective-permute-start.23) | collective-permute-done | bytes 884768 | tf_op jit(solution)/shard_map/ppermute | solution.py:376
  68.5 4.0 %shard_map.112 = (bf16[4,16,8,13824]{3,2,1,0:T(8,128)(2,1)}, f32[8,128]{1,0:T(8,128)S(1)}) custom-call(s32[4]{0:T(128)S(1)} %pad_add_fusion.place_ref, bf16[4,4,8,6912]{3,2,1,0:T(8,128)(2,1)S(1)} %shard_map.108.x_ref.refs_0_, bf16[4,4,8,6912]{3,2,1,0:T(8,128)(2,1)S(1)} %shard_map.106.x_ref.refs_1_, ...), custom_call_target="tpu_custom_call", output_to_operand_aliasing={{0}: (7, {})} | custom-call | bytes 14155776 | tf_op jit(solution)/shard_map/pallas_call | solution.py:358
  72.5 4.5 %collective-permute-done.27.x_ref = bf16[2,4,8,6912]{3,2,1,0:T(8,128)(2,1)S(1)} collective-permute-done((bf16[2,4,8,6912]{3,2,1,0:T(8,128)(2,1)S(1)}, bf16[2,4,8,6912]{3,2,1,0:T(8,128)(2,1)S(1)}, u32[]{:S(2)}, u32[]{:S(2)}) %collective-permute-start.27) | collective-permute-done | bytes 884768 | tf_op jit(solution)/shard_map/ppermute | solution.py:376
  77.0 1.2 %collective-permute-start.28 = (bf16[2,4,8,6912]{3,2,1,0:T(8,128)(2,1)S(1)}, bf16[2,4,8,6912]{3,2,1,0:T(8,128)(2,1)S(1)}, u32[]{:S(2)}, u32[]{:S(2)}) collective-permute-start(bf16[2,4,8,6912]{3,2,1,0:T(8,128)(2,1)S(1)} %shard_map.114.refs_1_), channel_id=1, source_target_pairs={{0,16},{1,17},{2,18},{3,19},{4,20},{5,21},{6,22},{7,23},{8,24},{9,... | collective-permute-start | bytes 2654216 | tf_op jit(solution)/shard_map/ppermute | solution.py:376
  78.3 2.5 %shard_map.115 = (bf16[4,16,8,13824]{3,2,1,0:T(8,128)(2,1)}, f32[8,128]{1,0:T(8,128)}) custom-call(s32[4]{0:T(128)S(1)} %pad_add_fusion.place_ref, bf16[2,4,8,6912]{3,2,1,0:T(8,128)(2,1)S(1)} %shard_map.113.refs_0_, bf16[2,4,8,6912]{3,2,1,0:T(8,128)(2,1)S(1)} %shard_map.114.refs_1_, ...), custom_call_target="tpu_custom_call", output_to_operand_aliasing={{0}: (3, {})} | custom-call | bytes 3538944 | tf_op jit(solution)/shard_map/pallas_call | solution.py:358
  80.8 0.7 collective-permute-done.26.refs_0_
  81.6 2.5 %shard_map.116 = (bf16[4,16,8,13824]{3,2,1,0:T(8,128)(2,1)}, f32[8,128]{1,0:T(8,128)}) custom-call(s32[4]{0:T(128)S(1)} %pad_add_fusion.place_ref, bf16[2,4,8,6912]{3,2,1,0:T(8,128)(2,1)S(1)} %collective-permute-done.26.refs_0_, bf16[2,4,8,6912]{3,2,1,0:T(8,128)(2,1)S(1)} %collective-permute-done.28.refs_1_, ...), custom_call_target="tpu_custom_call", output_to_operand_aliasing={{0}: (3, {})} | custom-call | bytes 3538944 | tf_op jit(solution)/shard_map/pallas_call | solution.py:358
  (33 shorter events, 1.1 us)
Async XLA Ops:
  3.6 3.7 %collective-permute-start = (bf16[4,8,6912]{2,1,0:T(8,128)(2,1)S(1)}, bf16[4,8,6912]{2,1,0:T(8,128)(2,1)S(1)}, u32[]{:S(2)}, u32[]{:S(2)}) collective-permute-start(bf16[4,8,6912]{2,1,0:T(8,128)(2,1)S(1)} %get-tuple-element.28), channel_id=1, source_target_pairs={{0,16},{1,17},{2,18},{3,19},{4,20},{5,21},{6,22},{7,23},{8,24},{9,... | collective-permute-start | bytes 1327112 | tf_op jit(solution)/shard_map/ppermute | solution.py:376
  7.4 7.2 %collective-permute-start.1 = (bf16[2,8,6912]{2,1,0:T(8,128)(2,1)S(1)}, bf16[2,8,6912]{2,1,0:T(8,128)(2,1)S(1)}, u32[]{:S(2)}, u32[]{:S(2)}) collective-permute-start(bf16[2,8,6912]{2,1,0:T(8,128)(2,1)S(1)} %get-tuple-element.29.mine_ref), channel_id=1, source_target_pairs={{0,32},{1,33},{2,34},{3,35},{4,36},{5,37},{6,38},{7,39},{8,40},{9,... | collective-permute-start | bytes 663560 | tf_op jit(solution)/shard_map/ppermute | solution.py:376
  11.3 6.0 %collective-permute-start.3 = (bf16[2,8,6912]{2,1,0:T(8,128)(2,1)S(1)}, bf16[2,8,6912]{2,1,0:T(8,128)(2,1)S(1)}, u32[]{:S(2)}, u32[]{:S(2)}) collective-permute-start(bf16[2,8,6912]{2,1,0:T(8,128)(2,1)S(1)} %get-tuple-element.31.mine_ref), channel_id=1, source_target_pairs={{0,32},{1,33},{2,34},{3,35},{4,36},{5,37},{6,38},{7,39},{8,40},{9,... | collective-permute-start | bytes 663560 | tf_op jit(solution)/shard_map/ppermute | solution.py:376
  14.7 5.2 %collective-permute-start.2 = (bf16[2,8,6912]{2,1,0:T(8,128)(2,1)S(1)}, bf16[2,8,6912]{2,1,0:T(8,128)(2,1)S(1)}, u32[]{:S(2)}, u32[]{:S(2)}) collective-permute-start(bf16[2,8,6912]{2,1,0:T(8,128)(2,1)S(1)} %shard_map.98.mine_ref), channel_id=1, source_target_pairs={{0,96},{1,97},{2,98},{3,99},{4,100},{5,101},{6,102},{7,103},{8,104... | collective-permute-start | bytes 663560 | tf_op jit(solution)/shard_map/ppermute | solution.py:376
  17.3 7.3 %collective-permute-start.7 = (bf16[2,8,6912]{2,1,0:T(8,128)(2,1)S(1)}, bf16[2,8,6912]{2,1,0:T(8,128)(2,1)S(1)}, u32[]{:S(2)}, u32[]{:S(2)}) collective-permute-start(bf16[2,8,6912]{2,1,0:T(8,128)(2,1)S(1)} %shard_map.99.refs_0_.mine_ref), channel_id=1, source_target_pairs={{0,96},{1,97},{2,98},{3,99},{4,100},{5,101},{6,102},{7,103},{8,104... | collective-permute-start | bytes 663560 | tf_op jit(solution)/shard_map/ppermute | solution.py:376
  20.2 7.7 %collective-permute-start.6 = (bf16[2,8,6912]{2,1,0:T(8,128)(2,1)S(1)}, bf16[2,8,6912]{2,1,0:T(8,128)(2,1)S(1)}, u32[]{:S(2)}, u32[]{:S(2)}) collective-permute-start(bf16[2,8,6912]{2,1,0:T(8,128)(2,1)S(1)} %shard_map.100.refs_0_), channel_id=1, source_target_pairs={{0,2},{1,3},{2,0},{3,1},{4,6},{5,7},{6,4},{7,5},{8,10},{9,11},{10,... | collective-permute-start | bytes 663560 | tf_op jit(solution)/shard_map/ppermute | solution.py:376
  23.2 6.4 %collective-permute-start.5 = (bf16[2,8,6912]{2,1,0:T(8,128)(2,1)S(1)}, bf16[2,8,6912]{2,1,0:T(8,128)(2,1)S(1)}, u32[]{:S(2)}, u32[]{:S(2)}) collective-permute-start(bf16[2,8,6912]{2,1,0:T(8,128)(2,1)S(1)} %shard_map.100.refs_0_), channel_id=1, source_target_pairs={{0,3},{1,0},{2,1},{3,2},{4,7},{5,4},{6,5},{7,6},{8,11},{9,8},{10,9... | collective-permute-start | bytes 663560 | tf_op jit(solution)/shard_map/ppermute | solution.py:376
  23.9 8.7 %collective-permute-start.4 = (bf16[2,8,6912]{2,1,0:T(8,128)(2,1)S(1)}, bf16[2,8,6912]{2,1,0:T(8,128)(2,1)S(1)}, u32[]{:S(2)}, u32[]{:S(2)}) collective-permute-start(bf16[2,8,6912]{2,1,0:T(8,128)(2,1)S(1)} %shard_map.100.refs_0_), channel_id=1, source_target_pairs={{0,1},{1,2},{2,3},{3,0},{4,5},{5,6},{6,7},{7,4},{8,9},{9,10},{10,1... | collective-permute-start | bytes 663560 | tf_op jit(solution)/shard_map/ppermute | solution.py:376
  25.0 7.6 %collective-permute-start.10 = (bf16[2,8,6912]{2,1,0:T(8,128)(2,1)S(1)}, bf16[2,8,6912]{2,1,0:T(8,128)(2,1)S(1)}, u32[]{:S(2)}, u32[]{:S(2)}) collective-permute-start(bf16[2,8,6912]{2,1,0:T(8,128)(2,1)S(1)} %shard_map.101.refs_4_), channel_id=1, source_target_pairs={{0,2},{1,3},{2,0},{3,1},{4,6},{5,7},{6,4},{7,5},{8,10},{9,11},{10,... | collective-permute-start | bytes 663560 | tf_op jit(solution)/shard_map/ppermute | solution.py:376
  25.8 8.5 %collective-permute-start.9 = (bf16[2,8,6912]{2,1,0:T(8,128)(2,1)S(1)}, bf16[2,8,6912]{2,1,0:T(8,128)(2,1)S(1)}, u32[]{:S(2)}, u32[]{:S(2)}) collective-permute-start(bf16[2,8,6912]{2,1,0:T(8,128)(2,1)S(1)} %shard_map.101.refs_4_), channel_id=1, source_target_pairs={{0,3},{1,0},{2,1},{3,2},{4,7},{5,4},{6,5},{7,6},{8,11},{9,8},{10,9... | collective-permute-start | bytes 663560 | tf_op jit(solution)/shard_map/ppermute | solution.py:376
  27.9 7.1 %collective-permute-start.8 = (bf16[2,8,6912]{2,1,0:T(8,128)(2,1)S(1)}, bf16[2,8,6912]{2,1,0:T(8,128)(2,1)S(1)}, u32[]{:S(2)}, u32[]{:S(2)}) collective-permute-start(bf16[2,8,6912]{2,1,0:T(8,128)(2,1)S(1)} %shard_map.101.refs_4_), channel_id=1, source_target_pairs={{0,1},{1,2},{2,3},{3,0},{4,5},{5,6},{6,7},{7,4},{8,9},{9,10},{10,1... | collective-permute-start | bytes 663560 | tf_op jit(solution)/shard_map/ppermute | solution.py:376
  35.6 22.9 %collective-permute-start.21 = (bf16[4,4,8,6912]{3,2,1,0:T(8,128)(2,1)S(1)}, bf16[4,4,8,6912]{3,2,1,0:T(8,128)(2,1)S(1)}, u32[]{:S(2)}, u32[]{:S(2)}) collective-permute-start(bf16[4,4,8,6912]{3,2,1,0:T(8,128)(2,1)S(1)} %shard_map.102.refs_0_), channel_id=1, source_target_pairs={{0,4},{1,5},{2,6},{3,7},{4,8},{5,9},{6,10},{7,11},{8,12},{9,13},{1... | collective-permute-start | bytes 5308424 | tf_op jit(solution)/shard_map/ppermute | solution.py:376
  36.6 26.1 %collective-permute-start.11 = (bf16[4,4,8,6912]{3,2,1,0:T(8,128)(2,1)S(1)}, bf16[4,4,8,6912]{3,2,1,0:T(8,128)(2,1)S(1)}, u32[]{:S(2)}, u32[]{:S(2)}) collective-permute-start(bf16[4,4,8,6912]{3,2,1,0:T(8,128)(2,1)S(1)} %shard_map.102.refs_0_), channel_id=1, source_target_pairs={{0,12},{1,13},{2,14},{3,15},{4,0},{5,1},{6,2},{7,3},{8,4},{9,5},{1... | collective-permute-start | bytes 5308424 | tf_op jit(solution)/shard_map/ppermute | solution.py:376
  38.4 4.7 %collective-permute-start.12 = (bf16[2,8,6912]{2,1,0:T(8,128)(2,1)S(1)}, bf16[2,8,6912]{2,1,0:T(8,128)(2,1)S(1)}, u32[]{:S(2)}, u32[]{:S(2)}) collective-permute-start(bf16[2,8,6912]{2,1,0:T(8,128)(2,1)S(1)} %shard_map.100.refs_0_), channel_id=1, source_target_pairs={{0,16},{1,17},{2,18},{3,19},{4,20},{5,21},{6,22},{7,23},{8,24},{9,... | collective-permute-start | bytes 663560 | tf_op jit(solution)/shard_map/ppermute | solution.py:376
  42.0 1.5 %collective-permute-start.16 = (bf16[2,8,6912]{2,1,0:T(8,128)(2,1)S(1)}, bf16[2,8,6912]{2,1,0:T(8,128)(2,1)S(1)}, u32[]{:S(2)}, u32[]{:S(2)}) collective-permute-start(bf16[2,8,6912]{2,1,0:T(8,128)(2,1)S(1)} %shard_map.101.refs_4_), channel_id=1, source_target_pairs={{0,16},{1,17},{2,18},{3,19},{4,20},{5,21},{6,22},{7,23},{8,24},{9,... | collective-permute-start | bytes 663560 | tf_op jit(solution)/shard_map/ppermute | solution.py:376
  42.0 1.8 %collective-permute-start.15 = (bf16[2,8,6912]{2,1,0:T(8,128)(2,1)S(1)}, bf16[2,8,6912]{2,1,0:T(8,128)(2,1)S(1)}, u32[]{:S(2)}, u32[]{:S(2)}) collective-permute-start(bf16[2,8,6912]{2,1,0:T(8,128)(2,1)S(1)} %collective-permute-done.6.refs_3_), channel_id=1, source_target_pairs={{0,16},{1,17},{2,18},{3,19},{4,20},{5,21},{6,22},{7,23},{8,24},{9,... | collective-permute-start | bytes 663560 | tf_op jit(solution)/shard_map/ppermute | solution.py:376
  43.1 1.5 %collective-permute-start.14 = (bf16[2,8,6912]{2,1,0:T(8,128)(2,1)S(1)}, bf16[2,8,6912]{2,1,0:T(8,128)(2,1)S(1)}, u32[]{:S(2)}, u32[]{:S(2)}) collective-permute-start(bf16[2,8,6912]{2,1,0:T(8,128)(2,1)S(1)} %collective-permute-done.5.refs_2_), channel_id=1, source_target_pairs={{0,16},{1,17},{2,18},{3,19},{4,20},{5,21},{6,22},{7,23},{8,24},{9,... | collective-permute-start | bytes 663560 | tf_op jit(solution)/shard_map/ppermute | solution.py:376
  43.5 1.5 %collective-permute-start.13 = (bf16[2,8,6912]{2,1,0:T(8,128)(2,1)S(1)}, bf16[2,8,6912]{2,1,0:T(8,128)(2,1)S(1)}, u32[]{:S(2)}, u32[]{:S(2)}) collective-permute-start(bf16[2,8,6912]{2,1,0:T(8,128)(2,1)S(1)} %collective-permute-done.4.refs_1_), channel_id=1, source_target_pairs={{0,16},{1,17},{2,18},{3,19},{4,20},{5,21},{6,22},{7,23},{8,24},{9,... | collective-permute-start | bytes 663560 | tf_op jit(solution)/shard_map/ppermute | solution.py:376
  43.8 8.8 %collective-permute-start.19 = (bf16[2,8,6912]{2,1,0:T(8,128)(2,1)S(1)}, bf16[2,8,6912]{2,1,0:T(8,128)(2,1)S(1)}, u32[]{:S(2)}, u32[]{:S(2)}) collective-permute-start(bf16[2,8,6912]{2,1,0:T(8,128)(2,1)S(1)} %collective-permute-done.10.refs_7_), channel_id=1, source_target_pairs={{0,16},{1,17},{2,18},{3,19},{4,20},{5,21},{6,22},{7,23},{8,24},{9,... | collective-permute-start | bytes 663560 | tf_op jit(solution)/shard_map/ppermute | solution.py:376
  44.6 8.1 %collective-permute-start.18 = (bf16[2,8,6912]{2,1,0:T(8,128)(2,1)S(1)}, bf16[2,8,6912]{2,1,0:T(8,128)(2,1)S(1)}, u32[]{:S(2)}, u32[]{:S(2)}) collective-permute-start(bf16[2,8,6912]{2,1,0:T(8,128)(2,1)S(1)} %collective-permute-done.9.refs_6_), channel_id=1, source_target_pairs={{0,16},{1,17},{2,18},{3,19},{4,20},{5,21},{6,22},{7,23},{8,24},{9,... | collective-permute-start | bytes 663560 | tf_op jit(solution)/shard_map/ppermute | solution.py:376
  45.0 7.7 %collective-permute-start.17 = (bf16[2,8,6912]{2,1,0:T(8,128)(2,1)S(1)}, bf16[2,8,6912]{2,1,0:T(8,128)(2,1)S(1)}, u32[]{:S(2)}, u32[]{:S(2)}) collective-permute-start(bf16[2,8,6912]{2,1,0:T(8,128)(2,1)S(1)} %collective-permute-done.8.refs_5_), channel_id=1, source_target_pairs={{0,16},{1,17},{2,18},{3,19},{4,20},{5,21},{6,22},{7,23},{8,24},{9,... | collective-permute-start | bytes 663560 | tf_op jit(solution)/shard_map/ppermute | solution.py:376
  58.7 6.1 %collective-permute-start.22 = (bf16[2,4,8,6912]{3,2,1,0:T(8,128)(2,1)S(1)}, bf16[2,4,8,6912]{3,2,1,0:T(8,128)(2,1)S(1)}, u32[]{:S(2)}, u32[]{:S(2)}) collective-permute-start(bf16[2,4,8,6912]{3,2,1,0:T(8,128)(2,1)S(1)} %shard_map.109), channel_id=1, source_target_pairs={{0,16},{1,17},{2,18},{3,19},{4,20},{5,21},{6,22},{7,23},{8,24},{9,... | collective-permute-start | bytes 2654216 | tf_op jit(solution)/shard_map/ppermute | solution.py:376
  62.9 3.4 %collective-permute-start.25 = (bf16[2,4,8,6912]{3,2,1,0:T(8,128)(2,1)S(1)}, bf16[2,4,8,6912]{3,2,1,0:T(8,128)(2,1)S(1)}, u32[]{:S(2)}, u32[]{:S(2)}) collective-permute-start(bf16[2,4,8,6912]{3,2,1,0:T(8,128)(2,1)S(1)} %shard_map.111), channel_id=1, source_target_pairs={{0,16},{1,17},{2,18},{3,19},{4,20},{5,21},{6,22},{7,23},{8,24},{9,... | collective-permute-start | bytes 2654216 | tf_op jit(solution)/shard_map/ppermute | solution.py:376
  63.1 4.1 %collective-permute-start.24 = (bf16[2,4,8,6912]{3,2,1,0:T(8,128)(2,1)S(1)}, bf16[2,4,8,6912]{3,2,1,0:T(8,128)(2,1)S(1)}, u32[]{:S(2)}, u32[]{:S(2)}) collective-permute-start(bf16[2,4,8,6912]{3,2,1,0:T(8,128)(2,1)S(1)} %shard_map.110), channel_id=1, source_target_pairs={{0,16},{1,17},{2,18},{3,19},{4,20},{5,21},{6,22},{7,23},{8,24},{9,... | collective-permute-start | bytes 2654216 | tf_op jit(solution)/shard_map/ppermute | solution.py:376
  63.5 5.0 %collective-permute-start.23 = (bf16[2,4,8,6912]{3,2,1,0:T(8,128)(2,1)S(1)}, bf16[2,4,8,6912]{3,2,1,0:T(8,128)(2,1)S(1)}, u32[]{:S(2)}, u32[]{:S(2)}) collective-permute-start(bf16[2,4,8,6912]{3,2,1,0:T(8,128)(2,1)S(1)} %shard_map.107), channel_id=1, source_target_pairs={{0,16},{1,17},{2,18},{3,19},{4,20},{5,21},{6,22},{7,23},{8,24},{9,... | collective-permute-start | bytes 2654216 | tf_op jit(solution)/shard_map/ppermute | solution.py:376
  63.6 13.4 %collective-permute-start.27 = (bf16[2,4,8,6912]{3,2,1,0:T(8,128)(2,1)S(1)}, bf16[2,4,8,6912]{3,2,1,0:T(8,128)(2,1)S(1)}, u32[]{:S(2)}, u32[]{:S(2)}) collective-permute-start(bf16[2,4,8,6912]{3,2,1,0:T(8,128)(2,1)S(1)} %shard_map.110), channel_id=1, source_target_pairs={{0,4},{1,5},{2,6},{3,7},{4,8},{5,9},{6,10},{7,11},{8,12},{9,13},{1... | collective-permute-start | bytes 2654216 | tf_op jit(solution)/shard_map/ppermute | solution.py:376
  64.7 13.5 %collective-permute-start.20 = (bf16[2,4,8,6912]{3,2,1,0:T(8,128)(2,1)S(1)}, bf16[2,4,8,6912]{3,2,1,0:T(8,128)(2,1)S(1)}, u32[]{:S(2)}, u32[]{:S(2)}) collective-permute-start(bf16[2,4,8,6912]{3,2,1,0:T(8,128)(2,1)S(1)} %shard_map.107), channel_id=1, source_target_pairs={{0,12},{1,13},{2,14},{3,15},{4,0},{5,1},{6,2},{7,3},{8,4},{9,5},{1... | collective-permute-start | bytes 2654216 | tf_op jit(solution)/shard_map/ppermute | solution.py:376
  77.0 3.8 %collective-permute-start.28 = (bf16[2,4,8,6912]{3,2,1,0:T(8,128)(2,1)S(1)}, bf16[2,4,8,6912]{3,2,1,0:T(8,128)(2,1)S(1)}, u32[]{:S(2)}, u32[]{:S(2)}) collective-permute-start(bf16[2,4,8,6912]{3,2,1,0:T(8,128)(2,1)S(1)} %shard_map.114.refs_1_), channel_id=1, source_target_pairs={{0,16},{1,17},{2,18},{3,19},{4,20},{5,21},{6,22},{7,23},{8,24},{9,... | collective-permute-start | bytes 2654216 | tf_op jit(solution)/shard_map/ppermute | solution.py:376
  78.2 3.3 %collective-permute-start.26 = (bf16[2,4,8,6912]{3,2,1,0:T(8,128)(2,1)S(1)}, bf16[2,4,8,6912]{3,2,1,0:T(8,128)(2,1)S(1)}, u32[]{:S(2)}, u32[]{:S(2)}) collective-permute-start(bf16[2,4,8,6912]{3,2,1,0:T(8,128)(2,1)S(1)} %shard_map.113.refs_0_), channel_id=1, source_target_pairs={{0,16},{1,17},{2,18},{3,19},{4,20},{5,21},{6,22},{7,23},{8,24},{9,... | collective-permute-start | bytes 2654216 | tf_op jit(solution)/shard_map/ppermute | solution.py:376
